TPU v7x, 32 devices: a whole 2x2x4 slice. The times are simulated.
32 devices in a mesh: fsdp: 32 (over z, y, x, core).
Axes of the slice: x: 2, y: 2, z: 4, core: 2. Of those that a mesh axis runs over, the one named last changes fastest.
Arguments:
- latents: bfloat16 [64, 256, 16], P('fsdp'), may hold values from -6 to 6
- noise_draw: bfloat16 [64, 256, 16], P('fsdp'), may hold values from -6 to 6
- timesteps: int32 [64], P('fsdp'), may hold values from 0 to 999
- labels: int32 [64], P('fsdp'), may hold values from 0 to 999
- weights_in: float32 [1024, 17408], P('fsdp'), may hold values from -2 to 2, as said below
- weights_down: float32 [4096, 1024], P('fsdp'), may hold values from -0.09375 to 0.09375
- weights_side: float32 [1024, 1288], P('fsdp'), may hold values from -4 to 4, as said below
- biases: float32 [19456], P('fsdp'), may hold values from -1 to 1
- first_in: float32 [1024, 17408], P('fsdp'), may hold values from -24 to 24
- first_down: float32 [4096, 1024], P('fsdp'), may hold values from -24 to 24
- first_side: float32 [1024, 1288], P('fsdp'), may hold values from -24 to 24
- first_bias: float32 [19456], P('fsdp'), may hold values from -24 to 24
- second_in: float32 [1024, 17408], P('fsdp'), may hold values from 14.0625 to 56.25
- second_down: float32 [4096, 1024], P('fsdp'), may hold values from 14.0625 to 56.25
- second_side: float32 [1024, 1288], P('fsdp'), may hold values from 14.0625 to 56.25
- second_bias: float32 [19456], P('fsdp'), may hold values from 14.0625 to 56.25
Outputs:
- loss_sum: float32 [], replicated
- updated_in: float32 [1024, 17408], P('fsdp')
- updated_down: float32 [4096, 1024], P('fsdp')
- updated_side: float32 [1024, 1288], P('fsdp')
- updated_bias: float32 [19456], P('fsdp')
- first_in_new: float32 [1024, 17408], P('fsdp')
- first_down_new: float32 [4096, 1024], P('fsdp')
- first_side_new: float32 [1024, 1288], P('fsdp')
- first_bias_new: float32 [19456], P('fsdp')
- second_in_new: float32 [1024, 17408], P('fsdp')
- second_down_new: float32 [4096, 1024], P('fsdp')
- second_side_new: float32 [1024, 1288], P('fsdp')
- second_bias_new: float32 [19456], P('fsdp')
- trust_ratios: float32 [12], replicated
- weight_norms: float32 [12], replicated
- update_norms: float32 [12], replicated
Inputs may be any that keep to these rules, and one draw needn't show every extreme that they name: `weights_in`: weights of order one over the root of their fan-in; the attention output columns W_out max(sqrt(256) / 2, 1) times larger. `weights_side`: weights of order one over the root of their fan-in, class embeddings of order one.
All inputs are finite; a program needn't handle non-finite values.
Results may differ from a plain program's by a relative error of at most 0.0083.
The roundings to bfloat16 on the way count: a program that leaves them out, or rounds other values in their place, can miss the bound.
Values may be sent and summed in bfloat16 or wider, within the bound.
No kernel may reach another device: no remote copies, remote signals or barrier semaphores. Data moves between devices by JAX's collectives and lax.ppermute only.
A program may use at most 512 MiB of HBM per device.

v0:
```python
from functools import partial
import math

import jax
import jax.numpy as jnp
from jax import lax
from jax.sharding import PartitionSpec as P

D = 1024
HEADS = 16
HEAD_DIM = 64
FF = 4096
CLASSES = 1000
PATCH_FEAT = 16
TFREQ = 256
GRID = 16
TOK = 256
MICRO = 2
STEP = 10
IMG_DEV = 1
SIDE = 1288


BETA_ONE = 0.5
BETA_TWO = 0.5
EPSILON = 1e-06
DECAY = 0.01
RATE = 0.25
NORM_EPS = 1e-06
ROW_SPLIT = 8


def matmul(left, right):
    return jnp.dot(left, right, preferred_element_type=jnp.float32)


def dot_tail(left, right):
    return lax.dot_general(
        left, right, (((1,), (1,)), ((), ())), preferred_element_type=jnp.float32
    )


def dot_head(left, right):
    return lax.dot_general(
        left, right, (((0,), (0,)), ((), ())), preferred_element_type=jnp.float32
    )


def layer_norm(values):
    center = values - jnp.mean(values, axis=-1, keepdims=True)
    return center * lax.rsqrt(jnp.mean(center * center, axis=-1, keepdims=True) + NORM_EPS)


def modulate(values, shift, scale):
    return layer_norm(values) * (1.0 + scale[:, None, :]) + shift[:, None, :]


def noise_scales(steps_part):
    phase = (steps_part.astype(jnp.float32) / 1000.0 + 0.008) / 1.008 * (math.pi / 2.0)
    signal = jnp.cos(phase) * jnp.cos(phase)
    return (jnp.sqrt(signal), jnp.sqrt(1.0 - signal))


def time_features(steps_part):
    half_width = TFREQ // 2
    freqs = jnp.exp(-math.log(10000.0) * jnp.arange(half_width, dtype=jnp.float32) / half_width)
    angles = steps_part.astype(jnp.float32)[:, None] * freqs[None, :]
    return jnp.concatenate([jnp.cos(angles), jnp.sin(angles)], axis=1)


def positions():
    quarter = D // 4
    omega = 1.0 / 10000.0 ** (jnp.arange(quarter, dtype=jnp.float32) / quarter)
    cells = jnp.arange(TOK, dtype=jnp.int32)
    row_pos = (cells // GRID).astype(jnp.float32)[:, None] * omega[None, :]
    col_pos = (cells % GRID).astype(jnp.float32)[:, None] * omega[None, :]
    return jnp.concatenate(
        [jnp.sin(row_pos), jnp.cos(row_pos), jnp.sin(col_pos), jnp.cos(col_pos)], axis=1
    )


def column_blocks():
    return [
        (0, 0, 3 * D),
        (0, 3 * D, 4 * D),
        (0, 4 * D, 4 * D + FF),
        (0, 4 * D + FF, 10 * D + FF),
        (0, 10 * D + FF, 12 * D + FF),
        (0, 12 * D + FF, 13 * D + FF),
        (1, 0, 0),
        (2, 0, TFREQ),
        (2, TFREQ, TFREQ + PATCH_FEAT),
        (2, TFREQ + PATCH_FEAT, TFREQ + PATCH_FEAT + CLASSES),
        (2, TFREQ + PATCH_FEAT + CLASSES, SIDE),
        (3, 0, 0),
    ]


def block_squares(arrays):
    totals = []
    for kind, start, stop in column_blocks():
        if kind in (0, 2):
            piece = arrays[kind][:, start:stop]
        else:
            piece = arrays[kind]
        totals.append(jnp.sum(piece * piece))
    return jnp.stack(totals)


def block_factors(trust):
    rows_in, rows_side = ([], [])
    for index, (kind, start, stop) in enumerate(column_blocks()):
        if kind == 0:
            rows_in.append(jnp.full((stop - start,), trust[index], jnp.float32))
        if kind == 2:
            rows_side.append(jnp.full((stop - start,), trust[index], jnp.float32))
    return (
        jnp.concatenate(rows_in)[None, :],
        trust[6],
        jnp.concatenate(rows_side)[None, :],
        trust[11],
    )


def adam_direction(weight, grad, first, second):
    first_new = BETA_ONE * first + (1.0 - BETA_ONE) * grad
    second_new = BETA_TWO * second + (1.0 - BETA_TWO) * grad * grad
    direction = (
        first_new
        / (1.0 - BETA_ONE**STEP)
        / (jnp.sqrt(second_new / (1.0 - BETA_TWO**STEP)) + EPSILON)
        + DECAY * weight
    )
    return (first_new, second_new, direction)


def split_weights(gathered):
    weights_in, weights_down, weights_side, biases = gathered
    bias_full = biases.astype(jnp.float32)
    named = {
        "w_qkv": weights_in[:, : 3 * D],
        "w_out": weights_in[:, 3 * D : 4 * D],
        "w_up": weights_in[:, 4 * D : 4 * D + FF],
        "w_mod": weights_in[:, 4 * D + FF : 10 * D + FF],
        "w_final": weights_in[:, 10 * D + FF : 12 * D + FF],
        "w_time": weights_in[:, 12 * D + FF :],
        "w_down": weights_down,
        "t_first": weights_side[:, :TFREQ],
        "w_patch": weights_side[:, TFREQ : TFREQ + PATCH_FEAT],
        "w_class": weights_side[:, TFREQ + PATCH_FEAT : TFREQ + PATCH_FEAT + CLASSES],
        "w_head": weights_side[:, TFREQ + PATCH_FEAT + CLASSES :],
        "b_query": bias_full[:D],
        "b_value": bias_full[D : 2 * D],
        "b_out": bias_full[2 * D : 3 * D],
        "b_up": bias_full[3 * D : 3 * D + FF],
        "b_down": bias_full[3 * D + FF : 4 * D + FF],
        "b_mod": bias_full[4 * D + FF : 10 * D + FF],
        "b_final": bias_full[10 * D + FF : 12 * D + FF],
        "b_tfirst": bias_full[12 * D + FF : 13 * D + FF],
        "b_time": bias_full[13 * D + FF : 14 * D + FF],
        "b_patch": bias_full[14 * D + FF :],
    }
    return named


def attention_scores(queries, keys_all):
    scores = jnp.einsum("bqhd,bkhd->bhqk", queries, keys_all, preferred_element_type=jnp.float32)
    return scores * HEAD_DIM ** (-0.5)


def forward(gathered, latent, noise_part, steps_part, label_part, image_total):
    named = split_weights(gathered)
    count = latent.shape[0]
    rows_all = count * TOK
    signal, spread = noise_scales(steps_part)
    noise_rows = noise_part.astype(jnp.float32)
    noisy = signal[:, None, None] * latent.astype(jnp.float32) + spread[:, None, None] * noise_rows
    noisy = noisy.astype(jnp.bfloat16).reshape(rows_all, PATCH_FEAT)
    hidden = (
        dot_tail(noisy, named["w_patch"]) + named["b_patch"] + jnp.tile(positions(), (count, 1))
    )
    feats = time_features(steps_part).astype(jnp.bfloat16)
    time_pre = dot_tail(feats, named["t_first"]) + named["b_tfirst"]
    time_act = jax.nn.silu(time_pre).astype(jnp.bfloat16)
    onehot = (label_part[:, None] == jnp.arange(CLASSES, dtype=jnp.int32)[None, :]).astype(
        jnp.bfloat16
    )
    cond = matmul(time_act, named["w_time"]) + named["b_time"] + dot_tail(onehot, named["w_class"])
    cond_act = jax.nn.silu(cond).astype(jnp.bfloat16)
    mods = matmul(cond_act, named["w_mod"]) + named["b_mod"]
    finals = matmul(cond_act, named["w_final"]) + named["b_final"]
    resid_in = hidden.reshape(count, TOK, D)
    normed_a = (
        modulate(resid_in, mods[:, :D], mods[:, D : 2 * D])
        .astype(jnp.bfloat16)
        .reshape(rows_all, D)
    )
    proj = matmul(normed_a, named["w_qkv"])
    head_shape = (count, TOK, HEADS, HEAD_DIM)
    queries = (proj[:, :D] + named["b_query"]).astype(jnp.bfloat16).reshape(head_shape)
    keys_all = proj[:, D : 2 * D].astype(jnp.bfloat16).reshape(head_shape)
    values_all = (proj[:, 2 * D :] + named["b_value"]).astype(jnp.bfloat16).reshape(head_shape)
    scores = attention_scores(queries, keys_all)
    log_total = jax.nn.logsumexp(scores, axis=-1)
    probs = jnp.exp(scores - log_total[..., None]).astype(jnp.bfloat16)
    mixed = jnp.einsum("bhqk,bkhd->bqhd", probs, values_all, preferred_element_type=jnp.float32)
    mixed = mixed.astype(jnp.bfloat16).reshape(rows_all, D)
    attended = matmul(mixed, named["w_out"]) + named["b_out"]
    resid_mid = resid_in + mods[:, 2 * D : 3 * D][:, None, :] * attended.reshape(count, TOK, D)
    normed_b = (
        modulate(resid_mid, mods[:, 3 * D : 4 * D], mods[:, 4 * D : 5 * D])
        .astype(jnp.bfloat16)
        .reshape(rows_all, D)
    )
    upper = matmul(normed_b, named["w_up"]) + named["b_up"]
    active = jax.nn.gelu(upper, approximate=True).astype(jnp.bfloat16)
    lowered = matmul(active, named["w_down"]) + named["b_down"]
    resid_out = resid_mid + mods[:, 5 * D :][:, None, :] * lowered.reshape(count, TOK, D)
    normed_c = (
        modulate(resid_out, finals[:, :D], finals[:, D:]).astype(jnp.bfloat16).reshape(rows_all, D)
    )
    predicted = matmul(normed_c, named["w_head"])
    error = predicted - noise_rows.reshape(rows_all, PATCH_FEAT)
    grad_pred = (2.0 / image_total * error).astype(jnp.bfloat16)
    cache = {
        "noisy": noisy,
        "feats": feats,
        "time_pre": time_pre,
        "time_act": time_act,
        "onehot": onehot.astype(jnp.float32),
        "cond": cond,
        "cond_act": cond_act,
        "mods": mods,
        "finals": finals,
        "resid_in": resid_in,
        "normed_a": normed_a,
        "queries": queries,
        "keys_all": keys_all,
        "values_all": values_all,
        "log_total": log_total,
        "mixed": mixed,
        "attended": attended,
        "resid_mid": resid_mid,
        "normed_b": normed_b,
        "upper": upper,
        "active": active,
        "lowered": lowered,
        "resid_out": resid_out,
        "normed_c": normed_c,
        "grad_pred": grad_pred,
    }
    return (jnp.sum(error * error), cache)


def backward(gathered, cache):
    named = split_weights(gathered)
    mods = cache["mods"]
    finals = cache["finals"]
    count = mods.shape[0]
    rows_all = count * TOK
    grad_pred = cache["grad_pred"]
    grad_head = dot_head(cache["normed_c"], grad_pred)
    grad_normed_c = dot_tail(grad_pred, named["w_head"]).reshape(count, TOK, D)
    _, pull_final = jax.vjp(modulate, cache["resid_out"], finals[:, :D], finals[:, D:])
    grad_out, grad_shift_f, grad_scale_f = pull_final(grad_normed_c)
    lowered = cache["lowered"].reshape(count, TOK, D)
    grad_gate_b = jnp.sum(grad_out * lowered, axis=1)
    grad_lowered = (grad_out * mods[:, 5 * D :][:, None, :]).reshape(rows_all, D)
    grad_b_down = jnp.sum(grad_lowered, axis=0)
    lowered_bf = grad_lowered.astype(jnp.bfloat16)
    grad_w_down = dot_head(cache["active"], lowered_bf)
    grad_active = dot_tail(lowered_bf, named["w_down"])
    _, pull_gelu = jax.vjp(partial(jax.nn.gelu, approximate=True), cache["upper"])
    grad_upper = pull_gelu(grad_active)[0]
    grad_b_up = jnp.sum(grad_upper, axis=0)
    upper_bf = grad_upper.astype(jnp.bfloat16)
    grad_w_up = dot_head(cache["normed_b"], upper_bf)
    grad_normed_b = dot_tail(upper_bf, named["w_up"]).reshape(count, TOK, D)
    _, pull_mid = jax.vjp(
        modulate, cache["resid_mid"], mods[:, 3 * D : 4 * D], mods[:, 4 * D : 5 * D]
    )
    grad_mid_norm, grad_shift_b, grad_scale_b = pull_mid(grad_normed_b)
    grad_mid = grad_out + grad_mid_norm
    attended = cache["attended"].reshape(count, TOK, D)
    grad_gate_a = jnp.sum(grad_mid * attended, axis=1)
    grad_attended = (grad_mid * mods[:, 2 * D : 3 * D][:, None, :]).reshape(rows_all, D)
    grad_b_out = jnp.sum(grad_attended, axis=0)
    attended_bf = grad_attended.astype(jnp.bfloat16)
    grad_w_out = dot_head(cache["mixed"], attended_bf)
    head_shape = (count, TOK, HEADS, HEAD_DIM)
    grad_mixed = dot_tail(attended_bf, named["w_out"]).astype(jnp.bfloat16).reshape(head_shape)
    queries = cache["queries"]
    keys_all = cache["keys_all"]
    values_all = cache["values_all"]
    scores = attention_scores(queries, keys_all)
    probs_full = jnp.exp(scores - cache["log_total"][..., None])
    grad_probs = jnp.einsum(
        "bqhd,bkhd->bhqk", grad_mixed, values_all, preferred_element_type=jnp.float32
    )
    inner = jnp.sum(probs_full * grad_probs, axis=-1, keepdims=True)
    grad_scores = (probs_full * (grad_probs - inner)).astype(jnp.bfloat16)
    scale = HEAD_DIM ** (-0.5)
    grad_queries = (
        jnp.einsum("bhqk,bkhd->bqhd", grad_scores, keys_all, preferred_element_type=jnp.float32)
        * scale
    )
    grad_keys = (
        jnp.einsum("bhqk,bqhd->bkhd", grad_scores, queries, preferred_element_type=jnp.float32)
        * scale
    )
    grad_values = jnp.einsum(
        "bhqk,bqhd->bkhd",
        probs_full.astype(jnp.bfloat16),
        grad_mixed,
        preferred_element_type=jnp.float32,
    )
    grad_queries = grad_queries.reshape(rows_all, D)
    grad_keys = grad_keys.reshape(rows_all, D)
    grad_values = grad_values.reshape(rows_all, D)
    grad_b_query = jnp.sum(grad_queries, axis=0)
    grad_b_value = jnp.sum(grad_values, axis=0)
    proj_bf = jnp.concatenate([grad_queries, grad_keys, grad_values], axis=1).astype(jnp.bfloat16)
    grad_w_qkv = dot_head(cache["normed_a"], proj_bf)
    grad_normed_a = dot_tail(proj_bf, named["w_qkv"]).reshape(count, TOK, D)
    _, pull_first = jax.vjp(modulate, cache["resid_in"], mods[:, :D], mods[:, D : 2 * D])
    grad_in_norm, grad_shift_a, grad_scale_a = pull_first(grad_normed_a)
    grad_hidden = (grad_mid + grad_in_norm).reshape(rows_all, D)
    grad_b_patch = jnp.sum(grad_hidden, axis=0)
    grad_w_patch = dot_head(grad_hidden.astype(jnp.bfloat16), cache["noisy"])
    grad_mods = jnp.concatenate(
        [grad_shift_a, grad_scale_a, grad_gate_a, grad_shift_b, grad_scale_b, grad_gate_b], axis=1
    )
    grad_finals = jnp.concatenate([grad_shift_f, grad_scale_f], axis=1)
    grad_b_mod = jnp.sum(grad_mods, axis=0)
    grad_b_final = jnp.sum(grad_finals, axis=0)
    mods_bf = grad_mods.astype(jnp.bfloat16)
    finals_bf = grad_finals.astype(jnp.bfloat16)
    grad_w_mod = dot_head(cache["cond_act"], mods_bf)
    grad_w_final = dot_head(cache["cond_act"], finals_bf)
    grad_cond_act = dot_tail(mods_bf, named["w_mod"]) + dot_tail(finals_bf, named["w_final"])
    _, pull_cond = jax.vjp(jax.nn.silu, cache["cond"])
    grad_cond = pull_cond(grad_cond_act)[0]
    grad_w_class = dot_head(grad_cond, cache["onehot"])
    grad_b_time = jnp.sum(grad_cond, axis=0)
    cond_bf = grad_cond.astype(jnp.bfloat16)
    grad_w_time = dot_head(cache["time_act"], cond_bf)
    grad_time_act = dot_tail(cond_bf, named["w_time"])
    _, pull_time = jax.vjp(jax.nn.silu, cache["time_pre"])
    grad_time_pre = pull_time(grad_time_act)[0]
    grad_b_tfirst = jnp.sum(grad_time_pre, axis=0)
    grad_t_first = dot_head(grad_time_pre.astype(jnp.bfloat16), cache["feats"])
    grad_in = jnp.concatenate(
        [grad_w_qkv, grad_w_out, grad_w_up, grad_w_mod, grad_w_final, grad_w_time], axis=1
    )
    grad_side = jnp.concatenate([grad_t_first, grad_w_patch, grad_w_class, grad_head], axis=1)
    grad_bias = jnp.concatenate(
        [
            grad_b_query,
            grad_b_value,
            grad_b_out,
            grad_b_up,
            grad_b_down,
            grad_b_mod,
            grad_b_final,
            grad_b_tfirst,
            grad_b_time,
            grad_b_patch,
        ]
    )
    return (grad_in, grad_w_down, grad_side, grad_bias)


def fetch(shards):
    return (
        lax.all_gather(shards[0], "fsdp", axis=0, tiled=True),
        lax.all_gather(shards[1], "fsdp", axis=0, tiled=True),
        lax.all_gather(shards[2], "fsdp", axis=0, tiled=True),
        lax.all_gather(shards[3], "fsdp", axis=0, tiled=True),
    )


def refetch(shards):
    return (
        lax.all_gather(shards[0], "fsdp", axis=0, tiled=True),
        lax.all_gather(shards[1], "fsdp", axis=0, tiled=True),
        lax.all_gather(shards[2], "fsdp", axis=0, tiled=True),
        lax.all_gather(shards[3], "fsdp", axis=0, tiled=True),
    )


def per_device(
    latents,
    noise_draw,
    timesteps,
    labels,
    weights_in,
    weights_down,
    weights_side,
    biases,
    first_in,
    first_down,
    first_side,
    first_bias,
    second_in,
    second_down,
    second_side,
    second_bias,
):
    image_total = IMG_DEV * MICRO * lax.axis_size("fsdp")
    masters = (weights_in, weights_down, weights_side, biases)
    shards = tuple((item.astype(jnp.bfloat16) for item in masters))
    loss_local = jnp.zeros((), jnp.float32)
    totals = None
    for micro_index in range(MICRO):
        first_row = micro_index * IMG_DEV
        last_row = first_row + IMG_DEV
        ahead = fetch(shards)
        loss_part, cache = forward(
            ahead,
            latents[first_row:last_row],
            noise_draw[first_row:last_row],
            timesteps[first_row:last_row],
            labels[first_row:last_row],
            image_total,
        )
        behind = refetch(shards)
        grads = backward(behind, cache)
        if totals is None:
            totals = grads
        else:
            totals = tuple((total + grad for total, grad in zip(totals, grads)))
        loss_local = loss_local + loss_part
    packed_in = totals[0].reshape(totals[0].shape[0] * ROW_SPLIT, totals[0].shape[1] // ROW_SPLIT)
    packed_side = totals[2].reshape(totals[2].shape[0] * ROW_SPLIT, totals[2].shape[1] // ROW_SPLIT)
    summed = (
        lax.psum_scatter(packed_in, "fsdp", scatter_dimension=0, tiled=True),
        lax.psum_scatter(totals[1], "fsdp", scatter_dimension=0, tiled=True),
        lax.psum_scatter(packed_side, "fsdp", scatter_dimension=0, tiled=True),
        lax.psum_scatter(totals[3], "fsdp", scatter_dimension=0, tiled=True),
    )
    reduced = (
        summed[0].reshape(weights_in.shape[0], weights_in.shape[1]),
        summed[1],
        summed[2].reshape(weights_side.shape[0], weights_side.shape[1]),
        summed[3],
    )
    firsts = (first_in, first_down, first_side, first_bias)
    seconds = (second_in, second_down, second_side, second_bias)
    results = [
        adam_direction(masters[index], reduced[index], firsts[index], seconds[index])
        for index in range(4)
    ]
    directions = [item[2] for item in results]
    update_local = block_squares(directions)
    loss_sum, weight_sq, update_sq = lax.psum(
        (loss_local, block_squares(masters), update_local), "fsdp"
    )
    weight_norms = jnp.sqrt(weight_sq)
    update_norms = jnp.sqrt(update_sq)
    trust = weight_norms / update_norms
    factors = block_factors(trust)
    updated = [masters[index] - RATE * factors[index] * directions[index] for index in range(4)]
    return (
        loss_sum,
        updated[0],
        updated[1],
        updated[2],
        updated[3],
        results[0][0],
        results[1][0],
        results[2][0],
        results[3][0],
        results[0][1],
        results[1][1],
        results[2][1],
        results[3][1],
        trust,
        weight_norms,
        update_norms,
    )


def solution(mesh):
    placed = (
        P("fsdp", None, None),
        P("fsdp", None, None),
        P("fsdp"),
        P("fsdp"),
        P("fsdp", None),
        P("fsdp", None),
        P("fsdp", None),
        P("fsdp"),
        P("fsdp", None),
        P("fsdp", None),
        P("fsdp", None),
        P("fsdp"),
        P("fsdp", None),
        P("fsdp", None),
        P("fsdp", None),
        P("fsdp"),
    )
    return jax.shard_map(
        per_device,
        mesh=mesh,
        in_specs=placed,
        out_specs=(
            P(),
            P("fsdp", None),
            P("fsdp", None),
            P("fsdp", None),
            P("fsdp"),
            P("fsdp", None),
            P("fsdp", None),
            P("fsdp", None),
            P("fsdp"),
            P("fsdp", None),
            P("fsdp", None),
            P("fsdp", None),
            P("fsdp"),
            P(),
            P(),
            P(),
        ),
        check_vma=False,
    )
```

profile of v0, /device:TPU:0, one launch (start us, length us, event | category | flops | bytes accessed | tf_op | source)
XLA Modules:
  0.0 1798.4 jit_solution(15723618536933730577)
XLA Ops:
  15.1 42.6 %all-reduce = bf16[19456]{0:T(1024)(128)(2,1)S(1)} all-reduce(bf16[19456]{0:T(1024)(128)(2,1)S(1)} %dynamic-update-slice), channel_id=1, replica_groups=mesh['fsdp'=32] {'fsdp'}, use_global_device_ids=true, to_apply=%add | all-reduce | flops 19456 | bytes 77824
  64.1 8.6 all-gather.4.cloned.1.call-done
  79.2 200.5 %all-gather.6.cloned.1.call-done = bf16[1024,17408]{1,0:T(8,128)(2,1)} async-done(((bf16[32,17408]{1,0:T(8,128)(2,1)}), bf16[1024,17408]{1,0:T(8,128)(2,1)}) %all-gather.6.cloned.1.call-update) | async-done | bytes 35651600 | tf_op jit(solution)/shard_map/all_gather | solution.py:375
  308.3 7.9 fusion.19
  316.2 42.6 %all-gather.8.cloned.1.call-done = bf16[4096,1024]{1,0:T(8,128)(2,1)} async-done(((bf16[128,1024]{1,0:T(8,128)(2,1)}), bf16[4096,1024]{1,0:T(8,128)(2,1)}) %all-gather.8.cloned.1.call-update) | async-done | bytes 8388624 | tf_op jit(solution)/shard_map/all_gather | solution.py:376
  358.8 7.6 fusion.200
  511.8 7.3 concatenate.112
  519.0 7.3 concatenate.111
  526.3 7.5 add.683
  533.8 10.1 add.684
  544.6 11.3 fusion.174
  555.9 11.0 convolution_add_fusion
  567.5 8.0 convolution_dynamic-update-slice_fusion.3
  578.4 8.3 convolution_dynamic-update-slice_fusion.1
  586.7 11.6 multiply_dynamic-update-slice_fusion.1
  614.3 8.5 convolution_dynamic-update-slice_fusion
  622.9 11.7 multiply_dynamic-update-slice_fusion
  640.7 70.7 %add.668 = f32[1024,17408]{1,0:T(8,128)} add(f32[1024,17408]{1,0:T(8,128)} %multiply_dynamic-update-slice_fusion.5, f32[1024,17408]{1,0:T(8,128)} %multiply_dynamic-update-slice_fusion.4) | non-fusion elementwise | flops 17825792 | bytes 213909504 | tf_op jit(solution)/shard_map/add | solution.py:431
  711.4 73.2 %add.669 = f32[8192,2176]{1,0:T(8,128)} reshape(f32[1024,17408]{1,0:T(8,128)} %add.668) | data formatting | bytes 142606336 | tf_op jit(solution)/shard_map/add | solution.py:431
  798.1 160.5 %reduce-scatter.6.cloned.1.call-done = f32[128,1024]{1,0:T(8,128)} async-done(((f32[4096,1024]{1,0:T(8,128)}), f32[128,1024]{1,0:T(8,128)}) %reduce-scatter.6.cloned.1.call-update) | async-done | bytes 524304 | tf_op jit(solution)/shard_map/reduce_scatter | solution.py:437
  961.8 7.8 stack.90
  969.6 738.2 %reduce-scatter.4.cloned.1.call-done = f32[256,2176]{1,0:T(8,128)} async-done(((f32[8192,2176]{1,0:T(8,128)}), f32[256,2176]{1,0:T(8,128)}) %reduce-scatter.4.cloned.1.call-update) | async-done | bytes 2228240 | tf_op jit(solution)/shard_map/reduce_scatter | solution.py:436
  1720.8 7.8 stack.103
  1728.7 47.2 %all-reduce.2 = (f32[]{:T(128)}, f32[12]{0:T(128)S(1)}, f32[12]{0:T(128)S(1)}) all-reduce(f32[]{:T(128)S(6)} %add.663, f32[12]{0:T(128)S(1)} %stack.90, f32[12]{0:T(128)S(1)} %stack.103), channel_id=1, replica_groups=mesh['fsdp'=32] {'fsdp'}, use_global_device_ids=true, to_apply=%region_18.19 | all-reduce | flops 25 | bytes 200 | tf_op jit(solution)/shard_map/psum | solution.py:455
  (495 shorter events, 260.0 us)
Async XLA Ops:
  7.2 51.9 %copy-start.98 = (s32[2]{0:T(128)S(1)}, s32[2]{0:T(128)}, u32[]{:S(2)}) copy-start(s32[2]{0:T(128)} %param.19) | copy-start | bytes 28
  7.2 67.6 %copy-start.65 = (bf16[2,256,16]{1,2,0:T(8,128)(2,1)S(1)}, bf16[2,256,16]{1,2,0:T(8,128)(2,1)}, u32[]{:S(2)}) copy-start(bf16[2,256,16]{1,2,0:T(8,128)(2,1)} %param.17) | copy-start | bytes 49156
  7.2 67.6 %copy-start.81 = (bf16[2,256,16]{1,2,0:T(8,128)(2,1)S(1)}, bf16[2,256,16]{1,2,0:T(8,128)(2,1)}, u32[]{:S(2)}) copy-start(bf16[2,256,16]{1,2,0:T(8,128)(2,1)} %param.16) | copy-start | bytes 49156
  7.2 65.5 %all-gather.4.cloned.1.call-start = ((), (), s32[]{:S(2)}) async-start(), calls=%async_computation.3 | async-start | bytes 2973696 | tf_op jit(solution)/shard_map/all_gather | solution.py:377
  9.0 270.7 %all-gather.6.cloned.1.call-start = ((), (), s32[]{:S(2)}) async-start(), calls=%async_computation.4 | async-start | bytes 36765696 | tf_op jit(solution)/shard_map/all_gather | solution.py:375
  11.8 347.0 %all-gather.8.cloned.1.call-start = ((), (), s32[]{:S(2)}) async-start(), calls=%async_computation.5 | async-start | bytes 8650752 | tf_op jit(solution)/shard_map/all_gather | solution.py:376
  12.6 779.8 %all-reduce.5.cloned.1.call-start = ((), (), s32[]{:S(2)}) async-start(), calls=%async_computation.9 | async-start | bytes 155648
  76.9 326.3 %copy-start.6 = (f32[256,1024]{1,0:T(8,128)}, f32[256,1024]{1,0:T(8,128)S(1)}, u32[]{:S(2)}) copy-start(f32[256,1024]{1,0:T(8,128)S(1)} %get-tuple-element.178) | copy-start | bytes 3145732
  76.9 326.3 %copy-start.70 = (f32[256]{0:T(256)}, f32[256]{0:T(256)S(1)}, u32[]{:S(2)}) copy-start(f32[256]{0:T(256)S(1)} %broadcast_multiply_fusion.8) | copy-start | bytes 3076
  77.2 326.0 %copy-start.77 = (f32[256]{0:T(256)}, f32[256]{0:T(256)S(1)}, u32[]{:S(2)}) copy-start(f32[256]{0:T(256)S(1)} %fusion.149) | copy-start | bytes 3076
  288.4 95.3 %copy-start.56 = (f32[1,1024]{1,0:T(1,128)}, f32[1,1024]{1,0:T(1,128)S(1)}, u32[]{:S(2)}) copy-start(f32[1,1024]{1,0:T(1,128)S(1)} %get-tuple-element.137) | copy-start | bytes 12292
  288.4 114.9 %copy-start.54 = (f32[1,1024]{1,0:T(1,128)}, f32[1,1024]{1,0:T(1,128)S(1)}, u32[]{:S(2)}) copy-start(f32[1,1024]{1,0:T(1,128)S(1)} %get-tuple-element.139) | copy-start | bytes 12292
  288.4 116.7 %copy-start.66 = (f32[1,1024]{1,0:T(1,128)}, f32[1,1024]{1,0:T(1,128)S(1)}, u32[]{:S(2)}) copy-start(f32[1,1024]{1,0:T(1,128)S(1)} %get-tuple-element.140) | copy-start | bytes 12292
  305.0 78.6 %copy-start.8 = (f32[256,1024]{1,0:T(8,128)}, f32[256,1024]{1,0:T(8,128)S(1)}, u32[]{:S(2)}) copy-start(f32[256,1024]{1,0:T(8,128)S(1)} %get-tuple-element.109) | copy-start | bytes 3145732
  305.0 78.6 %copy-start.74 = (f32[256]{0:T(256)}, f32[256]{0:T(256)S(1)}, u32[]{:S(2)}) copy-start(f32[256]{0:T(256)S(1)} %broadcast_multiply_fusion.7) | copy-start | bytes 3076
  305.3 78.4 %copy-start.79 = (f32[256]{0:T(256)}, f32[256]{0:T(256)S(1)}, u32[]{:S(2)}) copy-start(f32[256]{0:T(256)S(1)} %fusion.150) | copy-start | bytes 3076
  384.5 20.5 %copy-start.10 = (f32[256,1024]{1,0:T(8,128)}, f32[256,1024]{1,0:T(8,128)S(1)}, u32[]{:S(2)}) copy-start(f32[256,1024]{1,0:T(8,128)S(1)} %get-tuple-element.118) | copy-start | bytes 3145732
  506.8 287.2 %reduce-scatter.8.cloned.1.call-start = ((), (), s32[]{:S(2)}) async-start(), calls=%async_computation.8 | async-start | bytes 8650752 | tf_op jit(solution)/shard_map/reduce_scatter | solution.py:438
  544.0 414.6 %reduce-scatter.6.cloned.1.call-start = ((), (), s32[]{:S(2)}) async-start(), calls=%async_computation.7 | async-start | bytes 17301504 | tf_op jit(solution)/shard_map/reduce_scatter | solution.py:437
  567.0 1140.8 %reduce-scatter.4.cloned.1.call-start = ((), (), s32[]{:S(2)}) async-start(), calls=%async_computation.6 | async-start | bytes 73531392 | tf_op jit(solution)/shard_map/reduce_scatter | solution.py:436
  784.7 174.0 %copy-start.30 = (f32[128,1024]{1,0:T(8,128)S(1)}, f32[128,1024]{1,0:T(8,128)}, u32[]{:S(2)}) copy-start(f32[128,1024]{1,0:T(8,128)} %param.21) | copy-start | bytes 1572868
  794.0 995.7 %copy-start.82 = (f32[608]{0:T(1024)}, f32[608]{0:T(1024)S(1)}, u32[]{:S(2)}) copy-start(f32[608]{0:T(1024)S(1)} %get-tuple-element.90) | copy-start | bytes 7300
  794.0 995.7 %copy-start.83 = (f32[608]{0:T(1024)}, f32[608]{0:T(1024)S(1)}, u32[]{:S(2)}) copy-start(f32[608]{0:T(1024)S(1)} %get-tuple-element.91) | copy-start | bytes 7300
  961.8 828.5 %copy-start.47 = (f32[128,1024]{1,0:T(8,128)}, f32[128,1024]{1,0:T(8,128)S(1)}, u32[]{:S(2)}) copy-start(f32[128,1024]{1,0:T(8,128)S(1)} %get-tuple-element.100) | copy-start | bytes 1572868
  (85 other events, 452.0 us)
Sparse Core Ops, SparseCore 0:
  11.5 61.1 all-gather.3
  76.1 203.5 all-gather.5
  283.2 75.6 all-gather.7
  506.9 117.4 all-reduce.4
  626.5 150.5 reduce-scatter.7
  779.2 179.3 reduce-scatter.5
  961.0 746.7 reduce-scatter.3
where the time goes:
time: 1810 us; the launch traced here: 1800 us
  waiting for transfers between devices  1150 us (64%)
  matrix products  221 us (12%)
  other arithmetic  178 us (10%)
  local copies, waits for them, and re-layouts  137 us (8%)
  blocking collectives  89.8 us (5%)
  between operations  20.4 us (1%)
    reduce_scatter x1, waiting for transfers between devices, per_device(): lax.psum_scatter(packed_in, 'fsdp', scatter_dimension=0, tiled=True)  738 us
    all_gather x1, waiting for transfers between devices, fetch(): lax.all_gather(shards[0], 'fsdp', axis=0, tiled=True)  200 us
    reduce_scatter x1, waiting for transfers between devices, per_device(): lax.psum_scatter(totals[1], 'fsdp', scatter_dimension=0, tiled=True)  161 us
    add x2, local copies, waits for them, and re-layouts, per_device(): totals = tuple((total + grad for total, grad in zip(totals, grads)))  83.3 us
    add x3, other arithmetic, per_device(): totals = tuple((total + grad for total, grad in zip(totals, grads)))  78.8 us
    dot_general x22, matrix products, dot_tail(): lax.dot_general(left, right, (((1,), (1,)), ((), ())), preferred_element_...  71.2 us
    dot_general x16, matrix products, matmul(): return jnp.dot(left, right, preferred_element_type=jnp.float32)  66.9 us
    dot_general x12, matrix products, dot_head(): lax.dot_general(left, right, (((0,), (0,)), ((), ())), preferred_element_...  64.5 us
  transfers between devices with their start and end apart: 7, of which 5 were waited for; matrix products, arithmetic and copies ran while one was open for 19% of the time, Pallas kernels for 0%

commit v1 on v0

v1 whole, which is shorter than its diff:
```python
from functools import partial
import math

import jax
import jax.numpy as jnp
from jax import lax
from jax.experimental import pallas as pl
from jax.experimental.pallas import tpu as pltpu
from jax.sharding import PartitionSpec as P

D = 1024
HEADS = 16
HEAD_DIM = 64
FF = 4096
CLASSES = 1000
PATCH_FEAT = 16
TFREQ = 256
GRID = 16
TOK = 256
MICRO = 2
STEP = 10
IMG_DEV = 1
SIDE = 1288


BETA_ONE = 0.5
BETA_TWO = 0.5
EPSILON = 1e-06
DECAY = 0.01
RATE = 0.25
NORM_EPS = 1e-06
SMALL_ROWS = 16
AXIS = "fsdp"


def matmul(left, right):
    return jnp.dot(left, right, preferred_element_type=jnp.float32)


def dot_tail(left, right):
    return lax.dot_general(
        left, right, (((1,), (1,)), ((), ())), preferred_element_type=jnp.float32
    )


def dot_head(left, right):
    return lax.dot_general(
        left, right, (((0,), (0,)), ((), ())), preferred_element_type=jnp.float32
    )


def layer_norm(values):
    center = values - jnp.mean(values, axis=-1, keepdims=True)
    return center * lax.rsqrt(jnp.mean(center * center, axis=-1, keepdims=True) + NORM_EPS)


def modulate(values, shift, scale):
    return layer_norm(values) * (1.0 + scale[:, None, :]) + shift[:, None, :]


def noise_scales(steps_part):
    phase = (steps_part.astype(jnp.float32) / 1000.0 + 0.008) / 1.008 * (math.pi / 2.0)
    signal = jnp.cos(phase) * jnp.cos(phase)
    return (jnp.sqrt(signal), jnp.sqrt(1.0 - signal))


def time_features(steps_part):
    half_width = TFREQ // 2
    freqs = jnp.exp(-math.log(10000.0) * jnp.arange(half_width, dtype=jnp.float32) / half_width)
    angles = steps_part.astype(jnp.float32)[:, None] * freqs[None, :]
    return jnp.concatenate([jnp.cos(angles), jnp.sin(angles)], axis=1)


def positions():
    quarter = D // 4
    omega = 1.0 / 10000.0 ** (jnp.arange(quarter, dtype=jnp.float32) / quarter)
    cells = jnp.arange(TOK, dtype=jnp.int32)
    row_pos = (cells // GRID).astype(jnp.float32)[:, None] * omega[None, :]
    col_pos = (cells % GRID).astype(jnp.float32)[:, None] * omega[None, :]
    return jnp.concatenate(
        [jnp.sin(row_pos), jnp.cos(row_pos), jnp.sin(col_pos), jnp.cos(col_pos)], axis=1
    )


def column_blocks():
    return [
        (0, 0, 3 * D),
        (0, 3 * D, 4 * D),
        (0, 4 * D, 4 * D + FF),
        (0, 4 * D + FF, 10 * D + FF),
        (0, 10 * D + FF, 12 * D + FF),
        (0, 12 * D + FF, 13 * D + FF),
        (1, 0, 0),
        (2, 0, TFREQ),
        (2, TFREQ, TFREQ + PATCH_FEAT),
        (2, TFREQ + PATCH_FEAT, TFREQ + PATCH_FEAT + CLASSES),
        (2, TFREQ + PATCH_FEAT + CLASSES, SIDE),
        (3, 0, 0),
    ]


def block_squares(arrays):
    totals = []
    for kind, start, stop in column_blocks():
        if kind in (0, 2):
            piece = arrays[kind][:, start:stop]
        else:
            piece = arrays[kind]
        totals.append(jnp.sum(piece * piece))
    return jnp.stack(totals)


def block_factors(trust):
    rows_in, rows_side = ([], [])
    for index, (kind, start, stop) in enumerate(column_blocks()):
        if kind == 0:
            rows_in.append(jnp.full((stop - start,), trust[index], jnp.float32))
        if kind == 2:
            rows_side.append(jnp.full((stop - start,), trust[index], jnp.float32))
    return (
        jnp.concatenate(rows_in)[None, :],
        trust[6],
        jnp.concatenate(rows_side)[None, :],
        trust[11],
    )


def adam_direction(weight, grad, first, second):
    first_new = BETA_ONE * first + (1.0 - BETA_ONE) * grad
    second_new = BETA_TWO * second + (1.0 - BETA_TWO) * grad * grad
    direction = (
        first_new
        / (1.0 - BETA_ONE**STEP)
        / (jnp.sqrt(second_new / (1.0 - BETA_TWO**STEP)) + EPSILON)
        + DECAY * weight
    )
    return (first_new, second_new, direction)


class Grid:
    def __init__(self, count):
        if count == 32:
            self.sizes = (4, 2, 2, 2)
        elif count == 256:
            self.sizes = (8, 4, 4, 2)
        else:
            self.sizes = (count, 1, 1, 1)
        self.count = count
        index = lax.axis_index(AXIS)
        coords = []
        for size in reversed(self.sizes):
            coords.append(index % size)
            index = index // size
        self.coords = tuple(reversed(coords))

    def ahead(self, values, axis, shift):
        stride = math.prod(self.sizes[axis + 1 :])
        size = self.sizes[axis]
        pairs = []
        for source in range(self.count):
            place = source // stride % size
            pairs.append((source, source + ((place - shift) % size - place) * stride))
        return lax.ppermute(values, AXIS, pairs)

    def flip(self, values, axis, bit):
        stride = math.prod(self.sizes[axis + 1 :])
        pairs = []
        for source in range(self.count):
            place = source // stride % self.sizes[axis]
            pairs.append((source, source + ((place ^ bit) - place) * stride))
        return lax.ppermute(values, AXIS, pairs)

    def place(self, axis, shift):
        return (self.coords[axis] + shift) % self.sizes[axis]


def in_order(grid, pieces, axis):
    size = grid.sizes[axis]
    if size == 1:
        return pieces[0][None]
    if size == 2:
        lower = grid.coords[axis] == 0
        return jnp.stack(
            [jnp.where(lower, pieces[0], pieces[1]), jnp.where(lower, pieces[1], pieces[0])]
        )
    twice = jnp.stack(pieces + pieces)
    return lax.dynamic_slice_in_dim(twice, (size - grid.coords[axis]) % size, size, 0)


def gather_small(grid, values, order):
    for axis in order:
        pieces = [values]
        for shift in range(1, grid.sizes[axis]):
            pieces.append(grid.ahead(values, axis, shift))
        values = in_order(grid, pieces, axis)
    return values


def scatter_axis(grid, values, axis, dim):
    def entry(shift):
        return lax.dynamic_index_in_dim(values, grid.place(axis, shift), dim, keepdims=False)

    total = entry(0)
    for shift in range(1, grid.sizes[axis]):
        total = total + grid.ahead(entry(-shift), axis, shift)
    return total


def scatter_small(grid, values):
    values = scatter_axis(grid, values, 3, 3)
    values = scatter_axis(grid, values, 2, 2)
    values = scatter_axis(grid, values, 1, 1)
    return scatter_axis(grid, values, 0, 0)


def sum_small(grid, values):
    for axis in (3, 2, 1, 0):
        bit = 1
        while bit < grid.sizes[axis]:
            values = values + grid.flip(values, axis, bit)
            bit *= 2
    return values


def place_kernel(moves, where, *refs):
    pieces, full, sems = refs[:-2], refs[-2], refs[-1]
    copies = []
    for number, (piece, entry, spot) in enumerate(moves):
        place = tuple(where[slot] for slot in spot)
        copies.append(
            pltpu.make_async_copy(pieces[piece].at[entry], full.at[place], sems.at[number])
        )
    for copy in copies:
        copy.start()
    for copy in copies:
        copy.wait()


def gather_bulk(grid, shard, order):
    rows, columns = shard.shape
    first, second, third = order
    sizes = grid.sizes
    pieces = [shard]
    for _ in range(1, sizes[first]):
        pieces.append(grid.ahead(pieces[-1], first, 1))
    tagged = [((), jnp.stack(pieces))]
    for axis in (second, third, 3):
        reached = []
        for tag, piece in tagged:
            reached.append((tag + (0,), piece))
            for shift in range(1, sizes[axis]):
                piece = grid.ahead(piece, axis, 1)
                reached.append((tag + (shift,), piece))
        tagged = reached
    offsets = []
    for axis in range(4):
        offsets.append(sum(sizes[:axis]))
    moves = []
    for number, (tag, _) in enumerate(tagged):
        for entry in range(sizes[first]):
            shifts = {first: entry, second: tag[0], third: tag[1], 3: tag[2]}
            spot = tuple(offsets[axis] + shifts[axis] for axis in range(4))
            moves.append((number, entry, spot))
    where = jnp.stack(
        [grid.place(axis, shift) for axis in range(4) for shift in range(sizes[axis])]
    ).astype(jnp.int32)
    if rows % 16 == 0:
        full = pl.pallas_call(
            partial(place_kernel, moves),
            out_shape=jax.ShapeDtypeStruct(sizes + (rows, columns), shard.dtype),
            in_specs=[pl.BlockSpec(memory_space=pltpu.SMEM)]
            + [pl.BlockSpec(memory_space=pl.ANY)] * len(tagged),
            out_specs=pl.BlockSpec(memory_space=pl.ANY),
            scratch_shapes=[pltpu.SemaphoreType.DMA((len(moves),))],
            cost_estimate=pl.CostEstimate(
                flops=0, bytes_accessed=4 * grid.count * rows * columns, transcendentals=0
            ),
        )(where, *[piece for _, piece in tagged])
    else:
        full = jnp.zeros(sizes + (rows, columns), shard.dtype)
        for number, entry, spot in moves:
            place = tuple(where[slot] for slot in spot) + (0, 0)
            block = tagged[number][1][entry].reshape((1, 1, 1, 1, rows, columns))
            full = lax.dynamic_update_slice(full, block, place)
    return full.reshape(grid.count * rows, columns)


def scatter_bulk(grid, table, order):
    rows = table.shape[0] // grid.count
    current = table.reshape(grid.sizes + (rows, table.shape[1]))
    axes = (3,) + tuple(reversed(order))
    for axis in axes:
        size = grid.sizes[axis]

        def entry(shift, current=current, axis=axis):
            return lax.dynamic_index_in_dim(current, grid.place(axis, shift), axis)

        total = entry(1)
        for step in range(1, size):
            sent = grid.ahead(total.astype(jnp.bfloat16), axis, 1)
            total = sent.astype(jnp.float32) + entry(1 + step).astype(jnp.float32)
            if step < size - 1 or axis != axes[-1]:
                total = total.astype(jnp.bfloat16)
        current = total
    return current.reshape(rows, table.shape[1]).astype(jnp.float32)


def attention_scores(queries, keys_all):
    scores = jnp.einsum("bqhd,bkhd->bhqk", queries, keys_all, preferred_element_type=jnp.float32)
    return scores * HEAD_DIM ** (-0.5)


XZY = (2, 0, 1)
YZX = (1, 0, 2)
ZXY = (0, 2, 1)
ZYX = (0, 1, 2)
PLANS = (ZXY, YZX, XZY, YZX, XZY, ZYX)


def per_device(
    latents,
    noise_draw,
    timesteps,
    labels,
    weights_in,
    weights_down,
    weights_side,
    biases,
    first_in,
    first_down,
    first_side,
    first_bias,
    second_in,
    second_down,
    second_side,
    second_bias,
):
    bf16 = jnp.bfloat16
    count_all = lax.axis_size(AXIS)
    grid = Grid(count_all)
    sizes = grid.sizes
    count = latents.shape[0]
    rows_all = count * TOK
    image_total = count * count_all
    rows = weights_in.shape[0]
    bias_rows = biases.shape[0]
    my_rows = lax.axis_index(AXIS) * rows
    masters = (weights_in, weights_down, weights_side, biases)
    in_bf = weights_in.astype(bf16)
    down_bf = weights_down.astype(bf16)
    side_bf = weights_side.astype(bf16)
    t_first = side_bf[:, :TFREQ]
    patch_at = TFREQ
    class_at = TFREQ + PATCH_FEAT
    head_at = class_at + CLASSES
    w_class = side_bf[:, class_at:head_at]
    w_mods = in_bf[:, 4 * D + FF : 12 * D + FF]
    w_time = in_bf[:, 12 * D + FF :]

    numbers = jnp.concatenate([timesteps, labels])
    packed = jnp.concatenate(
        [
            biases.astype(bf16),
            side_bf[:, patch_at:class_at].reshape(-1),
            side_bf[:, head_at:].reshape(-1),
            (numbers // 32).astype(bf16),
            (numbers % 32).astype(bf16),
        ]
    )
    width = packed.shape[0]
    tall = -(-width // (SMALL_ROWS * 128)) * SMALL_ROWS
    packed = jnp.pad(packed, (0, tall * 128 - width)).reshape(tall, 128)
    spread_all = gather_small(grid, packed, (3, 2, 1, 0)).reshape(count_all, tall * 128)
    bias_full = spread_all[:, :bias_rows].reshape(-1).astype(jnp.float32)
    at = bias_rows
    w_patch = spread_all[:, at : at + rows * PATCH_FEAT].reshape(D, PATCH_FEAT)
    at += rows * PATCH_FEAT
    w_head = spread_all[:, at : at + rows * PATCH_FEAT].reshape(D, PATCH_FEAT)
    at += rows * PATCH_FEAT
    numbers = spread_all[:, at : at + 4 * count].astype(jnp.float32)
    numbers = numbers[:, : 2 * count] * 32.0 + numbers[:, 2 * count :]
    numbers = numbers.reshape(sizes + (2 * count,)).transpose(3, 2, 1, 0, 4)
    numbers = numbers.reshape(count_all, 2 * count)
    steps_all = numbers[:, :count].reshape(image_total)
    labels_all = numbers[:, count:].reshape(image_total).astype(jnp.int32)

    table_qk = gather_bulk(grid, in_bf[:, : 2 * D], PLANS[0])
    table_vo = gather_bulk(grid, in_bf[:, 2 * D : 4 * D], PLANS[1])
    half = FF // 2
    up_parts = (
        gather_bulk(grid, in_bf[:, 4 * D : 4 * D + half], PLANS[2]),
        gather_bulk(grid, in_bf[:, 4 * D + half : 4 * D + FF], PLANS[3]),
    )
    down_parts = (
        gather_bulk(grid, down_bf[:, : D // 2], PLANS[4]),
        gather_bulk(grid, down_bf[:, D // 2 :], PLANS[5]),
    )
    w_value, w_out = table_vo[:, :D], table_vo[:, D:]

    b_query = bias_full[:D]
    b_value = bias_full[D : 2 * D]
    b_out = bias_full[2 * D : 3 * D]
    b_up = bias_full[3 * D : 3 * D + FF]
    b_down = bias_full[3 * D + FF : 4 * D + FF]
    b_mods = bias_full[4 * D + FF : 12 * D + FF]
    b_tfirst = lax.dynamic_slice_in_dim(bias_full[12 * D + FF : 13 * D + FF], my_rows, rows)
    b_time = lax.dynamic_slice_in_dim(bias_full[13 * D + FF : 14 * D + FF], my_rows, rows)
    b_patch = bias_full[14 * D + FF :]

    feats = time_features(steps_all).astype(bf16)
    time_pre = dot_tail(t_first, feats) + b_tfirst[:, None]
    time_act = jax.nn.silu(time_pre).astype(bf16)
    onehot = labels_all[:, None] == jnp.arange(CLASSES, dtype=jnp.int32)[None, :]
    cond_part = lax.dot_general(
        w_time, time_act, (((0,), (0,)), ((), ())), preferred_element_type=jnp.float32
    )
    cond = scatter_small(grid, cond_part.reshape(sizes + (rows, image_total)))
    cond = cond + b_time[:, None] + dot_tail(w_class, onehot.astype(bf16))
    cond_act = jax.nn.silu(cond).astype(bf16)

    def scatter_mods(part):
        shape = (sizes[3], sizes[2], sizes[1], sizes[0] * count, part.shape[1])
        part = part.reshape(shape)
        for axis in (3, 2, 1):
            part = scatter_axis(grid, part, axis, 0)
        part = part.reshape(sizes[0], count * part.shape[1] // 128, 128)
        return scatter_axis(grid, part, 0, 0).reshape(count, -1)

    mods_first = scatter_mods(dot_head(cond_act, w_mods[:, : 2 * D])) + b_mods[: 2 * D]
    mods_later = scatter_mods(dot_head(cond_act, w_mods[:, 2 * D :])) + b_mods[2 * D :]
    shift_a, scale_a = mods_first[:, :D], mods_first[:, D:]
    gate_a, shift_b, scale_b, gate_b, shift_f, scale_f = jnp.split(mods_later, 6, axis=1)

    signal, spread = noise_scales(timesteps)
    noise_rows = noise_draw.astype(jnp.float32)
    noisy = signal[:, None, None] * latents.astype(jnp.float32) + spread[:, None, None] * noise_rows
    noisy = noisy.astype(bf16).reshape(rows_all, PATCH_FEAT)
    hidden = dot_tail(noisy, w_patch) + b_patch + jnp.tile(positions(), (count, 1))
    resid_in = hidden.reshape(count, TOK, D)
    normed_a = modulate(resid_in, shift_a, scale_a).astype(bf16).reshape(rows_all, D)
    head_shape = (count, TOK, HEADS, HEAD_DIM)
    proj_qk = matmul(normed_a, table_qk)
    queries = (proj_qk[:, :D] + b_query).astype(bf16).reshape(head_shape)
    keys_all = proj_qk[:, D:].astype(bf16).reshape(head_shape)
    values_all = (matmul(normed_a, w_value) + b_value).astype(bf16).reshape(head_shape)
    scores = attention_scores(queries, keys_all)
    log_total = jax.nn.logsumexp(scores, axis=-1)
    probs = jnp.exp(scores - log_total[..., None]).astype(bf16)
    mixed = jnp.einsum("bhqk,bkhd->bqhd", probs, values_all, preferred_element_type=jnp.float32)
    mixed = mixed.astype(bf16).reshape(rows_all, D)
    attended = (matmul(mixed, w_out) + b_out).reshape(count, TOK, D)
    resid_mid = resid_in + gate_a[:, None, :] * attended
    normed_b = modulate(resid_mid, shift_b, scale_b).astype(bf16).reshape(rows_all, D)
    uppers = [
        matmul(normed_b, part) + b_up[index * half : (index + 1) * half]
        for index, part in enumerate(up_parts)
    ]
    actives = [jax.nn.gelu(upper, approximate=True).astype(bf16) for upper in uppers]
    active = jnp.concatenate(actives, axis=1)
    lowered = jnp.concatenate([matmul(active, part) for part in down_parts], axis=1) + b_down
    lowered = lowered.reshape(count, TOK, D)
    resid_out = resid_mid + gate_b[:, None, :] * lowered
    normed_c = modulate(resid_out, shift_f, scale_f).astype(bf16).reshape(rows_all, D)
    predicted = matmul(normed_c, w_head)
    error = predicted - noise_rows.reshape(rows_all, PATCH_FEAT)
    loss_local = jnp.sum(error * error)
    grad_pred = (2.0 / image_total * error).astype(bf16)

    grad_head = dot_head(normed_c, grad_pred)
    grad_normed_c = dot_tail(grad_pred, w_head).reshape(count, TOK, D)
    _, pull_final = jax.vjp(modulate, resid_out, shift_f, scale_f)
    grad_out, grad_shift_f, grad_scale_f = pull_final(grad_normed_c)
    grad_gate_b = jnp.sum(grad_out * lowered, axis=1)
    grad_lowered = (grad_out * gate_b[:, None, :]).reshape(rows_all, D)
    grad_b_down = jnp.sum(grad_lowered, axis=0)
    lowered_bf = grad_lowered.astype(bf16)
    sum_down = [
        scatter_bulk(grid, dot_head(active, part).astype(bf16), PLANS[4 + index])
        for index, part in enumerate(jnp.split(lowered_bf, 2, axis=1))
    ]
    grad_active = dot_tail(lowered_bf[:, : D // 2], down_parts[0]) + dot_tail(
        lowered_bf[:, D // 2 :], down_parts[1]
    )
    gelu = partial(jax.nn.gelu, approximate=True)
    grad_uppers = [
        jax.vjp(gelu, upper)[1](grad_active[:, index * half : (index + 1) * half])[0]
        for index, upper in enumerate(uppers)
    ]
    grad_b_up = jnp.concatenate([jnp.sum(part, axis=0) for part in grad_uppers])
    upper_bf = [part.astype(bf16) for part in grad_uppers]
    sum_up = [
        scatter_bulk(grid, dot_head(normed_b, part).astype(bf16), PLANS[2 + index])
        for index, part in enumerate(upper_bf)
    ]
    grad_normed_b = (
        dot_tail(upper_bf[0], up_parts[0]) + dot_tail(upper_bf[1], up_parts[1])
    ).reshape(count, TOK, D)
    _, pull_mid = jax.vjp(modulate, resid_mid, shift_b, scale_b)
    grad_mid_norm, grad_shift_b, grad_scale_b = pull_mid(grad_normed_b)
    grad_mid = grad_out + grad_mid_norm
    grad_gate_a = jnp.sum(grad_mid * attended, axis=1)
    grad_attended = (grad_mid * gate_a[:, None, :]).reshape(rows_all, D)
    grad_b_out = jnp.sum(grad_attended, axis=0)
    attended_bf = grad_attended.astype(bf16)
    grad_w_out = dot_head(mixed, attended_bf)
    grad_mixed = dot_tail(attended_bf, w_out).astype(bf16).reshape(head_shape)
    scores = attention_scores(queries, keys_all)
    probs_full = jnp.exp(scores - log_total[..., None])
    grad_probs = jnp.einsum(
        "bqhd,bkhd->bhqk", grad_mixed, values_all, preferred_element_type=jnp.float32
    )
    inner = jnp.sum(probs_full * grad_probs, axis=-1, keepdims=True)
    grad_scores = (probs_full * (grad_probs - inner)).astype(bf16)
    scale = HEAD_DIM ** (-0.5)
    grad_queries = (
        jnp.einsum("bhqk,bkhd->bqhd", grad_scores, keys_all, preferred_element_type=jnp.float32)
        * scale
    ).reshape(rows_all, D)
    grad_keys = (
        jnp.einsum("bhqk,bqhd->bkhd", grad_scores, queries, preferred_element_type=jnp.float32)
        * scale
    ).reshape(rows_all, D)
    grad_values = jnp.einsum(
        "bhqk,bqhd->bkhd", probs_full.astype(bf16), grad_mixed, preferred_element_type=jnp.float32
    ).reshape(rows_all, D)
    grad_b_query = jnp.sum(grad_queries, axis=0)
    grad_b_value = jnp.sum(grad_values, axis=0)
    qk_bf = jnp.concatenate([grad_queries, grad_keys], axis=1).astype(bf16)
    values_bf = grad_values.astype(bf16)
    sum_vo = scatter_bulk(
        grid,
        jnp.concatenate([dot_head(normed_a, values_bf), grad_w_out], axis=1).astype(bf16),
        PLANS[1],
    )
    sum_qk = scatter_bulk(grid, dot_head(normed_a, qk_bf).astype(bf16), PLANS[0])
    grad_normed_a = (dot_tail(qk_bf, table_qk) + dot_tail(values_bf, w_value)).reshape(
        count, TOK, D
    )
    _, pull_first = jax.vjp(modulate, resid_in, shift_a, scale_a)
    grad_in_norm, grad_shift_a, grad_scale_a = pull_first(grad_normed_a)
    grad_hidden = (grad_mid + grad_in_norm).reshape(rows_all, D)
    grad_b_patch = jnp.sum(grad_hidden, axis=0)
    grad_w_patch = dot_head(grad_hidden.astype(bf16), noisy)

    grad_mods = jnp.concatenate(
        [
            grad_shift_a,
            grad_scale_a,
            grad_gate_a,
            grad_shift_b,
            grad_scale_b,
            grad_gate_b,
            grad_shift_f,
            grad_scale_f,
        ],
        axis=1,
    )
    grad_b_mods = jnp.sum(grad_mods, axis=0)
    mods_bf = gather_small(grid, grad_mods.astype(bf16).reshape(-1, 128), (0, 1, 2, 3))
    mods_bf = mods_bf.reshape(image_total, 8 * D)
    grad_w_mods = matmul(cond_act, mods_bf)
    grad_cond_act = dot_tail(w_mods, mods_bf)
    grad_cond = jax.vjp(jax.nn.silu, cond)[1](grad_cond_act)[0]
    grad_w_class = jnp.dot(
        grad_cond,
        onehot.astype(jnp.float32),
        precision=lax.Precision.HIGHEST,
        preferred_element_type=jnp.float32,
    )
    grad_b_time = jnp.sum(grad_cond, axis=1)
    cond_bf = gather_small(grid, grad_cond.astype(bf16), (3, 2, 1, 0)).reshape(D, image_total)
    grad_w_time = dot_tail(time_act, cond_bf)
    grad_time_act = matmul(w_time, cond_bf)
    grad_time_pre = jax.vjp(jax.nn.silu, time_pre)[1](grad_time_act)[0]
    grad_b_tfirst = jnp.sum(grad_time_pre, axis=1)
    grad_t_first = matmul(grad_time_pre.astype(bf16), feats)

    def spread_rows(part):
        return lax.dynamic_update_slice(jnp.zeros((D,), jnp.float32), part, (my_rows,))

    grad_bias = jnp.concatenate(
        [
            grad_b_query,
            grad_b_value,
            grad_b_out,
            grad_b_up,
            grad_b_down,
            grad_b_mods,
            spread_rows(grad_b_tfirst),
            spread_rows(grad_b_time),
            grad_b_patch,
        ]
    )
    small = jnp.concatenate(
        [
            grad_bias.reshape(count_all, bias_rows),
            grad_w_patch.reshape(count_all, rows * PATCH_FEAT),
            grad_head.reshape(count_all, rows * PATCH_FEAT),
        ],
        axis=1,
    )
    tall = -(-small.shape[1] // 1024) * 8
    small = jnp.pad(small, ((0, 0), (0, tall * 128 - small.shape[1])))
    small = scatter_small(grid, small.reshape(sizes + (tall, 128))).reshape(-1)
    at = bias_rows
    sum_patch = small[at : at + rows * PATCH_FEAT].reshape(rows, PATCH_FEAT)
    at += rows * PATCH_FEAT
    sum_head = small[at : at + rows * PATCH_FEAT].reshape(rows, PATCH_FEAT)

    reduced = (
        jnp.concatenate([sum_qk, sum_vo, *sum_up, grad_w_mods, grad_w_time], axis=1),
        jnp.concatenate(sum_down, axis=1),
        jnp.concatenate([grad_t_first, sum_patch, grad_w_class, sum_head], axis=1),
        small[:bias_rows],
    )
    firsts = (first_in, first_down, first_side, first_bias)
    seconds = (second_in, second_down, second_side, second_bias)
    results = [
        adam_direction(masters[index], reduced[index], firsts[index], seconds[index])
        for index in range(4)
    ]
    directions = [item[2] for item in results]
    early = sum_small(grid, jnp.concatenate([loss_local[None], block_squares(masters)]))
    loss_sum, weight_sq = early[0], early[1:]
    update_sq = sum_small(grid, block_squares(directions))
    weight_norms = jnp.sqrt(weight_sq)
    update_norms = jnp.sqrt(update_sq)
    trust = weight_norms / update_norms
    factors = block_factors(trust)
    updated = [masters[index] - RATE * factors[index] * directions[index] for index in range(4)]
    return (
        loss_sum,
        updated[0],
        updated[1],
        updated[2],
        updated[3],
        results[0][0],
        results[1][0],
        results[2][0],
        results[3][0],
        results[0][1],
        results[1][1],
        results[2][1],
        results[3][1],
        trust,
        weight_norms,
        update_norms,
    )


def solution(mesh):
    placed = (
        P("fsdp", None, None),
        P("fsdp", None, None),
        P("fsdp"),
        P("fsdp"),
        P("fsdp", None),
        P("fsdp", None),
        P("fsdp", None),
        P("fsdp"),
        P("fsdp", None),
        P("fsdp", None),
        P("fsdp", None),
        P("fsdp"),
        P("fsdp", None),
        P("fsdp", None),
        P("fsdp", None),
        P("fsdp"),
    )
    return jax.shard_map(
        per_device,
        mesh=mesh,
        in_specs=placed,
        out_specs=(
            P(),
            P("fsdp", None),
            P("fsdp", None),
            P("fsdp", None),
            P("fsdp"),
            P("fsdp", None),
            P("fsdp", None),
            P("fsdp", None),
            P("fsdp"),
            P("fsdp", None),
            P("fsdp", None),
            P("fsdp", None),
            P("fsdp"),
            P(),
            P(),
            P(),
        ),
        check_vma=False,
    )
```

time: 1810 us -> 1540 us (0.85)
  waiting for transfers between devices: 1150 us -> 214 us
  Pallas kernels: 0 us -> 775 us
  starting transfers between devices: 0.91 us -> 181 us
  matrix products: 221 us -> 104 us
  blocking collectives: 89.8 us -> 0 us
  other arithmetic: 178 us -> 117 us
    reduce_scatter x3 -> x0, waiting for transfers between devices: 899 us -> none  [the longest x1 738 us: per_device(): lax.psum_scatter(packed_in, 'fsdp', scatter_dimension=0, tiled=True)]
    pallas_call x0 -> x6, Pallas kernels: none -> 775 us  [gather_bulk(): pl.pallas_call(partial(place_kernel, moves), out_shape=jax.ShapeDtypeStru...]
    all_gather x3 -> x0, waiting for transfers between devices: 252 us -> none  [the longest x1 200 us: fetch(): lax.all_gather(shards[0], 'fsdp', axis=0, tiled=True)]
    ppermute x0 -> x172, waiting for transfers between devices: none -> 214 us  [the longest x162 208 us: ahead(): return lax.ppermute(values, AXIS, pairs)]
    ppermute x0 -> x172, starting transfers between devices: none -> 181 us  [the longest x162 169 us: ahead(): return lax.ppermute(values, AXIS, pairs)]
    add x2 -> x3, local copies, waits for them, and re-layouts: 83.3 us -> 0.04 us  [layer_norm(): jnp.mean(center * center, axis=-1, keepdims=True) + NORM_EPS]
    add x9 -> x31, other arithmetic: 78.9 us -> 7.39 us  [the longest x15 5.88 us: scatter_axis(): total = total + grid.ahead(entry(-shift), axis, shift)]
    psum x1 -> x0, blocking collectives: 47.2 us -> none  [per_device(): lax.psum((loss_local, block_squares(masters), update_local), 'fsdp')]
  transfers between devices with their start and end apart: 7 -> 172, of which waited for: 5 -> 62; matrix products, arithmetic and copies ran while one was open for 19% -> 14% of each run, Pallas kernels for 0% -> 42%
where the time goes in v1:
time: 1540 us; the launch traced here: 1530 us
  Pallas kernels  775 us (50%)
  waiting for transfers between devices  214 us (14%)
  starting transfers between devices  181 us (12%)
  local copies, waits for them, and re-layouts  128 us (8%)
  other arithmetic  117 us (8%)
  matrix products  104 us (7%)
    pallas_call x6, Pallas kernels, gather_bulk(): pl.pallas_call(partial(place_kernel, moves), out_shape=jax.ShapeDtypeStru...  775 us
    ppermute x162, waiting for transfers between devices, ahead(): return lax.ppermute(values, AXIS, pairs)  208 us
    ppermute x162, starting transfers between devices, ahead(): return lax.ppermute(values, AXIS, pairs)  169 us
    dot_general x11, matrix products, matmul(): return jnp.dot(left, right, preferred_element_type=jnp.float32)  34.3 us
  transfers between devices with their start and end apart: 172, of which 62 were waited for; matrix products, arithmetic and copies ran while one was open for 14% of the time, Pallas kernels for 42%

profile of v1, /device:TPU:0, one launch (start us, length us, event | category | flops | bytes accessed | tf_op | source)
XLA Modules:
  0.0 1525.2 jit_solution(11860748149869785365)
XLA Ops:
  45.8 5.7 collective-permute-done.5
  129.1 5.8 collective-permute-done.32.refs_8_
  173.8 5.8 collective-permute-start.78
  223.8 129.2 %shard_map.279 = bf16[4,2,2,2,32,2048]{5,4,3,2,1,0:T(8,128)(2,1)} custom-call(s32[10]{0:T(128)} %stack.387.where, bf16[2,32,2048]{2,1,0:T(8,128)(2,1)} %copy-done.70, bf16[2,32,2048]{2,1,0:T(8,128)(2,1)} %copy-done.98, bf16[2,32,2048]{2,1,0:T(8,128)(2,1)} %copy-done.97, bf16[2,32,2048]{2,1,0:T(8,128)(2,1)} %copy-done.108, bf16[2,32,2048]{2,1,0:T(8,128)(2,1)} %copy-done.96, ...), custom_call_target="tpu_custom_call" | custom-call | bytes 8388608 | tf_op jit(solution)/shard_map/pallas_call | solution.py:268
  367.7 129.1 %shard_map.281 = bf16[4,2,2,2,32,2048]{5,4,3,2,1,0:T(8,128)(2,1)} custom-call(s32[10]{0:T(128)} %stack.387.where, bf16[2,32,2048]{2,1,0:T(8,128)(2,1)} %copy-done.67, bf16[2,32,2048]{2,1,0:T(8,128)(2,1)} %copy-done.90, bf16[2,32,2048]{2,1,0:T(8,128)(2,1)} %copy-done.89, bf16[2,32,2048]{2,1,0:T(8,128)(2,1)} %copy-done.102, bf16[2,32,2048]{2,1,0:T(8,128)(2,1)} %copy-done.88, ...), custom_call_target="tpu_custom_call" | custom-call | bytes 8388608 | tf_op jit(solution)/shard_map/pallas_call | solution.py:268
  496.8 129.1 %shard_map.282 = bf16[4,2,2,2,32,2048]{5,4,3,2,1,0:T(8,128)(2,1)} custom-call(s32[10]{0:T(128)} %stack.387.where, bf16[2,32,2048]{2,1,0:T(8,128)(2,1)} %copy-done.68, bf16[2,32,2048]{2,1,0:T(8,128)(2,1)} %copy-done.94, bf16[2,32,2048]{2,1,0:T(8,128)(2,1)} %copy-done.93, bf16[2,32,2048]{2,1,0:T(8,128)(2,1)} %copy-done.106, bf16[2,32,2048]{2,1,0:T(8,128)(2,1)} %copy-done.91, ...), custom_call_target="tpu_custom_call" | custom-call | bytes 8388608 | tf_op jit(solution)/shard_map/pallas_call | solution.py:268
  626.0 129.1 %shard_map.283 = bf16[4,2,2,2,128,512]{5,4,3,2,1,0:T(8,128)(2,1)} custom-call(s32[10]{0:T(128)} %stack.387.where, bf16[2,128,512]{2,1,0:T(8,128)(2,1)} %copy-done.69, bf16[2,128,512]{2,1,0:T(8,128)(2,1)} %copy-done.95, bf16[2,128,512]{2,1,0:T(8,128)(2,1)} %collective-permute-done.84.refs_2_, bf16[2,128,512]{2,1,0:T(8,128)(2,1)} %collective-permute-done.85.refs_3_, ...), custom_call_target="tpu_custom_call" | custom-call | bytes 8388608 | tf_op jit(solution)/shard_map/pallas_call | solution.py:268
  759.4 11.6 collective-permute-done.102.refs_2_
  771.5 9.2 collective-permute-done.106.refs_6_
  780.7 129.1 %shard_map.280 = bf16[4,2,2,2,32,2048]{5,4,3,2,1,0:T(8,128)(2,1)} custom-call(s32[10]{0:T(128)} %stack.387.where, bf16[4,32,2048]{2,1,0:T(8,128)(2,1)} %pad_maximum_fusion.3.refs_0_, bf16[4,32,2048]{2,1,0:T(8,128)(2,1)} %collective-permute-done.43.refs_1_, bf16[4,32,2048]{2,1,0:T(8,128)(2,1)} %collective-permute-done.44.refs_2_, ...), custom_call_target="tpu_custom_call" | custom-call | bytes 8388608 | tf_op jit(solution)/shard_map/pallas_call | solution.py:268
  948.3 5.3 multiply_convert_fusion.2
  953.6 5.3 multiply_convert_fusion.1
  962.3 129.1 %shard_map.284 = bf16[4,2,2,2,128,512]{5,4,3,2,1,0:T(8,128)(2,1)} custom-call(s32[10]{0:T(128)} %stack.387.where, bf16[4,128,512]{2,1,0:T(8,128)(2,1)} %pad_maximum_fusion.4.refs_0_, bf16[4,128,512]{2,1,0:T(8,128)(2,1)} %collective-permute-done.101.refs_1_, bf16[4,128,512]{2,1,0:T(8,128)(2,1)} %collective-permute-done.102.refs_2_, ...), custom_call_target="tpu_custom_call" | custom-call | bytes 8388608 | tf_op jit(solution)/shard_map/pallas_call | solution.py:268
  1091.5 5.9 fusion.155
  1119.5 9.0 fusion.165
  1157.1 5.2 multiply_reduce_fusion
  1196.1 5.9 convolution_convert_fusion.2
  1241.5 5.9 collective-permute-done.141
  1330.3 8.9 collective-permute-done.132
  1344.1 17.6 %collective-permute-done.120 = bf16[4,2,1,1,32,2048]{5,4,3,2,1,0:T(8,128)(2,1)S(1)} collective-permute-done((bf16[4,2,1,1,32,2048]{5,4,3,2,1,0:T(8,128)(2,1)S(1)}, bf16[4,2,1,1,32,2048]{5,4,3,2,1,0:T(8,128)(2,1)S(1)}, u32[]{:S(2)}, u32[]{:S(2)}) %collective-permute-start.120) | collective-permute-done | bytes 1048608 | tf_op jit(solution)/shard_map/ppermute | solution.py:163
  1366.6 19.4 %collective-permute-done.150 = bf16[4,1,2,1,128,512]{5,4,3,2,1,0:T(8,128)(2,1)S(1)} collective-permute-done((bf16[4,1,2,1,128,512]{5,4,3,2,1,0:T(8,128)(2,1)S(1)}, bf16[4,1,2,1,128,512]{5,4,3,2,1,0:T(8,128)(2,1)S(1)}, u32[]{:S(2)}, u32[]{:S(2)}) %collective-permute-start.150) | collective-permute-done | bytes 1048608 | tf_op jit(solution)/shard_map/ppermute | solution.py:163
  1428.6 19.6 %collective-permute-done.117 = bf16[1,1,1,1,32,2048]{5,4,3,2,1,0:T(8,128)(2,1)S(1)} collective-permute-done((bf16[1,1,1,1,32,2048]{5,4,3,2,1,0:T(8,128)(2,1)S(1)}, bf16[1,1,1,1,32,2048]{5,4,3,2,1,0:T(8,128)(2,1)S(1)}, u32[]{:S(2)}, u32[]{:S(2)}) %collective-permute-start.117) | collective-permute-done | bytes 131104 | tf_op jit(solution)/shard_map/ppermute | solution.py:163
  1474.8 7.6 stack.461
  1482.5 8.2 concatenate.79
  (1092 shorter events, 582.5 us)
Async XLA Ops:
  3.6 61.2 %collective-permute-start.50 = (bf16[32,2048]{1,0:T(8,128)(2,1)}, bf16[32,2048]{1,0:T(8,128)(2,1)}, u32[]{:S(2)}, u32[]{:S(2)}) collective-permute-start(bf16[32,2048]{1,0:T(8,128)(2,1)} %get-tuple-element.82), channel_id=1, source_target_pairs={{0,2},{1,3},{2,0},{3,1},{4,6},{5,7},{6,4},{7,5},{8,10},{9,11},{10,... | collective-permute-start | bytes 393224 | tf_op jit(solution)/shard_map/ppermute | solution.py:163
  6.6 69.1 %collective-permute-start.40 = (bf16[32,2048]{1,0:T(8,128)(2,1)}, bf16[32,2048]{1,0:T(8,128)(2,1)}, u32[]{:S(2)}, u32[]{:S(2)}) collective-permute-start(bf16[32,2048]{1,0:T(8,128)(2,1)} %get-tuple-element.83), channel_id=1, source_target_pairs={{0,24},{1,25},{2,26},{3,27},{4,28},{5,29},{6,30},{7,31},{8,0},{9,1... | collective-permute-start | bytes 393224 | tf_op jit(solution)/shard_map/ppermute | solution.py:163
  16.4 51.1 %collective-permute-start.24 = (bf16[32,2048]{1,0:T(8,128)(2,1)}, bf16[32,2048]{1,0:T(8,128)(2,1)}, u32[]{:S(2)}, u32[]{:S(2)}) collective-permute-start(bf16[32,2048]{1,0:T(8,128)(2,1)} %get-tuple-element.84), channel_id=1, source_target_pairs={{0,4},{1,5},{2,6},{3,7},{4,0},{5,1},{6,2},{7,3},{8,12},{9,13},{10,... | collective-permute-start | bytes 393224 | tf_op jit(solution)/shard_map/ppermute | solution.py:163
  18.0 56.7 %collective-permute-start.66 = (bf16[32,2048]{1,0:T(8,128)(2,1)}, bf16[32,2048]{1,0:T(8,128)(2,1)}, u32[]{:S(2)}, u32[]{:S(2)}) collective-permute-start(bf16[32,2048]{1,0:T(8,128)(2,1)} %get-tuple-element.81), channel_id=1, source_target_pairs={{0,4},{1,5},{2,6},{3,7},{4,0},{5,1},{6,2},{7,3},{8,12},{9,13},{10,... | collective-permute-start | bytes 393224 | tf_op jit(solution)/shard_map/ppermute | solution.py:163
  214.9 138.2 %collective-permute-start.65 = (bf16[2,32,2048]{2,1,0:T(8,128)(2,1)}, bf16[2,32,2048]{2,1,0:T(8,128)(2,1)}, u32[]{:S(2)}, u32[]{:S(2)}) collective-permute-start(bf16[2,32,2048]{2,1,0:T(8,128)(2,1)} %collective-permute-done.64.refs_14_), channel_id=1, source_target_pairs={{0,1},{1,0},{2,3},{3,2},{4,5},{5,4},{6,7},{7,6},{8,9},{9,8},{10,11... | collective-permute-start | bytes 786440 | tf_op jit(solution)/shard_map/ppermute | solution.py:163
  218.6 134.8 %collective-permute-start.81 = (bf16[2,32,2048]{2,1,0:T(8,128)(2,1)}, bf16[2,32,2048]{2,1,0:T(8,128)(2,1)}, u32[]{:S(2)}, u32[]{:S(2)}) collective-permute-start(bf16[2,32,2048]{2,1,0:T(8,128)(2,1)} %copy-done.119), channel_id=1, source_target_pairs={{0,1},{1,0},{2,3},{3,2},{4,5},{5,4},{6,7},{7,6},{8,9},{9,8},{10,11... | collective-permute-start | bytes 786440 | tf_op jit(solution)/shard_map/ppermute | solution.py:163
  218.6 134.8 %collective-permute-start.97 = (bf16[2,128,512]{2,1,0:T(8,128)(2,1)}, bf16[2,128,512]{2,1,0:T(8,128)(2,1)}, u32[]{:S(2)}, u32[]{:S(2)}) collective-permute-start(bf16[2,128,512]{2,1,0:T(8,128)(2,1)} %collective-permute-done.96.refs_14_), channel_id=1, source_target_pairs={{0,1},{1,0},{2,3},{3,2},{4,5},{5,4},{6,7},{7,6},{8,9},{9,8},{10,11... | collective-permute-start | bytes 786440 | tf_op jit(solution)/shard_map/ppermute | solution.py:163
  219.8 135.5 %collective-permute-start.15 = (f32[96,128]{1,0:T(8,128)}, f32[96,128]{1,0:T(8,128)}, u32[]{:S(2)}, u32[]{:S(2)}) collective-permute-start(f32[96,128]{1,0:T(8,128)} %get-tuple-element.95), channel_id=1, source_target_pairs={{0,24},{1,25},{2,26},{3,27},{4,28},{5,29},{6,30},{7,31},{8,0},{9,1... | collective-permute-start | bytes 147464 | tf_op jit(solution)/shard_map/ppermute | solution.py:163
  221.8 133.7 %collective-permute-start.16 = (f32[96,128]{1,0:T(8,128)S(1)}, f32[96,128]{1,0:T(8,128)}, u32[]{:S(2)}, u32[]{:S(2)}) collective-permute-start(f32[96,128]{1,0:T(8,128)S(1)} %get-tuple-element.97), channel_id=1, source_target_pairs={{0,16},{1,17},{2,18},{3,19},{4,20},{5,21},{6,22},{7,23},{8,24},{9,... | collective-permute-start | bytes 147464 | tf_op jit(solution)/shard_map/ppermute | solution.py:163
  353.1 404.3 %collective-permute-start.44 = (bf16[4,32,2048]{2,1,0:T(8,128)(2,1)}, bf16[4,32,2048]{2,1,0:T(8,128)(2,1)}, u32[]{:S(2)}, u32[]{:S(2)}) collective-permute-start(bf16[4,32,2048]{2,1,0:T(8,128)(2,1)} %pad_maximum_fusion.3.refs_0_), channel_id=1, source_target_pairs={{0,4},{1,5},{2,6},{3,7},{4,0},{5,1},{6,2},{7,3},{8,12},{9,13},{10,... | collective-permute-start | bytes 1572872 | tf_op jit(solution)/shard_map/ppermute | solution.py:163
  353.4 404.1 %collective-permute-start.43 = (bf16[4,32,2048]{2,1,0:T(8,128)(2,1)}, bf16[4,32,2048]{2,1,0:T(8,128)(2,1)}, u32[]{:S(2)}, u32[]{:S(2)}) collective-permute-start(bf16[4,32,2048]{2,1,0:T(8,128)(2,1)} %pad_maximum_fusion.3.refs_0_), channel_id=1, source_target_pairs={{0,1},{1,0},{2,3},{3,2},{4,5},{5,4},{6,7},{7,6},{8,9},{9,8},{10,11... | collective-permute-start | bytes 1572872 | tf_op jit(solution)/shard_map/ppermute | solution.py:163
  353.5 404.5 %collective-permute-start.104 = (bf16[4,128,512]{2,1,0:T(8,128)(2,1)}, bf16[4,128,512]{2,1,0:T(8,128)(2,1)}, u32[]{:S(2)}, u32[]{:S(2)}) collective-permute-start(bf16[4,128,512]{2,1,0:T(8,128)(2,1)} %pad_maximum_fusion.4.refs_0_), channel_id=1, source_target_pairs={{0,4},{1,5},{2,6},{3,7},{4,0},{5,1},{6,2},{7,3},{8,12},{9,13},{10,... | collective-permute-start | bytes 1572872 | tf_op jit(solution)/shard_map/ppermute | solution.py:163
  355.3 404.0 %collective-permute-start.48 = (bf16[4,32,2048]{2,1,0:T(8,128)(2,1)}, bf16[4,32,2048]{2,1,0:T(8,128)(2,1)}, u32[]{:S(2)}, u32[]{:S(2)}) collective-permute-start(bf16[4,32,2048]{2,1,0:T(8,128)(2,1)} %collective-permute-done.46.refs_4_), channel_id=1, source_target_pairs={{0,4},{1,5},{2,6},{3,7},{4,0},{5,1},{6,2},{7,3},{8,12},{9,13},{10,... | collective-permute-start | bytes 1572872 | tf_op jit(solution)/shard_map/ppermute | solution.py:163
  355.6 399.6 %collective-permute-start.17 = (f32[96,128]{1,0:T(8,128)S(1)}, f32[96,128]{1,0:T(8,128)S(1)}, u32[]{:S(2)}, u32[]{:S(2)}) collective-permute-start(f32[96,128]{1,0:T(8,128)S(1)} %get-tuple-element.96), channel_id=1, source_target_pairs={{0,8},{1,9},{2,10},{3,11},{4,12},{5,13},{6,14},{7,15},{8,16},{9,17... | collective-permute-start | bytes 147464 | tf_op jit(solution)/shard_map/ppermute | solution.py:163
  770.9 191.4 %collective-permute-start.101 = (bf16[4,128,512]{2,1,0:T(8,128)(2,1)}, bf16[4,128,512]{2,1,0:T(8,128)(2,1)}, u32[]{:S(2)}, u32[]{:S(2)}) collective-permute-start(bf16[4,128,512]{2,1,0:T(8,128)(2,1)} %pad_maximum_fusion.4.refs_0_), channel_id=1, source_target_pairs={{0,1},{1,0},{2,3},{3,2},{4,5},{5,4},{6,7},{7,6},{8,9},{9,8},{10,11... | collective-permute-start | bytes 1572872 | tf_op jit(solution)/shard_map/ppermute | solution.py:163
  770.9 191.4 %collective-permute-start.105 = (bf16[4,128,512]{2,1,0:T(8,128)(2,1)}, bf16[4,128,512]{2,1,0:T(8,128)(2,1)}, u32[]{:S(2)}, u32[]{:S(2)}) collective-permute-start(bf16[4,128,512]{2,1,0:T(8,128)(2,1)} %collective-permute-done.104.refs_4_), channel_id=1, source_target_pairs={{0,1},{1,0},{2,3},{3,2},{4,5},{5,4},{6,7},{7,6},{8,9},{9,8},{10,11... | collective-permute-start | bytes 1572872 | tf_op jit(solution)/shard_map/ppermute | solution.py:163
  771.4 190.9 %collective-permute-start.103 = (bf16[4,128,512]{2,1,0:T(8,128)(2,1)}, bf16[4,128,512]{2,1,0:T(8,128)(2,1)}, u32[]{:S(2)}, u32[]{:S(2)}) collective-permute-start(bf16[4,128,512]{2,1,0:T(8,128)(2,1)} %collective-permute-done.102.refs_2_), channel_id=1, source_target_pairs={{0,1},{1,0},{2,3},{3,2},{4,5},{5,4},{6,7},{7,6},{8,9},{9,8},{10,11... | collective-permute-start | bytes 1572872 | tf_op jit(solution)/shard_map/ppermute | solution.py:163
  780.7 181.6 %collective-permute-start.107 = (bf16[4,128,512]{2,1,0:T(8,128)(2,1)}, bf16[4,128,512]{2,1,0:T(8,128)(2,1)}, u32[]{:S(2)}, u32[]{:S(2)}) collective-permute-start(bf16[4,128,512]{2,1,0:T(8,128)(2,1)} %collective-permute-done.106.refs_6_), channel_id=1, source_target_pairs={{0,1},{1,0},{2,3},{3,2},{4,5},{5,4},{6,7},{7,6},{8,9},{9,8},{10,11... | collective-permute-start | bytes 1572872 | tf_op jit(solution)/shard_map/ppermute | solution.py:163
  1220.7 88.4 %collective-permute-start.131 = (bf16[4,2,2,1,32,2048]{5,4,3,2,1,0:T(8,128)(2,1)}, bf16[4,2,2,1,32,2048]{5,4,3,2,1,0:T(8,128)(2,1)}, u32[]{:S(2)}, u32[]{:S(2)}) collective-permute-start(bf16[4,2,2,1,32,2048]{5,4,3,2,1,0:T(8,128)(2,1)} %constant_dynamic-slice_fusion.17), channel_id=1, source_target_pairs={{0,1},{1,0},{2,3},{3,2},{4,5},{5,4},{6,7},{7,6},{8,9},{9,8},{10,11... | collective-permute-start | bytes 6291464 | tf_op jit(solution)/shard_map/ppermute | solution.py:163
  1222.2 90.9 %collective-permute-start.125 = (bf16[4,2,2,1,32,2048]{5,4,3,2,1,0:T(8,128)(2,1)}, bf16[4,2,2,1,32,2048]{5,4,3,2,1,0:T(8,128)(2,1)}, u32[]{:S(2)}, u32[]{:S(2)}) collective-permute-start(bf16[4,2,2,1,32,2048]{5,4,3,2,1,0:T(8,128)(2,1)} %constant_dynamic-slice_fusion.21), channel_id=1, source_target_pairs={{0,1},{1,0},{2,3},{3,2},{4,5},{5,4},{6,7},{7,6},{8,9},{9,8},{10,11... | collective-permute-start | bytes 6291464 | tf_op jit(solution)/shard_map/ppermute | solution.py:163
  1328.1 57.9 %collective-permute-start.150 = (bf16[4,1,2,1,128,512]{5,4,3,2,1,0:T(8,128)(2,1)S(1)}, bf16[4,1,2,1,128,512]{5,4,3,2,1,0:T(8,128)(2,1)S(1)}, u32[]{:S(2)}, u32[]{:S(2)}) collective-permute-start(bf16[4,1,2,1,128,512]{5,4,3,2,1,0:T(8,128)(2,1)S(1)} %constant_dynamic-slice_fusion.10), channel_id=1, source_target_pairs={{0,4},{1,5},{2,6},{3,7},{4,0},{5,1},{6,2},{7,3},{8,12},{9,13},{10,... | collective-permute-start | bytes 3145736 | tf_op jit(solution)/shard_map/ppermute | solution.py:163
  1339.2 48.8 %collective-permute-start.156 = (bf16[4,2,1,1,128,512]{5,4,3,2,1,0:T(8,128)(2,1)S(1)}, bf16[4,2,1,1,128,512]{5,4,3,2,1,0:T(8,128)(2,1)S(1)}, u32[]{:S(2)}, u32[]{:S(2)}) collective-permute-start(bf16[4,2,1,1,128,512]{5,4,3,2,1,0:T(8,128)(2,1)S(1)} %constant_dynamic-slice_fusion.6), channel_id=1, source_target_pairs={{0,2},{1,3},{2,0},{3,1},{4,6},{5,7},{6,4},{7,5},{8,10},{9,11},{10,... | collective-permute-start | bytes 3145736 | tf_op jit(solution)/shard_map/ppermute | solution.py:163
  1342.2 47.6 %collective-permute-start.133 = (bf16[1,2,1,1,32,2048]{5,4,3,2,1,0:T(8,128)(2,1)S(1)}, bf16[1,2,1,1,32,2048]{5,4,3,2,1,0:T(8,128)(2,1)S(1)}, u32[]{:S(2)}, u32[]{:S(2)}) collective-permute-start(bf16[1,2,1,1,32,2048]{5,4,3,2,1,0:T(8,128)(2,1)S(1)} %constant_dynamic-slice_fusion.15), channel_id=1, source_target_pairs={{0,24},{1,25},{2,26},{3,27},{4,28},{5,29},{6,30},{7,31},{8,0},{9,1... | collective-permute-start | bytes 786440 | tf_op jit(solution)/shard_map/ppermute | solution.py:163
  1408.5 49.7 %collective-permute-start.135 = (bf16[1,2,1,1,32,2048]{5,4,3,2,1,0:T(8,128)(2,1)S(1)}, bf16[1,2,1,1,32,2048]{5,4,3,2,1,0:T(8,128)(2,1)S(1)}, u32[]{:S(2)}, u32[]{:S(2)}) collective-permute-start(bf16[1,2,1,1,32,2048]{5,4,3,2,1,0:T(8,128)(2,1)S(1)} %add_convert_fusion.19), channel_id=1, source_target_pairs={{0,24},{1,25},{2,26},{3,27},{4,28},{5,29},{6,30},{7,31},{8,0},{9,1... | collective-permute-start | bytes 786440 | tf_op jit(solution)/shard_map/ppermute | solution.py:163
  (334 other events, 4552.2 us)

commit v2 on v1

--- a/solution.py
+++ b/solution.py
@@ -107,7 +107,15 @@
         else:
             piece = arrays[kind]
         totals.append(jnp.sum(piece * piece))
-    return jnp.stack(totals)
+    return totals
+
+
+def as_vector(scalars):
+    places = jnp.arange(32, dtype=jnp.int32)
+    vector = jnp.zeros((32,), jnp.float32)
+    for index, value in enumerate(scalars):
+        vector = jnp.where(places == index, value, vector)
+    return vector
 
 
 def block_factors(trust):
@@ -137,38 +145,60 @@
     return (first_new, second_new, direction)
 
 
+Z_AXIS, Y_AXIS, X_AXIS, CORE, MIX_P, MIX_Q = range(6)
+
+
 class Grid:
     def __init__(self, count):
         if count == 32:
-            self.sizes = (4, 2, 2, 2)
+            sizes = (4, 2, 2, 2)
         elif count == 256:
-            self.sizes = (8, 4, 4, 2)
+            sizes = (8, 4, 4, 2)
         else:
-            self.sizes = (count, 1, 1, 1)
+            sizes = (count, 1, 1, 1)
         self.count = count
+        self.shape = sizes
+        self.sizes = sizes + (sizes[X_AXIS], sizes[Y_AXIS])
         index = lax.axis_index(AXIS)
+        self.coords = self.split(index)
+        mixed = [
+            jnp.where(self.coords[CORE] == 0, self.coords[X_AXIS], self.coords[Y_AXIS]),
+            jnp.where(self.coords[CORE] == 0, self.coords[Y_AXIS], self.coords[X_AXIS]),
+        ]
+        self.coords = self.coords + tuple(mixed)
+
+    def split(self, index):
         coords = []
-        for size in reversed(self.sizes):
+        for size in reversed(self.shape):
             coords.append(index % size)
             index = index // size
-        self.coords = tuple(reversed(coords))
-
-    def ahead(self, values, axis, shift):
-        stride = math.prod(self.sizes[axis + 1 :])
-        size = self.sizes[axis]
+        return tuple(reversed(coords))
+
+    def join(self, coords):
+        index = 0
+        for size, place in zip(self.shape, coords):
+            index = index * size + place
+        return index
+
+    def move(self, values, axis, change):
         pairs = []
         for source in range(self.count):
-            place = source // stride % size
-            pairs.append((source, source + ((place - shift) % size - place) * stride))
+            coords = list(self.split(source))
+            real = axis
+            if axis == MIX_P:
+                real = X_AXIS if coords[CORE] == 0 else Y_AXIS
+            if axis == MIX_Q:
+                real = Y_AXIS if coords[CORE] == 0 else X_AXIS
+            coords[real] = change(coords[real])
+            pairs.append((source, self.join(coords)))
         return lax.ppermute(values, AXIS, pairs)
 
+    def ahead(self, values, axis, shift):
+        size = self.sizes[axis]
+        return self.move(values, axis, lambda place: (place - shift) % size)
+
     def flip(self, values, axis, bit):
-        stride = math.prod(self.sizes[axis + 1 :])
-        pairs = []
-        for source in range(self.count):
-            place = source // stride % self.sizes[axis]
-            pairs.append((source, source + ((place ^ bit) - place) * stride))
-        return lax.ppermute(values, AXIS, pairs)
+        return self.move(values, axis, lambda place: place ^ bit)
 
     def place(self, axis, shift):
         return (self.coords[axis] + shift) % self.sizes[axis]
@@ -225,10 +255,11 @@
 def place_kernel(moves, where, *refs):
     pieces, full, sems = refs[:-2], refs[-2], refs[-1]
     copies = []
-    for number, (piece, entry, spot) in enumerate(moves):
-        place = tuple(where[slot] for slot in spot)
+    for number, (piece, entry) in enumerate(moves):
         copies.append(
-            pltpu.make_async_copy(pieces[piece].at[entry], full.at[place], sems.at[number])
+            pltpu.make_async_copy(
+                pieces[piece].at[entry], full.at[where[number]], sems.at[number]
+            )
         )
     for copy in copies:
         copy.start()
@@ -238,70 +269,74 @@
 
 def gather_bulk(grid, shard, order):
     rows, columns = shard.shape
-    first, second, third = order
-    sizes = grid.sizes
-    pieces = [shard]
-    for _ in range(1, sizes[first]):
-        pieces.append(grid.ahead(pieces[-1], first, 1))
-    tagged = [((), jnp.stack(pieces))]
-    for axis in (second, third, 3):
-        reached = []
-        for tag, piece in tagged:
-            reached.append((tag + (0,), piece))
-            for shift in range(1, sizes[axis]):
-                piece = grid.ahead(piece, axis, 1)
-                reached.append((tag + (shift,), piece))
-        tagged = reached
-    offsets = []
-    for axis in range(4):
-        offsets.append(sum(sizes[:axis]))
-    moves = []
-    for number, (tag, _) in enumerate(tagged):
-        for entry in range(sizes[first]):
-            shifts = {first: entry, second: tag[0], third: tag[1], 3: tag[2]}
-            spot = tuple(offsets[axis] + shifts[axis] for axis in range(4))
-            moves.append((number, entry, spot))
-    where = jnp.stack(
-        [grid.place(axis, shift) for axis in range(4) for shift in range(sizes[axis])]
+    parts = [shard]
+    for axis in order:
+        sent = jnp.stack(parts).reshape((-1, rows, columns))
+        parts = [sent]
+        for _ in range(1, grid.sizes[axis]):
+            parts.append(grid.ahead(parts[-1], axis, 1))
+    if grid.sizes[CORE] == 2:
+        parts = parts + [grid.ahead(part, CORE, 1) for part in parts]
+    dims = (grid.sizes[CORE],) + tuple(grid.sizes[axis] for axis in reversed(order))
+    number = jnp.arange(grid.count, dtype=jnp.int32)
+    shifts = {}
+    for axis, size in reversed(list(zip((CORE,) + tuple(reversed(order)), dims))):
+        shifts[axis] = number % size
+        number = number // size
+    core = (grid.coords[CORE] + shifts[CORE]) % grid.sizes[CORE]
+    x_ahead = jnp.where(core == 0, shifts[MIX_P], shifts[MIX_Q])
+    y_ahead = jnp.where(core == 0, shifts[MIX_Q], shifts[MIX_P])
+    where = grid.join(
+        (
+            (grid.coords[Z_AXIS] + shifts[Z_AXIS]) % grid.sizes[Z_AXIS],
+            (grid.coords[Y_AXIS] + y_ahead) % grid.sizes[Y_AXIS],
+            (grid.coords[X_AXIS] + x_ahead) % grid.sizes[X_AXIS],
+            core,
+        )
     ).astype(jnp.int32)
+    entries = parts[0].shape[0]
+    moves = [(piece, entry) for piece in range(len(parts)) for entry in range(entries)]
     if rows % 16 == 0:
         full = pl.pallas_call(
             partial(place_kernel, moves),
-            out_shape=jax.ShapeDtypeStruct(sizes + (rows, columns), shard.dtype),
+            out_shape=jax.ShapeDtypeStruct((grid.count, rows, columns), shard.dtype),
             in_specs=[pl.BlockSpec(memory_space=pltpu.SMEM)]
-            + [pl.BlockSpec(memory_space=pl.ANY)] * len(tagged),
-            out_specs=pl.BlockSpec(memory_space=pl.ANY),
+            + [pl.BlockSpec(memory_space=pl.ANY)] * len(parts),
+            out_specs=pl.BlockSpec(memory_space=pltpu.VMEM),
             scratch_shapes=[pltpu.SemaphoreType.DMA((len(moves),))],
+            compiler_params=pltpu.CompilerParams(vmem_limit_bytes=24 * 2**20),
             cost_estimate=pl.CostEstimate(
                 flops=0, bytes_accessed=4 * grid.count * rows * columns, transcendentals=0
             ),
-        )(where, *[piece for _, piece in tagged])
+        )(where, *parts)
     else:
-        full = jnp.zeros(sizes + (rows, columns), shard.dtype)
-        for number, entry, spot in moves:
-            place = tuple(where[slot] for slot in spot) + (0, 0)
-            block = tagged[number][1][entry].reshape((1, 1, 1, 1, rows, columns))
-            full = lax.dynamic_update_slice(full, block, place)
+        stacked = jnp.stack(parts).reshape((grid.count, rows, columns))
+        full = jnp.zeros((grid.count, rows, columns), shard.dtype).at[where].set(stacked)
     return full.reshape(grid.count * rows, columns)
 
 
 def scatter_bulk(grid, table, order):
     rows = table.shape[0] // grid.count
-    current = table.reshape(grid.sizes + (rows, table.shape[1]))
-    axes = (3,) + tuple(reversed(order))
-    for axis in axes:
+    current = table.reshape(grid.shape + (rows, table.shape[1]))
+    first = grid.coords[CORE] == 0
+
+    def entry(axis, shift):
+        place = grid.place(axis, shift)
+        if axis in (MIX_P, MIX_Q):
+            return lax.dynamic_index_in_dim(current, place, X_AXIS if axis == MIX_P else Y_AXIS)
+        return lax.dynamic_index_in_dim(current, place, axis)
+
+    for axis in (CORE,) + tuple(reversed(order)):
         size = grid.sizes[axis]
-
-        def entry(shift, current=current, axis=axis):
-            return lax.dynamic_index_in_dim(current, grid.place(axis, shift), axis)
-
-        total = entry(1)
+        total = entry(axis, 1)
         for step in range(1, size):
-            sent = grid.ahead(total.astype(jnp.bfloat16), axis, 1)
-            total = sent.astype(jnp.float32) + entry(1 + step).astype(jnp.float32)
-            if step < size - 1 or axis != axes[-1]:
+            sent = grid.ahead(total, axis, 1)
+            total = sent.astype(jnp.float32) + entry(axis, 1 + step).astype(jnp.float32)
+            if step < size - 1 or axis != order[0]:
                 total = total.astype(jnp.bfloat16)
         current = total
+        if axis == CORE:
+            current = jnp.where(first, current, jnp.swapaxes(current, Y_AXIS, X_AXIS))
     return current.reshape(rows, table.shape[1]).astype(jnp.float32)
 
 
@@ -310,11 +345,12 @@
     return scores * HEAD_DIM ** (-0.5)
 
 
-XZY = (2, 0, 1)
-YZX = (1, 0, 2)
-ZXY = (0, 2, 1)
-ZYX = (0, 1, 2)
-PLANS = (ZXY, YZX, XZY, YZX, XZY, ZYX)
+OUTER = (MIX_P, Z_AXIS, MIX_Q)
+DEEP = (Z_AXIS, MIX_P, MIX_Q)
+
+
+def after(values, *others):
+    return lax.optimization_barrier((values,) + others)[0]
 
 
 def per_device(
@@ -338,7 +374,7 @@
     bf16 = jnp.bfloat16
     count_all = lax.axis_size(AXIS)
     grid = Grid(count_all)
-    sizes = grid.sizes
+    sizes = grid.shape
     count = latents.shape[0]
     rows_all = count * TOK
     image_total = count * count_all
@@ -379,22 +415,17 @@
     at += rows * PATCH_FEAT
     numbers = spread_all[:, at : at + 4 * count].astype(jnp.float32)
     numbers = numbers[:, : 2 * count] * 32.0 + numbers[:, 2 * count :]
-    numbers = numbers.reshape(sizes + (2 * count,)).transpose(3, 2, 1, 0, 4)
-    numbers = numbers.reshape(count_all, 2 * count)
+    numbers = numbers.reshape(sizes + (2 * count,))
+    numbers = jnp.stack(
+        [numbers[:, :, :, core].transpose((1, 2, 0, 3) if core else (2, 1, 0, 3)) for core in range(sizes[CORE])]
+    ).reshape(count_all, 2 * count)
     steps_all = numbers[:, :count].reshape(image_total)
     labels_all = numbers[:, count:].reshape(image_total).astype(jnp.int32)
 
-    table_qk = gather_bulk(grid, in_bf[:, : 2 * D], PLANS[0])
-    table_vo = gather_bulk(grid, in_bf[:, 2 * D : 4 * D], PLANS[1])
-    half = FF // 2
-    up_parts = (
-        gather_bulk(grid, in_bf[:, 4 * D : 4 * D + half], PLANS[2]),
-        gather_bulk(grid, in_bf[:, 4 * D + half : 4 * D + FF], PLANS[3]),
-    )
-    down_parts = (
-        gather_bulk(grid, down_bf[:, : D // 2], PLANS[4]),
-        gather_bulk(grid, down_bf[:, D // 2 :], PLANS[5]),
-    )
+    table_qk = gather_bulk(grid, in_bf[:, : 2 * D], OUTER)
+    table_vo = gather_bulk(grid, in_bf[:, 2 * D : 4 * D], OUTER)
+    table_up = gather_bulk(grid, in_bf[:, 4 * D : 4 * D + FF], OUTER)
+    table_down = gather_bulk(grid, down_bf, DEEP)
     w_value, w_out = table_vo[:, :D], table_vo[:, D:]
 
     b_query = bias_full[:D]
@@ -418,18 +449,15 @@
     cond = cond + b_time[:, None] + dot_tail(w_class, onehot.astype(bf16))
     cond_act = jax.nn.silu(cond).astype(bf16)
 
-    def scatter_mods(part):
-        shape = (sizes[3], sizes[2], sizes[1], sizes[0] * count, part.shape[1])
-        part = part.reshape(shape)
-        for axis in (3, 2, 1):
-            part = scatter_axis(grid, part, axis, 0)
-        part = part.reshape(sizes[0], count * part.shape[1] // 128, 128)
-        return scatter_axis(grid, part, 0, 0).reshape(count, -1)
-
-    mods_first = scatter_mods(dot_head(cond_act, w_mods[:, : 2 * D])) + b_mods[: 2 * D]
-    mods_later = scatter_mods(dot_head(cond_act, w_mods[:, 2 * D :])) + b_mods[2 * D :]
-    shift_a, scale_a = mods_first[:, :D], mods_first[:, D:]
-    gate_a, shift_b, scale_b, gate_b, shift_f, scale_f = jnp.split(mods_later, 6, axis=1)
+    mods = dot_head(cond_act, w_mods)
+    mods = mods.reshape(sizes[CORE], sizes[X_AXIS], sizes[Y_AXIS], sizes[Z_AXIS] * count, 8 * D)
+    for axis in (CORE, MIX_P, MIX_Q):
+        mods = scatter_axis(grid, mods, axis, 0)
+    mods = mods.reshape(sizes[Z_AXIS], count * 8 * D // 128, 128)
+    mods = scatter_axis(grid, mods, Z_AXIS, 0).reshape(count, 8 * D) + b_mods
+    shift_a, scale_a, gate_a, shift_b, scale_b, gate_b, shift_f, scale_f = jnp.split(
+        mods, 8, axis=1
+    )
 
     signal, spread = noise_scales(timesteps)
     noise_rows = noise_draw.astype(jnp.float32)
@@ -451,13 +479,9 @@
     attended = (matmul(mixed, w_out) + b_out).reshape(count, TOK, D)
     resid_mid = resid_in + gate_a[:, None, :] * attended
     normed_b = modulate(resid_mid, shift_b, scale_b).astype(bf16).reshape(rows_all, D)
-    uppers = [
-        matmul(normed_b, part) + b_up[index * half : (index + 1) * half]
-        for index, part in enumerate(up_parts)
-    ]
-    actives = [jax.nn.gelu(upper, approximate=True).astype(bf16) for upper in uppers]
-    active = jnp.concatenate(actives, axis=1)
-    lowered = jnp.concatenate([matmul(active, part) for part in down_parts], axis=1) + b_down
+    upper = matmul(normed_b, table_up) + b_up
+    active = jax.nn.gelu(upper, approximate=True).astype(bf16)
+    lowered = matmul(active, table_down) + b_down
     lowered = lowered.reshape(count, TOK, D)
     resid_out = resid_mid + gate_b[:, None, :] * lowered
     normed_c = modulate(resid_out, shift_f, scale_f).astype(bf16).reshape(rows_all, D)
@@ -474,27 +498,18 @@
     grad_lowered = (grad_out * gate_b[:, None, :]).reshape(rows_all, D)
     grad_b_down = jnp.sum(grad_lowered, axis=0)
     lowered_bf = grad_lowered.astype(bf16)
-    sum_down = [
-        scatter_bulk(grid, dot_head(active, part).astype(bf16), PLANS[4 + index])
-        for index, part in enumerate(jnp.split(lowered_bf, 2, axis=1))
-    ]
-    grad_active = dot_tail(lowered_bf[:, : D // 2], down_parts[0]) + dot_tail(
-        lowered_bf[:, D // 2 :], down_parts[1]
-    )
+    grad_w_down = dot_head(active, lowered_bf).astype(bf16)
+    sum_down = scatter_bulk(grid, grad_w_down, OUTER)
+    lowered_bf = after(lowered_bf, grad_w_down)
+    grad_active = dot_tail(lowered_bf, table_down)
     gelu = partial(jax.nn.gelu, approximate=True)
-    grad_uppers = [
-        jax.vjp(gelu, upper)[1](grad_active[:, index * half : (index + 1) * half])[0]
-        for index, upper in enumerate(uppers)
-    ]
-    grad_b_up = jnp.concatenate([jnp.sum(part, axis=0) for part in grad_uppers])
-    upper_bf = [part.astype(bf16) for part in grad_uppers]
-    sum_up = [
-        scatter_bulk(grid, dot_head(normed_b, part).astype(bf16), PLANS[2 + index])
-        for index, part in enumerate(upper_bf)
-    ]
-    grad_normed_b = (
-        dot_tail(upper_bf[0], up_parts[0]) + dot_tail(upper_bf[1], up_parts[1])
-    ).reshape(count, TOK, D)
+    grad_upper = jax.vjp(gelu, upper)[1](grad_active)[0]
+    grad_b_up = jnp.sum(grad_upper, axis=0)
+    upper_bf = grad_upper.astype(bf16)
+    grad_w_up = dot_head(normed_b, upper_bf).astype(bf16)
+    sum_up = scatter_bulk(grid, grad_w_up, OUTER)
+    upper_bf = after(upper_bf, grad_w_up)
+    grad_normed_b = dot_tail(upper_bf, table_up).reshape(count, TOK, D)
     _, pull_mid = jax.vjp(modulate, resid_mid, shift_b, scale_b)
     grad_mid_norm, grad_shift_b, grad_scale_b = pull_mid(grad_normed_b)
     grad_mid = grad_out + grad_mid_norm
@@ -527,12 +542,11 @@
     grad_b_value = jnp.sum(grad_values, axis=0)
     qk_bf = jnp.concatenate([grad_queries, grad_keys], axis=1).astype(bf16)
     values_bf = grad_values.astype(bf16)
-    sum_vo = scatter_bulk(
-        grid,
-        jnp.concatenate([dot_head(normed_a, values_bf), grad_w_out], axis=1).astype(bf16),
-        PLANS[1],
-    )
-    sum_qk = scatter_bulk(grid, dot_head(normed_a, qk_bf).astype(bf16), PLANS[0])
+    grad_vo = jnp.concatenate([dot_head(normed_a, values_bf), grad_w_out], axis=1).astype(bf16)
+    grad_qk = dot_head(normed_a, qk_bf).astype(bf16)
+    sum_vo = scatter_bulk(grid, grad_vo, OUTER)
+    sum_qk = scatter_bulk(grid, grad_qk, OUTER)
+    qk_bf = after(qk_bf, grad_vo, grad_qk)
     grad_normed_a = (dot_tail(qk_bf, table_qk) + dot_tail(values_bf, w_value)).reshape(
         count, TOK, D
     )
@@ -556,7 +570,7 @@
         axis=1,
     )
     grad_b_mods = jnp.sum(grad_mods, axis=0)
-    mods_bf = gather_small(grid, grad_mods.astype(bf16).reshape(-1, 128), (0, 1, 2, 3))
+    mods_bf = gather_small(grid, grad_mods.astype(bf16).reshape(-1, 128), (Z_AXIS, MIX_Q, MIX_P, CORE))
     mods_bf = mods_bf.reshape(image_total, 8 * D)
     grad_w_mods = matmul(cond_act, mods_bf)
     grad_cond_act = dot_tail(w_mods, mods_bf)
@@ -608,8 +622,8 @@
     sum_head = small[at : at + rows * PATCH_FEAT].reshape(rows, PATCH_FEAT)
 
     reduced = (
-        jnp.concatenate([sum_qk, sum_vo, *sum_up, grad_w_mods, grad_w_time], axis=1),
-        jnp.concatenate(sum_down, axis=1),
+        jnp.concatenate([sum_qk, sum_vo, sum_up, grad_w_mods, grad_w_time], axis=1),
+        sum_down,
         jnp.concatenate([grad_t_first, sum_patch, grad_w_class, sum_head], axis=1),
         small[:bias_rows],
     )
@@ -620,9 +634,8 @@
         for index in range(4)
     ]
     directions = [item[2] for item in results]
-    early = sum_small(grid, jnp.concatenate([loss_local[None], block_squares(masters)]))
-    loss_sum, weight_sq = early[0], early[1:]
-    update_sq = sum_small(grid, block_squares(directions))
+    sums = sum_small(grid, as_vector([loss_local] + block_squares(masters) + block_squares(directions)))
+    loss_sum, weight_sq, update_sq = sums[0], sums[1:13], sums[13:25]
     weight_norms = jnp.sqrt(weight_sq)
     update_norms = jnp.sqrt(update_sq)
     trust = weight_norms / update_norms

time: 1540 us -> 742 us (0.48)
  Pallas kernels: 775 us -> 17.6 us
  starting transfers between devices: 181 us -> 103 us
  other arithmetic: 117 us -> 164 us
    pallas_call x6 -> x4, Pallas kernels: 775 us -> 17.6 us  [gather_bulk(): pl.pallas_call(partial(place_kernel, moves), out_shape=jax.ShapeDtypeStru...]
    ppermute x172 -> x93, starting transfers between devices: 181 us -> 103 us  [move(): return lax.ppermute(values, AXIS, pairs)]
    add x9 -> x5, other arithmetic: 0.03 us -> 31.1 us  [sum_small(): values = values + grid.flip(values, axis, bit)]
    select_n x0 -> x5, other arithmetic: none -> 16.5 us  [the longest x1 15.5 us: as_vector(): vector = jnp.where(places == index, value, vector)]
    dot_general x11 -> x9, matrix products: 34.3 us -> 20.8 us  [matmul(): return jnp.dot(left, right, preferred_element_type=jnp.float32)]
    dot_general x13 -> x11, matrix products: 24.8 us -> 34.2 us  [dot_tail(): lax.dot_general(left, right, (((1,), (1,)), ((), ())), preferred_element_...]
    ppermute x172 -> x93, waiting for transfers between devices: 214 us -> 222 us  [move(): return lax.ppermute(values, AXIS, pairs)]
    dot_general x11 -> x8, matrix products: 29.3 us -> 33.9 us  [dot_head(): lax.dot_general(left, right, (((0,), (0,)), ((), ())), preferred_element_...]
  transfers between devices with their start and end apart: 172 -> 93, of which waited for: 62 -> 48; matrix products, arithmetic and copies ran while one was open for 14% -> 26% of each run, Pallas kernels for 42% -> 1%
where the time goes in v2:
time: 742 us; the launch traced here: 731 us
  waiting for transfers between devices  222 us (30%)
  other arithmetic  164 us (22%)
  local copies, waits for them, and re-layouts  117 us (16%)
  starting transfers between devices  103 us (14%)
  matrix products  103 us (14%)
  Pallas kernels  17.6 us (2%)
    ppermute x93, waiting for transfers between devices, move(): return lax.ppermute(values, AXIS, pairs)  222 us
    ppermute x93, starting transfers between devices, move(): return lax.ppermute(values, AXIS, pairs)  103 us
    dot_general x11, matrix products, dot_tail(): lax.dot_general(left, right, (((1,), (1,)), ((), ())), preferred_element_...  34.2 us
    unnamed x294, local copies, waits for them, and re-layouts  34 us
    dot_general x8, matrix products, dot_head(): lax.dot_general(left, right, (((0,), (0,)), ((), ())), preferred_element_...  33.9 us
    add x5, other arithmetic, sum_small(): values = values + grid.flip(values, axis, bit)  31.1 us
    dot_general x9, matrix products, matmul(): return jnp.dot(left, right, preferred_element_type=jnp.float32)  20.8 us
    convert_element_type x20, other arithmetic, scatter_bulk(): total = total.astype(jnp.bfloat16)  18 us
  transfers between devices with their start and end apart: 93, of which 48 were waited for; matrix products, arithmetic and copies ran while one was open for 26% of the time, Pallas kernels for 1%

profile of v2, /device:TPU:0, one launch (start us, length us, event | category | flops | bytes accessed | tf_op | source)
XLA Modules:
  0.0 731.1 jit_solution(7267591300937000426)
XLA Ops:
  51.2 5.7 collective-permute-done.5
  95.6 12.6 %collective-permute-done.40 = bf16[1,128,1024]{2,1,0:T(8,128)(2,1)} collective-permute-done((bf16[1,128,1024]{2,1,0:T(8,128)(2,1)}, bf16[1,128,1024]{2,1,0:T(8,128)(2,1)}, u32[]{:S(2)}, u32[]{:S(2)}) %collective-permute-start.40) | collective-permute-done | bytes 262176 | tf_op jit(solution)/shard_map/ppermute | solution.py:194
  138.7 6.0 collective-permute-done.34
  148.5 8.2 %collective-permute-done.35 = bf16[2,32,4096]{2,1,0:T(8,128)(2,1)S(1)} collective-permute-done((bf16[2,32,4096]{2,1,0:T(8,128)(2,1)S(1)}, bf16[2,32,4096]{2,1,0:T(8,128)(2,1)S(1)}, u32[]{:S(2)}, u32[]{:S(2)}) %collective-permute-start.35) | collective-permute-done | bytes 524320 | tf_op jit(solution)/shard_map/ppermute | solution.py:194
  251.9 6.7 shard_map.282
  258.6 6.9 fusion.164
  280.1 13.7 %convolution_convert_fusion.1 = bf16[4096,1024]{1,0:T(8,128)(2,1)} fusion(bf16[512,1024]{1,0:T(8,128)(2,1)} %bitcast.512, f32[512,4096]{1,0:T(8,128)} %copy-done.31, f32[4096]{0:T(1024)S(1)} %copy-done.89), kind=kOutput, calls=%fused_computation.17 | convolution fusion | flops 4320133120 | bytes 17842176 | tf_op jit(solution)/shard_map/dot_general | solution.py:47
  293.8 14.1 %fusion.160 = (f32[4096]{0:T(1024)}, bf16[512,4096]{1,0:T(8,128)(2,1)}) fusion(f32[512,4096]{1,0:T(8,128)} %copy-done.31, f32[4096]{0:T(1024)S(1)} %copy-done.89, bf16[512,1024]{1,0:T(8,128)(2,1)} %bitcast.513, bf16[4096,1024]{1,0:T(8,128)(2,1)S(1)} %bitcast.461), kind=kOutput, calls=%fused_computation.581 | convolution fusion | flops 4341100544 | bytes 22052864 | tf_op jit(solution)/shard_map/dot_general | solution.py:41
  307.9 10.6 %convolution_convert_fusion = bf16[1024,4096]{1,0:T(8,128)(2,1)} fusion(bf16[512,1024]{1,0:T(8,128)(2,1)} %copy-done.57, bf16[512,4096]{1,0:T(8,128)(2,1)} %get-tuple-element.20), kind=kOutput, calls=%fused_computation.16 | convolution fusion | flops 4299161600 | bytes 13631488 | tf_op jit(solution)/shard_map/dot_general | solution.py:47
  318.5 6.8 multiply_reduce_fusion.7
  386.6 7.8 %constant_dynamic-slice_fusion.3 = (bf16[4,2,2,1,32,4096]{5,4,3,2,1,0:T(8,128)(2,1)}, bf16[4,2,2,1,32,4096]{5,4,3,2,1,0:T(8,128)(2,1)}) fusion(bf16[4,2,2,2,32,4096]{5,4,3,2,1,0:T(8,128)(2,1)} %bitcast.489, s32[]{:T(128)S(6)} %select_n.912, s32[]{:T(128)S(6)} %select_n.910), kind=kLoop, calls=%fused_computation.316 | loop fusion | bytes 16777224 | tf_op jit(solution)/shard_map/jit(dynamic_index_in_dim)/dynamic_slice | solution.py:327
  450.7 7.0 constant_dynamic-slice_fusion.16
  487.0 8.7 %collective-permute-done.77 = bf16[4,1,2,1,32,2048]{5,4,3,2,1,0:T(8,128)(2,1)S(1)} collective-permute-done((bf16[4,1,2,1,32,2048]{5,4,3,2,1,0:T(8,128)(2,1)S(1)}, bf16[4,1,2,1,32,2048]{5,4,3,2,1,0:T(8,128)(2,1)S(1)}, u32[]{:S(2)}, u32[]{:S(2)}) %collective-permute-start.77) | collective-permute-done | bytes 1048608 | tf_op jit(solution)/shard_map/ppermute | solution.py:194
  498.1 8.8 %collective-permute-done.71 = bf16[4,1,2,1,32,2048]{5,4,3,2,1,0:T(8,128)(2,1)S(1)} collective-permute-done((bf16[4,1,2,1,32,2048]{5,4,3,2,1,0:T(8,128)(2,1)S(1)}, bf16[4,1,2,1,32,2048]{5,4,3,2,1,0:T(8,128)(2,1)S(1)}, u32[]{:S(2)}, u32[]{:S(2)}) %collective-permute-start.71) | collective-permute-done | bytes 1048608 | tf_op jit(solution)/shard_map/ppermute | solution.py:194
  509.6 7.1 collective-permute-done.72
  545.5 18.6 %collective-permute-done.83 = bf16[4,1,2,1,32,4096]{5,4,3,2,1,0:T(8,128)(2,1)S(1)} collective-permute-done((bf16[4,1,2,1,32,4096]{5,4,3,2,1,0:T(8,128)(2,1)S(1)}, bf16[4,1,2,1,32,4096]{5,4,3,2,1,0:T(8,128)(2,1)S(1)}, u32[]{:S(2)}, u32[]{:S(2)}) %collective-permute-start.83) | collective-permute-done | bytes 2097184 | tf_op jit(solution)/shard_map/ppermute | solution.py:194
  566.0 20.5 %collective-permute-done.65 = bf16[4,1,2,1,128,1024]{5,4,3,2,1,0:T(8,128)(2,1)S(1)} collective-permute-done((bf16[4,1,2,1,128,1024]{5,4,3,2,1,0:T(8,128)(2,1)S(1)}, bf16[4,1,2,1,128,1024]{5,4,3,2,1,0:T(8,128)(2,1)S(1)}, u32[]{:S(2)}, u32[]{:S(2)}) %collective-permute-start.65) | collective-permute-done | bytes 2097184 | tf_op jit(solution)/shard_map/ppermute | solution.py:194
  588.0 14.6 %collective-permute-done.66 = bf16[1,1,2,1,128,1024]{5,4,3,2,1,0:T(8,128)(2,1)S(1)} collective-permute-done((bf16[1,1,2,1,128,1024]{5,4,3,2,1,0:T(8,128)(2,1)S(1)}, bf16[1,1,2,1,128,1024]{5,4,3,2,1,0:T(8,128)(2,1)S(1)}, u32[]{:S(2)}, u32[]{:S(2)}) %collective-permute-start.66) | collective-permute-done | bytes 524320 | tf_op jit(solution)/shard_map/ppermute | solution.py:194
  604.6 9.1 %collective-permute-done.85 = bf16[1,1,2,1,32,4096]{5,4,3,2,1,0:T(8,128)(2,1)S(1)} collective-permute-done((bf16[1,1,2,1,32,4096]{5,4,3,2,1,0:T(8,128)(2,1)S(1)}, bf16[1,1,2,1,32,4096]{5,4,3,2,1,0:T(8,128)(2,1)S(1)}, u32[]{:S(2)}, u32[]{:S(2)}) %collective-permute-start.85) | collective-permute-done | bytes 524320 | tf_op jit(solution)/shard_map/ppermute | solution.py:194
  616.7 8.3 %collective-permute-done.67 = bf16[1,1,2,1,128,1024]{5,4,3,2,1,0:T(8,128)(2,1)S(1)} collective-permute-done((bf16[1,1,2,1,128,1024]{5,4,3,2,1,0:T(8,128)(2,1)S(1)}, bf16[1,1,2,1,128,1024]{5,4,3,2,1,0:T(8,128)(2,1)S(1)}, u32[]{:S(2)}, u32[]{:S(2)}) %collective-permute-start.67) | collective-permute-done | bytes 524320 | tf_op jit(solution)/shard_map/ppermute | solution.py:194
  627.4 7.2 collective-permute-done.86
  651.7 15.5 %compare_select_fusion.44 = f32[32]{0:T(128)S(1)} fusion(f32[]{:T(128)} %get-tuple-element.142, f32[]{:T(128)} %multiply_reduce_fusion.18, f32[]{:T(128)} %get-tuple-element.29, f32[]{:T(128)} %multiply_reduce_fusion.15, f32[]{:T(128)} %multiply_reduce_fusion.14, f32[]{:T(128)} %multiply_reduce_fusion.19, f32[]{:T(128)} %get-tuple-element.28, ...), kind=kLoop, calls=%fused_computation.504 | loop fusion | flops 1600 | bytes 228 | tf_op jit(solution)/shard_map/jit(_where)/select_n | solution.py:117
  668.5 15.5 %fusion.228 = f32[32]{0:T(128)S(1)} fusion(f32[32]{0:T(128)S(1)} %collective-permute-done.88, f32[]{:T(128)} %get-tuple-element.142, f32[]{:T(128)} %multiply_reduce_fusion.18, f32[]{:T(128)} %get-tuple-element.29, f32[]{:T(128)} %multiply_reduce_fusion.15, f32[]{:T(128)} %multiply_reduce_fusion.14, f32[]{:T(128)} %multiply_reduce_fusion.19, ...), kind=kLoop, calls=%fused_computation.599 | loop fusion | flops 1632 | bytes 356 | tf_op jit(solution)/shard_map/add | solution.py:250
  687.6 15.5 %fusion.229 = f32[32]{0:T(128)S(1)} fusion(f32[32]{0:T(128)S(1)} %collective-permute-done.89, f32[32]{0:T(128)S(1)} %collective-permute-done.88, f32[]{:T(128)} %get-tuple-element.142, f32[]{:T(128)} %multiply_reduce_fusion.18, f32[]{:T(128)} %get-tuple-element.29, f32[]{:T(128)} %multiply_reduce_fusion.15, f32[]{:T(128)} %multiply_reduce_fusion.14, ...), kind=kLoop, calls=%fused_computation.600 | loop fusion | flops 1664 | bytes 484 | tf_op jit(solution)/shard_map/add | solution.py:250
  (768 shorter events, 470.6 us)
Async XLA Ops:
  3.3 77.0 %collective-permute-start.32 = (bf16[1,32,4096]{2,1,0:T(8,128)(2,1)}, bf16[1,32,4096]{2,1,0:T(8,128)(2,1)}, u32[]{:S(2)}, u32[]{:S(2)}) collective-permute-start(bf16[1,32,4096]{2,1,0:T(8,128)(2,1)} %get-tuple-element.84), channel_id=1, source_target_pairs={{0,2},{1,5},{2,0},{3,7},{4,6},{5,1},{6,4},{7,3},{8,10},{9,13},{10,... | collective-permute-start | bytes 786440 | tf_op jit(solution)/shard_map/ppermute | solution.py:194
  7.1 61.2 %collective-permute-start.18 = (bf16[1,32,2048]{2,1,0:T(8,128)(2,1)}, bf16[1,32,2048]{2,1,0:T(8,128)(2,1)}, u32[]{:S(2)}, u32[]{:S(2)}) collective-permute-start(bf16[1,32,2048]{2,1,0:T(8,128)(2,1)} %get-tuple-element.86), channel_id=1, source_target_pairs={{0,2},{1,5},{2,0},{3,7},{4,6},{5,1},{6,4},{7,3},{8,10},{9,13},{10,... | collective-permute-start | bytes 393224 | tf_op jit(solution)/shard_map/ppermute | solution.py:194
  14.5 57.6 %collective-permute-start.25 = (bf16[1,32,2048]{2,1,0:T(8,128)(2,1)}, bf16[1,32,2048]{2,1,0:T(8,128)(2,1)}, u32[]{:S(2)}, u32[]{:S(2)}) collective-permute-start(bf16[1,32,2048]{2,1,0:T(8,128)(2,1)} %get-tuple-element.87), channel_id=1, source_target_pairs={{0,2},{1,5},{2,0},{3,7},{4,6},{5,1},{6,4},{7,3},{8,10},{9,13},{10,... | collective-permute-start | bytes 393224 | tf_op jit(solution)/shard_map/ppermute | solution.py:194
  18.5 65.7 %collective-permute-start.39 = (bf16[1,128,1024]{2,1,0:T(8,128)(2,1)}, bf16[1,128,1024]{2,1,0:T(8,128)(2,1)}, u32[]{:S(2)}, u32[]{:S(2)}) collective-permute-start(bf16[1,128,1024]{2,1,0:T(8,128)(2,1)} %get-tuple-element.98), channel_id=1, source_target_pairs={{0,24},{1,25},{2,26},{3,27},{4,28},{5,29},{6,30},{7,31},{8,0},{9,1... | collective-permute-start | bytes 786440 | tf_op jit(solution)/shard_map/ppermute | solution.py:194
  80.3 41.6 %collective-permute-start.12 = (f32[2,2,8,8192]{3,2,1,0:T(8,128)S(1)}, f32[2,2,8,8192]{3,2,1,0:T(8,128)}, u32[]{:S(2)}, u32[]{:S(2)}) collective-permute-start(f32[2,2,8,8192]{3,2,1,0:T(8,128)S(1)} %dynamic-slice_bitcast_fusion), channel_id=1, source_target_pairs={{0,1},{1,0},{2,3},{3,2},{4,5},{5,4},{6,7},{7,6},{8,9},{9,8},{10,11... | collective-permute-start | bytes 3145736 | tf_op jit(solution)/shard_map/ppermute | solution.py:194
  82.6 38.5 %collective-permute-start.33 = (bf16[2,32,4096]{2,1,0:T(8,128)(2,1)}, bf16[2,32,4096]{2,1,0:T(8,128)(2,1)}, u32[]{:S(2)}, u32[]{:S(2)}) collective-permute-start(bf16[2,32,4096]{2,1,0:T(8,128)(2,1)} %get-tuple-element.96), channel_id=1, source_target_pairs={{0,24},{1,25},{2,26},{3,27},{4,28},{5,29},{6,30},{7,31},{8,0},{9,1... | collective-permute-start | bytes 1572872 | tf_op jit(solution)/shard_map/ppermute | solution.py:194
  85.8 28.1 %collective-permute-start.20 = (bf16[2,32,2048]{2,1,0:T(8,128)(2,1)}, bf16[2,32,2048]{2,1,0:T(8,128)(2,1)}, u32[]{:S(2)}, u32[]{:S(2)}) collective-permute-start(bf16[2,32,2048]{2,1,0:T(8,128)(2,1)} %collective-permute-done.19), channel_id=1, source_target_pairs={{0,24},{1,25},{2,26},{3,27},{4,28},{5,29},{6,30},{7,31},{8,0},{9,1... | collective-permute-start | bytes 786440 | tf_op jit(solution)/shard_map/ppermute | solution.py:194
  91.4 28.1 %collective-permute-start.27 = (bf16[2,32,2048]{2,1,0:T(8,128)(2,1)}, bf16[2,32,2048]{2,1,0:T(8,128)(2,1)}, u32[]{:S(2)}, u32[]{:S(2)}) collective-permute-start(bf16[2,32,2048]{2,1,0:T(8,128)(2,1)} %collective-permute-done.26), channel_id=1, source_target_pairs={{0,24},{1,25},{2,26},{3,27},{4,28},{5,29},{6,30},{7,31},{8,0},{9,1... | collective-permute-start | bytes 786440 | tf_op jit(solution)/shard_map/ppermute | solution.py:194
  127.5 42.4 %collective-permute-start.42 = (bf16[4,128,1024]{2,1,0:T(8,128)(2,1)}, bf16[4,128,1024]{2,1,0:T(8,128)(2,1)}, u32[]{:S(2)}, u32[]{:S(2)}) collective-permute-start(bf16[4,128,1024]{2,1,0:T(8,128)(2,1)} %get-tuple-element.92), channel_id=1, source_target_pairs={{0,2},{1,5},{2,0},{3,7},{4,6},{5,1},{6,4},{7,3},{8,10},{9,13},{10,... | collective-permute-start | bytes 3145736 | tf_op jit(solution)/shard_map/ppermute | solution.py:194
  132.7 40.4 %collective-permute-start.22 = (bf16[8,32,2048]{2,1,0:T(8,128)(2,1)}, bf16[8,32,2048]{2,1,0:T(8,128)(2,1)}, u32[]{:S(2)}, u32[]{:S(2)}) collective-permute-start(bf16[8,32,2048]{2,1,0:T(8,128)(2,1)} %bitcast.55.refs_0_), channel_id=1, source_target_pairs={{0,4},{1,3},{2,6},{3,1},{4,0},{5,7},{6,2},{7,5},{8,12},{9,11},{10,... | collective-permute-start | bytes 3145736 | tf_op jit(solution)/shard_map/ppermute | solution.py:194
  137.5 40.7 %collective-permute-start.29 = (bf16[8,32,2048]{2,1,0:T(8,128)(2,1)S(1)}, bf16[8,32,2048]{2,1,0:T(8,128)(2,1)}, u32[]{:S(2)}, u32[]{:S(2)}) collective-permute-start(bf16[8,32,2048]{2,1,0:T(8,128)(2,1)S(1)} %bitcast.478), channel_id=1, source_target_pairs={{0,4},{1,3},{2,6},{3,1},{4,0},{5,7},{6,2},{7,5},{8,12},{9,11},{10,... | collective-permute-start | bytes 3145736 | tf_op jit(solution)/shard_map/ppermute | solution.py:194
  178.1 34.4 %collective-permute-start.30 = (bf16[8,32,2048]{2,1,0:T(8,128)(2,1)S(1)}, bf16[8,32,2048]{2,1,0:T(8,128)(2,1)}, u32[]{:S(2)}, u32[]{:S(2)}) collective-permute-start(bf16[8,32,2048]{2,1,0:T(8,128)(2,1)S(1)} %bitcast.479), channel_id=1, source_target_pairs={{0,1},{1,0},{2,3},{3,2},{4,5},{5,4},{6,7},{7,6},{8,9},{9,8},{10,11... | collective-permute-start | bytes 3145736 | tf_op jit(solution)/shard_map/ppermute | solution.py:194
  178.2 50.0 %collective-permute-start.36 = (bf16[8,32,4096]{2,1,0:T(8,128)(2,1)S(1)}, bf16[8,32,4096]{2,1,0:T(8,128)(2,1)}, u32[]{:S(2)}, u32[]{:S(2)}) collective-permute-start(bf16[8,32,4096]{2,1,0:T(8,128)(2,1)S(1)} %bitcast.472), channel_id=1, source_target_pairs={{0,4},{1,3},{2,6},{3,1},{4,0},{5,7},{6,2},{7,5},{8,12},{9,11},{10,... | collective-permute-start | bytes 6291464 | tf_op jit(solution)/shard_map/ppermute | solution.py:194
  179.4 33.3 %collective-permute-start.31 = (bf16[8,32,2048]{2,1,0:T(8,128)(2,1)}, bf16[8,32,2048]{2,1,0:T(8,128)(2,1)}, u32[]{:S(2)}, u32[]{:S(2)}) collective-permute-start(bf16[8,32,2048]{2,1,0:T(8,128)(2,1)} %collective-permute-done.29.refs_1_), channel_id=1, source_target_pairs={{0,1},{1,0},{2,3},{3,2},{4,5},{5,4},{6,7},{7,6},{8,9},{9,8},{10,11... | collective-permute-start | bytes 3145736 | tf_op jit(solution)/shard_map/ppermute | solution.py:194
  188.3 55.0 %collective-permute-start.37 = (bf16[8,32,4096]{2,1,0:T(8,128)(2,1)S(1)}, bf16[8,32,4096]{2,1,0:T(8,128)(2,1)}, u32[]{:S(2)}, u32[]{:S(2)}) collective-permute-start(bf16[8,32,4096]{2,1,0:T(8,128)(2,1)S(1)} %bitcast.473), channel_id=1, source_target_pairs={{0,1},{1,0},{2,3},{3,2},{4,5},{5,4},{6,7},{7,6},{8,9},{9,8},{10,11... | collective-permute-start | bytes 6291464 | tf_op jit(solution)/shard_map/ppermute | solution.py:194
  188.4 41.9 %collective-permute-start.43 = (bf16[8,128,1024]{2,1,0:T(8,128)(2,1)}, bf16[8,128,1024]{2,1,0:T(8,128)(2,1)}, u32[]{:S(2)}, u32[]{:S(2)}) collective-permute-start(bf16[8,128,1024]{2,1,0:T(8,128)(2,1)} %bitcast.475), channel_id=1, source_target_pairs={{0,4},{1,3},{2,6},{3,1},{4,0},{5,7},{6,2},{7,5},{8,12},{9,11},{10,... | collective-permute-start | bytes 6291464 | tf_op jit(solution)/shard_map/ppermute | solution.py:194
  212.5 39.3 %collective-permute-start.44 = (bf16[8,128,1024]{2,1,0:T(8,128)(2,1)}, bf16[8,128,1024]{2,1,0:T(8,128)(2,1)}, u32[]{:S(2)}, u32[]{:S(2)}) collective-permute-start(bf16[8,128,1024]{2,1,0:T(8,128)(2,1)} %bitcast.476), channel_id=1, source_target_pairs={{0,1},{1,0},{2,3},{3,2},{4,5},{5,4},{6,7},{7,6},{8,9},{9,8},{10,11... | collective-permute-start | bytes 6291464 | tf_op jit(solution)/shard_map/ppermute | solution.py:194
  400.4 132.1 %collective-permute-start.82 = (bf16[4,2,2,1,32,4096]{5,4,3,1,2,0:T(8,128)(2,1)}, bf16[4,2,2,1,32,4096]{5,4,3,1,2,0:T(8,128)(2,1)}, u32[]{:S(2)}, u32[]{:S(2)}) collective-permute-start(bf16[4,2,2,1,32,4096]{5,4,3,1,2,0:T(8,128)(2,1)} %copy.267), channel_id=1, source_target_pairs={{0,1},{1,0},{2,3},{3,2},{4,5},{5,4},{6,7},{7,6},{8,9},{9,8},{10,11... | collective-permute-start | bytes 12582920 | tf_op jit(solution)/shard_map/ppermute | solution.py:194
  420.2 57.5 %collective-permute-start.76 = (bf16[4,2,2,1,32,2048]{5,4,3,2,1,0:T(8,128)(2,1)}, bf16[4,2,2,1,32,2048]{5,4,3,2,1,0:T(8,128)(2,1)}, u32[]{:S(2)}, u32[]{:S(2)}) collective-permute-start(bf16[4,2,2,1,32,2048]{5,4,3,2,1,0:T(8,128)(2,1)} %fusion.14), channel_id=1, source_target_pairs={{0,1},{1,0},{2,3},{3,2},{4,5},{5,4},{6,7},{7,6},{8,9},{9,8},{10,11... | collective-permute-start | bytes 6291464 | tf_op jit(solution)/shard_map/ppermute | solution.py:194
  470.5 68.7 %collective-permute-start.64 = (bf16[4,2,2,1,128,1024]{5,4,3,1,2,0:T(8,128)(2,1)}, bf16[4,2,2,1,128,1024]{5,4,3,1,2,0:T(8,128)(2,1)}, u32[]{:S(2)}, u32[]{:S(2)}) collective-permute-start(bf16[4,2,2,1,128,1024]{5,4,3,1,2,0:T(8,128)(2,1)} %copy.263), channel_id=1, source_target_pairs={{0,1},{1,0},{2,3},{3,2},{4,5},{5,4},{6,7},{7,6},{8,9},{9,8},{10,11... | collective-permute-start | bytes 12582920 | tf_op jit(solution)/shard_map/ppermute | solution.py:194
  536.6 27.5 %collective-permute-start.83 = (bf16[4,1,2,1,32,4096]{5,4,3,2,1,0:T(8,128)(2,1)S(1)}, bf16[4,1,2,1,32,4096]{5,4,3,2,1,0:T(8,128)(2,1)S(1)}, u32[]{:S(2)}, u32[]{:S(2)}) collective-permute-start(bf16[4,1,2,1,32,4096]{5,4,3,2,1,0:T(8,128)(2,1)S(1)} %constant_dynamic-slice_fusion.2), channel_id=1, source_target_pairs={{0,4},{1,3},{2,6},{3,1},{4,0},{5,7},{6,2},{7,5},{8,12},{9,11},{10,... | collective-permute-start | bytes 6291464 | tf_op jit(solution)/shard_map/ppermute | solution.py:194
  538.2 77.6 %collective-permute-start.81 = (bf16[1,1,1,1,32,2048]{5,4,3,2,1,0:T(8,128)(2,1)}, bf16[1,1,1,1,32,2048]{5,4,3,2,1,0:T(8,128)(2,1)}, u32[]{:S(2)}, u32[]{:S(2)}) collective-permute-start(bf16[1,1,1,1,32,2048]{5,4,3,2,1,0:T(8,128)(2,1)} %constant_dynamic-slice_fusion.5), channel_id=1, source_target_pairs={{0,2},{1,5},{2,0},{3,7},{4,6},{5,1},{6,4},{7,3},{8,10},{9,13},{10,... | collective-permute-start | bytes 393224 | tf_op jit(solution)/shard_map/ppermute | solution.py:194
  543.3 43.2 %collective-permute-start.65 = (bf16[4,1,2,1,128,1024]{5,4,3,2,1,0:T(8,128)(2,1)S(1)}, bf16[4,1,2,1,128,1024]{5,4,3,2,1,0:T(8,128)(2,1)S(1)}, u32[]{:S(2)}, u32[]{:S(2)}) collective-permute-start(bf16[4,1,2,1,128,1024]{5,4,3,2,1,0:T(8,128)(2,1)S(1)} %constant_dynamic-slice_fusion.15), channel_id=1, source_target_pairs={{0,4},{1,3},{2,6},{3,1},{4,0},{5,7},{6,2},{7,5},{8,12},{9,11},{10,... | collective-permute-start | bytes 6291464 | tf_op jit(solution)/shard_map/ppermute | solution.py:194
  587.8 25.9 %collective-permute-start.85 = (bf16[1,1,2,1,32,4096]{5,4,3,2,1,0:T(8,128)(2,1)S(1)}, bf16[1,1,2,1,32,4096]{5,4,3,2,1,0:T(8,128)(2,1)S(1)}, u32[]{:S(2)}, u32[]{:S(2)}) collective-permute-start(bf16[1,1,2,1,32,4096]{5,4,3,2,1,0:T(8,128)(2,1)S(1)} %add_convert_fusion.11), channel_id=1, source_target_pairs={{0,24},{1,25},{2,26},{3,27},{4,28},{5,29},{6,30},{7,31},{8,0},{9,1... | collective-permute-start | bytes 1572872 | tf_op jit(solution)/shard_map/ppermute | solution.py:194
  (193 other events, 2478.8 us)

commit v3 on v2

--- a/solution.py
+++ b/solution.py
@@ -99,40 +99,6 @@
     ]
 
 
-def block_squares(arrays):
-    totals = []
-    for kind, start, stop in column_blocks():
-        if kind in (0, 2):
-            piece = arrays[kind][:, start:stop]
-        else:
-            piece = arrays[kind]
-        totals.append(jnp.sum(piece * piece))
-    return totals
-
-
-def as_vector(scalars):
-    places = jnp.arange(32, dtype=jnp.int32)
-    vector = jnp.zeros((32,), jnp.float32)
-    for index, value in enumerate(scalars):
-        vector = jnp.where(places == index, value, vector)
-    return vector
-
-
-def block_factors(trust):
-    rows_in, rows_side = ([], [])
-    for index, (kind, start, stop) in enumerate(column_blocks()):
-        if kind == 0:
-            rows_in.append(jnp.full((stop - start,), trust[index], jnp.float32))
-        if kind == 2:
-            rows_side.append(jnp.full((stop - start,), trust[index], jnp.float32))
-    return (
-        jnp.concatenate(rows_in)[None, :],
-        trust[6],
-        jnp.concatenate(rows_side)[None, :],
-        trust[11],
-    )
-
-
 def adam_direction(weight, grad, first, second):
     first_new = BETA_ONE * first + (1.0 - BETA_ONE) * grad
     second_new = BETA_TWO * second + (1.0 - BETA_TWO) * grad * grad
@@ -143,6 +109,75 @@
         + DECAY * weight
     )
     return (first_new, second_new, direction)
+
+
+def direction_kernel(widths, *refs):
+    weights, firsts, seconds = refs[0:4], refs[4:8], refs[8:12]
+    grads, outs = refs[12:-13], refs[-13:]
+    lanes = lax.broadcasted_iota(jnp.int32, (8, 128), 1)
+    lines = lax.broadcasted_iota(jnp.int32, (8, 128), 0)
+    sums = jnp.zeros((8, 128), jnp.float32)
+    pieces = []
+    at = 0
+    for number, width in enumerate(widths):
+        pieces.append((number, at, at + width))
+        at += width
+    for block, (kind, start, stop) in enumerate(column_blocks()):
+        if stop == 0:
+            stop = weights[kind].shape[1]
+        if kind == 0:
+            spans = [
+                (grads[number], max(start, low) - low, max(start, low), min(stop, high))
+                for number, low, high in pieces
+                if max(start, low) < min(stop, high)
+            ]
+        else:
+            spans = [(grads[len(widths) + kind - 1], start, start, stop)]
+        for grad_ref, offset, low, high in spans:
+            weight = weights[kind][:, low:high]
+            first_new, second_new, direction = adam_direction(
+                weight,
+                grad_ref[:, offset : offset + high - low],
+                firsts[kind][:, low:high],
+                seconds[kind][:, low:high],
+            )
+            outs[kind][:, low:high] = first_new
+            outs[4 + kind][:, low:high] = second_new
+            outs[8 + kind][:, low:high] = direction
+            here = lanes == block
+            sums = sums + jnp.where(here & (lines == 0), jnp.sum(weight * weight), 0.0)
+            sums = sums + jnp.where(here & (lines == 1), jnp.sum(direction * direction), 0.0)
+    outs[12][...] = sums
+
+
+def update_kernel(sums_ref, *refs):
+    weights, directions, outs = refs[0:4], refs[4:8], refs[8:]
+    norms = jnp.sqrt(sums_ref[...])
+    trust = norms[0:1] / norms[1:2]
+    line = lax.broadcasted_iota(jnp.int32, (8, 128), 0)
+    outs[4][...] = jnp.where(line == 2, trust, norms)
+    for block, (kind, start, stop) in enumerate(column_blocks()):
+        if stop == 0:
+            stop = weights[kind].shape[1]
+        factor = RATE * trust[0:1, block : block + 1]
+        outs[kind][:, start:stop] = (
+            weights[kind][:, start:stop] - factor * directions[kind][:, start:stop]
+        )
+
+
+def whole_kernel(kernel, args, shapes):
+    vmem = pl.BlockSpec(memory_space=pltpu.VMEM)
+    size = sum(arg.size for arg in args) + sum(math.prod(shape) for shape in shapes)
+    return pl.pallas_call(
+        kernel,
+        out_shape=[jax.ShapeDtypeStruct(shape, jnp.float32) for shape in shapes],
+        in_specs=[vmem] * len(args),
+        out_specs=[vmem] * len(shapes),
+        compiler_params=pltpu.CompilerParams(vmem_limit_bytes=40 * 2**20),
+        cost_estimate=pl.CostEstimate(
+            flops=10 * size, bytes_accessed=4 * size, transcendentals=size // 8
+        ),
+    )(*args)
 
 
 Z_AXIS, Y_AXIS, X_AXIS, CORE, MIX_P, MIX_Q = range(6)
@@ -204,6 +239,10 @@
         return (self.coords[axis] + shift) % self.sizes[axis]
 
 
+def after(values, *others):
+    return lax.optimization_barrier((values,) + others)[0] if others else values
+
+
 def in_order(grid, pieces, axis):
     size = grid.sizes[axis]
     if size == 1:
@@ -217,8 +256,9 @@
     return lax.dynamic_slice_in_dim(twice, (size - grid.coords[axis]) % size, size, 0)
 
 
-def gather_small(grid, values, order):
+def gather_small(grid, values, order, before=None):
     for axis in order:
+        values = after(values, *(before or {}).get(axis, ()))
         pieces = [values]
         for shift in range(1, grid.sizes[axis]):
             pieces.append(grid.ahead(values, axis, shift))
@@ -236,11 +276,11 @@
     return total
 
 
-def scatter_small(grid, values):
-    values = scatter_axis(grid, values, 3, 3)
-    values = scatter_axis(grid, values, 2, 2)
-    values = scatter_axis(grid, values, 1, 1)
-    return scatter_axis(grid, values, 0, 0)
+def scatter_small(grid, values, before=None):
+    for axis in (CORE, X_AXIS, Y_AXIS, Z_AXIS):
+        values = after(values, *(before or {}).get(axis, ()))
+        values = scatter_axis(grid, values, axis, axis)
+    return values
 
 
 def sum_small(grid, values):
@@ -250,6 +290,26 @@
             values = values + grid.flip(values, axis, bit)
             bit *= 2
     return values
+
+
+def relative_places(grid, order):
+    dims = (CORE,) + tuple(reversed(order))
+    number = jnp.arange(grid.count, dtype=jnp.int32)
+    shifts = {}
+    for axis in reversed(dims):
+        shifts[axis] = number % grid.sizes[axis]
+        number = number // grid.sizes[axis]
+    core = (grid.coords[CORE] + shifts[CORE]) % grid.sizes[CORE]
+    x_ahead = jnp.where(core == 0, shifts[MIX_P], shifts[MIX_Q])
+    y_ahead = jnp.where(core == 0, shifts[MIX_Q], shifts[MIX_P])
+    return grid.join(
+        (
+            (grid.coords[Z_AXIS] + shifts[Z_AXIS]) % grid.sizes[Z_AXIS],
+            (grid.coords[Y_AXIS] + y_ahead) % grid.sizes[Y_AXIS],
+            (grid.coords[X_AXIS] + x_ahead) % grid.sizes[X_AXIS],
+            core,
+        )
+    ).astype(jnp.int32)
 
 
 def place_kernel(moves, where, *refs):
@@ -275,25 +335,10 @@
         parts = [sent]
         for _ in range(1, grid.sizes[axis]):
             parts.append(grid.ahead(parts[-1], axis, 1))
+            yield parts[-1]
     if grid.sizes[CORE] == 2:
         parts = parts + [grid.ahead(part, CORE, 1) for part in parts]
-    dims = (grid.sizes[CORE],) + tuple(grid.sizes[axis] for axis in reversed(order))
-    number = jnp.arange(grid.count, dtype=jnp.int32)
-    shifts = {}
-    for axis, size in reversed(list(zip((CORE,) + tuple(reversed(order)), dims))):
-        shifts[axis] = number % size
-        number = number // size
-    core = (grid.coords[CORE] + shifts[CORE]) % grid.sizes[CORE]
-    x_ahead = jnp.where(core == 0, shifts[MIX_P], shifts[MIX_Q])
-    y_ahead = jnp.where(core == 0, shifts[MIX_Q], shifts[MIX_P])
-    where = grid.join(
-        (
-            (grid.coords[Z_AXIS] + shifts[Z_AXIS]) % grid.sizes[Z_AXIS],
-            (grid.coords[Y_AXIS] + y_ahead) % grid.sizes[Y_AXIS],
-            (grid.coords[X_AXIS] + x_ahead) % grid.sizes[X_AXIS],
-            core,
-        )
-    ).astype(jnp.int32)
+    where = relative_places(grid, order)
     entries = parts[0].shape[0]
     moves = [(piece, entry) for piece in range(len(parts)) for entry in range(entries)]
     if rows % 16 == 0:
@@ -312,45 +357,188 @@
     else:
         stacked = jnp.stack(parts).reshape((grid.count, rows, columns))
         full = jnp.zeros((grid.count, rows, columns), shard.dtype).at[where].set(stacked)
-    return full.reshape(grid.count * rows, columns)
-
-
-def scatter_bulk(grid, table, order):
-    rows = table.shape[0] // grid.count
-    current = table.reshape(grid.shape + (rows, table.shape[1]))
-    first = grid.coords[CORE] == 0
-
-    def entry(axis, shift):
-        place = grid.place(axis, shift)
-        if axis in (MIX_P, MIX_Q):
-            return lax.dynamic_index_in_dim(current, place, X_AXIS if axis == MIX_P else Y_AXIS)
-        return lax.dynamic_index_in_dim(current, place, axis)
-
-    for axis in (CORE,) + tuple(reversed(order)):
+    yield full.reshape(grid.count * rows, columns)
+
+
+def pick_kernel(base, places, *refs):
+    tables, picked, sems = refs[:-2], refs[-2], refs[-1]
+    copies = []
+    for number in range(picked.shape[0]):
+        at = 0
+        for table in tables:
+            width = table.shape[2]
+            copies.append(
+                pltpu.make_async_copy(
+                    table.at[places[base + number]],
+                    picked.at[number, :, pl.ds(at, width)],
+                    sems.at[len(copies)],
+                )
+            )
+            at += width
+    for copy in copies:
+        copy.start()
+    for copy in copies:
+        copy.wait()
+
+
+def pick_rows(tables, places, base, count):
+    rows = tables[0].shape[1]
+    columns = sum(table.shape[2] for table in tables)
+    if rows % 16:
+        return jnp.concatenate([table[places[base : base + count]] for table in tables], axis=2)
+    return pl.pallas_call(
+        partial(pick_kernel, base),
+        out_shape=jax.ShapeDtypeStruct((count, rows, columns), jnp.bfloat16),
+        in_specs=[pl.BlockSpec(memory_space=pltpu.SMEM)]
+        + [pl.BlockSpec(memory_space=pl.ANY)] * len(tables),
+        out_specs=pl.BlockSpec(memory_space=pltpu.VMEM),
+        scratch_shapes=[pltpu.SemaphoreType.DMA((count * len(tables),))],
+        compiler_params=pltpu.CompilerParams(vmem_limit_bytes=24 * 2**20),
+        cost_estimate=pl.CostEstimate(
+            flops=0, bytes_accessed=4 * count * rows * columns, transcendentals=0
+        ),
+    )(places, *tables)
+
+
+def scatter_bulk(grid, tables, order):
+    rows = tables[0].shape[0] // grid.count
+    columns = sum(table.shape[1] for table in tables)
+    places = relative_places(grid, order)
+    tables = [table.reshape(grid.count, rows, table.shape[1]) for table in tables]
+    kept = grid.count // grid.sizes[CORE]
+    axes = tuple(reversed(order))
+    dims = tuple(grid.sizes[axis] for axis in axes) + (rows, columns)
+    terms = []
+    for core in reversed(range(grid.sizes[CORE])):
+        picked = pick_rows(tables, places, core * kept, kept)
+        if core > 0:
+            picked = grid.ahead(picked, CORE, core)
+            yield picked
+        terms.append(picked.reshape(dims))
+
+    def entry(place):
+        return sum(term[place].astype(jnp.float32) for term in terms)
+
+    for axis in axes:
         size = grid.sizes[axis]
-        total = entry(axis, 1)
+        total = None
         for step in range(1, size):
-            sent = grid.ahead(total, axis, 1)
-            total = sent.astype(jnp.float32) + entry(axis, 1 + step).astype(jnp.float32)
-            if step < size - 1 or axis != order[0]:
-                total = total.astype(jnp.bfloat16)
-        current = total
-        if axis == CORE:
-            current = jnp.where(first, current, jnp.swapaxes(current, Y_AXIS, X_AXIS))
-    return current.reshape(rows, table.shape[1]).astype(jnp.float32)
-
-
-def attention_scores(queries, keys_all):
-    scores = jnp.einsum("bqhd,bkhd->bhqk", queries, keys_all, preferred_element_type=jnp.float32)
-    return scores * HEAD_DIM ** (-0.5)
+            total = entry(step) if total is None else total.astype(jnp.float32) + entry(step)
+            total = grid.ahead(total.astype(jnp.bfloat16), axis, 1)
+            yield total
+        terms = [term[0] for term in terms] + ([] if total is None else [total])
+    yield sum(term.astype(jnp.float32) for term in terms)
+
+
+def last(steps):
+    return list(steps)[-1]
+
+
+HEAD_COLS = 4 * HEAD_DIM
+
+
+def head_probs(query, key):
+    scores = dot_tail(query, key) * HEAD_DIM ** (-0.5)
+    weights = jnp.exp(scores - jnp.max(scores, axis=-1, keepdims=True))
+    return weights * (1.0 / jnp.sum(weights, axis=-1, keepdims=True))
+
+
+def head_masks():
+    lanes = lax.broadcasted_iota(jnp.int32, (1, 2 * HEAD_DIM), 1)
+    first = lanes < HEAD_DIM
+    return first, (first.astype(jnp.bfloat16), (~first).astype(jnp.bfloat16))
+
+
+def attend_kernel(query_ref, key_ref, value_ref, mixed_ref):
+    first, masks = head_masks()
+    for at in range(0, HEAD_COLS, 2 * HEAD_DIM):
+        pair = slice(at, at + 2 * HEAD_DIM)
+        query, key, value = query_ref[:, pair], key_ref[:, pair], value_ref[:, pair]
+        mixed = [
+            matmul(head_probs(query * mask, key).astype(jnp.bfloat16), value) for mask in masks
+        ]
+        mixed_ref[:, pair] = jnp.where(first, mixed[0], mixed[1]).astype(jnp.bfloat16)
+
+
+def attend_back_kernel(query_ref, key_ref, value_ref, grad_ref, out_ref, bias_ref):
+    first, masks = head_masks()
+
+    @pl.when(pl.program_id(1) == 0)
+    def _():
+        bias_ref[...] = jnp.zeros_like(bias_ref)
+
+    for at in range(0, HEAD_COLS, 2 * HEAD_DIM):
+        pair = slice(at, at + 2 * HEAD_DIM)
+        query, key, value = query_ref[:, pair], key_ref[:, pair], value_ref[:, pair]
+        grad = grad_ref[:, pair]
+        parts = []
+        for mask in masks:
+            probs = head_probs(query * mask, key)
+            grad_probs = dot_tail(grad * mask, value)
+            inner = jnp.sum(probs * grad_probs, axis=-1, keepdims=True)
+            grad_scores = (probs * (grad_probs - inner)).astype(jnp.bfloat16)
+            parts.append(
+                (
+                    matmul(grad_scores, key) * HEAD_DIM ** (-0.5),
+                    dot_head(grad_scores, query) * HEAD_DIM ** (-0.5),
+                    dot_head(probs.astype(jnp.bfloat16), grad),
+                )
+            )
+        whole = [jnp.where(first, one, two) for one, two in zip(*parts)]
+        for index in range(3):
+            out_ref[index, :, pair] = whole[index].astype(jnp.bfloat16)
+        bias_ref[0:1, pair] += jnp.sum(whole[0], axis=0, keepdims=True)
+        bias_ref[1:2, pair] += jnp.sum(whole[2], axis=0, keepdims=True)
+
+
+def head_specs():
+    groups = D // HEAD_COLS
+    return [
+        pl.BlockSpec((TOK, HEAD_COLS), lambda group, image, part=part: (image, part * groups + group))
+        for part in range(3)
+    ]
+
+
+def attend(proj):
+    count = proj.shape[0] // TOK
+    flops = 4 * count * HEADS * TOK * TOK * HEAD_DIM
+    return pl.pallas_call(
+        attend_kernel,
+        grid=(D // HEAD_COLS, count),
+        out_shape=jax.ShapeDtypeStruct((proj.shape[0], D), jnp.bfloat16),
+        in_specs=head_specs(),
+        out_specs=pl.BlockSpec((TOK, HEAD_COLS), lambda group, image: (image, group)),
+        compiler_params=pltpu.CompilerParams(vmem_limit_bytes=24 * 2**20),
+        cost_estimate=pl.CostEstimate(
+            flops=4 * flops, bytes_accessed=8 * proj.size, transcendentals=flops // 256
+        ),
+    )(proj, proj, proj)
+
+
+def attend_back(proj, grad_mixed):
+    count = proj.shape[0] // TOK
+    flops = 12 * count * HEADS * TOK * TOK * HEAD_DIM
+    block = pl.BlockSpec((TOK, HEAD_COLS), lambda group, image: (image, group))
+    return pl.pallas_call(
+        attend_back_kernel,
+        grid=(D // HEAD_COLS, count),
+        out_shape=[
+            jax.ShapeDtypeStruct((3, proj.shape[0], D), jnp.bfloat16),
+            jax.ShapeDtypeStruct((8, D), jnp.float32),
+        ],
+        in_specs=head_specs() + [block],
+        out_specs=[
+            pl.BlockSpec((3, TOK, HEAD_COLS), lambda group, image: (0, image, group)),
+            pl.BlockSpec((8, HEAD_COLS), lambda group, image: (0, group)),
+        ],
+        compiler_params=pltpu.CompilerParams(vmem_limit_bytes=24 * 2**20),
+        cost_estimate=pl.CostEstimate(
+            flops=3 * flops, bytes_accessed=16 * proj.size, transcendentals=flops // 512
+        ),
+    )(proj, proj, proj, grad_mixed)
 
 
 OUTER = (MIX_P, Z_AXIS, MIX_Q)
-DEEP = (Z_AXIS, MIX_P, MIX_Q)
-
-
-def after(values, *others):
-    return lax.optimization_barrier((values,) + others)[0]
 
 
 def per_device(
@@ -406,7 +594,16 @@
     width = packed.shape[0]
     tall = -(-width // (SMALL_ROWS * 128)) * SMALL_ROWS
     packed = jnp.pad(packed, (0, tall * 128 - width)).reshape(tall, 128)
-    spread_all = gather_small(grid, packed, (3, 2, 1, 0)).reshape(count_all, tall * 128)
+    head_in = weights_in[:, : 4 * D].astype(bf16)
+    table_qkvo = lax.all_gather(head_in, AXIS, axis=0, tiled=True)
+    half = FF // 2
+    up_bf = weights_in[:, 4 * D : 4 * D + FF].astype(bf16)
+    table_first = lax.all_gather(up_bf[:, :half], AXIS, axis=0, tiled=True)
+    get_down = gather_bulk(grid, down_bf, OUTER)
+    get_up = gather_bulk(grid, up_bf[:, half:], OUTER)
+    before = {Y_AXIS: [next(get_down), next(get_up)]}
+    spread_all = gather_small(grid, packed, (CORE, X_AXIS, Y_AXIS, Z_AXIS), before)
+    spread_all = spread_all.reshape(count_all, tall * 128)
     bias_full = spread_all[:, :bias_rows].reshape(-1).astype(jnp.float32)
     at = bias_rows
     w_patch = spread_all[:, at : at + rows * PATCH_FEAT].reshape(D, PATCH_FEAT)
@@ -422,14 +619,7 @@
     steps_all = numbers[:, :count].reshape(image_total)
     labels_all = numbers[:, count:].reshape(image_total).astype(jnp.int32)
 
-    table_qk = gather_bulk(grid, in_bf[:, : 2 * D], OUTER)
-    table_vo = gather_bulk(grid, in_bf[:, 2 * D : 4 * D], OUTER)
-    table_up = gather_bulk(grid, in_bf[:, 4 * D : 4 * D + FF], OUTER)
-    table_down = gather_bulk(grid, down_bf, DEEP)
-    w_value, w_out = table_vo[:, :D], table_vo[:, D:]
-
-    b_query = bias_full[:D]
-    b_value = bias_full[D : 2 * D]
+    b_qkv = jnp.concatenate([bias_full[:D], jnp.zeros((D,), jnp.float32), bias_full[D : 2 * D]])
     b_out = bias_full[2 * D : 3 * D]
     b_up = bias_full[3 * D : 3 * D + FF]
     b_down = bias_full[3 * D + FF : 4 * D + FF]
@@ -445,19 +635,25 @@
     cond_part = lax.dot_general(
         w_time, time_act, (((0,), (0,)), ((), ())), preferred_element_type=jnp.float32
     )
-    cond = scatter_small(grid, cond_part.reshape(sizes + (rows, image_total)))
+    cond = cond_part.reshape(sizes + (rows, image_total))
+    before = {CORE: [next(get_down), next(get_up)], Z_AXIS: [next(get_down), next(get_up)]}
+    cond = scatter_small(grid, cond, before)
     cond = cond + b_time[:, None] + dot_tail(w_class, onehot.astype(bf16))
     cond_act = jax.nn.silu(cond).astype(bf16)
 
     mods = dot_head(cond_act, w_mods)
     mods = mods.reshape(sizes[CORE], sizes[X_AXIS], sizes[Y_AXIS], sizes[Z_AXIS] * count, 8 * D)
-    for axis in (CORE, MIX_P, MIX_Q):
-        mods = scatter_axis(grid, mods, axis, 0)
+    mods = scatter_axis(grid, mods, CORE, 0)
+    mods = scatter_axis(grid, mods, MIX_P, 0)
+    ready = [next(get_down), next(get_up)]
+    mods = scatter_axis(grid, after(mods, *ready), MIX_Q, 0)
     mods = mods.reshape(sizes[Z_AXIS], count * 8 * D // 128, 128)
     mods = scatter_axis(grid, mods, Z_AXIS, 0).reshape(count, 8 * D) + b_mods
     shift_a, scale_a, gate_a, shift_b, scale_b, gate_b, shift_f, scale_f = jnp.split(
         mods, 8, axis=1
     )
+
+    w_qkv, w_out = table_qkvo[:, : 3 * D], table_qkvo[:, 3 * D :]
 
     signal, spread = noise_scales(timesteps)
     noise_rows = noise_draw.astype(jnp.float32)
@@ -466,21 +662,19 @@
     hidden = dot_tail(noisy, w_patch) + b_patch + jnp.tile(positions(), (count, 1))
     resid_in = hidden.reshape(count, TOK, D)
     normed_a = modulate(resid_in, shift_a, scale_a).astype(bf16).reshape(rows_all, D)
-    head_shape = (count, TOK, HEADS, HEAD_DIM)
-    proj_qk = matmul(normed_a, table_qk)
-    queries = (proj_qk[:, :D] + b_query).astype(bf16).reshape(head_shape)
-    keys_all = proj_qk[:, D:].astype(bf16).reshape(head_shape)
-    values_all = (matmul(normed_a, w_value) + b_value).astype(bf16).reshape(head_shape)
-    scores = attention_scores(queries, keys_all)
-    log_total = jax.nn.logsumexp(scores, axis=-1)
-    probs = jnp.exp(scores - log_total[..., None]).astype(bf16)
-    mixed = jnp.einsum("bhqk,bkhd->bqhd", probs, values_all, preferred_element_type=jnp.float32)
-    mixed = mixed.astype(bf16).reshape(rows_all, D)
+    proj = (matmul(normed_a, w_qkv) + b_qkv).astype(bf16)
+    proj = after(proj, next(get_down), next(get_up))
+    mixed = attend(proj)
     attended = (matmul(mixed, w_out) + b_out).reshape(count, TOK, D)
     resid_mid = resid_in + gate_a[:, None, :] * attended
     normed_b = modulate(resid_mid, shift_b, scale_b).astype(bf16).reshape(rows_all, D)
-    upper = matmul(normed_b, table_up) + b_up
-    active = jax.nn.gelu(upper, approximate=True).astype(bf16)
+    table_up, table_down = (table_first, last(get_up)), last(get_down)
+    uppers = [
+        matmul(normed_b, part) + b_up[index * half : (index + 1) * half]
+        for index, part in enumerate(table_up)
+    ]
+    actives = [jax.nn.gelu(upper, approximate=True).astype(bf16) for upper in uppers]
+    active = jnp.concatenate(actives, axis=1)
     lowered = matmul(active, table_down) + b_down
     lowered = lowered.reshape(count, TOK, D)
     resid_out = resid_mid + gate_b[:, None, :] * lowered
@@ -499,17 +693,23 @@
     grad_b_down = jnp.sum(grad_lowered, axis=0)
     lowered_bf = grad_lowered.astype(bf16)
     grad_w_down = dot_head(active, lowered_bf).astype(bf16)
-    sum_down = scatter_bulk(grid, grad_w_down, OUTER)
+    sum_down = lax.psum_scatter(grad_w_down, AXIS, scatter_dimension=0, tiled=True)
     lowered_bf = after(lowered_bf, grad_w_down)
     grad_active = dot_tail(lowered_bf, table_down)
     gelu = partial(jax.nn.gelu, approximate=True)
-    grad_upper = jax.vjp(gelu, upper)[1](grad_active)[0]
-    grad_b_up = jnp.sum(grad_upper, axis=0)
-    upper_bf = grad_upper.astype(bf16)
-    grad_w_up = dot_head(normed_b, upper_bf).astype(bf16)
-    sum_up = scatter_bulk(grid, grad_w_up, OUTER)
-    upper_bf = after(upper_bf, grad_w_up)
-    grad_normed_b = dot_tail(upper_bf, table_up).reshape(count, TOK, D)
+    grad_uppers = [
+        jax.vjp(gelu, upper)[1](grad_active[:, index * half : (index + 1) * half])[0]
+        for index, upper in enumerate(uppers)
+    ]
+    grad_b_up = jnp.concatenate([jnp.sum(part, axis=0) for part in grad_uppers])
+    upper_bf = [part.astype(bf16) for part in grad_uppers]
+    grad_w_up = [dot_head(normed_b, part).astype(bf16) for part in upper_bf]
+    put_up = scatter_bulk(grid, grad_w_up, OUTER)
+    upper_bf[0] = after(upper_bf[0], *grad_w_up)
+    grad_normed_b = (
+        dot_tail(upper_bf[0], table_up[0]) + dot_tail(upper_bf[1], table_up[1])
+    ).reshape(count, TOK, D)
+    grad_normed_b = after(grad_normed_b, next(put_up))
     _, pull_mid = jax.vjp(modulate, resid_mid, shift_b, scale_b)
     grad_mid_norm, grad_shift_b, grad_scale_b = pull_mid(grad_normed_b)
     grad_mid = grad_out + grad_mid_norm
@@ -517,39 +717,18 @@
     grad_attended = (grad_mid * gate_a[:, None, :]).reshape(rows_all, D)
     grad_b_out = jnp.sum(grad_attended, axis=0)
     attended_bf = grad_attended.astype(bf16)
-    grad_w_out = dot_head(mixed, attended_bf)
-    grad_mixed = dot_tail(attended_bf, w_out).astype(bf16).reshape(head_shape)
-    scores = attention_scores(queries, keys_all)
-    probs_full = jnp.exp(scores - log_total[..., None])
-    grad_probs = jnp.einsum(
-        "bqhd,bkhd->bhqk", grad_mixed, values_all, preferred_element_type=jnp.float32
-    )
-    inner = jnp.sum(probs_full * grad_probs, axis=-1, keepdims=True)
-    grad_scores = (probs_full * (grad_probs - inner)).astype(bf16)
-    scale = HEAD_DIM ** (-0.5)
-    grad_queries = (
-        jnp.einsum("bhqk,bkhd->bqhd", grad_scores, keys_all, preferred_element_type=jnp.float32)
-        * scale
-    ).reshape(rows_all, D)
-    grad_keys = (
-        jnp.einsum("bhqk,bqhd->bkhd", grad_scores, queries, preferred_element_type=jnp.float32)
-        * scale
-    ).reshape(rows_all, D)
-    grad_values = jnp.einsum(
-        "bhqk,bqhd->bkhd", probs_full.astype(bf16), grad_mixed, preferred_element_type=jnp.float32
-    ).reshape(rows_all, D)
-    grad_b_query = jnp.sum(grad_queries, axis=0)
-    grad_b_value = jnp.sum(grad_values, axis=0)
-    qk_bf = jnp.concatenate([grad_queries, grad_keys], axis=1).astype(bf16)
-    values_bf = grad_values.astype(bf16)
-    grad_vo = jnp.concatenate([dot_head(normed_a, values_bf), grad_w_out], axis=1).astype(bf16)
-    grad_qk = dot_head(normed_a, qk_bf).astype(bf16)
-    sum_vo = scatter_bulk(grid, grad_vo, OUTER)
-    sum_qk = scatter_bulk(grid, grad_qk, OUTER)
-    qk_bf = after(qk_bf, grad_vo, grad_qk)
-    grad_normed_a = (dot_tail(qk_bf, table_qk) + dot_tail(values_bf, w_value)).reshape(
-        count, TOK, D
-    )
+    grad_w_out = dot_head(mixed, attended_bf).astype(bf16)
+    grad_mixed = dot_tail(attended_bf, w_out).astype(bf16)
+    proj_bf, proj_sums = attend_back(proj, grad_mixed)
+    grad_b_query, grad_b_value = proj_sums[0], proj_sums[1]
+    grad_qkv = [dot_head(normed_a, proj_bf[part]).astype(bf16) for part in range(3)]
+    put_vo = scatter_bulk(grid, [grad_qkv[2], grad_w_out], OUTER)
+    put_qk = scatter_bulk(grid, grad_qkv[:2], OUTER)
+    proj_bf = after(proj_bf, *grad_qkv, next(put_up))
+    grad_normed_a = sum(
+        dot_tail(proj_bf[part], w_qkv[:, part * D : (part + 1) * D]) for part in range(3)
+    ).reshape(count, TOK, D)
+    grad_normed_a = after(grad_normed_a, next(put_up), next(put_vo), next(put_qk))
     _, pull_first = jax.vjp(modulate, resid_in, shift_a, scale_a)
     grad_in_norm, grad_shift_a, grad_scale_a = pull_first(grad_normed_a)
     grad_hidden = (grad_mid + grad_in_norm).reshape(rows_all, D)
@@ -570,7 +749,12 @@
         axis=1,
     )
     grad_b_mods = jnp.sum(grad_mods, axis=0)
-    mods_bf = gather_small(grid, grad_mods.astype(bf16).reshape(-1, 128), (Z_AXIS, MIX_Q, MIX_P, CORE))
+    before = {
+        MIX_Q: [next(put_up), next(put_vo)],
+        CORE: [next(put_qk), next(put_up)],
+    }
+    mods_bf = grad_mods.astype(bf16).reshape(-1, 128)
+    mods_bf = gather_small(grid, mods_bf, (Z_AXIS, MIX_Q, MIX_P, CORE), before)
     mods_bf = mods_bf.reshape(image_total, 8 * D)
     grad_w_mods = matmul(cond_act, mods_bf)
     grad_cond_act = dot_tail(w_mods, mods_bf)
@@ -582,7 +766,9 @@
         preferred_element_type=jnp.float32,
     )
     grad_b_time = jnp.sum(grad_cond, axis=1)
-    cond_bf = gather_small(grid, grad_cond.astype(bf16), (3, 2, 1, 0)).reshape(D, image_total)
+    before = {X_AXIS: [next(put_vo), next(put_up)], Z_AXIS: [next(put_qk)]}
+    cond_bf = gather_small(grid, grad_cond.astype(bf16), (CORE, X_AXIS, Y_AXIS, Z_AXIS), before)
+    cond_bf = cond_bf.reshape(D, image_total)
     grad_w_time = dot_tail(time_act, cond_bf)
     grad_time_act = matmul(w_time, cond_bf)
     grad_time_pre = jax.vjp(jax.nn.silu, time_pre)[1](grad_time_act)[0]
@@ -615,49 +801,58 @@
     )
     tall = -(-small.shape[1] // 1024) * 8
     small = jnp.pad(small, ((0, 0), (0, tall * 128 - small.shape[1])))
-    small = scatter_small(grid, small.reshape(sizes + (tall, 128))).reshape(-1)
+    before = {
+        CORE: [next(put_vo)],
+        X_AXIS: [next(put_qk)],
+        Y_AXIS: [next(put_vo)],
+        Z_AXIS: [next(put_qk)],
+    }
+    small = scatter_small(grid, small.reshape(sizes + (tall, 128)), before).reshape(-1)
     at = bias_rows
     sum_patch = small[at : at + rows * PATCH_FEAT].reshape(rows, PATCH_FEAT)
     at += rows * PATCH_FEAT
     sum_head = small[at : at + rows * PATCH_FEAT].reshape(rows, PATCH_FEAT)
 
-    reduced = (
-        jnp.concatenate([sum_qk, sum_vo, sum_up, grad_w_mods, grad_w_time], axis=1),
+    sum_vo, sum_qk, sum_up = last(put_vo), last(put_qk), last(put_up)
+    sum_down = sum_down.astype(jnp.float32)
+    grads_in = (sum_qk, sum_vo, sum_up, grad_w_mods, grad_w_time)
+    grads_other = (
         sum_down,
         jnp.concatenate([grad_t_first, sum_patch, grad_w_class, sum_head], axis=1),
-        small[:bias_rows],
-    )
-    firsts = (first_in, first_down, first_side, first_bias)
-    seconds = (second_in, second_down, second_side, second_bias)
-    results = [
-        adam_direction(masters[index], reduced[index], firsts[index], seconds[index])
-        for index in range(4)
-    ]
-    directions = [item[2] for item in results]
-    sums = sum_small(grid, as_vector([loss_local] + block_squares(masters) + block_squares(directions)))
-    loss_sum, weight_sq, update_sq = sums[0], sums[1:13], sums[13:25]
-    weight_norms = jnp.sqrt(weight_sq)
-    update_norms = jnp.sqrt(update_sq)
-    trust = weight_norms / update_norms
-    factors = block_factors(trust)
-    updated = [masters[index] - RATE * factors[index] * directions[index] for index in range(4)]
+        small[None, :bias_rows],
+    )
+    masters = (weights_in, weights_down, weights_side, biases[None])
+    firsts = (first_in, first_down, first_side, first_bias[None])
+    seconds = (second_in, second_down, second_side, second_bias[None])
+    shapes = [master.shape for master in masters]
+    results = whole_kernel(
+        partial(direction_kernel, [grad.shape[1] for grad in grads_in]),
+        masters + firsts + seconds + grads_in + grads_other,
+        shapes * 3 + [(8, 128)],
+    )
+    loss_spot = jnp.arange(8, dtype=jnp.int32)[:, None] == 3
+    sums = sum_small(grid, results[12] + jnp.where(loss_spot, loss_local, 0.0))
+    updated = whole_kernel(
+        update_kernel, (sums,) + masters + tuple(results[8:12]), shapes + [(8, 128)]
+    )
+    norms = updated[4]
     return (
-        loss_sum,
+        sums[3, 0],
         updated[0],
         updated[1],
         updated[2],
-        updated[3],
-        results[0][0],
-        results[1][0],
-        results[2][0],
+        updated[3][0],
+        results[0],
+        results[1],
+        results[2],
         results[3][0],
-        results[0][1],
-        results[1][1],
-        results[2][1],
-        results[3][1],
-        trust,
-        weight_norms,
-        update_norms,
+        results[4],
+        results[5],
+        results[6],
+        results[7][0],
+        norms[2, :12],
+        norms[0, :12],
+        norms[1, :12],
     )
 
 

time: 742 us -> 584 us (0.79)
  other arithmetic: 164 us -> 85.3 us
  local copies, waits for them, and re-layouts: 117 us -> 64 us
  waiting for transfers between devices: 222 us -> 172 us
  Pallas kernels: 17.6 us -> 62.8 us
  matrix products: 103 us -> 86 us
  starting transfers between devices: 103 us -> 89.1 us
  between operations: 4.95 us -> 16.6 us
    pallas_call x0 -> x10, Pallas kernels: none -> 55 us  [the longest x1 20.1 us: attend_back(): pl.pallas_call(attend_back_kernel, grid=(D // HEAD_COLS, count), out_shap...]
    ppermute x93 -> x73, waiting for transfers between devices: 222 us -> 172 us  [move(): return lax.ppermute(values, AXIS, pairs)]
    add x5, other arithmetic: 31.1 us -> 0.08 us  [sum_small(): values = values + grid.flip(values, axis, bit)]
    reshape x8 -> x0, local copies, waits for them, and re-layouts: 28 us -> none  [the longest x2 7.58 us: per_device(): keys_all = proj_qk[:, D:].astype(bf16).reshape(head_shape)]
    dynamic_slice x15 -> x0, local copies, waits for them, and re-layouts: 18.8 us -> none  [the longest x7 17.5 us: entry(): return lax.dynamic_index_in_dim(current, place, axis)]
    dot_general x9, matrix products: 20.8 us -> 36.2 us  [matmul(): return jnp.dot(left, right, preferred_element_type=jnp.float32)]
    select_n x6 -> x1, other arithmetic: 16.5 us -> 1.16 us  [per_device(): sums = sum_small(grid, results[12] + jnp.where(loss_spot, loss_local, 0.0))]
    dot_general x8 -> x10, matrix products: 33.9 us -> 19 us  [dot_head(): lax.dot_general(left, right, (((0,), (0,)), ((), ())), preferred_element_...]
  transfers between devices with their start and end apart: 93 -> 76, of which waited for: 48 -> 39; matrix products, arithmetic and copies ran while one was open for 26% -> 23% of each run, Pallas kernels for 1% -> 5%
where the time goes in v3:
time: 584 us; the launch traced here: 576 us
  waiting for transfers between devices  172 us (29%)
  starting transfers between devices  89.1 us (15%)
  matrix products  86 us (15%)
  other arithmetic  85.3 us (15%)
  local copies, waits for them, and re-layouts  64 us (11%)
  Pallas kernels  62.8 us (11%)
  between operations  16.6 us (3%)
    ppermute x73, waiting for transfers between devices, move(): return lax.ppermute(values, AXIS, pairs)  172 us
    ppermute x73, starting transfers between devices, move(): return lax.ppermute(values, AXIS, pairs)  89 us
    unnamed x318, local copies, waits for them, and re-layouts  44.6 us
    dot_general x9, matrix products, matmul(): return jnp.dot(left, right, preferred_element_type=jnp.float32)  36.2 us
    dot_general x13, matrix products, dot_tail(): lax.dot_general(left, right, (((1,), (1,)), ((), ())), preferred_element_...  29.6 us
    convert_element_type x15, other arithmetic, scatter_bulk(): total = grid.ahead(total.astype(jnp.bfloat16), axis, 1)  28.3 us
    pallas_call x1, Pallas kernels, attend_back(): pl.pallas_call(attend_back_kernel, grid=(D // HEAD_COLS, count), out_shap...  20.1 us
    dot_general x10, matrix products, dot_head(): lax.dot_general(left, right, (((0,), (0,)), ((), ())), preferred_element_...  19 us
  transfers between devices with their start and end apart: 76, of which 39 were waited for; matrix products, arithmetic and copies ran while one was open for 23% of the time, Pallas kernels for 5%

profile of v3, /device:TPU:0, one launch (start us, length us, event | category | flops | bytes accessed | tf_op | source)
XLA Modules:
  0.0 575.6 jit_solution(15538342771805839927)
XLA Ops:
  31.5 16.2 %collective-permute-done.5 = bf16[2,2,2,16,128]{4,3,2,1,0:T(8,128)(2,1)S(1)} collective-permute-done((bf16[2,2,2,16,128]{4,3,2,1,0:T(8,128)(2,1)S(1)}, bf16[2,2,2,16,128]{4,3,2,1,0:T(8,128)(2,1)S(1)}, u32[]{:S(2)}, u32[]{:S(2)}) %collective-permute-start.5) | collective-permute-done | bytes 32800 | tf_op jit(solution)/shard_map/ppermute | solution.py:229
  64.8 7.7 %collective-permute-done.14 = bf16[2,32,2048]{2,1,0:T(8,128)(2,1)S(1)} collective-permute-done((bf16[2,32,2048]{2,1,0:T(8,128)(2,1)}, bf16[2,32,2048]{2,1,0:T(8,128)(2,1)S(1)}, u32[]{:S(2)}, u32[]{:S(2)}) %collective-permute-start.14) | collective-permute-done | bytes 262176 | tf_op jit(solution)/shard_map/ppermute | solution.py:229
  72.5 13.6 %collective-permute-done.13 = bf16[2,128,1024]{2,1,0:T(8,128)(2,1)S(1)} collective-permute-done((bf16[2,128,1024]{2,1,0:T(8,128)(2,1)S(1)}, bf16[2,128,1024]{2,1,0:T(8,128)(2,1)S(1)}, u32[]{:S(2)}, u32[]{:S(2)}) %collective-permute-start.13) | collective-permute-done | bytes 524320 | tf_op jit(solution)/shard_map/ppermute | solution.py:229
  109.2 10.6 %collective-permute-done.21 = bf16[2,32,2048]{2,1,0:T(8,128)(2,1)S(1)} collective-permute-done((bf16[2,32,2048]{2,1,0:T(8,128)(2,1)S(1)}, bf16[2,32,2048]{2,1,0:T(8,128)(2,1)S(1)}, u32[]{:S(2)}, u32[]{:S(2)}) %collective-permute-start.21) | collective-permute-done | bytes 262176 | tf_op jit(solution)/shard_map/ppermute | solution.py:229
  124.3 10.6 %collective-permute-done.20 = bf16[2,128,1024]{2,1,0:T(8,128)(2,1)S(1)} collective-permute-done((bf16[2,128,1024]{2,1,0:T(8,128)(2,1)S(1)}, bf16[2,128,1024]{2,1,0:T(8,128)(2,1)S(1)}, u32[]{:S(2)}, u32[]{:S(2)}) %collective-permute-start.20) | collective-permute-done | bytes 524320 | tf_op jit(solution)/shard_map/ppermute | solution.py:229
  158.7 9.7 %collective-permute-done.26.refs_1_ = bf16[8,128,1024]{2,1,0:T(8,128)(2,1)} collective-permute-done((bf16[8,128,1024]{2,1,0:T(8,128)(2,1)S(1)}, bf16[8,128,1024]{2,1,0:T(8,128)(2,1)}, u32[]{:S(2)}, u32[]{:S(2)}) %collective-permute-start.26) | collective-permute-done | bytes 2097184 | tf_op jit(solution)/shard_map/ppermute | solution.py:229
  180.0 6.6 %add_convert_fusion.query_ref.key_ref.value_ref = bf16[512,3072]{1,0:T(8,128)(2,1)S(1)} fusion(bf16[512,1024]{1,0:T(8,128)(2,1)} %fusion.27, bf16[1024,4096]{1,0:T(8,128)(2,1)} %all-gather.3.cloned.1.call-done, f32[3072]{0:T(1024)S(1)} %pad_maximum_fusion.22), kind=kOutput, calls=%fused_computation.3 | convolution fusion | flops 3224371200 | bytes 10498048 | tf_op jit(solution)/shard_map/dot_general | solution.py:37
  186.6 9.8 %shard_map.279 = bf16[512,1024]{1,0:T(8,128)(2,1)S(1)} custom-call(bf16[512,3072]{1,0:T(8,128)(2,1)S(1)} %add_convert_fusion.query_ref.key_ref.value_ref, bf16[512,3072]{1,0:T(8,128)(2,1)S(1)} %add_convert_fusion.query_ref.key_ref.value_ref, bf16[512,3072]{1,0:T(8,128)(2,1)S(1)} %add_convert_fusion.query_ref.key_ref.value_ref), custom_call_target="tpu_custom_call" | custom-call | flops 2147483648 | bytes 12582912 | tf_op jit(solution)/shard_map/pallas_call | solution.py:505
  204.5 5.9 %multiply_convert_fusion = (bf16[512,2048]{1,0:T(8,128)(2,1)}, f32[512,2048]{1,0:T(8,128)}) fusion(f32[2048]{0:T(1024)S(1)} %copy-done.111, bf16[512,1024]{1,0:T(8,128)(2,1)S(1)} %fusion.24, bf16[1024,2048]{1,0:T(8,128)(2,1)S(1)} %bitcast.500), kind=kOutput, calls=%fused_computation.22 | convolution fusion | flops 2157969408 | bytes 11542528 | tf_op jit(solution)/shard_map/dot_general | solution.py:37
  210.4 7.8 %multiply_convert_fusion.1 = (bf16[512,2048]{1,0:T(8,128)(2,1)S(1)}, f32[512,2048]{1,0:T(8,128)}) fusion(f32[2048]{0:T(1024)S(1)} %copy-done.112, bf16[512,1024]{1,0:T(8,128)(2,1)} %copy-done.78, bf16[1024,2048]{1,0:T(8,128)(2,1)} %all-gather.5.cloned.1.call-done), kind=kOutput, calls=%fused_computation.23 | convolution fusion | flops 2157969408 | bytes 11542528 | tf_op jit(solution)/shard_map/dot_general | solution.py:37
  218.3 6.4 %fusion.160 = (f32[512]{0:T(512)S(1)}, f32[512,1024]{1,0:T(8,128)}, f32[512,1024]{1,0:T(8,128)}) fusion(f32[512,1024]{1,0:T(8,128)S(1)} %copy-done.53, f32[2,1024]{1,0:T(2,128)S(1)} %get-tuple-element.165, f32[1024]{0:T(1024)S(1)} %copy-done.117, bf16[4096,1024]{1,0:T(8,128)(2,1)S(1)} %bitcast.481, bf16[512,2048]{1,0:T(8,128)(2,1)S(1)} %copy-done.68, ...), kind=kOutput, calls=%fused_computation.455 | convolution fusion | flops 4305452544 | bytes 18888704 | tf_op jit(solution)/shard_map/dot_general | solution.py:37
  236.0 7.2 %convolution_convert_fusion = bf16[4096,1024]{1,0:T(8,128)(2,1)} fusion(bf16[512,1024]{1,0:T(8,128)(2,1)S(1)} %bitcast.522, bf16[512,2048]{1,0:T(8,128)(2,1)S(1)} %copy-done.69, bf16[512,2048]{1,0:T(8,128)(2,1)S(1)} %copy-done.71), kind=kOutput, calls=%fused_computation | convolution fusion | flops 4307550208 | bytes 13631488 | tf_op jit(solution)/shard_map/dot_general | solution.py:47
  243.2 7.4 %fusion.177 = f32[512,4096]{1,0:T(8,128)S(1)} fusion(bf16[512,1024]{1,0:T(8,128)(2,1)} %bitcast.523, bf16[4096,1024]{1,0:T(8,128)(2,1)} %bitcast.478), kind=kOutput, calls=%fused_computation.470 | convolution fusion | flops 4294967296 | bytes 17825792 | tf_op jit(solution)/shard_map/dot_general | solution.py:41
  250.7 6.7 %fusion.155 = (f32[2048]{0:T(1024)S(1)}, bf16[512,2048]{1,0:T(8,128)(2,1)S(1)}, f32[2048]{0:T(1024)S(1)}, bf16[512,2048]{1,0:T(8,128)(2,1)S(1)}) fusion(f32[512,2048]{1,0:T(8,128)S(1)} %copy-done.64, f32[2048]{0:T(1024)S(1)} %copy-done.111, f32[512,4096]{1,0:T(8,128)S(1)} %fusion.177, f32[512,2048]{1,0:T(8,128)S(1)} %copy-done.65, f32[2048]{0:T(1024)S(1)} %copy-done.112), kind=kLoop, calls=%fused_computation.452 | loop fusion | flops 46133248 | bytes 21004288 | tf_op jit(solution)/shard_map/reduce_sum | solution.py:704
  275.7 5.3 fusion.178
  291.6 20.1 %shard_map.283 = (bf16[3,512,1024]{2,1,0:T(8,128)(2,1)S(1)}, f32[8,1024]{1,0:T(8,128)S(1)}) custom-call(bf16[512,3072]{1,0:T(8,128)(2,1)S(1)} %add_convert_fusion.query_ref.key_ref.value_ref, bf16[512,3072]{1,0:T(8,128)(2,1)S(1)} %add_convert_fusion.query_ref.key_ref.value_ref, bf16[512,3072]{1,0:T(8,128)(2,1)S(1)} %add_convert_fusion.query_ref.key_ref.value_ref, ...), custom_call_target="tpu_custom_call" | custom-call | flops 4831838208 | bytes 25165824 | tf_op jit(solution)/shard_map/pallas_call | solution.py:522
  311.8 4.8 add_convert_fusion.1
  340.2 6.4 %collective-permute-done.45 = bf16[4,2,32,4096]{3,2,1,0:T(8,128)(2,1)} collective-permute-done((bf16[4,2,32,4096]{3,2,1,0:T(8,128)(2,1)}, bf16[4,2,32,4096]{3,2,1,0:T(8,128)(2,1)}, u32[]{:S(2)}, u32[]{:S(2)}) %collective-permute-start.45) | collective-permute-done | bytes 2097184 | tf_op jit(solution)/shard_map/ppermute | solution.py:229
  371.7 4.8 fusion.62
  378.1 4.4 collective-permute-start.51
  394.8 11.3 %collective-permute-done.47 = bf16[2,32,4096]{2,1,0:T(8,128)(2,1)S(1)} collective-permute-done((bf16[2,32,4096]{2,1,0:T(8,128)(2,1)}, bf16[2,32,4096]{2,1,0:T(8,128)(2,1)S(1)}, u32[]{:S(2)}, u32[]{:S(2)}) %collective-permute-start.47) | collective-permute-done | bytes 524320 | tf_op jit(solution)/shard_map/ppermute | solution.py:229
  417.5 18.1 %collective-permute-done.35 = bf16[2,32,2048]{2,1,0:T(8,128)(2,1)S(1)} collective-permute-done((bf16[2,32,2048]{2,1,0:T(8,128)(2,1)S(1)}, bf16[2,32,2048]{2,1,0:T(8,128)(2,1)S(1)}, u32[]{:S(2)}, u32[]{:S(2)}) %collective-permute-start.35) | collective-permute-done | bytes 262176 | tf_op jit(solution)/shard_map/ppermute | solution.py:229
  466.4 5.7 collective-permute-done.43
  534.3 7.6 %shard_map.289 = (f32[32,17408]{1,0:T(8,128)}, f32[128,1024]{1,0:T(8,128)}, f32[32,1288]{1,0:T(8,128)}, f32[1,608]{1,0:T(1,128)S(1)}, f32[32,17408]{1,0:T(8,128)...) custom-call(f32[32,17408]{1,0:T(8,128)S(1)} %copy-done.1, ...), custom_call_target="tpu_custom_call" | custom-call | flops 51106880 | bytes 20442752 | tf_op jit(solution)/shard_map/pallas_call | solution.py:171
  (693 shorter events, 344.3 us)
Async XLA Ops:
  7.2 172.8 %all-gather.3.cloned.1.call-start = ((), (), s32[]{:S(2)}) async-start(), calls=%async_computation.1 | async-start | bytes 8650752 | tf_op jit(solution)/shard_map/all_gather | solution.py:598
  9.9 200.4 %all-gather.5.cloned.1.call-start = ((), (), s32[]{:S(2)}) async-start(), calls=%async_computation.2 | async-start | bytes 4325376 | tf_op jit(solution)/shard_map/all_gather | solution.py:601
  14.5 508.3 %reduce-scatter.2.cloned.1.call-start = ((), (), s32[]{:S(2)}) async-start(), calls=%async_computation.3 | async-start | bytes 8650752 | tf_op jit(solution)/shard_map/reduce_scatter | solution.py:696
  20.5 31.3 %collective-permute-start.9 = (bf16[2,32,2048]{2,1,0:T(8,128)(2,1)}, bf16[2,32,2048]{2,1,0:T(8,128)(2,1)}, u32[]{:S(2)}, u32[]{:S(2)}) collective-permute-start(bf16[2,32,2048]{2,1,0:T(8,128)(2,1)} %get-tuple-element.138), channel_id=1, source_target_pairs={{0,24},{1,25},{2,26},{3,27},{4,28},{5,29},{6,30},{7,31},{8,0},{9,1... | collective-permute-start | bytes 786440 | tf_op jit(solution)/shard_map/ppermute | solution.py:229
  27.0 24.8 %collective-permute-start.8 = (bf16[2,128,1024]{2,1,0:T(8,128)(2,1)S(1)}, bf16[2,128,1024]{2,1,0:T(8,128)(2,1)S(1)}, u32[]{:S(2)}, u32[]{:S(2)}) collective-permute-start(bf16[2,128,1024]{2,1,0:T(8,128)(2,1)S(1)} %get-tuple-element.132), channel_id=1, source_target_pairs={{0,24},{1,25},{2,26},{3,27},{4,28},{5,29},{6,30},{7,31},{8,0},{9,1... | collective-permute-start | bytes 1572872 | tf_op jit(solution)/shard_map/ppermute | solution.py:229
  28.4 20.1 %collective-permute-start.6 = (bf16[2,2,2,16,128]{4,3,2,1,0:T(8,128)(2,1)S(1)}, bf16[2,2,2,16,128]{4,3,2,1,0:T(8,128)(2,1)S(1)}, u32[]{:S(2)}, u32[]{:S(2)}) collective-permute-start(bf16[2,2,2,16,128]{4,3,2,1,0:T(8,128)(2,1)S(1)} %pad_maximum_fusion.14), channel_id=1, source_target_pairs={{0,16},{1,17},{2,18},{3,19},{4,20},{5,21},{6,22},{7,23},{8,24},{9,... | collective-permute-start | bytes 98312 | tf_op jit(solution)/shard_map/ppermute | solution.py:229
  28.5 19.2 %collective-permute-start.5 = (bf16[2,2,2,16,128]{4,3,2,1,0:T(8,128)(2,1)S(1)}, bf16[2,2,2,16,128]{4,3,2,1,0:T(8,128)(2,1)S(1)}, u32[]{:S(2)}, u32[]{:S(2)}) collective-permute-start(bf16[2,2,2,16,128]{4,3,2,1,0:T(8,128)(2,1)S(1)} %pad_maximum_fusion.14), channel_id=1, source_target_pairs={{0,24},{1,25},{2,26},{3,27},{4,28},{5,29},{6,30},{7,31},{8,0},{9,1... | collective-permute-start | bytes 98312 | tf_op jit(solution)/shard_map/ppermute | solution.py:229
  57.8 28.3 %collective-permute-start.13 = (bf16[2,128,1024]{2,1,0:T(8,128)(2,1)S(1)}, bf16[2,128,1024]{2,1,0:T(8,128)(2,1)S(1)}, u32[]{:S(2)}, u32[]{:S(2)}) collective-permute-start(bf16[2,128,1024]{2,1,0:T(8,128)(2,1)S(1)} %collective-permute-done.8), channel_id=1, source_target_pairs={{0,24},{1,25},{2,26},{3,27},{4,28},{5,29},{6,30},{7,31},{8,0},{9,1... | collective-permute-start | bytes 1572872 | tf_op jit(solution)/shard_map/ppermute | solution.py:229
  120.9 19.6 %collective-permute-start.27 = (bf16[8,32,2048]{2,1,0:T(8,128)(2,1)S(1)}, bf16[8,32,2048]{2,1,0:T(8,128)(2,1)}, u32[]{:S(2)}, u32[]{:S(2)}) collective-permute-start(bf16[8,32,2048]{2,1,0:T(8,128)(2,1)S(1)} %bitcast.497), channel_id=1, source_target_pairs={{0,4},{1,3},{2,6},{3,1},{4,0},{5,7},{6,2},{7,5},{8,12},{9,11},{10,... | collective-permute-start | bytes 3145736 | tf_op jit(solution)/shard_map/ppermute | solution.py:229
  139.6 28.7 %collective-permute-start.26 = (bf16[8,128,1024]{2,1,0:T(8,128)(2,1)S(1)}, bf16[8,128,1024]{2,1,0:T(8,128)(2,1)}, u32[]{:S(2)}, u32[]{:S(2)}) collective-permute-start(bf16[8,128,1024]{2,1,0:T(8,128)(2,1)S(1)} %bitcast.494), channel_id=1, source_target_pairs={{0,4},{1,3},{2,6},{3,1},{4,0},{5,7},{6,2},{7,5},{8,12},{9,11},{10,... | collective-permute-start | bytes 6291464 | tf_op jit(solution)/shard_map/ppermute | solution.py:229
  148.3 20.0 %collective-permute-start.23 = (f32[128,128]{1,0:T(8,128)S(1)}, f32[128,128]{1,0:T(8,128)S(1)}, u32[]{:S(2)}, u32[]{:S(2)}) collective-permute-start(f32[128,128]{1,0:T(8,128)S(1)} %get-tuple-element.139), channel_id=1, source_target_pairs={{0,24},{1,25},{2,26},{3,27},{4,28},{5,29},{6,30},{7,31},{8,0},{9,1... | collective-permute-start | bytes 196616 | tf_op jit(solution)/shard_map/ppermute | solution.py:229
  152.5 20.0 %collective-permute-start.30 = (bf16[8,128,1024]{2,1,0:T(8,128)(2,1)S(1)}, bf16[8,128,1024]{2,1,0:T(8,128)(2,1)}, u32[]{:S(2)}, u32[]{:S(2)}) collective-permute-start(bf16[8,128,1024]{2,1,0:T(8,128)(2,1)S(1)} %bitcast.495), channel_id=1, source_target_pairs={{0,1},{1,0},{2,3},{3,2},{4,5},{5,4},{6,7},{7,6},{8,9},{9,8},{10,11... | collective-permute-start | bytes 6291464 | tf_op jit(solution)/shard_map/ppermute | solution.py:229
  316.6 30.0 %collective-permute-start.45 = (bf16[4,2,32,4096]{3,2,1,0:T(8,128)(2,1)}, bf16[4,2,32,4096]{3,2,1,0:T(8,128)(2,1)}, u32[]{:S(2)}, u32[]{:S(2)}) collective-permute-start(bf16[4,2,32,4096]{3,2,1,0:T(8,128)(2,1)} %bitcast.110), channel_id=1, source_target_pairs={{0,4},{1,3},{2,6},{3,1},{4,0},{5,7},{6,2},{7,5},{8,12},{9,11},{10,... | collective-permute-start | bytes 6291464 | tf_op jit(solution)/shard_map/ppermute | solution.py:229
  325.0 26.0 %collective-permute-start.33 = (bf16[16,32,2048]{2,1,0:T(8,128)(2,1)}, bf16[16,32,2048]{2,1,0:T(8,128)(2,1)}, u32[]{:S(2)}, u32[]{:S(2)}) collective-permute-start(bf16[16,32,2048]{2,1,0:T(8,128)(2,1)} %shard_map.284), channel_id=1, source_target_pairs={{0,1},{1,0},{2,3},{3,2},{4,5},{5,4},{6,7},{7,6},{8,9},{9,8},{10,11... | collective-permute-start | bytes 6291464 | tf_op jit(solution)/shard_map/ppermute | solution.py:229
  330.7 24.6 %collective-permute-start.39 = (bf16[16,32,2048]{2,1,0:T(8,128)(2,1)}, bf16[16,32,2048]{2,1,0:T(8,128)(2,1)}, u32[]{:S(2)}, u32[]{:S(2)}) collective-permute-start(bf16[16,32,2048]{2,1,0:T(8,128)(2,1)} %shard_map.286), channel_id=1, source_target_pairs={{0,1},{1,0},{2,3},{3,2},{4,5},{5,4},{6,7},{7,6},{8,9},{9,8},{10,11... | collective-permute-start | bytes 6291464 | tf_op jit(solution)/shard_map/ppermute | solution.py:229
  348.2 18.8 %collective-permute-start.46 = (bf16[2,32,4096]{2,1,0:T(8,128)(2,1)S(1)}, bf16[2,32,4096]{2,1,0:T(8,128)(2,1)S(1)}, u32[]{:S(2)}, u32[]{:S(2)}) collective-permute-start(bf16[2,32,4096]{2,1,0:T(8,128)(2,1)S(1)} %fusion.46), channel_id=1, source_target_pairs={{0,24},{1,25},{2,26},{3,27},{4,28},{5,29},{6,30},{7,31},{8,0},{9,1... | collective-permute-start | bytes 1572872 | tf_op jit(solution)/shard_map/ppermute | solution.py:229
  353.6 56.4 %collective-permute-start.34 = (bf16[4,2,32,2048]{3,2,1,0:T(8,128)(2,1)}, bf16[4,2,32,2048]{3,2,1,0:T(8,128)(2,1)}, u32[]{:S(2)}, u32[]{:S(2)}) collective-permute-start(bf16[4,2,32,2048]{3,2,1,0:T(8,128)(2,1)} %bitcast.87), channel_id=1, source_target_pairs={{0,4},{1,3},{2,6},{3,1},{4,0},{5,7},{6,2},{7,5},{8,12},{9,11},{10,... | collective-permute-start | bytes 3145736 | tf_op jit(solution)/shard_map/ppermute | solution.py:229
  358.3 53.4 %collective-permute-start.40 = (bf16[4,2,32,2048]{3,2,1,0:T(8,128)(2,1)}, bf16[4,2,32,2048]{3,2,1,0:T(8,128)(2,1)}, u32[]{:S(2)}, u32[]{:S(2)}) collective-permute-start(bf16[4,2,32,2048]{3,2,1,0:T(8,128)(2,1)} %bitcast.100), channel_id=1, source_target_pairs={{0,4},{1,3},{2,6},{3,1},{4,0},{5,7},{6,2},{7,5},{8,12},{9,11},{10,... | collective-permute-start | bytes 3145736 | tf_op jit(solution)/shard_map/ppermute | solution.py:229
  386.8 19.3 %collective-permute-start.47 = (bf16[2,32,4096]{2,1,0:T(8,128)(2,1)}, bf16[2,32,4096]{2,1,0:T(8,128)(2,1)S(1)}, u32[]{:S(2)}, u32[]{:S(2)}) collective-permute-start(bf16[2,32,4096]{2,1,0:T(8,128)(2,1)} %fusion.45), channel_id=1, source_target_pairs={{0,24},{1,25},{2,26},{3,27},{4,28},{5,29},{6,30},{7,31},{8,0},{9,1... | collective-permute-start | bytes 1572872 | tf_op jit(solution)/shard_map/ppermute | solution.py:229
  407.7 37.2 %collective-permute-start.48 = (bf16[2,32,4096]{2,1,0:T(8,128)(2,1)S(1)}, bf16[2,32,4096]{2,1,0:T(8,128)(2,1)S(1)}, u32[]{:S(2)}, u32[]{:S(2)}) collective-permute-start(bf16[2,32,4096]{2,1,0:T(8,128)(2,1)S(1)} %fusion.43), channel_id=1, source_target_pairs={{0,24},{1,25},{2,26},{3,27},{4,28},{5,29},{6,30},{7,31},{8,0},{9,1... | collective-permute-start | bytes 1572872 | tf_op jit(solution)/shard_map/ppermute | solution.py:229
  411.2 24.5 %collective-permute-start.35 = (bf16[2,32,2048]{2,1,0:T(8,128)(2,1)S(1)}, bf16[2,32,2048]{2,1,0:T(8,128)(2,1)S(1)}, u32[]{:S(2)}, u32[]{:S(2)}) collective-permute-start(bf16[2,32,2048]{2,1,0:T(8,128)(2,1)S(1)} %fusion.74), channel_id=1, source_target_pairs={{0,24},{1,25},{2,26},{3,27},{4,28},{5,29},{6,30},{7,31},{8,0},{9,1... | collective-permute-start | bytes 786440 | tf_op jit(solution)/shard_map/ppermute | solution.py:229
  412.9 28.9 %collective-permute-start.41 = (bf16[2,32,2048]{2,1,0:T(8,128)(2,1)S(1)}, bf16[2,32,2048]{2,1,0:T(8,128)(2,1)S(1)}, u32[]{:S(2)}, u32[]{:S(2)}) collective-permute-start(bf16[2,32,2048]{2,1,0:T(8,128)(2,1)S(1)} %fusion.69), channel_id=1, source_target_pairs={{0,24},{1,25},{2,26},{3,27},{4,28},{5,29},{6,30},{7,31},{8,0},{9,1... | collective-permute-start | bytes 786440 | tf_op jit(solution)/shard_map/ppermute | solution.py:229
  417.5 27.4 %collective-permute-start.54 = (bf16[2,4,128,128]{3,2,1,0:T(8,128)(2,1)S(1)}, bf16[2,4,128,128]{3,2,1,0:T(8,128)(2,1)S(1)}, u32[]{:S(2)}, u32[]{:S(2)}) collective-permute-start(bf16[2,4,128,128]{3,2,1,0:T(8,128)(2,1)S(1)} %pad_maximum_fusion.12), channel_id=1, source_target_pairs={{0,2},{1,5},{2,0},{3,7},{4,6},{5,1},{6,4},{7,3},{8,10},{9,13},{10,... | collective-permute-start | bytes 786440 | tf_op jit(solution)/shard_map/ppermute | solution.py:229
  446.4 34.1 %collective-permute-start.49 = (bf16[32,4096]{1,0:T(8,128)(2,1)S(1)}, bf16[32,4096]{1,0:T(8,128)(2,1)}, u32[]{:S(2)}, u32[]{:S(2)}) collective-permute-start(bf16[32,4096]{1,0:T(8,128)(2,1)S(1)} %fusion.63), channel_id=1, source_target_pairs={{0,2},{1,5},{2,0},{3,7},{4,6},{5,1},{6,4},{7,3},{8,10},{9,13},{10,... | collective-permute-start | bytes 786440 | tf_op jit(solution)/shard_map/ppermute | solution.py:229
  (193 other events, 1666.9 us)
Sparse Core Ops, SparseCore 0:
  11.5 113.8 all-gather.2
  128.9 62.4 all-gather.4
  331.9 162.5 reduce-scatter.1

commit v4 on v3

--- a/solution.py
+++ b/solution.py
@@ -111,73 +111,169 @@
     return (first_new, second_new, direction)
 
 
-def direction_kernel(widths, *refs):
+def column_chunks(edges, shapes):
+    blocks = column_blocks()
+    chunks = []
+    for kind in (1, 2, 3):
+        parts = [
+            (block, start, stop or shapes[kind][1])
+            for block, (other, start, stop) in enumerate(blocks)
+            if other == kind
+        ]
+        chunks.append((kind, len(edges) - 2 + kind, 0, 0, shapes[kind][1], parts))
+    for number in range(len(edges) - 1):
+        for low in range(edges[number], edges[number + 1], 4 * D):
+            high = min(low + 4 * D, edges[number + 1])
+            parts = [
+                (block, max(start, low), min(stop, high))
+                for block, (kind, start, stop) in enumerate(blocks)
+                if kind == 0 and max(start, low) < min(stop, high)
+            ]
+            chunks.append((0, number, low - edges[number], low, high, parts))
+    return chunks
+
+
+def span(ref, low, high):
+    return ref if (low, high) == (0, ref.shape[1]) else ref.at[:, pl.ds(low, high - low)]
+
+
+def direction_kernel(edges, shapes, *refs):
     weights, firsts, seconds = refs[0:4], refs[4:8], refs[8:12]
-    grads, outs = refs[12:-13], refs[-13:]
+    count = len(edges) - 1 + 3
+    grads, outs = refs[12 : 12 + count], refs[12 + count : 25 + count]
+    scratch, in_sems, out_sems = refs[25 + count : -2], refs[-2], refs[-1]
     lanes = lax.broadcasted_iota(jnp.int32, (8, 128), 1)
     lines = lax.broadcasted_iota(jnp.int32, (8, 128), 0)
     sums = jnp.zeros((8, 128), jnp.float32)
-    pieces = []
-    at = 0
-    for number, width in enumerate(widths):
-        pieces.append((number, at, at + width))
-        at += width
-    for block, (kind, start, stop) in enumerate(column_blocks()):
-        if stop == 0:
-            stop = weights[kind].shape[1]
-        if kind == 0:
-            spans = [
-                (grads[number], max(start, low) - low, max(start, low), min(stop, high))
-                for number, low, high in pieces
-                if max(start, low) < min(stop, high)
+    chunks = column_chunks(edges, shapes)
+    loads, stores = [], []
+    for index, (kind, number, at, low, high, _) in enumerate(chunks):
+        sources = [span(group[kind], low, high) for group in (weights, firsts, seconds)]
+        sources.append(span(grads[number], at, at + high - low))
+        held = scratch[7 * kind : 7 * kind + 4]
+        loads.append(
+            [
+                pltpu.make_async_copy(
+                    source, span(held[slot], low, high), in_sems.at[index, slot]
+                )
+                for slot, source in enumerate(sources)
             ]
-        else:
-            spans = [(grads[len(widths) + kind - 1], start, start, stop)]
-        for grad_ref, offset, low, high in spans:
-            weight = weights[kind][:, low:high]
-            first_new, second_new, direction = adam_direction(
-                weight,
-                grad_ref[:, offset : offset + high - low],
-                firsts[kind][:, low:high],
-                seconds[kind][:, low:high],
+        )
+        for copy in loads[-1]:
+            copy.start()
+    for index, (kind, _, _, low, high, parts) in enumerate(chunks):
+        held, made = scratch[7 * kind : 7 * kind + 4], scratch[7 * kind + 4 : 7 * kind + 7]
+        for copy in loads[index]:
+            copy.wait()
+        for block, start, stop in parts:
+            columns = slice(start, stop)
+            weight = held[0][:, columns]
+            results = adam_direction(
+                weight, held[3][:, columns], held[1][:, columns], held[2][:, columns]
             )
-            outs[kind][:, low:high] = first_new
-            outs[4 + kind][:, low:high] = second_new
-            outs[8 + kind][:, low:high] = direction
+            for target, result in zip(made, results):
+                target[:, columns] = result
             here = lanes == block
             sums = sums + jnp.where(here & (lines == 0), jnp.sum(weight * weight), 0.0)
-            sums = sums + jnp.where(here & (lines == 1), jnp.sum(direction * direction), 0.0)
+            sums = sums + jnp.where(here & (lines == 1), jnp.sum(results[2] * results[2]), 0.0)
+        for slot in range(3):
+            stores.append(
+                pltpu.make_async_copy(
+                    span(made[slot], low, high),
+                    span(outs[4 * slot + kind], low, high),
+                    out_sems.at[index, slot],
+                )
+            )
+            stores[-1].start()
     outs[12][...] = sums
-
-
-def update_kernel(sums_ref, *refs):
-    weights, directions, outs = refs[0:4], refs[4:8], refs[8:]
+    for copy in stores:
+        copy.wait()
+
+
+def lamb_call(kernel, args, first_specs, shapes, held, slots):
+    any_space = pl.BlockSpec(memory_space=pl.ANY)
+    size = sum(arg.size for arg in args) + sum(math.prod(shape) for shape in shapes)
+    return pl.pallas_call(
+        kernel,
+        out_shape=[jax.ShapeDtypeStruct(shape, jnp.float32) for shape in shapes],
+        in_specs=first_specs + [any_space] * (len(args) - len(first_specs)),
+        out_specs=[any_space] * (len(shapes) - 1) + [pl.BlockSpec(memory_space=pltpu.VMEM)],
+        scratch_shapes=[pltpu.VMEM(shape, jnp.float32) for shape in held]
+        + [pltpu.SemaphoreType.DMA(slot) for slot in slots],
+        compiler_params=pltpu.CompilerParams(vmem_limit_bytes=60 * 2**20),
+        cost_estimate=pl.CostEstimate(
+            flops=10 * size, bytes_accessed=4 * size, transcendentals=size // 8
+        ),
+    )(*args)
+
+
+def directions(masters, firsts, seconds, grads_in, grads_other):
+    edges = [0]
+    for grad in grads_in:
+        edges.append(edges[-1] + grad.shape[1])
+    shapes = [master.shape for master in masters]
+    return lamb_call(
+        partial(direction_kernel, edges, shapes),
+        masters + firsts + seconds + grads_in + grads_other,
+        [],
+        shapes * 3 + [(8, 128)],
+        [shape for shape in shapes for _ in range(7)],
+        [(len(column_chunks(edges, shapes)), slot) for slot in (4, 3)],
+    )
+
+
+def update_kernel(edges, shapes, sums_ref, *refs):
+    weights, steps, outs = refs[0:4], refs[4:8], refs[8:13]
+    scratch, in_sems, out_sems = refs[13:-2], refs[-2], refs[-1]
     norms = jnp.sqrt(sums_ref[...])
     trust = norms[0:1] / norms[1:2]
     line = lax.broadcasted_iota(jnp.int32, (8, 128), 0)
     outs[4][...] = jnp.where(line == 2, trust, norms)
-    for block, (kind, start, stop) in enumerate(column_blocks()):
-        if stop == 0:
-            stop = weights[kind].shape[1]
-        factor = RATE * trust[0:1, block : block + 1]
-        outs[kind][:, start:stop] = (
-            weights[kind][:, start:stop] - factor * directions[kind][:, start:stop]
+    chunks = column_chunks(edges, shapes)
+    loads, stores = [], []
+    for index, (kind, _, _, low, high, _) in enumerate(chunks):
+        loads.append(
+            [
+                pltpu.make_async_copy(
+                    span(source[kind], low, high),
+                    span(scratch[3 * kind + slot], low, high),
+                    in_sems.at[index, slot],
+                )
+                for slot, source in enumerate((weights, steps))
+            ]
         )
-
-
-def whole_kernel(kernel, args, shapes):
-    vmem = pl.BlockSpec(memory_space=pltpu.VMEM)
-    size = sum(arg.size for arg in args) + sum(math.prod(shape) for shape in shapes)
-    return pl.pallas_call(
-        kernel,
-        out_shape=[jax.ShapeDtypeStruct(shape, jnp.float32) for shape in shapes],
-        in_specs=[vmem] * len(args),
-        out_specs=[vmem] * len(shapes),
-        compiler_params=pltpu.CompilerParams(vmem_limit_bytes=40 * 2**20),
-        cost_estimate=pl.CostEstimate(
-            flops=10 * size, bytes_accessed=4 * size, transcendentals=size // 8
-        ),
-    )(*args)
+        for copy in loads[-1]:
+            copy.start()
+    for index, (kind, _, _, low, high, parts) in enumerate(chunks):
+        held, made = scratch[3 * kind : 3 * kind + 2], scratch[3 * kind + 2]
+        for copy in loads[index]:
+            copy.wait()
+        for block, start, stop in parts:
+            columns = slice(start, stop)
+            factor = RATE * trust[0:1, block : block + 1]
+            made[:, columns] = held[0][:, columns] - factor * held[1][:, columns]
+        stores.append(
+            pltpu.make_async_copy(
+                span(made, low, high), span(outs[kind], low, high), out_sems.at[index]
+            )
+        )
+        stores[-1].start()
+    for copy in stores:
+        copy.wait()
+
+
+def updates(sums, masters, steps):
+    edges = [0, masters[0].shape[1]]
+    shapes = [master.shape for master in masters]
+    chunks = len(column_chunks(edges, shapes))
+    return lamb_call(
+        partial(update_kernel, edges, shapes),
+        (sums,) + masters + tuple(steps),
+        [pl.BlockSpec(memory_space=pltpu.VMEM)],
+        shapes + [(8, 128)],
+        [shape for shape in shapes for _ in range(3)],
+        [(chunks, 2), (chunks,)],
+    )
 
 
 Z_AXIS, Y_AXIS, X_AXIS, CORE, MIX_P, MIX_Q = range(6)
@@ -190,7 +286,7 @@
         elif count == 256:
             sizes = (8, 4, 4, 2)
         else:
-            sizes = (count, 1, 1, 1)
+            sizes = (count // 2, 1, 1, 2)
         self.count = count
         self.shape = sizes
         self.sizes = sizes + (sizes[X_AXIS], sizes[Y_AXIS])
@@ -243,44 +339,84 @@
     return lax.optimization_barrier((values,) + others)[0] if others else values
 
 
-def in_order(grid, pieces, axis):
-    size = grid.sizes[axis]
-    if size == 1:
-        return pieces[0][None]
-    if size == 2:
-        lower = grid.coords[axis] == 0
-        return jnp.stack(
-            [jnp.where(lower, pieces[0], pieces[1]), jnp.where(lower, pieces[1], pieces[0])]
-        )
-    twice = jnp.stack(pieces + pieces)
-    return lax.dynamic_slice_in_dim(twice, (size - grid.coords[axis]) % size, size, 0)
-
-
-def gather_small(grid, values, order, before=None):
+def gather_small(grid, values, order):
     for axis in order:
-        values = after(values, *(before or {}).get(axis, ()))
-        pieces = [values]
-        for shift in range(1, grid.sizes[axis]):
-            pieces.append(grid.ahead(values, axis, shift))
-        values = in_order(grid, pieces, axis)
+        values = values[None]
+        bit = 1
+        while bit < grid.sizes[axis]:
+            other = grid.flip(values, axis, bit)
+            lower = grid.coords[axis] // bit % 2 == 0
+            values = jnp.concatenate(
+                [jnp.where(lower, values, other), jnp.where(lower, other, values)]
+            )
+            bit *= 2
     return values
 
 
 def scatter_axis(grid, values, axis, dim):
-    def entry(shift):
-        return lax.dynamic_index_in_dim(values, grid.place(axis, shift), dim, keepdims=False)
-
-    total = entry(0)
-    for shift in range(1, grid.sizes[axis]):
-        total = total + grid.ahead(entry(-shift), axis, shift)
-    return total
-
-
-def scatter_small(grid, values, before=None):
+    bit = grid.sizes[axis]
+    while bit > 1:
+        bit //= 2
+        upper = grid.coords[axis] // bit % 2
+        kept = lax.dynamic_slice_in_dim(values, upper * bit, bit, dim)
+        sent = lax.dynamic_slice_in_dim(values, (1 - upper) * bit, bit, dim)
+        values = kept + grid.flip(sent, axis, bit)
+    return lax.squeeze(values, (dim,))
+
+
+def scatter_small(grid, values):
     for axis in (CORE, X_AXIS, Y_AXIS, Z_AXIS):
-        values = after(values, *(before or {}).get(axis, ()))
         values = scatter_axis(grid, values, axis, axis)
     return values
+
+
+def gather_and_scatter(grid, values, table, ready):
+    turned = jnp.swapaxes(table, Y_AXIS, X_AXIS)
+    table = jnp.where(grid.coords[CORE] == 0, table, turned)
+    for axis in (Z_AXIS, MIX_Q, MIX_P, CORE):
+        values = values[None]
+        bit = 1
+        while bit < grid.sizes[axis]:
+            lower = grid.coords[axis] // bit % 2 == 0
+            halves = table.reshape((table.shape[0] // 2, 2) + table.shape[1:])
+            even, odd = halves[:, 0], halves[:, 1]
+            kept = jnp.where(lower, even, odd)
+            sent = jnp.where(lower, odd, even).astype(values.dtype)
+            count = values.size // 128
+            packed = jnp.concatenate([values.reshape(-1, 128), sent.reshape(-1, 128)])
+            packed = grid.flip(packed, axis, bit)
+            other = packed[:count].reshape(values.shape)
+            values = jnp.concatenate(
+                [jnp.where(lower, values, other), jnp.where(lower, other, values)]
+            )
+            table = kept + packed[count:].reshape(kept.shape).astype(jnp.float32)
+            bit *= 2
+        table = table[0]
+        values = meet(values, *ready.get(axis, ()))
+    return values, table
+
+
+class Flow:
+    def __init__(self, steps):
+        self.steps = steps
+        self.out = next(steps)
+
+
+def meet(values, *flows):
+    given = [values] + [array for flow in flows for array in flow.out]
+    given = list(lax.optimization_barrier(tuple(given)))
+    values = given.pop(0)
+    for flow in flows:
+        count = len(flow.out)
+        flow.out = flow.steps.send(given[:count])
+        given = given[count:]
+    return values
+
+
+def last(flow):
+    while isinstance(flow.out, list):
+        flow.out = flow.steps.send(flow.out)
+    return flow.out
 
 
 def sum_small(grid, values):
@@ -292,7 +428,7 @@
     return values
 
 
-def relative_places(grid, order):
+def relative_places(grid, order, crossed=False):
     dims = (CORE,) + tuple(reversed(order))
     number = jnp.arange(grid.count, dtype=jnp.int32)
     shifts = {}
@@ -300,77 +436,110 @@
         shifts[axis] = number % grid.sizes[axis]
         number = number // grid.sizes[axis]
     core = (grid.coords[CORE] + shifts[CORE]) % grid.sizes[CORE]
-    x_ahead = jnp.where(core == 0, shifts[MIX_P], shifts[MIX_Q])
-    y_ahead = jnp.where(core == 0, shifts[MIX_Q], shifts[MIX_P])
+    first = core == 0
+
+    def place(axis, own):
+        if axis == Z_AXIS and crossed:
+            return own ^ shifts[axis]
+        return (own + shifts[axis]) % grid.sizes[axis]
+
+    x_own, y_own = grid.coords[X_AXIS], grid.coords[Y_AXIS]
+    p_place = place(MIX_P, jnp.where(first, x_own, y_own))
+    q_place = place(MIX_Q, jnp.where(first, y_own, x_own))
     return grid.join(
         (
-            (grid.coords[Z_AXIS] + shifts[Z_AXIS]) % grid.sizes[Z_AXIS],
-            (grid.coords[Y_AXIS] + y_ahead) % grid.sizes[Y_AXIS],
-            (grid.coords[X_AXIS] + x_ahead) % grid.sizes[X_AXIS],
+            place(Z_AXIS, grid.coords[Z_AXIS]),
+            jnp.where(first, q_place, p_place),
+            jnp.where(first, p_place, q_place),
             core,
         )
     ).astype(jnp.int32)
 
 
-def place_kernel(moves, where, *refs):
-    pieces, full, sems = refs[:-2], refs[-2], refs[-1]
+def place_kernel(layout, places, *refs):
+    parts, tables, sems = refs[: -1 - len(layout)], refs[-1 - len(layout) : -1], refs[-1]
     copies = []
-    for number, (piece, entry) in enumerate(moves):
-        copies.append(
-            pltpu.make_async_copy(
-                pieces[piece].at[entry], full.at[where[number]], sems.at[number]
-            )
-        )
+    entries, rows = parts[0].shape[0], parts[0].shape[1]
+    for number, part in enumerate(parts):
+        for entry in range(entries):
+            place = places[number * entries + entry]
+            at = 0
+            for table, groups in zip(tables, layout):
+                for group in range(groups):
+                    copies.append(
+                        pltpu.make_async_copy(
+                            part.at[entry, :, pl.ds(at, table.shape[2])],
+                            table.at[place, pl.ds(group * rows, rows)],
+                            sems.at[len(copies)],
+                        )
+                    )
+                    at += table.shape[2]
     for copy in copies:
         copy.start()
     for copy in copies:
         copy.wait()
 
 
-def gather_bulk(grid, shard, order):
-    rows, columns = shard.shape
-    parts = [shard]
+def gather_bulk(grid, shards, order):
+    rows = min(shard.shape[0] for shard in shards)
+    layout = [shard.shape[0] // rows for shard in shards]
+    pieces = [
+        shard[group * rows : (group + 1) * rows]
+        for shard, groups in zip(shards, layout)
+        for group in range(groups)
+    ]
+    parts = [jnp.concatenate(pieces, axis=1)]
+    columns = parts[0].shape[1]
     for axis in order:
         sent = jnp.stack(parts).reshape((-1, rows, columns))
         parts = [sent]
         for _ in range(1, grid.sizes[axis]):
-            parts.append(grid.ahead(parts[-1], axis, 1))
-            yield parts[-1]
-    if grid.sizes[CORE] == 2:
-        parts = parts + [grid.ahead(part, CORE, 1) for part in parts]
-    where = relative_places(grid, order)
-    entries = parts[0].shape[0]
-    moves = [(piece, entry) for piece in range(len(parts)) for entry in range(entries)]
+            parts = parts + (yield [grid.ahead(parts[-1], axis, 1)])
+    received = yield [grid.ahead(part, CORE, 1) for part in parts]
+    parts = parts + received
+    places = relative_places(grid, order)
+    shapes = [
+        (grid.count, groups * rows, shard.shape[1]) for shard, groups in zip(shards, layout)
+    ]
     if rows % 16 == 0:
-        full = pl.pallas_call(
-            partial(place_kernel, moves),
-            out_shape=jax.ShapeDtypeStruct((grid.count, rows, columns), shard.dtype),
+        tables = pl.pallas_call(
+            partial(place_kernel, layout),
+            out_shape=[jax.ShapeDtypeStruct(shape, parts[0].dtype) for shape in shapes],
             in_specs=[pl.BlockSpec(memory_space=pltpu.SMEM)]
             + [pl.BlockSpec(memory_space=pl.ANY)] * len(parts),
-            out_specs=pl.BlockSpec(memory_space=pltpu.VMEM),
-            scratch_shapes=[pltpu.SemaphoreType.DMA((len(moves),))],
-            compiler_params=pltpu.CompilerParams(vmem_limit_bytes=24 * 2**20),
+            out_specs=[pl.BlockSpec(memory_space=pltpu.VMEM)] * len(shapes),
+            scratch_shapes=[pltpu.SemaphoreType.DMA((grid.count * sum(layout),))],
+            compiler_params=pltpu.CompilerParams(vmem_limit_bytes=32 * 2**20),
             cost_estimate=pl.CostEstimate(
                 flops=0, bytes_accessed=4 * grid.count * rows * columns, transcendentals=0
             ),
-        )(where, *parts)
+        )(places, *parts)
     else:
         stacked = jnp.stack(parts).reshape((grid.count, rows, columns))
-        full = jnp.zeros((grid.count, rows, columns), shard.dtype).at[where].set(stacked)
-    yield full.reshape(grid.count * rows, columns)
-
-
-def pick_kernel(base, places, *refs):
-    tables, picked, sems = refs[:-2], refs[-2], refs[-1]
+        stacked = jnp.zeros_like(stacked).at[places].set(stacked)
+        tables = []
+        for shape, groups in zip(shapes, layout):
+            width = groups * shape[2]
+            table = stacked[:, :, :width].reshape((grid.count, rows, groups, shape[2]))
+            tables.append(table.transpose((0, 2, 1, 3)).reshape(shape))
+            stacked = stacked[:, :, width:]
+    yield tuple(table.reshape((-1, table.shape[2])) for table in tables)
+
+
+def pick_kernel(places, *refs):
+    tables, picked, sems = refs[:-3], refs[-3:-1], refs[-1]
     copies = []
-    for number in range(picked.shape[0]):
+    for number in range(sum(half.shape[0] for half in picked)):
+        half, entry = picked[0], number
+        if number >= half.shape[0]:
+            half, entry = picked[1], number - half.shape[0]
         at = 0
         for table in tables:
             width = table.shape[2]
             copies.append(
                 pltpu.make_async_copy(
-                    table.at[places[base + number]],
-                    picked.at[number, :, pl.ds(at, width)],
+                    table.at[places[number]],
+                    half.at[entry, :, pl.ds(at, width)],
                     sems.at[len(copies)],
                 )
             )
@@ -381,19 +550,21 @@
         copy.wait()
 
 
-def pick_rows(tables, places, base, count):
-    rows = tables[0].shape[1]
+def pick_rows(tables, places):
+    count, rows = tables[0].shape[:2]
     columns = sum(table.shape[2] for table in tables)
+    half = (count // 2, rows, columns)
     if rows % 16:
-        return jnp.concatenate([table[places[base : base + count]] for table in tables], axis=2)
+        picked = jnp.concatenate([table[places] for table in tables], axis=2)
+        return picked[: count // 2], picked[count // 2 :]
     return pl.pallas_call(
-        partial(pick_kernel, base),
-        out_shape=jax.ShapeDtypeStruct((count, rows, columns), jnp.bfloat16),
+        pick_kernel,
+        out_shape=[jax.ShapeDtypeStruct(half, jnp.bfloat16)] * 2,
         in_specs=[pl.BlockSpec(memory_space=pltpu.SMEM)]
         + [pl.BlockSpec(memory_space=pl.ANY)] * len(tables),
-        out_specs=pl.BlockSpec(memory_space=pltpu.VMEM),
+        out_specs=[pl.BlockSpec(memory_space=pltpu.VMEM)] * 2,
         scratch_shapes=[pltpu.SemaphoreType.DMA((count * len(tables),))],
-        compiler_params=pltpu.CompilerParams(vmem_limit_bytes=24 * 2**20),
+        compiler_params=pltpu.CompilerParams(vmem_limit_bytes=32 * 2**20),
         cost_estimate=pl.CostEstimate(
             flops=0, bytes_accessed=4 * count * rows * columns, transcendentals=0
         ),
@@ -403,35 +574,35 @@
 def scatter_bulk(grid, tables, order):
     rows = tables[0].shape[0] // grid.count
     columns = sum(table.shape[1] for table in tables)
-    places = relative_places(grid, order)
+    places = relative_places(grid, order, True)
     tables = [table.reshape(grid.count, rows, table.shape[1]) for table in tables]
-    kept = grid.count // grid.sizes[CORE]
     axes = tuple(reversed(order))
     dims = tuple(grid.sizes[axis] for axis in axes) + (rows, columns)
-    terms = []
-    for core in reversed(range(grid.sizes[CORE])):
-        picked = pick_rows(tables, places, core * kept, kept)
-        if core > 0:
-            picked = grid.ahead(picked, CORE, core)
-            yield picked
-        terms.append(picked.reshape(dims))
+    kept, sent = pick_rows(tables, places)
+    received = yield [grid.ahead(sent, CORE, 1)]
+    terms = [kept.reshape(dims), received[0].reshape(dims)]
 
     def entry(place):
         return sum(term[place].astype(jnp.float32) for term in terms)
 
     for axis in axes:
-        size = grid.sizes[axis]
+        if axis == Z_AXIS:
+            bit = 1
+            while bit < grid.sizes[axis]:
+                terms = [term.reshape((-1, 2) + term.shape[1:]) for term in terms]
+                sent = sum(term[:, 1].astype(jnp.float32) for term in terms)
+                received = yield [grid.flip(sent.astype(jnp.bfloat16), axis, bit)]
+                terms = [term[:, 0] for term in terms] + received
+                bit *= 2
+            terms = [term[0] for term in terms]
+            continue
         total = None
-        for step in range(1, size):
-            total = entry(step) if total is None else total.astype(jnp.float32) + entry(step)
-            total = grid.ahead(total.astype(jnp.bfloat16), axis, 1)
-            yield total
-        terms = [term[0] for term in terms] + ([] if total is None else [total])
+        for place in range(1, grid.sizes[axis]):
+            here = entry(place)
+            total = here if total is None else here + total.astype(jnp.float32)
+            total = (yield [grid.ahead(total.astype(jnp.bfloat16), axis, 1)])[0]
+        terms = [term[0] for term in terms] + [total]
     yield sum(term.astype(jnp.float32) for term in terms)
-
-
-def last(steps):
-    return list(steps)[-1]
 
 
 HEAD_COLS = 4 * HEAD_DIM
@@ -538,7 +709,7 @@
     )(proj, proj, proj, grad_mixed)
 
 
-OUTER = (MIX_P, Z_AXIS, MIX_Q)
+ORDER = (Z_AXIS, MIX_P, MIX_Q)
 
 
 def per_device(
@@ -596,13 +767,10 @@
     packed = jnp.pad(packed, (0, tall * 128 - width)).reshape(tall, 128)
     head_in = weights_in[:, : 4 * D].astype(bf16)
     table_qkvo = lax.all_gather(head_in, AXIS, axis=0, tiled=True)
-    half = FF // 2
     up_bf = weights_in[:, 4 * D : 4 * D + FF].astype(bf16)
-    table_first = lax.all_gather(up_bf[:, :half], AXIS, axis=0, tiled=True)
-    get_down = gather_bulk(grid, down_bf, OUTER)
-    get_up = gather_bulk(grid, up_bf[:, half:], OUTER)
-    before = {Y_AXIS: [next(get_down), next(get_up)]}
-    spread_all = gather_small(grid, packed, (CORE, X_AXIS, Y_AXIS, Z_AXIS), before)
+    table_up = lax.all_gather(up_bf, AXIS, axis=0, tiled=True)
+    get = Flow(gather_bulk(grid, [down_bf], ORDER))
+    spread_all = gather_small(grid, packed, (CORE, X_AXIS, Y_AXIS, Z_AXIS))
     spread_all = spread_all.reshape(count_all, tall * 128)
     bias_full = spread_all[:, :bias_rows].reshape(-1).astype(jnp.float32)
     at = bias_rows
@@ -636,19 +804,29 @@
         w_time, time_act, (((0,), (0,)), ((), ())), preferred_element_type=jnp.float32
     )
     cond = cond_part.reshape(sizes + (rows, image_total))
-    before = {CORE: [next(get_down), next(get_up)], Z_AXIS: [next(get_down), next(get_up)]}
-    cond = scatter_small(grid, cond, before)
+    cond = scatter_small(grid, cond)
     cond = cond + b_time[:, None] + dot_tail(w_class, onehot.astype(bf16))
     cond_act = jax.nn.silu(cond).astype(bf16)
 
-    mods = dot_head(cond_act, w_mods)
-    mods = mods.reshape(sizes[CORE], sizes[X_AXIS], sizes[Y_AXIS], sizes[Z_AXIS] * count, 8 * D)
+    def own_columns(part):
+        wide = jnp.zeros((image_total, D), jnp.float32)
+        return lax.dynamic_update_slice(wide, part.T, (0, my_rows))
+
+    mods = jnp.concatenate(
+        [dot_head(cond_act, w_mods), own_columns(cond), own_columns(time_pre)], axis=1
+    )
+    mods = mods.reshape(sizes[CORE], sizes[X_AXIS], sizes[Y_AXIS], sizes[Z_AXIS] * count, 10 * D)
     mods = scatter_axis(grid, mods, CORE, 0)
-    mods = scatter_axis(grid, mods, MIX_P, 0)
-    ready = [next(get_down), next(get_up)]
-    mods = scatter_axis(grid, after(mods, *ready), MIX_Q, 0)
-    mods = mods.reshape(sizes[Z_AXIS], count * 8 * D // 128, 128)
-    mods = scatter_axis(grid, mods, Z_AXIS, 0).reshape(count, 8 * D) + b_mods
+    mods = meet(scatter_axis(grid, mods, MIX_P, 0), get)
+    mods = meet(scatter_axis(grid, mods, MIX_Q, 0), get)
+    mods = mods.reshape(sizes[Z_AXIS], count * 10 * D // 128, 128)
+    total = lax.dynamic_index_in_dim(mods, grid.coords[Z_AXIS], 0, keepdims=False)
+    for shift in range(1, sizes[Z_AXIS]):
+        part = lax.dynamic_index_in_dim(mods, grid.place(Z_AXIS, -shift), 0, keepdims=False)
+        total = total + grid.ahead(part, Z_AXIS, shift)
+    mods = meet(total.reshape(count, 10 * D), get)
+    cond_own, time_own = mods[:, 8 * D : 9 * D], mods[:, 9 * D :]
+    mods = mods[:, : 8 * D] + b_mods
     shift_a, scale_a, gate_a, shift_b, scale_b, gate_b, shift_f, scale_f = jnp.split(
         mods, 8, axis=1
     )
@@ -663,18 +841,16 @@
     resid_in = hidden.reshape(count, TOK, D)
     normed_a = modulate(resid_in, shift_a, scale_a).astype(bf16).reshape(rows_all, D)
     proj = (matmul(normed_a, w_qkv) + b_qkv).astype(bf16)
-    proj = after(proj, next(get_down), next(get_up))
-    mixed = attend(proj)
+    mixed = meet(attend(meet(proj, get)), get)
+    tail_bf = after(in_bf[:, 4 * D + FF :], mixed)
+    table_cond = lax.all_gather(tail_bf, AXIS, axis=0, tiled=True)
     attended = (matmul(mixed, w_out) + b_out).reshape(count, TOK, D)
     resid_mid = resid_in + gate_a[:, None, :] * attended
     normed_b = modulate(resid_mid, shift_b, scale_b).astype(bf16).reshape(rows_all, D)
-    table_up, table_down = (table_first, last(get_up)), last(get_down)
-    uppers = [
-        matmul(normed_b, part) + b_up[index * half : (index + 1) * half]
-        for index, part in enumerate(table_up)
-    ]
-    actives = [jax.nn.gelu(upper, approximate=True).astype(bf16) for upper in uppers]
-    active = jnp.concatenate(actives, axis=1)
+    normed_b = meet(normed_b, get)
+    (table_down,) = last(get)
+    upper = matmul(normed_b, table_up) + b_up
+    active = jax.nn.gelu(upper, approximate=True).astype(bf16)
     lowered = matmul(active, table_down) + b_down
     lowered = lowered.reshape(count, TOK, D)
     resid_out = resid_mid + gate_b[:, None, :] * lowered
@@ -693,23 +869,18 @@
     grad_b_down = jnp.sum(grad_lowered, axis=0)
     lowered_bf = grad_lowered.astype(bf16)
     grad_w_down = dot_head(active, lowered_bf).astype(bf16)
-    sum_down = lax.psum_scatter(grad_w_down, AXIS, scatter_dimension=0, tiled=True)
+    put_down = Flow(scatter_bulk(grid, [grad_w_down], ORDER))
     lowered_bf = after(lowered_bf, grad_w_down)
     grad_active = dot_tail(lowered_bf, table_down)
     gelu = partial(jax.nn.gelu, approximate=True)
-    grad_uppers = [
-        jax.vjp(gelu, upper)[1](grad_active[:, index * half : (index + 1) * half])[0]
-        for index, upper in enumerate(uppers)
-    ]
-    grad_b_up = jnp.concatenate([jnp.sum(part, axis=0) for part in grad_uppers])
-    upper_bf = [part.astype(bf16) for part in grad_uppers]
-    grad_w_up = [dot_head(normed_b, part).astype(bf16) for part in upper_bf]
-    put_up = scatter_bulk(grid, grad_w_up, OUTER)
-    upper_bf[0] = after(upper_bf[0], *grad_w_up)
-    grad_normed_b = (
-        dot_tail(upper_bf[0], table_up[0]) + dot_tail(upper_bf[1], table_up[1])
-    ).reshape(count, TOK, D)
-    grad_normed_b = after(grad_normed_b, next(put_up))
+    grad_upper = jax.vjp(gelu, upper)[1](grad_active)[0]
+    grad_b_up = jnp.sum(grad_upper, axis=0)
+    upper_bf = grad_upper.astype(bf16)
+    upper_bf = meet(upper_bf, put_down)
+    grad_w_up = dot_head(normed_b, upper_bf).astype(bf16)
+    put_up = Flow(scatter_bulk(grid, [grad_w_up], ORDER))
+    upper_bf = after(upper_bf, grad_w_up)
+    grad_normed_b = dot_tail(upper_bf, table_up).reshape(count, TOK, D)
     _, pull_mid = jax.vjp(modulate, resid_mid, shift_b, scale_b)
     grad_mid_norm, grad_shift_b, grad_scale_b = pull_mid(grad_normed_b)
     grad_mid = grad_out + grad_mid_norm
@@ -719,16 +890,18 @@
     attended_bf = grad_attended.astype(bf16)
     grad_w_out = dot_head(mixed, attended_bf).astype(bf16)
     grad_mixed = dot_tail(attended_bf, w_out).astype(bf16)
+    grad_mixed = meet(grad_mixed, put_down, put_up)
     proj_bf, proj_sums = attend_back(proj, grad_mixed)
     grad_b_query, grad_b_value = proj_sums[0], proj_sums[1]
+    proj_bf = meet(proj_bf, put_down, put_up)
     grad_qkv = [dot_head(normed_a, proj_bf[part]).astype(bf16) for part in range(3)]
-    put_vo = scatter_bulk(grid, [grad_qkv[2], grad_w_out], OUTER)
-    put_qk = scatter_bulk(grid, grad_qkv[:2], OUTER)
-    proj_bf = after(proj_bf, *grad_qkv, next(put_up))
+    grad_qkv[0] = meet(grad_qkv[0], put_down, put_up)
+    put_rest = Flow(scatter_bulk(grid, grad_qkv + [grad_w_out], ORDER))
+    proj_bf = meet(after(proj_bf, *grad_qkv), put_down)
     grad_normed_a = sum(
         dot_tail(proj_bf[part], w_qkv[:, part * D : (part + 1) * D]) for part in range(3)
     ).reshape(count, TOK, D)
-    grad_normed_a = after(grad_normed_a, next(put_up), next(put_vo), next(put_qk))
+    grad_normed_a = meet(grad_normed_a, put_up, put_rest)
     _, pull_first = jax.vjp(modulate, resid_in, shift_a, scale_a)
     grad_in_norm, grad_shift_a, grad_scale_a = pull_first(grad_normed_a)
     grad_hidden = (grad_mid + grad_in_norm).reshape(rows_all, D)
@@ -748,36 +921,14 @@
         ],
         axis=1,
     )
-    grad_b_mods = jnp.sum(grad_mods, axis=0)
-    before = {
-        MIX_Q: [next(put_up), next(put_vo)],
-        CORE: [next(put_qk), next(put_up)],
-    }
-    mods_bf = grad_mods.astype(bf16).reshape(-1, 128)
-    mods_bf = gather_small(grid, mods_bf, (Z_AXIS, MIX_Q, MIX_P, CORE), before)
-    mods_bf = mods_bf.reshape(image_total, 8 * D)
-    grad_w_mods = matmul(cond_act, mods_bf)
-    grad_cond_act = dot_tail(w_mods, mods_bf)
-    grad_cond = jax.vjp(jax.nn.silu, cond)[1](grad_cond_act)[0]
-    grad_w_class = jnp.dot(
-        grad_cond,
-        onehot.astype(jnp.float32),
-        precision=lax.Precision.HIGHEST,
-        preferred_element_type=jnp.float32,
-    )
-    grad_b_time = jnp.sum(grad_cond, axis=1)
-    before = {X_AXIS: [next(put_vo), next(put_up)], Z_AXIS: [next(put_qk)]}
-    cond_bf = gather_small(grid, grad_cond.astype(bf16), (CORE, X_AXIS, Y_AXIS, Z_AXIS), before)
-    cond_bf = cond_bf.reshape(D, image_total)
-    grad_w_time = dot_tail(time_act, cond_bf)
-    grad_time_act = matmul(w_time, cond_bf)
-    grad_time_pre = jax.vjp(jax.nn.silu, time_pre)[1](grad_time_act)[0]
-    grad_b_tfirst = jnp.sum(grad_time_pre, axis=1)
-    grad_t_first = matmul(grad_time_pre.astype(bf16), feats)
-
-    def spread_rows(part):
-        return lax.dynamic_update_slice(jnp.zeros((D,), jnp.float32), part, (my_rows,))
-
+    grad_mods = meet(grad_mods, put_up)
+    mods_bf = grad_mods.astype(bf16)
+    grad_cond = jax.vjp(jax.nn.silu, cond_own)[1](dot_tail(mods_bf, table_cond[:, : 8 * D]))[0]
+    cond_bf = grad_cond.astype(bf16)
+    grad_time_act = dot_tail(cond_bf, table_cond[:, 8 * D :])
+    grad_time_pre = jax.vjp(jax.nn.silu, time_own)[1](grad_time_act)[0]
+    image_grads = jnp.concatenate([mods_bf, cond_bf, grad_time_pre.astype(bf16)], axis=1)
+    image_grads = meet(image_grads, put_rest).reshape(-1, 128)
     grad_bias = jnp.concatenate(
         [
             grad_b_query,
@@ -785,9 +936,7 @@
             grad_b_out,
             grad_b_up,
             grad_b_down,
-            grad_b_mods,
-            spread_rows(grad_b_tfirst),
-            spread_rows(grad_b_time),
+            jnp.zeros((10 * D,), jnp.float32),
             grad_b_patch,
         ]
     )
@@ -799,42 +948,56 @@
         ],
         axis=1,
     )
-    tall = -(-small.shape[1] // 1024) * 8
+    tall = -(-small.shape[1] // 2048) * SMALL_ROWS
     small = jnp.pad(small, ((0, 0), (0, tall * 128 - small.shape[1])))
-    before = {
-        CORE: [next(put_vo)],
-        X_AXIS: [next(put_qk)],
-        Y_AXIS: [next(put_vo)],
-        Z_AXIS: [next(put_qk)],
-    }
-    small = scatter_small(grid, small.reshape(sizes + (tall, 128)), before).reshape(-1)
+    small = small.reshape(sizes + (tall, 128))
+    ready = {axis: (put_rest,) for axis in (Z_AXIS, MIX_P, CORE)}
+    image_grads, small = gather_and_scatter(grid, image_grads, small, ready)
+    small = small.reshape(-1)
+    image_grads = image_grads.reshape(image_total, 10 * D)
+    mods_bf, cond_bf = image_grads[:, : 8 * D], image_grads[:, 8 * D : 9 * D]
+    grad_w_mods = matmul(cond_act, mods_bf)
+    grad_w_time = matmul(time_act, cond_bf)
+    grad_w_class = lax.dot_general(
+        lax.dynamic_slice_in_dim(cond_bf, my_rows, rows, 1).astype(jnp.float32),
+        onehot.astype(jnp.float32),
+        (((0,), (0,)), ((), ())),
+        precision=lax.Precision.HIGHEST,
+        preferred_element_type=jnp.float32,
+    )
+    own_pre = lax.dynamic_slice_in_dim(image_grads, 9 * D + my_rows, rows, 1)
+    grad_t_first = dot_head(own_pre, feats)
+    sums = jnp.sum(image_grads.astype(jnp.float32), axis=0)
+    known = jnp.concatenate(
+        [
+            jnp.zeros((4 * D + FF,), jnp.float32),
+            sums[: 8 * D],
+            sums[9 * D :],
+            sums[8 * D : 9 * D],
+            jnp.zeros((D,), jnp.float32),
+        ]
+    )
+    known = lax.dynamic_slice_in_dim(known, lax.axis_index(AXIS) * bias_rows, bias_rows)
     at = bias_rows
     sum_patch = small[at : at + rows * PATCH_FEAT].reshape(rows, PATCH_FEAT)
     at += rows * PATCH_FEAT
     sum_head = small[at : at + rows * PATCH_FEAT].reshape(rows, PATCH_FEAT)
 
-    sum_vo, sum_qk, sum_up = last(put_vo), last(put_qk), last(put_up)
-    sum_down = sum_down.astype(jnp.float32)
-    grads_in = (sum_qk, sum_vo, sum_up, grad_w_mods, grad_w_time)
+    sum_rest, sum_up, sum_down = last(put_rest), last(put_up), last(put_down)
+    grads_in = (sum_rest, sum_up, grad_w_mods, grad_w_time)
     grads_other = (
         sum_down,
         jnp.concatenate([grad_t_first, sum_patch, grad_w_class, sum_head], axis=1),
-        small[None, :bias_rows],
+        (small[:bias_rows] + known)[None],
     )
     masters = (weights_in, weights_down, weights_side, biases[None])
     firsts = (first_in, first_down, first_side, first_bias[None])
     seconds = (second_in, second_down, second_side, second_bias[None])
     shapes = [master.shape for master in masters]
-    results = whole_kernel(
-        partial(direction_kernel, [grad.shape[1] for grad in grads_in]),
-        masters + firsts + seconds + grads_in + grads_other,
-        shapes * 3 + [(8, 128)],
-    )
+    results = directions(masters, firsts, seconds, grads_in, grads_other)
     loss_spot = jnp.arange(8, dtype=jnp.int32)[:, None] == 3
     sums = sum_small(grid, results[12] + jnp.where(loss_spot, loss_local, 0.0))
-    updated = whole_kernel(
-        update_kernel, (sums,) + masters + tuple(results[8:12]), shapes + [(8, 128)]
-    )
+    updated = updates(sums, masters, results[8:12])
     norms = updated[4]
     return (
         sums[3, 0],

time: 584 us -> 572 us (0.979)
  starting transfers between devices: 89.1 us -> 62.3 us
  waiting for transfers between devices: 172 us -> 194 us
  matrix products: 86 us -> 106 us
  local copies, waits for them, and re-layouts: 64 us -> 50.6 us
  other arithmetic: 85.3 us -> 74.1 us
    ppermute x73 -> x48, starting transfers between devices: 89 us -> 62.2 us  [move(): return lax.ppermute(values, AXIS, pairs)]
    unnamed x318 -> x246, local copies, waits for them, and re-layouts: 44.6 us -> 18.5 us
    ppermute x73 -> x48, waiting for transfers between devices: 172 us -> 194 us  [move(): return lax.ppermute(values, AXIS, pairs)]
    dot_general x13 -> x12, matrix products: 29.6 us -> 49.9 us  [dot_tail(): lax.dot_general(left, right, (((1,), (1,)), ((), ())), preferred_element_...]
    convert_element_type x17 -> x16, other arithmetic: 31.5 us -> 19.8 us  [the longest x6 15.9 us: scatter_bulk(): total = (yield [grid.ahead(total.astype(jnp.bfloat16), axis, 1)])[0]]
    reduce_sum x6 -> x3, other arithmetic: 14 us -> 4.72 us  [the longest x1 3.4 us: per_device(): grad_gate_a = jnp.sum(grad_mid * attended, axis=1)]
    slice x4 -> x21, local copies, waits for them, and re-layouts: 2.07 us -> 9.95 us  [the longest x9 8.03 us: scatter_bulk(): terms = [term[0] for term in terms] + [total]]
    another operation x6 -> x17, local copies, waits for them, and re-layouts: 0.65 us -> 7.12 us  [the longest x12 7.04 us: scatter_bulk(): terms = [term.reshape((-1, 2) + term.shape[1:]) for term in terms]]
  transfers between devices with their start and end apart: 76 -> 51, of which waited for: 39 -> 39; matrix products, arithmetic and copies ran while one was open for 23% -> 35% of each run, Pallas kernels for 5% -> 8%
where the time goes in v4:
time: 572 us; the launch traced here: 564 us
  waiting for transfers between devices  194 us (34%)
  matrix products  106 us (19%)
  other arithmetic  74.1 us (13%)
  starting transfers between devices  62.3 us (11%)
  Pallas kernels  61.3 us (11%)
  local copies, waits for them, and re-layouts  50.6 us (9%)
  between operations  16.6 us (3%)
    ppermute x48, waiting for transfers between devices, move(): return lax.ppermute(values, AXIS, pairs)  194 us
    ppermute x48, starting transfers between devices, move(): return lax.ppermute(values, AXIS, pairs)  62.2 us
    dot_general x12, matrix products, dot_tail(): lax.dot_general(left, right, (((1,), (1,)), ((), ())), preferred_element_...  49.9 us
    dot_general x7, matrix products, matmul(): return jnp.dot(left, right, preferred_element_type=jnp.float32)  29.9 us
    dot_general x10, matrix products, dot_head(): lax.dot_general(left, right, (((0,), (0,)), ((), ())), preferred_element_...  25.3 us
    pallas_call x1, Pallas kernels, attend_back(): pl.pallas_call(attend_back_kernel, grid=(D // HEAD_COLS, count), out_shap...  20.3 us
    unnamed x246, local copies, waits for them, and re-layouts  18.5 us
    convert_element_type x6, other arithmetic, scatter_bulk(): total = (yield [grid.ahead(total.astype(jnp.bfloat16), axis, 1)])[0]  15.9 us
  transfers between devices with their start and end apart: 51, of which 39 were waited for; matrix products, arithmetic and copies ran while one was open for 35% of the time, Pallas kernels for 8%

profile of v4, /device:TPU:0, one launch (start us, length us, event | category | flops | bytes accessed | tf_op | source)
XLA Modules:
  0.0 564.4 jit_solution(5886781817062960485)
XLA Ops:
  79.0 8.3 %collective-permute-done.11 = f32[1,2,8,10240]{3,2,1,0:T(8,128)} collective-permute-done((f32[1,2,8,10240]{3,2,1,0:T(8,128)}, f32[1,2,8,10240]{3,2,1,0:T(8,128)}, u32[]{:S(2)}, u32[]{:S(2)}) %collective-permute-start.11) | collective-permute-done | bytes 655392 | tf_op jit(solution)/shard_map/ppermute | solution.py:325
  111.7 6.7 %collective-permute-done.18 = bf16[1,128,1024]{2,1,0:T(8,128)(2,1)} collective-permute-done((bf16[1,128,1024]{2,1,0:T(8,128)(2,1)S(1)}, bf16[1,128,1024]{2,1,0:T(8,128)(2,1)}, u32[]{:S(2)}, u32[]{:S(2)}) %collective-permute-start.18) | collective-permute-done | bytes 262176 | tf_op jit(solution)/shard_map/ppermute | solution.py:325
  124.1 6.6 %add_convert_fusion.query_ref.key_ref.value_ref = bf16[512,3072]{1,0:T(8,128)(2,1)S(1)} fusion(bf16[512,1024]{1,0:T(8,128)(2,1)} %fusion.32, bf16[1024,4096]{1,0:T(8,128)(2,1)} %all-gather.4.cloned.1.call-done, f32[3072]{0:T(1024)S(1)} %copy-done.98), kind=kOutput, calls=%fused_computation.15 | convolution fusion | flops 3224371200 | bytes 10498048 | tf_op jit(solution)/shard_map/dot_general | solution.py:37
  130.7 12.4 %collective-permute-done.19 = bf16[4,128,1024]{2,1,0:T(8,128)(2,1)} collective-permute-done((bf16[4,128,1024]{2,1,0:T(8,128)(2,1)}, bf16[4,128,1024]{2,1,0:T(8,128)(2,1)}, u32[]{:S(2)}, u32[]{:S(2)}) %collective-permute-start.19) | collective-permute-done | bytes 1048608 | tf_op jit(solution)/shard_map/ppermute | solution.py:325
  146.5 9.8 %shard_map.279 = bf16[512,1024]{1,0:T(8,128)(2,1)S(1)} custom-call(bf16[512,3072]{1,0:T(8,128)(2,1)S(1)} %add_convert_fusion.query_ref.key_ref.value_ref, bf16[512,3072]{1,0:T(8,128)(2,1)S(1)} %add_convert_fusion.query_ref.key_ref.value_ref, bf16[512,3072]{1,0:T(8,128)(2,1)S(1)} %add_convert_fusion.query_ref.key_ref.value_ref), custom_call_target="tpu_custom_call" | custom-call | flops 2147483648 | bytes 12582912 | tf_op jit(solution)/shard_map/pallas_call | solution.py:676
  157.2 29.9 %collective-permute-done.20.refs_1_ = bf16[8,128,1024]{2,1,0:T(8,128)(2,1)} collective-permute-done((bf16[8,128,1024]{2,1,0:T(8,128)(2,1)}, bf16[8,128,1024]{2,1,0:T(8,128)(2,1)}, u32[]{:S(2)}, u32[]{:S(2)}) %collective-permute-start.20) | collective-permute-done | bytes 2097184 | tf_op jit(solution)/shard_map/ppermute | solution.py:325
  203.1 7.5 %fusion.159 = f32[512,4096]{1,0:T(8,128)S(1)} fusion(bf16[512,1024]{1,0:T(8,128)(2,1)} %fusion.16, bf16[1024,4096]{1,0:T(8,128)(2,1)} %all-gather.6.cloned.1.call-done), kind=kOutput, calls=%fused_computation.418 | convolution fusion | flops 4294967296 | bytes 17825792 | tf_op jit(solution)/shard_map/dot_general | solution.py:37
  210.7 7.4 %fusion.146 = (f32[512]{0:T(512)S(1)}, f32[512,1024]{1,0:T(8,128)}, f32[512,1024]{1,0:T(8,128)}) fusion(f32[512,1024]{1,0:T(8,128)S(1)} %copy-done.14, f32[2,1024]{1,0:T(2,128)S(1)} %get-tuple-element.221, f32[1024]{0:T(1024)S(1)} %copy-done.97, bf16[4096,1024]{1,0:T(8,128)(2,1)S(1)} %bitcast.467, f32[512,4096]{1,0:T(8,128)S(1)} %fusion.159, ...), kind=kOutput, calls=%fused_computation.407 | convolution fusion | flops 4318035456 | bytes 23099392 | tf_op jit(solution)/shard_map/dot_general | solution.py:37
  231.0 10.2 %convolution_convert_fusion.1 = bf16[4096,1024]{1,0:T(8,128)(2,1)S(1)} fusion(bf16[512,1024]{1,0:T(8,128)(2,1)S(1)} %bitcast.513, f32[512,4096]{1,0:T(8,128)} %copy-done.23, f32[4096]{0:T(1024)S(1)} %slice.702), kind=kOutput, calls=%fused_computation.12 | convolution fusion | flops 4320133120 | bytes 17842176 | tf_op jit(solution)/shard_map/dot_general | solution.py:47
  248.9 13.6 %fusion.142 = (f32[4096]{0:T(1024)S(1)}, bf16[512,4096]{1,0:T(8,128)(2,1)S(1)}) fusion(f32[512,4096]{1,0:T(8,128)} %copy-done.23, f32[4096]{0:T(1024)S(1)} %slice.702, bf16[512,1024]{1,0:T(8,128)(2,1)} %bitcast.514, bf16[4096,1024]{1,0:T(8,128)(2,1)} %bitcast.466), kind=kOutput, calls=%fused_computation.405 | convolution fusion | flops 4341100544 | bytes 22052864 | tf_op jit(solution)/shard_map/dot_general | solution.py:41
  282.2 11.2 %multiply_reduce_fusion.5 = (f32[512]{0:T(512)S(1)}, f32[512,1024]{1,0:T(8,128)}) fusion(f32[512,1024]{1,0:T(8,128)} %copy-done.13, f32[2,1024]{1,0:T(2,128)S(1)} %get-tuple-element.220, f32[512]{0:T(512)S(1)} %broadcast_multiply_fusion.1, bf16[512,4096]{1,0:T(8,128)(2,1)} %copy-done.32, bf16[1024,4096]{1,0:T(8,128)(2,1)} %all-gather.6.cloned.1.call-done), kind=kOutput, calls=%fused_computation.68 | convolution fusion | flops 4297063936 | bytes 16789504 | tf_op jit(solution)/shard_map/dot_general | solution.py:41
  312.6 14.9 %collective-permute-done.24 = bf16[2,4,128,1024]{3,2,1,0:T(8,128)(2,1)S(1)} collective-permute-done((bf16[2,4,128,1024]{3,2,1,0:T(8,128)(2,1)S(1)}, bf16[2,4,128,1024]{3,2,1,0:T(8,128)(2,1)S(1)}, u32[]{:S(2)}, u32[]{:S(2)}) %collective-permute-start.24) | collective-permute-done | bytes 2097184 | tf_op jit(solution)/shard_map/ppermute | solution.py:325
  334.2 20.3 %shard_map.283 = (bf16[3,512,1024]{2,1,0:T(8,128)(2,1)S(1)}, f32[8,1024]{1,0:T(8,128)S(1)}) custom-call(bf16[512,3072]{1,0:T(8,128)(2,1)S(1)} %add_convert_fusion.query_ref.key_ref.value_ref, bf16[512,3072]{1,0:T(8,128)(2,1)S(1)} %add_convert_fusion.query_ref.key_ref.value_ref, bf16[512,3072]{1,0:T(8,128)(2,1)S(1)} %add_convert_fusion.query_ref.key_ref.value_ref, ...), custom_call_target="tpu_custom_call" | custom-call | flops 4831838208 | bytes 25165824 | tf_op jit(solution)/shard_map/pallas_call | solution.py:693
  359.2 8.0 %collective-permute-done.27 = bf16[2,4,32,4096]{3,2,1,0:T(8,128)(2,1)S(1)} collective-permute-done((bf16[2,4,32,4096]{3,2,1,0:T(8,128)(2,1)S(1)}, bf16[2,4,32,4096]{3,2,1,0:T(8,128)(2,1)S(1)}, u32[]{:S(2)}, u32[]{:S(2)}) %collective-permute-start.27) | collective-permute-done | bytes 2097184 | tf_op jit(solution)/shard_map/ppermute | solution.py:325
  379.9 7.4 %collective-permute-done.28 = bf16[2,128,1024]{2,1,0:T(8,128)(2,1)S(1)} collective-permute-done((bf16[2,128,1024]{2,1,0:T(8,128)(2,1)S(1)}, bf16[2,128,1024]{2,1,0:T(8,128)(2,1)S(1)}, u32[]{:S(2)}, u32[]{:S(2)}) %collective-permute-start.28) | collective-permute-done | bytes 524320 | tf_op jit(solution)/shard_map/ppermute | solution.py:325
  437.1 6.0 %collective-permute-done.33 = bf16[1,32,4096]{2,1,0:T(8,128)(2,1)S(1)} collective-permute-done((bf16[1,32,4096]{2,1,0:T(8,128)(2,1)S(1)}, bf16[1,32,4096]{2,1,0:T(8,128)(2,1)S(1)}, u32[]{:S(2)}, u32[]{:S(2)}) %collective-permute-start.33) | collective-permute-done | bytes 262176 | tf_op jit(solution)/shard_map/ppermute | solution.py:325
  444.2 8.3 %fusion.107 = bf16[2,1024]{1,0:T(2,128)(2,1)S(1)} fusion(bf16[2,8192]{1,0:T(2,128)(2,1)S(1)} %constant_dynamic-update-slice_fusion, bf16[1024,9216]{1,0:T(8,128)(2,1)} %all-gather.8.cloned.1.call-done, f32[2,10240]{1,0:T(2,128)} %copy-done.64), kind=kOutput, calls=%fused_computation.291 | convolution fusion | flops 33574912 | bytes 16822272 | tf_op jit(solution)/shard_map/dot_general | solution.py:41
  454.8 6.7 %collective-permute-done.34 = bf16[2,4,32,4096]{3,2,1,0:T(8,128)(2,1)} collective-permute-done((bf16[2,4,32,4096]{3,2,1,0:T(8,128)(2,1)}, bf16[2,4,32,4096]{3,2,1,0:T(8,128)(2,1)}, u32[]{:S(2)}, u32[]{:S(2)}) %collective-permute-start.34) | collective-permute-done | bytes 2097184 | tf_op jit(solution)/shard_map/ppermute | solution.py:325
  468.1 7.3 %collective-permute-done.36 = bf16[448,128]{1,0:T(8,128)(2,1)S(1)} collective-permute-done((bf16[448,128]{1,0:T(8,128)(2,1)S(1)}, bf16[448,128]{1,0:T(8,128)(2,1)S(1)}, u32[]{:S(2)}, u32[]{:S(2)}) %collective-permute-start.36) | collective-permute-done | bytes 114720 | tf_op jit(solution)/shard_map/ppermute | solution.py:325
  475.5 7.1 %collective-permute-done.37 = bf16[4,32,4096]{2,1,0:T(8,128)(2,1)S(1)} collective-permute-done((bf16[4,32,4096]{2,1,0:T(8,128)(2,1)S(1)}, bf16[4,32,4096]{2,1,0:T(8,128)(2,1)S(1)}, u32[]{:S(2)}, u32[]{:S(2)}) %collective-permute-start.37) | collective-permute-done | bytes 1048608 | tf_op jit(solution)/shard_map/ppermute | solution.py:325
  489.0 7.0 %collective-permute-done.39 = bf16[1312,128]{1,0:T(8,128)(2,1)S(1)} collective-permute-done((bf16[1312,128]{1,0:T(8,128)(2,1)S(1)}, bf16[1312,128]{1,0:T(8,128)(2,1)S(1)}, u32[]{:S(2)}, u32[]{:S(2)}) %collective-permute-start.39) | collective-permute-done | bytes 335904 | tf_op jit(solution)/shard_map/ppermute | solution.py:325
  502.9 12.0 %collective-permute-done.42 = bf16[1,32,4096]{2,1,0:T(8,128)(2,1)S(1)} collective-permute-done((bf16[1,32,4096]{2,1,0:T(8,128)(2,1)S(1)}, bf16[1,32,4096]{2,1,0:T(8,128)(2,1)S(1)}, u32[]{:S(2)}, u32[]{:S(2)}) %collective-permute-start.42) | collective-permute-done | bytes 262176 | tf_op jit(solution)/shard_map/ppermute | solution.py:325
  521.8 8.9 %shard_map.285 = (f32[32,17408]{1,0:T(8,128)}, f32[128,1024]{1,0:T(8,128)}, f32[32,1288]{1,0:T(8,128)}, f32[1,608]{1,0:T(1,128)}, f32[32,17408]{1,0:T(8,128)}, /...) custom-call(f32[32,17408]{1,0:T(8,128)} %refs_0_.3, ...), custom_call_target="tpu_custom_call" | custom-call | flops 51106880 | bytes 20442752 | tf_op jit(solution)/shard_map/pallas_call | solution.py:196
  549.4 5.5 shard_map.286
  (595 shorter events, 304.6 us)
Async XLA Ops:
  7.2 116.9 %all-gather.4.cloned.1.call-start = ((), (), s32[]{:S(2)}) async-start(), calls=%async_computation | async-start | bytes 8650752 | tf_op jit(solution)/shard_map/all_gather | solution.py:769
  10.0 193.1 %all-gather.6.cloned.1.call-start = ((), (), s32[]{:S(2)}) async-start(), calls=%async_computation.1 | async-start | bytes 8650752 | tf_op jit(solution)/shard_map/all_gather | solution.py:771
  60.6 27.9 %collective-permute-start.12 = (bf16[1,128,1024]{2,1,0:T(8,128)(2,1)}, bf16[1,128,1024]{2,1,0:T(8,128)(2,1)}, u32[]{:S(2)}, u32[]{:S(2)}) collective-permute-start(bf16[1,128,1024]{2,1,0:T(8,128)(2,1)} %get-tuple-element.192), channel_id=1, source_target_pairs={{0,24},{1,25},{2,26},{3,27},{4,28},{5,29},{6,30},{7,31},{8,0},{9,1... | collective-permute-start | bytes 786440 | tf_op jit(solution)/shard_map/ppermute | solution.py:325
  63.9 380.3 %all-gather.8.cloned.1.call-start = ((), (), s32[]{:S(2)}) async-start(), calls=%async_computation.2 | async-start | bytes 19464192 | tf_op jit(solution)/shard_map/all_gather | solution.py:846
  70.3 17.1 %collective-permute-start.11 = (f32[1,2,8,10240]{3,2,1,0:T(8,128)}, f32[1,2,8,10240]{3,2,1,0:T(8,128)}, u32[]{:S(2)}, u32[]{:S(2)}) collective-permute-start(f32[1,2,8,10240]{3,2,1,0:T(8,128)} %dynamic-slice_bitcast_fusion), channel_id=1, source_target_pairs={{0,2},{1,5},{2,0},{3,7},{4,6},{5,1},{6,4},{7,3},{8,10},{9,13},{10,... | collective-permute-start | bytes 1966088 | tf_op jit(solution)/shard_map/ppermute | solution.py:325
  106.4 12.0 %collective-permute-start.18 = (bf16[1,128,1024]{2,1,0:T(8,128)(2,1)S(1)}, bf16[1,128,1024]{2,1,0:T(8,128)(2,1)}, u32[]{:S(2)}, u32[]{:S(2)}) collective-permute-start(bf16[1,128,1024]{2,1,0:T(8,128)(2,1)S(1)} %collective-permute-done.14), channel_id=1, source_target_pairs={{0,24},{1,25},{2,26},{3,27},{4,28},{5,29},{6,30},{7,31},{8,0},{9,1... | collective-permute-start | bytes 786440 | tf_op jit(solution)/shard_map/ppermute | solution.py:325
  120.9 22.2 %collective-permute-start.19 = (bf16[4,128,1024]{2,1,0:T(8,128)(2,1)}, bf16[4,128,1024]{2,1,0:T(8,128)(2,1)}, u32[]{:S(2)}, u32[]{:S(2)}) collective-permute-start(bf16[4,128,1024]{2,1,0:T(8,128)(2,1)} %get-tuple-element.188), channel_id=1, source_target_pairs={{0,2},{1,5},{2,0},{3,7},{4,6},{5,1},{6,4},{7,3},{8,10},{9,13},{10,... | collective-permute-start | bytes 3145736 | tf_op jit(solution)/shard_map/ppermute | solution.py:325
  145.9 41.3 %collective-permute-start.20 = (bf16[8,128,1024]{2,1,0:T(8,128)(2,1)}, bf16[8,128,1024]{2,1,0:T(8,128)(2,1)}, u32[]{:S(2)}, u32[]{:S(2)}) collective-permute-start(bf16[8,128,1024]{2,1,0:T(8,128)(2,1)} %bitcast.45.refs_0_), channel_id=1, source_target_pairs={{0,4},{1,3},{2,6},{3,1},{4,0},{5,7},{6,2},{7,5},{8,12},{9,11},{10,... | collective-permute-start | bytes 6291464 | tf_op jit(solution)/shard_map/ppermute | solution.py:325
  146.5 49.2 %collective-permute-start.21 = (bf16[8,128,1024]{2,1,0:T(8,128)(2,1)}, bf16[8,128,1024]{2,1,0:T(8,128)(2,1)}, u32[]{:S(2)}, u32[]{:S(2)}) collective-permute-start(bf16[8,128,1024]{2,1,0:T(8,128)(2,1)} %bitcast.45.refs_0_), channel_id=1, source_target_pairs={{0,1},{1,0},{2,3},{3,2},{4,5},{5,4},{6,7},{7,6},{8,9},{9,8},{10,11... | collective-permute-start | bytes 6291464 | tf_op jit(solution)/shard_map/ppermute | solution.py:325
  246.8 15.8 %collective-permute-start.23 = (bf16[16,128,1024]{2,1,0:T(8,128)(2,1)}, bf16[16,128,1024]{2,1,0:T(8,128)(2,1)}, u32[]{:S(2)}, u32[]{:S(2)}) collective-permute-start(bf16[16,128,1024]{2,1,0:T(8,128)(2,1)} %get-tuple-element.99), channel_id=1, source_target_pairs={{0,1},{1,0},{2,3},{3,2},{4,5},{5,4},{6,7},{7,6},{8,9},{9,8},{10,11... | collective-permute-start | bytes 12582920 | tf_op jit(solution)/shard_map/ppermute | solution.py:325
  273.4 54.1 %collective-permute-start.25 = (bf16[16,32,4096]{2,1,0:T(8,128)(2,1)}, bf16[16,32,4096]{2,1,0:T(8,128)(2,1)}, u32[]{:S(2)}, u32[]{:S(2)}) collective-permute-start(bf16[16,32,4096]{2,1,0:T(8,128)(2,1)} %get-tuple-element.104), channel_id=1, source_target_pairs={{0,1},{1,0},{2,3},{3,2},{4,5},{5,4},{6,7},{7,6},{8,9},{9,8},{10,11... | collective-permute-start | bytes 12582920 | tf_op jit(solution)/shard_map/ppermute | solution.py:325
  301.3 26.1 %collective-permute-start.24 = (bf16[2,4,128,1024]{3,2,1,0:T(8,128)(2,1)S(1)}, bf16[2,4,128,1024]{3,2,1,0:T(8,128)(2,1)S(1)}, u32[]{:S(2)}, u32[]{:S(2)}) collective-permute-start(bf16[2,4,128,1024]{3,2,1,0:T(8,128)(2,1)S(1)} %bitcast.504), channel_id=1, source_target_pairs={{0,4},{1,3},{2,6},{3,1},{4,0},{5,7},{6,2},{7,5},{8,12},{9,11},{10,... | collective-permute-start | bytes 6291464 | tf_op jit(solution)/shard_map/ppermute | solution.py:325
  329.9 37.3 %collective-permute-start.27 = (bf16[2,4,32,4096]{3,2,1,0:T(8,128)(2,1)S(1)}, bf16[2,4,32,4096]{3,2,1,0:T(8,128)(2,1)S(1)}, u32[]{:S(2)}, u32[]{:S(2)}) collective-permute-start(bf16[2,4,32,4096]{3,2,1,0:T(8,128)(2,1)S(1)} %bitcast.503), channel_id=1, source_target_pairs={{0,4},{1,3},{2,6},{3,1},{4,0},{5,7},{6,2},{7,5},{8,12},{9,11},{10,... | collective-permute-start | bytes 6291464 | tf_op jit(solution)/shard_map/ppermute | solution.py:325
  333.0 26.2 %collective-permute-start.26 = (bf16[4,128,1024]{2,1,0:T(8,128)(2,1)S(1)}, bf16[4,128,1024]{2,1,0:T(8,128)(2,1)S(1)}, u32[]{:S(2)}, u32[]{:S(2)}) collective-permute-start(bf16[4,128,1024]{2,1,0:T(8,128)(2,1)S(1)} %fusion.27), channel_id=1, source_target_pairs={{0,2},{1,5},{2,0},{3,7},{4,6},{5,1},{6,4},{7,3},{8,10},{9,13},{10,... | collective-permute-start | bytes 3145736 | tf_op jit(solution)/shard_map/ppermute | solution.py:325
  369.1 18.2 %collective-permute-start.29 = (bf16[4,32,4096]{2,1,0:T(8,128)(2,1)S(1)}, bf16[4,32,4096]{2,1,0:T(8,128)(2,1)S(1)}, u32[]{:S(2)}, u32[]{:S(2)}) collective-permute-start(bf16[4,32,4096]{2,1,0:T(8,128)(2,1)S(1)} %fusion.26), channel_id=1, source_target_pairs={{0,2},{1,5},{2,0},{3,7},{4,6},{5,1},{6,4},{7,3},{8,10},{9,13},{10,... | collective-permute-start | bytes 3145736 | tf_op jit(solution)/shard_map/ppermute | solution.py:325
  373.6 13.7 %collective-permute-start.28 = (bf16[2,128,1024]{2,1,0:T(8,128)(2,1)S(1)}, bf16[2,128,1024]{2,1,0:T(8,128)(2,1)S(1)}, u32[]{:S(2)}, u32[]{:S(2)}) collective-permute-start(bf16[2,128,1024]{2,1,0:T(8,128)(2,1)S(1)} %fusion.62), channel_id=1, source_target_pairs={{0,8},{1,9},{2,10},{3,11},{4,12},{5,13},{6,14},{7,15},{8,0},{9,1},... | collective-permute-start | bytes 1572872 | tf_op jit(solution)/shard_map/ppermute | solution.py:325
  387.6 14.0 %collective-permute-start.30 = (bf16[1,128,1024]{2,1,0:T(8,128)(2,1)S(1)}, bf16[1,128,1024]{2,1,0:T(8,128)(2,1)}, u32[]{:S(2)}, u32[]{:S(2)}) collective-permute-start(bf16[1,128,1024]{2,1,0:T(8,128)(2,1)S(1)} %fusion.67), channel_id=1, source_target_pairs={{0,16},{1,17},{2,18},{3,19},{4,20},{5,21},{6,22},{7,23},{8,24},{9,... | collective-permute-start | bytes 786440 | tf_op jit(solution)/shard_map/ppermute | solution.py:325
  396.7 15.9 %collective-permute-start.32 = (bf16[16,32,4096]{2,1,0:T(8,128)(2,1)S(1)}, bf16[16,32,4096]{2,1,0:T(8,128)(2,1)S(1)}, u32[]{:S(2)}, u32[]{:S(2)}) collective-permute-start(bf16[16,32,4096]{2,1,0:T(8,128)(2,1)S(1)} %get-tuple-element.119), channel_id=1, source_target_pairs={{0,1},{1,0},{2,3},{3,2},{4,5},{5,4},{6,7},{7,6},{8,9},{9,8},{10,11... | collective-permute-start | bytes 12582920 | tf_op jit(solution)/shard_map/ppermute | solution.py:325
  397.1 15.5 %collective-permute-start.31 = (bf16[2,32,4096]{2,1,0:T(8,128)(2,1)S(1)}, bf16[2,32,4096]{2,1,0:T(8,128)(2,1)S(1)}, u32[]{:S(2)}, u32[]{:S(2)}) collective-permute-start(bf16[2,32,4096]{2,1,0:T(8,128)(2,1)S(1)} %fusion.63), channel_id=1, source_target_pairs={{0,8},{1,9},{2,10},{3,11},{4,12},{5,13},{6,14},{7,15},{8,0},{9,1},... | collective-permute-start | bytes 1572872 | tf_op jit(solution)/shard_map/ppermute | solution.py:325
  428.3 14.9 %collective-permute-start.33 = (bf16[1,32,4096]{2,1,0:T(8,128)(2,1)S(1)}, bf16[1,32,4096]{2,1,0:T(8,128)(2,1)S(1)}, u32[]{:S(2)}, u32[]{:S(2)}) collective-permute-start(bf16[1,32,4096]{2,1,0:T(8,128)(2,1)S(1)} %fusion.68), channel_id=1, source_target_pairs={{0,16},{1,17},{2,18},{3,19},{4,20},{5,21},{6,22},{7,23},{8,24},{9,... | collective-permute-start | bytes 786440 | tf_op jit(solution)/shard_map/ppermute | solution.py:325
  435.2 26.4 %collective-permute-start.34 = (bf16[2,4,32,4096]{3,2,1,0:T(8,128)(2,1)}, bf16[2,4,32,4096]{3,2,1,0:T(8,128)(2,1)}, u32[]{:S(2)}, u32[]{:S(2)}) collective-permute-start(bf16[2,4,32,4096]{3,2,1,0:T(8,128)(2,1)} %bitcast.102), channel_id=1, source_target_pairs={{0,4},{1,3},{2,6},{3,1},{4,0},{5,7},{6,2},{7,5},{8,12},{9,11},{10,... | collective-permute-start | bytes 6291464 | tf_op jit(solution)/shard_map/ppermute | solution.py:325
  467.8 14.9 %collective-permute-start.37 = (bf16[4,32,4096]{2,1,0:T(8,128)(2,1)S(1)}, bf16[4,32,4096]{2,1,0:T(8,128)(2,1)S(1)}, u32[]{:S(2)}, u32[]{:S(2)}) collective-permute-start(bf16[4,32,4096]{2,1,0:T(8,128)(2,1)S(1)} %fusion.25), channel_id=1, source_target_pairs={{0,2},{1,5},{2,0},{3,7},{4,6},{5,1},{6,4},{7,3},{8,10},{9,13},{10,... | collective-permute-start | bytes 3145736 | tf_op jit(solution)/shard_map/ppermute | solution.py:325
  489.0 10.7 %collective-permute-start.40 = (bf16[2,32,4096]{2,1,0:T(8,128)(2,1)S(1)}, bf16[2,32,4096]{2,1,0:T(8,128)(2,1)S(1)}, u32[]{:S(2)}, u32[]{:S(2)}) collective-permute-start(bf16[2,32,4096]{2,1,0:T(8,128)(2,1)S(1)} %fusion.64), channel_id=1, source_target_pairs={{0,8},{1,9},{2,10},{3,11},{4,12},{5,13},{6,14},{7,15},{8,0},{9,1},... | collective-permute-start | bytes 1572872 | tf_op jit(solution)/shard_map/ppermute | solution.py:325
  500.0 15.0 %collective-permute-start.42 = (bf16[1,32,4096]{2,1,0:T(8,128)(2,1)S(1)}, bf16[1,32,4096]{2,1,0:T(8,128)(2,1)S(1)}, u32[]{:S(2)}, u32[]{:S(2)}) collective-permute-start(bf16[1,32,4096]{2,1,0:T(8,128)(2,1)S(1)} %fusion.69), channel_id=1, source_target_pairs={{0,16},{1,17},{2,18},{3,19},{4,20},{5,21},{6,22},{7,23},{8,24},{9,... | collective-permute-start | bytes 786440 | tf_op jit(solution)/shard_map/ppermute | solution.py:325
  (141 other events, 1305.0 us)
Sparse Core Ops, SparseCore 0:
  11.5 86.7 all-gather.3
  101.7 91.7 all-gather.5
  196.4 125.8 all-gather.7

commit v5 on v4

--- a/solution.py
+++ b/solution.py
@@ -765,12 +765,11 @@
     width = packed.shape[0]
     tall = -(-width // (SMALL_ROWS * 128)) * SMALL_ROWS
     packed = jnp.pad(packed, (0, tall * 128 - width)).reshape(tall, 128)
-    head_in = weights_in[:, : 4 * D].astype(bf16)
-    table_qkvo = lax.all_gather(head_in, AXIS, axis=0, tiled=True)
-    up_bf = weights_in[:, 4 * D : 4 * D + FF].astype(bf16)
-    table_up = lax.all_gather(up_bf, AXIS, axis=0, tiled=True)
+    main_bf = weights_in[:, : 4 * D + FF].astype(bf16)
+    table_main = lax.all_gather(main_bf, AXIS, axis=0, tiled=True)
     get = Flow(gather_bulk(grid, [down_bf], ORDER))
-    spread_all = gather_small(grid, packed, (CORE, X_AXIS, Y_AXIS, Z_AXIS))
+    spread_all = gather_small(grid, packed, (CORE, X_AXIS, Y_AXIS))
+    spread_all = gather_small(grid, meet(spread_all, get), (Z_AXIS,))
     spread_all = spread_all.reshape(count_all, tall * 128)
     bias_full = spread_all[:, :bias_rows].reshape(-1).astype(jnp.float32)
     at = bias_rows
@@ -804,7 +803,9 @@
         w_time, time_act, (((0,), (0,)), ((), ())), preferred_element_type=jnp.float32
     )
     cond = cond_part.reshape(sizes + (rows, image_total))
-    cond = scatter_small(grid, cond)
+    cond = scatter_axis(grid, scatter_axis(grid, cond, CORE, CORE), X_AXIS, X_AXIS)
+    cond = scatter_axis(grid, meet(cond, get), Y_AXIS, Y_AXIS)
+    cond = scatter_axis(grid, cond, Z_AXIS, Z_AXIS)
     cond = cond + b_time[:, None] + dot_tail(w_class, onehot.astype(bf16))
     cond_act = jax.nn.silu(cond).astype(bf16)
 
@@ -816,9 +817,9 @@
         [dot_head(cond_act, w_mods), own_columns(cond), own_columns(time_pre)], axis=1
     )
     mods = mods.reshape(sizes[CORE], sizes[X_AXIS], sizes[Y_AXIS], sizes[Z_AXIS] * count, 10 * D)
-    mods = scatter_axis(grid, mods, CORE, 0)
-    mods = meet(scatter_axis(grid, mods, MIX_P, 0), get)
-    mods = meet(scatter_axis(grid, mods, MIX_Q, 0), get)
+    mods = meet(scatter_axis(grid, mods, CORE, 0), get)
+    mods = scatter_axis(grid, mods, MIX_P, 0)
+    mods = scatter_axis(grid, mods, MIX_Q, 0)
     mods = mods.reshape(sizes[Z_AXIS], count * 10 * D // 128, 128)
     total = lax.dynamic_index_in_dim(mods, grid.coords[Z_AXIS], 0, keepdims=False)
     for shift in range(1, sizes[Z_AXIS]):
@@ -831,7 +832,8 @@
         mods, 8, axis=1
     )
 
-    w_qkv, w_out = table_qkvo[:, : 3 * D], table_qkvo[:, 3 * D :]
+    w_qkv, w_out = table_main[:, : 3 * D], table_main[:, 3 * D : 4 * D]
+    table_up = table_main[:, 4 * D :]
 
     signal, spread = noise_scales(timesteps)
     noise_rows = noise_draw.astype(jnp.float32)
@@ -841,7 +843,7 @@
     resid_in = hidden.reshape(count, TOK, D)
     normed_a = modulate(resid_in, shift_a, scale_a).astype(bf16).reshape(rows_all, D)
     proj = (matmul(normed_a, w_qkv) + b_qkv).astype(bf16)
-    mixed = meet(attend(meet(proj, get)), get)
+    mixed = meet(attend(proj), get)
     tail_bf = after(in_bf[:, 4 * D + FF :], mixed)
     table_cond = lax.all_gather(tail_bf, AXIS, axis=0, tiled=True)
     attended = (matmul(mixed, w_out) + b_out).reshape(count, TOK, D)
@@ -881,6 +883,7 @@
     put_up = Flow(scatter_bulk(grid, [grad_w_up], ORDER))
     upper_bf = after(upper_bf, grad_w_up)
     grad_normed_b = dot_tail(upper_bf, table_up).reshape(count, TOK, D)
+    grad_normed_b = meet(grad_normed_b, put_down)
     _, pull_mid = jax.vjp(modulate, resid_mid, shift_b, scale_b)
     grad_mid_norm, grad_shift_b, grad_scale_b = pull_mid(grad_normed_b)
     grad_mid = grad_out + grad_mid_norm
@@ -897,7 +900,7 @@
     grad_qkv = [dot_head(normed_a, proj_bf[part]).astype(bf16) for part in range(3)]
     grad_qkv[0] = meet(grad_qkv[0], put_down, put_up)
     put_rest = Flow(scatter_bulk(grid, grad_qkv + [grad_w_out], ORDER))
-    proj_bf = meet(after(proj_bf, *grad_qkv), put_down)
+    proj_bf = after(proj_bf, *grad_qkv)
     grad_normed_a = sum(
         dot_tail(proj_bf[part], w_qkv[:, part * D : (part + 1) * D]) for part in range(3)
     ).reshape(count, TOK, D)
@@ -927,7 +930,7 @@
     cond_bf = grad_cond.astype(bf16)
     grad_time_act = dot_tail(cond_bf, table_cond[:, 8 * D :])
     grad_time_pre = jax.vjp(jax.nn.silu, time_own)[1](grad_time_act)[0]
-    image_grads = jnp.concatenate([mods_bf, cond_bf, grad_time_pre.astype(bf16)], axis=1)
+    image_grads = jnp.concatenate([mods_bf, grad_time_pre.astype(bf16), cond_bf], axis=1)
     image_grads = meet(image_grads, put_rest).reshape(-1, 128)
     grad_bias = jnp.concatenate(
         [
@@ -955,7 +958,7 @@
     image_grads, small = gather_and_scatter(grid, image_grads, small, ready)
     small = small.reshape(-1)
     image_grads = image_grads.reshape(image_total, 10 * D)
-    mods_bf, cond_bf = image_grads[:, : 8 * D], image_grads[:, 8 * D : 9 * D]
+    mods_bf, cond_bf = image_grads[:, : 8 * D], image_grads[:, 9 * D :]
     grad_w_mods = matmul(cond_act, mods_bf)
     grad_w_time = matmul(time_act, cond_bf)
     grad_w_class = lax.dot_general(
@@ -965,18 +968,10 @@
         precision=lax.Precision.HIGHEST,
         preferred_element_type=jnp.float32,
     )
-    own_pre = lax.dynamic_slice_in_dim(image_grads, 9 * D + my_rows, rows, 1)
+    own_pre = lax.dynamic_slice_in_dim(image_grads, 8 * D + my_rows, rows, 1)
     grad_t_first = dot_head(own_pre, feats)
     sums = jnp.sum(image_grads.astype(jnp.float32), axis=0)
-    known = jnp.concatenate(
-        [
-            jnp.zeros((4 * D + FF,), jnp.float32),
-            sums[: 8 * D],
-            sums[9 * D :],
-            sums[8 * D : 9 * D],
-            jnp.zeros((D,), jnp.float32),
-        ]
-    )
+    known = jnp.pad(sums, (4 * D + FF, D))
     known = lax.dynamic_slice_in_dim(known, lax.axis_index(AXIS) * bias_rows, bias_rows)
     at = bias_rows
     sum_patch = small[at : at + rows * PATCH_FEAT].reshape(rows, PATCH_FEAT)

time: 572 us -> 544 us (0.951)
  waiting for transfers between devices: 194 us -> 178 us
    ppermute x48, waiting for transfers between devices: 194 us -> 178 us  [move(): return lax.ppermute(values, AXIS, pairs)]
    unnamed x246 -> x238, local copies, waits for them, and re-layouts: 18.5 us -> 13.8 us
  transfers between devices with their start and end apart: 51 -> 50, of which waited for: 39 -> 36; matrix products, arithmetic and copies ran while one was open for 35% -> 37% of each run, Pallas kernels for 8% -> 8%
where the time goes in v5:
time: 544 us; the launch traced here: 536 us
  waiting for transfers between devices  178 us (33%)
  matrix products  106 us (19%)
  other arithmetic  69.6 us (13%)
  Pallas kernels  59.3 us (11%)
  starting transfers between devices  58.7 us (11%)
  local copies, waits for them, and re-layouts  48.5 us (9%)
  between operations  16.5 us (3%)
    ppermute x48, waiting for transfers between devices, move(): return lax.ppermute(values, AXIS, pairs)  178 us
    ppermute x48, starting transfers between devices, move(): return lax.ppermute(values, AXIS, pairs)  58.6 us
    dot_general x12, matrix products, dot_tail(): lax.dot_general(left, right, (((1,), (1,)), ((), ())), preferred_element_...  48.9 us
    dot_general x7, matrix products, matmul(): return jnp.dot(left, right, preferred_element_type=jnp.float32)  30.7 us
    dot_general x10, matrix products, dot_head(): lax.dot_general(left, right, (((0,), (0,)), ((), ())), preferred_element_...  25.4 us
    pallas_call x1, Pallas kernels, attend_back(): pl.pallas_call(attend_back_kernel, grid=(D // HEAD_COLS, count), out_shap...  20.5 us
    convert_element_type x6, other arithmetic, scatter_bulk(): total = (yield [grid.ahead(total.astype(jnp.bfloat16), axis, 1)])[0]  18.3 us
    pallas_call x2, Pallas kernels, lamb_call(): pl.pallas_call(kernel, out_shape=[jax.ShapeDtypeStruct(shape, jnp.float32...  14.4 us
  transfers between devices with their start and end apart: 50, of which 36 were waited for; matrix products, arithmetic and copies ran while one was open for 37% of the time, Pallas kernels for 8%

profile of v5, /device:TPU:0, one launch (start us, length us, event | category | flops | bytes accessed | tf_op | source)
XLA Modules:
  0.0 535.6 jit_solution(14256024669821175338)
XLA Ops:
  22.5 10.3 %collective-permute-done.3 = bf16[1,128,1024]{2,1,0:T(8,128)(2,1)S(1)} collective-permute-done((bf16[1,128,1024]{2,1,0:T(8,128)(2,1)S(1)}, bf16[1,128,1024]{2,1,0:T(8,128)(2,1)S(1)}, u32[]{:S(2)}, u32[]{:S(2)}) %collective-permute-start.3) | collective-permute-done | bytes 262176 | tf_op jit(solution)/shard_map/ppermute | solution.py:325
  56.1 12.9 %collective-permute-done.8 = bf16[1,128,1024]{2,1,0:T(8,128)(2,1)S(1)} collective-permute-done((bf16[1,128,1024]{2,1,0:T(8,128)(2,1)S(1)}, bf16[1,128,1024]{2,1,0:T(8,128)(2,1)S(1)}, u32[]{:S(2)}, u32[]{:S(2)}) %collective-permute-start.8) | collective-permute-done | bytes 262176 | tf_op jit(solution)/shard_map/ppermute | solution.py:325
  73.6 5.3 collective-permute-done.10
  92.4 17.8 %collective-permute-done.13 = bf16[1,128,1024]{2,1,0:T(8,128)(2,1)S(1)} collective-permute-done((bf16[1,128,1024]{2,1,0:T(8,128)(2,1)}, bf16[1,128,1024]{2,1,0:T(8,128)(2,1)S(1)}, u32[]{:S(2)}, u32[]{:S(2)}) %collective-permute-start.13) | collective-permute-done | bytes 262176 | tf_op jit(solution)/shard_map/ppermute | solution.py:325
  116.7 6.4 %collective-permute-done.14 = f32[1,2,8,10240]{3,2,1,0:T(8,128)S(1)} collective-permute-done((f32[1,2,8,10240]{3,2,1,0:T(8,128)}, f32[1,2,8,10240]{3,2,1,0:T(8,128)S(1)}, u32[]{:S(2)}, u32[]{:S(2)}) %collective-permute-start.14) | collective-permute-done | bytes 655392 | tf_op jit(solution)/shard_map/ppermute | solution.py:325
  151.1 6.5 %add_convert_fusion.query_ref.key_ref.value_ref = bf16[512,3072]{1,0:T(8,128)(2,1)S(1)} fusion(bf16[512,1024]{1,0:T(8,128)(2,1)} %fusion.31, bf16[1024,8192]{1,0:T(8,128)(2,1)} %all-gather.3.cloned.1.call-done, f32[3072]{0:T(1024)S(1)} %pad_maximum_fusion.22), kind=kOutput, calls=%fused_computation.19 | convolution fusion | flops 3224371200 | bytes 10498048 | tf_op jit(solution)/shard_map/dot_general | solution.py:37
  157.7 9.8 %shard_map.279 = bf16[512,1024]{1,0:T(8,128)(2,1)S(1)} custom-call(bf16[512,3072]{1,0:T(8,128)(2,1)S(1)} %add_convert_fusion.query_ref.key_ref.value_ref, bf16[512,3072]{1,0:T(8,128)(2,1)S(1)} %add_convert_fusion.query_ref.key_ref.value_ref, bf16[512,3072]{1,0:T(8,128)(2,1)S(1)} %add_convert_fusion.query_ref.key_ref.value_ref), custom_call_target="tpu_custom_call" | custom-call | flops 2147483648 | bytes 12582912 | tf_op jit(solution)/shard_map/pallas_call | solution.py:676
  187.7 9.9 %fusion.10 = f32[512,4096]{1,0:T(8,128)S(1)} fusion(bf16[512,1024]{1,0:T(8,128)(2,1)S(1)} %fusion.28, bf16[1024,8192]{1,0:T(8,128)(2,1)} %all-gather.3.cloned.1.call-done), kind=kOutput, calls=%fused_computation.15 | convolution fusion | flops 4294967296 | bytes 17825792 | tf_op jit(solution)/shard_map/dot_general | solution.py:37
  197.7 7.2 %fusion.146 = (f32[512]{0:T(512)S(1)}, f32[512,1024]{1,0:T(8,128)}, f32[512,1024]{1,0:T(8,128)}) fusion(f32[512,1024]{1,0:T(8,128)S(1)} %get-tuple-element.178, f32[2,1024]{1,0:T(2,128)S(1)} %get-tuple-element.218, f32[1024]{0:T(1024)S(1)} %copy-done.96, bf16[4096,1024]{1,0:T(8,128)(2,1)S(1)} %bitcast.444, f32[512,4096]{1,0:T(8,128)S(1)} %fusion.10, ...), kind=kOutput, calls=%fused_computation.401 | convolution fusion | flops 4318035456 | bytes 23099392 | tf_op jit(solution)/shard_map/dot_general | solution.py:37
  215.8 10.2 %convolution_convert_fusion.1 = bf16[4096,1024]{1,0:T(8,128)(2,1)S(1)} fusion(bf16[512,1024]{1,0:T(8,128)(2,1)S(1)} %bitcast.492, f32[512,4096]{1,0:T(8,128)} %copy-done.21, f32[4096]{0:T(1024)S(1)} %copy-done.83), kind=kOutput, calls=%fused_computation.12 | convolution fusion | flops 4320133120 | bytes 17842176 | tf_op jit(solution)/shard_map/dot_general | solution.py:47
  241.5 15.2 %fusion.143 = (f32[4096]{0:T(1024)S(1)}, bf16[512,4096]{1,0:T(8,128)(2,1)S(1)}) fusion(f32[512,4096]{1,0:T(8,128)} %copy-done.21, f32[4096]{0:T(1024)S(1)} %copy-done.83, bf16[512,1024]{1,0:T(8,128)(2,1)} %bitcast.493, bf16[4096,1024]{1,0:T(8,128)(2,1)} %bitcast.445), kind=kOutput, calls=%fused_computation.399 | convolution fusion | flops 4341100544 | bytes 22052864 | tf_op jit(solution)/shard_map/dot_general | solution.py:41
  256.7 5.4 %add_convert_fusion.3 = bf16[8,128,1024]{2,1,0:T(8,128)(2,1)} fusion(bf16[16,128,1024]{2,1,0:T(8,128)(2,1)} %collective-permute-done.23, bf16[16,128,1024]{2,1,0:T(8,128)(2,1)S(1)} %copy-done.4), kind=kLoop, calls=%fused_computation.22 | loop fusion | flops 4194304 | bytes 6291456 | tf_op jit(solution)/shard_map/convert_element_type | solution.py:603
  274.4 7.1 %fusion.8 = f32[512,1024]{1,0:T(8,128)S(1)} fusion(bf16[512,4096]{1,0:T(8,128)(2,1)S(1)} %copy-done.110, bf16[1024,8192]{1,0:T(8,128)(2,1)} %all-gather.3.cloned.1.call-done), kind=kOutput, calls=%fused_computation.13 | convolution fusion | flops 4294967296 | bytes 14680064 | tf_op jit(solution)/shard_map/dot_general | solution.py:41
  281.6 17.9 %collective-permute-done.24 = bf16[2,4,128,1024]{3,2,1,0:T(8,128)(2,1)} collective-permute-done((bf16[2,4,128,1024]{3,2,1,0:T(8,128)(2,1)}, bf16[2,4,128,1024]{3,2,1,0:T(8,128)(2,1)}, u32[]{:S(2)}, u32[]{:S(2)}) %collective-permute-start.24) | collective-permute-done | bytes 2097184 | tf_op jit(solution)/shard_map/ppermute | solution.py:325
  323.3 20.5 %shard_map.283 = (bf16[3,512,1024]{2,1,0:T(8,128)(2,1)S(1)}, f32[8,1024]{1,0:T(8,128)S(1)}) custom-call(bf16[512,3072]{1,0:T(8,128)(2,1)S(1)} %add_convert_fusion.query_ref.key_ref.value_ref, bf16[512,3072]{1,0:T(8,128)(2,1)S(1)} %add_convert_fusion.query_ref.key_ref.value_ref, bf16[512,3072]{1,0:T(8,128)(2,1)S(1)} %add_convert_fusion.query_ref.key_ref.value_ref, ...), custom_call_target="tpu_custom_call" | custom-call | flops 4831838208 | bytes 25165824 | tf_op jit(solution)/shard_map/pallas_call | solution.py:693
  358.9 6.2 %collective-permute-done.30 = bf16[4,32,4096]{2,1,0:T(8,128)(2,1)S(1)} collective-permute-done((bf16[4,32,4096]{2,1,0:T(8,128)(2,1)S(1)}, bf16[4,32,4096]{2,1,0:T(8,128)(2,1)S(1)}, u32[]{:S(2)}, u32[]{:S(2)}) %collective-permute-start.30) | collective-permute-done | bytes 1048608 | tf_op jit(solution)/shard_map/ppermute | solution.py:325
  408.4 6.9 %collective-permute-done.33 = bf16[1,32,4096]{2,1,0:T(8,128)(2,1)S(1)} collective-permute-done((bf16[1,32,4096]{2,1,0:T(8,128)(2,1)S(1)}, bf16[1,32,4096]{2,1,0:T(8,128)(2,1)S(1)}, u32[]{:S(2)}, u32[]{:S(2)}) %collective-permute-start.33) | collective-permute-done | bytes 262176 | tf_op jit(solution)/shard_map/ppermute | solution.py:325
  416.3 8.1 %fusion.107 = bf16[2,1024]{1,0:T(2,128)(2,1)S(1)} fusion(bf16[2,8192]{1,0:T(2,128)(2,1)S(1)} %constant_dynamic-update-slice_fusion, bf16[1024,9216]{1,0:T(8,128)(2,1)} %all-gather.5.cloned.1.call-done, f32[2,10240]{1,0:T(2,128)} %copy-done.64), kind=kOutput, calls=%fused_computation.288 | convolution fusion | flops 33574912 | bytes 16822272 | tf_op jit(solution)/shard_map/dot_general | solution.py:41
  426.7 6.1 %collective-permute-done.34 = bf16[2,4,32,4096]{3,2,1,0:T(8,128)(2,1)} collective-permute-done((bf16[2,4,32,4096]{3,2,1,0:T(8,128)(2,1)}, bf16[2,4,32,4096]{3,2,1,0:T(8,128)(2,1)}, u32[]{:S(2)}, u32[]{:S(2)}) %collective-permute-start.34) | collective-permute-done | bytes 2097184 | tf_op jit(solution)/shard_map/ppermute | solution.py:325
  446.7 6.1 %collective-permute-done.37 = bf16[4,32,4096]{2,1,0:T(8,128)(2,1)S(1)} collective-permute-done((bf16[4,32,4096]{2,1,0:T(8,128)(2,1)S(1)}, bf16[4,32,4096]{2,1,0:T(8,128)(2,1)S(1)}, u32[]{:S(2)}, u32[]{:S(2)}) %collective-permute-start.37) | collective-permute-done | bytes 1048608 | tf_op jit(solution)/shard_map/ppermute | solution.py:325
  453.8 5.6 %collective-permute-done.38 = bf16[704,128]{1,0:T(8,128)(2,1)S(1)} collective-permute-done((bf16[704,128]{1,0:T(8,128)(2,1)S(1)}, bf16[704,128]{1,0:T(8,128)(2,1)S(1)}, u32[]{:S(2)}, u32[]{:S(2)}) %collective-permute-start.38) | collective-permute-done | bytes 180256 | tf_op jit(solution)/shard_map/ppermute | solution.py:325
  474.2 11.7 %collective-permute-done.42 = bf16[1,32,4096]{2,1,0:T(8,128)(2,1)S(1)} collective-permute-done((bf16[1,32,4096]{2,1,0:T(8,128)(2,1)S(1)}, bf16[1,32,4096]{2,1,0:T(8,128)(2,1)S(1)}, u32[]{:S(2)}, u32[]{:S(2)}) %collective-permute-start.42) | collective-permute-done | bytes 262176 | tf_op jit(solution)/shard_map/ppermute | solution.py:325
  493.0 8.9 %shard_map.285 = (f32[32,17408]{1,0:T(8,128)}, f32[128,1024]{1,0:T(8,128)}, f32[32,1288]{1,0:T(8,128)}, f32[1,608]{1,0:T(1,128)}, f32[32,17408]{1,0:T(8,128)}, /...) custom-call(f32[32,17408]{1,0:T(8,128)} %refs_0_.3, ...), custom_call_target="tpu_custom_call" | custom-call | flops 51106880 | bytes 20442752 | tf_op jit(solution)/shard_map/pallas_call | solution.py:196
  520.5 5.5 %shard_map.286 = (f32[32,17408]{1,0:T(8,128)}, f32[128,1024]{1,0:T(8,128)}, f32[32,1288]{1,0:T(8,128)}, f32[1,608]{1,0:T(1,128)}, f32[8,128]{1,0:T(8,128)}) custom-call(f32[8,128]{1,0:T(8,128)} %copy-done.89, f32[32,17408]{1,0:T(8,128)} %refs_0_.3, f32[128,1024]{1,0:T(8,128)} %refs_1_.3, f32[32,1288]{1,0:T(8,128)} %refs_2_.3, ...), custom_call_target="tpu_custom_call" | custom-call | flops 21919040 | bytes 8767616 | tf_op jit(solution)/shard_map/pallas_call | solution.py:196
  (581 shorter events, 291.5 us)
Async XLA Ops:
  7.2 143.9 %all-gather.3.cloned.1.call-start = ((), (), s32[]{:S(2)}) async-start(), calls=%async_computation | async-start | bytes 17301504 | tf_op jit(solution)/shard_map/all_gather | solution.py:769
  10.1 406.2 %all-gather.5.cloned.1.call-start = ((), (), s32[]{:S(2)}) async-start(), calls=%async_computation.1 | async-start | bytes 19464192 | tf_op jit(solution)/shard_map/all_gather | solution.py:848
  18.8 13.9 %collective-permute-start.3 = (bf16[1,128,1024]{2,1,0:T(8,128)(2,1)S(1)}, bf16[1,128,1024]{2,1,0:T(8,128)(2,1)S(1)}, u32[]{:S(2)}, u32[]{:S(2)}) collective-permute-start(bf16[1,128,1024]{2,1,0:T(8,128)(2,1)S(1)} %get-tuple-element.189), channel_id=1, source_target_pairs={{0,24},{1,25},{2,26},{3,27},{4,28},{5,29},{6,30},{7,31},{8,0},{9,1... | collective-permute-start | bytes 786440 | tf_op jit(solution)/shard_map/ppermute | solution.py:325
  48.4 20.6 %collective-permute-start.8 = (bf16[1,128,1024]{2,1,0:T(8,128)(2,1)S(1)}, bf16[1,128,1024]{2,1,0:T(8,128)(2,1)S(1)}, u32[]{:S(2)}, u32[]{:S(2)}) collective-permute-start(bf16[1,128,1024]{2,1,0:T(8,128)(2,1)S(1)} %collective-permute-done.3), channel_id=1, source_target_pairs={{0,24},{1,25},{2,26},{3,27},{4,28},{5,29},{6,30},{7,31},{8,0},{9,1... | collective-permute-start | bytes 786440 | tf_op jit(solution)/shard_map/ppermute | solution.py:325
  89.9 20.3 %collective-permute-start.13 = (bf16[1,128,1024]{2,1,0:T(8,128)(2,1)}, bf16[1,128,1024]{2,1,0:T(8,128)(2,1)S(1)}, u32[]{:S(2)}, u32[]{:S(2)}) collective-permute-start(bf16[1,128,1024]{2,1,0:T(8,128)(2,1)} %copy-done.69), channel_id=1, source_target_pairs={{0,24},{1,25},{2,26},{3,27},{4,28},{5,29},{6,30},{7,31},{8,0},{9,1... | collective-permute-start | bytes 786440 | tf_op jit(solution)/shard_map/ppermute | solution.py:325
  111.8 11.3 %collective-permute-start.14 = (f32[1,2,8,10240]{3,2,1,0:T(8,128)}, f32[1,2,8,10240]{3,2,1,0:T(8,128)S(1)}, u32[]{:S(2)}, u32[]{:S(2)}) collective-permute-start(f32[1,2,8,10240]{3,2,1,0:T(8,128)} %constant_dynamic-slice_fusion), channel_id=1, source_target_pairs={{0,2},{1,5},{2,0},{3,7},{4,6},{5,1},{6,4},{7,3},{8,10},{9,13},{10,... | collective-permute-start | bytes 1966088 | tf_op jit(solution)/shard_map/ppermute | solution.py:325
  126.4 18.2 %collective-permute-start.19 = (bf16[4,128,1024]{2,1,0:T(8,128)(2,1)}, bf16[4,128,1024]{2,1,0:T(8,128)(2,1)}, u32[]{:S(2)}, u32[]{:S(2)}) collective-permute-start(bf16[4,128,1024]{2,1,0:T(8,128)(2,1)} %get-tuple-element.185), channel_id=1, source_target_pairs={{0,2},{1,5},{2,0},{3,7},{4,6},{5,1},{6,4},{7,3},{8,10},{9,13},{10,... | collective-permute-start | bytes 3145736 | tf_op jit(solution)/shard_map/ppermute | solution.py:325
  147.4 26.4 %collective-permute-start.20 = (bf16[8,128,1024]{2,1,0:T(8,128)(2,1)}, bf16[8,128,1024]{2,1,0:T(8,128)(2,1)}, u32[]{:S(2)}, u32[]{:S(2)}) collective-permute-start(bf16[8,128,1024]{2,1,0:T(8,128)(2,1)} %bitcast.43.refs_0_), channel_id=1, source_target_pairs={{0,4},{1,3},{2,6},{3,1},{4,0},{5,7},{6,2},{7,5},{8,12},{9,11},{10,... | collective-permute-start | bytes 6291464 | tf_op jit(solution)/shard_map/ppermute | solution.py:325
  148.9 34.3 %collective-permute-start.21 = (bf16[8,128,1024]{2,1,0:T(8,128)(2,1)}, bf16[8,128,1024]{2,1,0:T(8,128)(2,1)}, u32[]{:S(2)}, u32[]{:S(2)}) collective-permute-start(bf16[8,128,1024]{2,1,0:T(8,128)(2,1)} %bitcast.43.refs_0_), channel_id=1, source_target_pairs={{0,1},{1,0},{2,3},{3,2},{4,5},{5,4},{6,7},{7,6},{8,9},{9,8},{10,11... | collective-permute-start | bytes 6291464 | tf_op jit(solution)/shard_map/ppermute | solution.py:325
  173.7 9.5 %collective-permute-start.22 = (bf16[8,128,1024]{2,1,0:T(8,128)(2,1)}, bf16[8,128,1024]{2,1,0:T(8,128)(2,1)}, u32[]{:S(2)}, u32[]{:S(2)}) collective-permute-start(bf16[8,128,1024]{2,1,0:T(8,128)(2,1)} %collective-permute-done.20.refs_1_), channel_id=1, source_target_pairs={{0,1},{1,0},{2,3},{3,2},{4,5},{5,4},{6,7},{7,6},{8,9},{9,8},{10,11... | collective-permute-start | bytes 6291464 | tf_op jit(solution)/shard_map/ppermute | solution.py:325
  231.6 25.1 %collective-permute-start.23 = (bf16[16,128,1024]{2,1,0:T(8,128)(2,1)}, bf16[16,128,1024]{2,1,0:T(8,128)(2,1)}, u32[]{:S(2)}, u32[]{:S(2)}) collective-permute-start(bf16[16,128,1024]{2,1,0:T(8,128)(2,1)} %get-tuple-element.99), channel_id=1, source_target_pairs={{0,1},{1,0},{2,3},{3,2},{4,5},{5,4},{6,7},{7,6},{8,9},{9,8},{10,11... | collective-permute-start | bytes 12582920 | tf_op jit(solution)/shard_map/ppermute | solution.py:325
  262.1 37.4 %collective-permute-start.24 = (bf16[2,4,128,1024]{3,2,1,0:T(8,128)(2,1)}, bf16[2,4,128,1024]{3,2,1,0:T(8,128)(2,1)}, u32[]{:S(2)}, u32[]{:S(2)}) collective-permute-start(bf16[2,4,128,1024]{3,2,1,0:T(8,128)(2,1)} %bitcast.57), channel_id=1, source_target_pairs={{0,4},{1,3},{2,6},{3,1},{4,0},{5,7},{6,2},{7,5},{8,12},{9,11},{10,... | collective-permute-start | bytes 6291464 | tf_op jit(solution)/shard_map/ppermute | solution.py:325
  270.3 46.7 %collective-permute-start.26 = (bf16[16,32,4096]{2,1,0:T(8,128)(2,1)S(1)}, bf16[16,32,4096]{2,1,0:T(8,128)(2,1)}, u32[]{:S(2)}, u32[]{:S(2)}) collective-permute-start(bf16[16,32,4096]{2,1,0:T(8,128)(2,1)S(1)} %get-tuple-element.106), channel_id=1, source_target_pairs={{0,1},{1,0},{2,3},{3,2},{4,5},{5,4},{6,7},{7,6},{8,9},{9,8},{10,11... | collective-permute-start | bytes 12582920 | tf_op jit(solution)/shard_map/ppermute | solution.py:325
  302.2 14.9 %collective-permute-start.25 = (bf16[4,128,1024]{2,1,0:T(8,128)(2,1)S(1)}, bf16[4,128,1024]{2,1,0:T(8,128)(2,1)S(1)}, u32[]{:S(2)}, u32[]{:S(2)}) collective-permute-start(bf16[4,128,1024]{2,1,0:T(8,128)(2,1)S(1)} %fusion.26), channel_id=1, source_target_pairs={{0,2},{1,5},{2,0},{3,7},{4,6},{5,1},{6,4},{7,3},{8,10},{9,13},{10,... | collective-permute-start | bytes 3145736 | tf_op jit(solution)/shard_map/ppermute | solution.py:325
  319.4 26.1 %collective-permute-start.28 = (bf16[2,4,32,4096]{3,2,1,0:T(8,128)(2,1)S(1)}, bf16[2,4,32,4096]{3,2,1,0:T(8,128)(2,1)S(1)}, u32[]{:S(2)}, u32[]{:S(2)}) collective-permute-start(bf16[2,4,32,4096]{3,2,1,0:T(8,128)(2,1)S(1)} %bitcast.485), channel_id=1, source_target_pairs={{0,4},{1,3},{2,6},{3,1},{4,0},{5,7},{6,2},{7,5},{8,12},{9,11},{10,... | collective-permute-start | bytes 6291464 | tf_op jit(solution)/shard_map/ppermute | solution.py:325
  321.5 23.2 %collective-permute-start.27 = (bf16[2,128,1024]{2,1,0:T(8,128)(2,1)S(1)}, bf16[2,128,1024]{2,1,0:T(8,128)(2,1)S(1)}, u32[]{:S(2)}, u32[]{:S(2)}) collective-permute-start(bf16[2,128,1024]{2,1,0:T(8,128)(2,1)S(1)} %fusion.60), channel_id=1, source_target_pairs={{0,8},{1,9},{2,10},{3,11},{4,12},{5,13},{6,14},{7,15},{8,0},{9,1},... | collective-permute-start | bytes 1572872 | tf_op jit(solution)/shard_map/ppermute | solution.py:325
  345.7 13.2 %collective-permute-start.29 = (bf16[1,128,1024]{2,1,0:T(8,128)(2,1)S(1)}, bf16[1,128,1024]{2,1,0:T(8,128)(2,1)S(1)}, u32[]{:S(2)}, u32[]{:S(2)}) collective-permute-start(bf16[1,128,1024]{2,1,0:T(8,128)(2,1)S(1)} %fusion.66), channel_id=1, source_target_pairs={{0,16},{1,17},{2,18},{3,19},{4,20},{5,21},{6,22},{7,23},{8,24},{9,... | collective-permute-start | bytes 786440 | tf_op jit(solution)/shard_map/ppermute | solution.py:325
  350.3 14.9 %collective-permute-start.30 = (bf16[4,32,4096]{2,1,0:T(8,128)(2,1)S(1)}, bf16[4,32,4096]{2,1,0:T(8,128)(2,1)S(1)}, u32[]{:S(2)}, u32[]{:S(2)}) collective-permute-start(bf16[4,32,4096]{2,1,0:T(8,128)(2,1)S(1)} %fusion.25), channel_id=1, source_target_pairs={{0,2},{1,5},{2,0},{3,7},{4,6},{5,1},{6,4},{7,3},{8,10},{9,13},{10,... | collective-permute-start | bytes 3145736 | tf_op jit(solution)/shard_map/ppermute | solution.py:325
  370.2 14.8 %collective-permute-start.32 = (bf16[16,32,4096]{2,1,0:T(8,128)(2,1)S(1)}, bf16[16,32,4096]{2,1,0:T(8,128)(2,1)S(1)}, u32[]{:S(2)}, u32[]{:S(2)}) collective-permute-start(bf16[16,32,4096]{2,1,0:T(8,128)(2,1)S(1)} %get-tuple-element.119), channel_id=1, source_target_pairs={{0,1},{1,0},{2,3},{3,2},{4,5},{5,4},{6,7},{7,6},{8,9},{9,8},{10,11... | collective-permute-start | bytes 12582920 | tf_op jit(solution)/shard_map/ppermute | solution.py:325
  370.6 14.4 %collective-permute-start.31 = (bf16[2,32,4096]{2,1,0:T(8,128)(2,1)S(1)}, bf16[2,32,4096]{2,1,0:T(8,128)(2,1)S(1)}, u32[]{:S(2)}, u32[]{:S(2)}) collective-permute-start(bf16[2,32,4096]{2,1,0:T(8,128)(2,1)S(1)} %fusion.61), channel_id=1, source_target_pairs={{0,8},{1,9},{2,10},{3,11},{4,12},{5,13},{6,14},{7,15},{8,0},{9,1},... | collective-permute-start | bytes 1572872 | tf_op jit(solution)/shard_map/ppermute | solution.py:325
  400.8 14.5 %collective-permute-start.33 = (bf16[1,32,4096]{2,1,0:T(8,128)(2,1)S(1)}, bf16[1,32,4096]{2,1,0:T(8,128)(2,1)S(1)}, u32[]{:S(2)}, u32[]{:S(2)}) collective-permute-start(bf16[1,32,4096]{2,1,0:T(8,128)(2,1)S(1)} %fusion.67), channel_id=1, source_target_pairs={{0,16},{1,17},{2,18},{3,19},{4,20},{5,21},{6,22},{7,23},{8,24},{9,... | collective-permute-start | bytes 786440 | tf_op jit(solution)/shard_map/ppermute | solution.py:325
  406.4 26.4 %collective-permute-start.34 = (bf16[2,4,32,4096]{3,2,1,0:T(8,128)(2,1)}, bf16[2,4,32,4096]{3,2,1,0:T(8,128)(2,1)}, u32[]{:S(2)}, u32[]{:S(2)}) collective-permute-start(bf16[2,4,32,4096]{3,2,1,0:T(8,128)(2,1)} %bitcast.100), channel_id=1, source_target_pairs={{0,4},{1,3},{2,6},{3,1},{4,0},{5,7},{6,2},{7,5},{8,12},{9,11},{10,... | collective-permute-start | bytes 6291464 | tf_op jit(solution)/shard_map/ppermute | solution.py:325
  438.0 14.9 %collective-permute-start.37 = (bf16[4,32,4096]{2,1,0:T(8,128)(2,1)S(1)}, bf16[4,32,4096]{2,1,0:T(8,128)(2,1)S(1)}, u32[]{:S(2)}, u32[]{:S(2)}) collective-permute-start(bf16[4,32,4096]{2,1,0:T(8,128)(2,1)S(1)} %fusion.24), channel_id=1, source_target_pairs={{0,2},{1,5},{2,0},{3,7},{4,6},{5,1},{6,4},{7,3},{8,10},{9,13},{10,... | collective-permute-start | bytes 3145736 | tf_op jit(solution)/shard_map/ppermute | solution.py:325
  470.7 15.2 %collective-permute-start.42 = (bf16[1,32,4096]{2,1,0:T(8,128)(2,1)S(1)}, bf16[1,32,4096]{2,1,0:T(8,128)(2,1)S(1)}, u32[]{:S(2)}, u32[]{:S(2)}) collective-permute-start(bf16[1,32,4096]{2,1,0:T(8,128)(2,1)S(1)} %fusion.68), channel_id=1, source_target_pairs={{0,16},{1,17},{2,18},{3,19},{4,20},{5,21},{6,22},{7,23},{8,24},{9,... | collective-permute-start | bytes 786440 | tf_op jit(solution)/shard_map/ppermute | solution.py:325
  (138 other events, 1135.7 us)
Sparse Core Ops, SparseCore 0:
  11.5 130.6 all-gather.2
  175.0 130.9 all-gather.4

commit v6 on v5

--- a/solution.py
+++ b/solution.py
@@ -370,6 +370,25 @@
     return values
 
 
+def beside_kernel(*refs):
+    parts, out = refs[:-1], refs[-1]
+    at = 0
+    for part in parts:
+        out[:, at : at + part.shape[1]] = part[...].astype(out.dtype)
+        at += part.shape[1]
+
+
+def beside(parts):
+    vmem = pl.BlockSpec(memory_space=pltpu.VMEM)
+    shape = (parts[0].shape[0], sum(part.shape[1] for part in parts))
+    return pl.pallas_call(
+        beside_kernel,
+        out_shape=jax.ShapeDtypeStruct(shape, jnp.bfloat16),
+        in_specs=[vmem] * len(parts),
+        out_specs=vmem,
+    )(*parts)
+
+
 def gather_and_scatter(grid, values, table, ready):
     turned = jnp.swapaxes(table, Y_AXIS, X_AXIS)
     table = jnp.where(grid.coords[CORE] == 0, table, turned)
@@ -580,29 +599,35 @@
     dims = tuple(grid.sizes[axis] for axis in axes) + (rows, columns)
     kept, sent = pick_rows(tables, places)
     received = yield [grid.ahead(sent, CORE, 1)]
-    terms = [kept.reshape(dims), received[0].reshape(dims)]
-
-    def entry(place):
-        return sum(term[place].astype(jnp.float32) for term in terms)
+    terms = [(kept.reshape(dims), (), 1), (received[0].reshape(dims), (), 1)]
+
+    def total(*index):
+        return sum(array[prefix + index].astype(jnp.float32) for array, prefix, _ in terms)
 
     for axis in axes:
         if axis == Z_AXIS:
             bit = 1
             while bit < grid.sizes[axis]:
-                terms = [term.reshape((-1, 2) + term.shape[1:]) for term in terms]
-                sent = sum(term[:, 1].astype(jnp.float32) for term in terms)
+                sent = sum(
+                    array[prefix + (slice(stride, None, 2 * stride),)].astype(jnp.float32)
+                    for array, prefix, stride in terms
+                )
                 received = yield [grid.flip(sent.astype(jnp.bfloat16), axis, bit)]
-                terms = [term[:, 0] for term in terms] + received
+                terms = [(array, prefix, 2 * stride) for array, prefix, stride in terms]
+                terms.append((received[0], (), 1))
                 bit *= 2
-            terms = [term[0] for term in terms]
+        else:
+            passing = None
+            for place in range(1, grid.sizes[axis]):
+                here = total(place)
+                if passing is not None:
+                    here = here + passing.astype(jnp.float32)
+                passing = (yield [grid.ahead(here.astype(jnp.bfloat16), axis, 1)])[0]
+            terms = [(array, prefix + (0,), 1) for array, prefix, _ in terms]
+            terms.append((passing, (), 1))
             continue
-        total = None
-        for place in range(1, grid.sizes[axis]):
-            here = entry(place)
-            total = here if total is None else here + total.astype(jnp.float32)
-            total = (yield [grid.ahead(total.astype(jnp.bfloat16), axis, 1)])[0]
-        terms = [term[0] for term in terms] + [total]
-    yield sum(term.astype(jnp.float32) for term in terms)
+        terms = [(array, prefix + (0,), 1) for array, prefix, _ in terms]
+    yield total()
 
 
 HEAD_COLS = 4 * HEAD_DIM
@@ -844,7 +869,7 @@
     normed_a = modulate(resid_in, shift_a, scale_a).astype(bf16).reshape(rows_all, D)
     proj = (matmul(normed_a, w_qkv) + b_qkv).astype(bf16)
     mixed = meet(attend(proj), get)
-    tail_bf = after(in_bf[:, 4 * D + FF :], mixed)
+    tail_bf = after(in_bf[:, 4 * D + FF :], mods)
     table_cond = lax.all_gather(tail_bf, AXIS, axis=0, tiled=True)
     attended = (matmul(mixed, w_out) + b_out).reshape(count, TOK, D)
     resid_mid = resid_in + gate_a[:, None, :] * attended
@@ -852,7 +877,9 @@
     normed_b = meet(normed_b, get)
     (table_down,) = last(get)
     upper = matmul(normed_b, table_up) + b_up
-    active = jax.nn.gelu(upper, approximate=True).astype(bf16)
+    active, pull_gelu = jax.vjp(partial(jax.nn.gelu, approximate=True), upper)
+    slope = pull_gelu(jnp.ones_like(upper))[0]
+    active, slope = lax.optimization_barrier((active.astype(bf16), slope))
     lowered = matmul(active, table_down) + b_down
     lowered = lowered.reshape(count, TOK, D)
     resid_out = resid_mid + gate_b[:, None, :] * lowered
@@ -874,8 +901,7 @@
     put_down = Flow(scatter_bulk(grid, [grad_w_down], ORDER))
     lowered_bf = after(lowered_bf, grad_w_down)
     grad_active = dot_tail(lowered_bf, table_down)
-    gelu = partial(jax.nn.gelu, approximate=True)
-    grad_upper = jax.vjp(gelu, upper)[1](grad_active)[0]
+    grad_upper = grad_active * slope
     grad_b_up = jnp.sum(grad_upper, axis=0)
     upper_bf = grad_upper.astype(bf16)
     upper_bf = meet(upper_bf, put_down)
@@ -911,7 +937,7 @@
     grad_b_patch = jnp.sum(grad_hidden, axis=0)
     grad_w_patch = dot_head(grad_hidden.astype(bf16), noisy)
 
-    grad_mods = jnp.concatenate(
+    mods_bf = beside(
         [
             grad_shift_a,
             grad_scale_a,
@@ -921,17 +947,14 @@
             grad_gate_b,
             grad_shift_f,
             grad_scale_f,
-        ],
-        axis=1,
-    )
-    grad_mods = meet(grad_mods, put_up)
-    mods_bf = grad_mods.astype(bf16)
+        ]
+    )
     grad_cond = jax.vjp(jax.nn.silu, cond_own)[1](dot_tail(mods_bf, table_cond[:, : 8 * D]))[0]
     cond_bf = grad_cond.astype(bf16)
     grad_time_act = dot_tail(cond_bf, table_cond[:, 8 * D :])
     grad_time_pre = jax.vjp(jax.nn.silu, time_own)[1](grad_time_act)[0]
-    image_grads = jnp.concatenate([mods_bf, grad_time_pre.astype(bf16), cond_bf], axis=1)
-    image_grads = meet(image_grads, put_rest).reshape(-1, 128)
+    image_grads = beside([mods_bf, grad_time_pre, grad_cond])
+    image_grads = meet(image_grads, put_up, put_rest).reshape(-1, 128)
     grad_bias = jnp.concatenate(
         [
             grad_b_query,

time: 544 us -> 531 us (0.976)
  local copies, waits for them, and re-layouts: 48.5 us -> 33.3 us
  other arithmetic: 69.6 us -> 79.2 us
  waiting for transfers between devices: 178 us -> 171 us
  Pallas kernels: 59.3 us -> 65.8 us
    slice x10 -> x1, local copies, waits for them, and re-layouts: 10.9 us -> 0.88 us  [per_device(): tail_bf = after(in_bf[:, 4 * D + FF:], mods)]
    convert_element_type x3 -> x6, other arithmetic: 1.96 us -> 9.84 us  [scatter_bulk(): received = (yield [grid.flip(sent.astype(jnp.bfloat16), axis, bit)])]
    another operation x14 -> x2, local copies, waits for them, and re-layouts: 7.25 us -> 0.04 us  [the longest x12 7.21 us: scatter_bulk(): terms = [term.reshape((-1, 2) + term.shape[1:]) for term in terms]]
    ppermute x48, waiting for transfers between devices: 178 us -> 171 us  [move(): return lax.ppermute(values, AXIS, pairs)]
    unnamed x238 -> x191, local copies, waits for them, and re-layouts: 13.8 us -> 17.6 us
  transfers between devices with their start and end apart: 50 -> 50, of which waited for: 36 -> 35; matrix products, arithmetic and copies ran while one was open for 37% -> 35% of each run, Pallas kernels for 8% -> 10%
where the time goes in v6:
time: 531 us; the launch traced here: 522 us
  waiting for transfers between devices  171 us (32%)
  matrix products  101 us (19%)
  other arithmetic  79.2 us (15%)
  Pallas kernels  65.8 us (12%)
  starting transfers between devices  55.4 us (10%)
  local copies, waits for them, and re-layouts  33.3 us (6%)
  between operations  16.1 us (3%)
    ppermute x48, waiting for transfers between devices, move(): return lax.ppermute(values, AXIS, pairs)  171 us
    ppermute x48, starting transfers between devices, move(): return lax.ppermute(values, AXIS, pairs)  55.3 us
    dot_general x12, matrix products, dot_tail(): lax.dot_general(left, right, (((1,), (1,)), ((), ())), preferred_element_...  46.2 us
    dot_general x7, matrix products, matmul(): return jnp.dot(left, right, preferred_element_type=jnp.float32)  33.4 us
    dot_general x10, matrix products, dot_head(): lax.dot_general(left, right, (((0,), (0,)), ((), ())), preferred_element_...  20.7 us
    pallas_call x1, Pallas kernels, attend_back(): pl.pallas_call(attend_back_kernel, grid=(D // HEAD_COLS, count), out_shap...  20.1 us
    unnamed x191, local copies, waits for them, and re-layouts  17.6 us
    convert_element_type x6, other arithmetic, scatter_bulk(): passing = (yield [grid.ahead(here.astype(jnp.bfloat16), axis, 1)])[0]  16.8 us
  transfers between devices with their start and end apart: 50, of which 35 were waited for; matrix products, arithmetic and copies ran while one was open for 35% of the time, Pallas kernels for 10%

profile of v6, /device:TPU:0, one launch (start us, length us, event | category | flops | bytes accessed | tf_op | source)
XLA Modules:
  0.0 521.8 jit_solution(14143115861169340526)
XLA Ops:
  22.5 10.2 %collective-permute-done.3 = bf16[1,128,1024]{2,1,0:T(8,128)(2,1)S(1)} collective-permute-done((bf16[1,128,1024]{2,1,0:T(8,128)(2,1)S(1)}, bf16[1,128,1024]{2,1,0:T(8,128)(2,1)S(1)}, u32[]{:S(2)}, u32[]{:S(2)}) %collective-permute-start.3) | collective-permute-done | bytes 262176 | tf_op jit(solution)/shard_map/ppermute | solution.py:325
  56.1 12.9 %collective-permute-done.8 = bf16[1,128,1024]{2,1,0:T(8,128)(2,1)S(1)} collective-permute-done((bf16[1,128,1024]{2,1,0:T(8,128)(2,1)S(1)}, bf16[1,128,1024]{2,1,0:T(8,128)(2,1)S(1)}, u32[]{:S(2)}, u32[]{:S(2)}) %collective-permute-start.8) | collective-permute-done | bytes 262176 | tf_op jit(solution)/shard_map/ppermute | solution.py:325
  73.6 5.4 %collective-permute-done.10 = f32[2,32,64]{2,1,0:T(8,128)S(1)} collective-permute-done((f32[2,32,64]{2,1,0:T(8,128)S(1)}, f32[2,32,64]{2,1,0:T(8,128)S(1)}, u32[]{:S(2)}, u32[]{:S(2)}) %collective-permute-start.10) | collective-permute-done | bytes 16416 | tf_op jit(solution)/shard_map/ppermute | solution.py:325
  92.0 13.3 %collective-permute-done.13 = bf16[1,128,1024]{2,1,0:T(8,128)(2,1)S(1)} collective-permute-done((bf16[1,128,1024]{2,1,0:T(8,128)(2,1)S(1)}, bf16[1,128,1024]{2,1,0:T(8,128)(2,1)S(1)}, u32[]{:S(2)}, u32[]{:S(2)}) %collective-permute-start.13) | collective-permute-done | bytes 262176 | tf_op jit(solution)/shard_map/ppermute | solution.py:325
  107.1 16.0 %collective-permute-done.14 = f32[1,2,8,10240]{3,2,1,0:T(8,128)S(1)} collective-permute-done((f32[1,2,8,10240]{3,2,1,0:T(8,128)S(1)}, f32[1,2,8,10240]{3,2,1,0:T(8,128)S(1)}, u32[]{:S(2)}, u32[]{:S(2)}) %collective-permute-start.14) | collective-permute-done | bytes 655392 | tf_op jit(solution)/shard_map/ppermute | solution.py:325
  156.8 7.0 %add_convert_fusion.query_ref.key_ref.value_ref = bf16[512,3072]{1,0:T(8,128)(2,1)S(1)} fusion(bf16[512,1024]{1,0:T(8,128)(2,1)S(1)} %fusion.31, bf16[1024,8192]{1,0:T(8,128)(2,1)} %all-gather.3.cloned.1.call-done, f32[3072]{0:T(1024)S(1)} %pad_maximum_fusion.21), kind=kOutput, calls=%fused_computation.20 | convolution fusion | flops 3224371200 | bytes 10498048 | tf_op jit(solution)/shard_map/dot_general | solution.py:37
  163.8 9.8 %shard_map.279 = bf16[512,1024]{1,0:T(8,128)(2,1)S(1)} custom-call(bf16[512,3072]{1,0:T(8,128)(2,1)S(1)} %add_convert_fusion.query_ref.key_ref.value_ref, bf16[512,3072]{1,0:T(8,128)(2,1)S(1)} %add_convert_fusion.query_ref.key_ref.value_ref, bf16[512,3072]{1,0:T(8,128)(2,1)S(1)} %add_convert_fusion.query_ref.key_ref.value_ref), custom_call_target="tpu_custom_call" | custom-call | flops 2147483648 | bytes 12582912 | tf_op jit(solution)/shard_map/pallas_call | solution.py:701
  173.6 7.8 %collective-permute-done.20.refs_1_ = bf16[8,128,1024]{2,1,0:T(8,128)(2,1)} collective-permute-done((bf16[8,128,1024]{2,1,0:T(8,128)(2,1)S(1)}, bf16[8,128,1024]{2,1,0:T(8,128)(2,1)}, u32[]{:S(2)}, u32[]{:S(2)}) %collective-permute-start.20) | collective-permute-done | bytes 2097184 | tf_op jit(solution)/shard_map/ppermute | solution.py:325
  189.9 13.8 %fusion.7 = (f32[512,4096]{1,0:T(8,128)}, bf16[512,4096]{1,0:T(8,128)(2,1)S(1)}) fusion(f32[4096]{0:T(1024)S(1)} %slice-done.3, bf16[512,1024]{1,0:T(8,128)(2,1)S(1)} %fusion.28, bf16[1024,8192]{1,0:T(8,128)(2,1)} %all-gather.3.cloned.1.call-done), kind=kOutput, calls=%fused_computation.9 | convolution fusion | flops 4336910336 | bytes 22036480 | tf_op jit(solution)/shard_map/dot_general | solution.py:37
  208.2 5.9 %fusion.148 = (f32[512]{0:T(512)S(1)}, f32[512,1024]{1,0:T(8,128)}, f32[512,1024]{1,0:T(8,128)S(1)}) fusion(f32[512,1024]{1,0:T(8,128)S(1)} %get-tuple-element.178, f32[2,1024]{1,0:T(2,128)S(1)} %get-tuple-element.222, f32[1024]{0:T(1024)S(1)} %copy-done.68, bf16[512,4096]{1,0:T(8,128)(2,1)S(1)} %get-tuple-element.97, bf16[4096,1024]{1,0:T(8,128)(2,1)S(1)} %bitcast.391), kind=kOutput, calls=%fused_computation.385 | convolution fusion | flops 4297063936 | bytes 18888704 | tf_op jit(solution)/shard_map/dot_general | solution.py:37
  226.2 6.7 %convolution_convert_fusion.1 = bf16[4096,1024]{1,0:T(8,128)(2,1)} fusion(bf16[512,4096]{1,0:T(8,128)(2,1)S(1)} %copy-done.28, bf16[512,1024]{1,0:T(8,128)(2,1)S(1)} %bitcast.441), kind=kOutput, calls=%fused_computation.12 | convolution fusion | flops 4299161600 | bytes 13631488 | tf_op jit(solution)/shard_map/dot_general | solution.py:47
  242.3 9.0 %fusion.152 = (f32[4096]{0:T(1024)S(1)}, bf16[512,4096]{1,0:T(8,128)(2,1)}) fusion(f32[512,4096]{1,0:T(8,128)} %get-tuple-element.101, bf16[512,1024]{1,0:T(8,128)(2,1)} %bitcast.442, bf16[4096,1024]{1,0:T(8,128)(2,1)S(1)} %bitcast.394), kind=kOutput, calls=%fused_computation.387 | convolution fusion | flops 4301254656 | bytes 22036480 | tf_op jit(solution)/shard_map/dot_general | solution.py:41
  266.3 8.3 %fusion.8 = f32[512,1024]{1,0:T(8,128)S(1)} fusion(bf16[512,4096]{1,0:T(8,128)(2,1)} %get-tuple-element.104, bf16[1024,8192]{1,0:T(8,128)(2,1)} %all-gather.3.cloned.1.call-done), kind=kOutput, calls=%fused_computation.13 | convolution fusion | flops 4294967296 | bytes 14680064 | tf_op jit(solution)/shard_map/dot_general | solution.py:41
  274.5 6.5 %collective-permute-done.24 = bf16[2,4,128,1024]{3,2,1,0:T(8,128)(2,1)} collective-permute-done((bf16[2,4,128,1024]{3,2,1,0:T(8,128)(2,1)S(1)}, bf16[2,4,128,1024]{3,2,1,0:T(8,128)(2,1)}, u32[]{:S(2)}, u32[]{:S(2)}) %collective-permute-start.24) | collective-permute-done | bytes 2097184 | tf_op jit(solution)/shard_map/ppermute | solution.py:325
  293.1 5.4 %collective-permute-done.25 = bf16[4,128,1024]{2,1,0:T(8,128)(2,1)S(1)} collective-permute-done((bf16[4,128,1024]{2,1,0:T(8,128)(2,1)S(1)}, bf16[4,128,1024]{2,1,0:T(8,128)(2,1)S(1)}, u32[]{:S(2)}, u32[]{:S(2)}) %collective-permute-start.25) | collective-permute-done | bytes 1048608 | tf_op jit(solution)/shard_map/ppermute | solution.py:325
  306.9 20.1 %shard_map.283 = (bf16[3,512,1024]{2,1,0:T(8,128)(2,1)S(1)}, f32[8,1024]{1,0:T(8,128)S(1)}) custom-call(bf16[512,3072]{1,0:T(8,128)(2,1)S(1)} %copy-done.2, bf16[512,3072]{1,0:T(8,128)(2,1)S(1)} %copy-done.2, bf16[512,3072]{1,0:T(8,128)(2,1)S(1)} %copy-done.2, bf16[512,1024]{1,0:T(8,128)(2,1)S(1)} %fusion.41.grad_ref), custom_call_target="tpu_custom_call" | custom-call | flops 4831838208 | bytes 25165824 | tf_op jit(solution)/shard_map/pallas_call | solution.py:718
  338.7 6.3 %collective-permute-done.29 = bf16[1,128,1024]{2,1,0:T(8,128)(2,1)S(1)} collective-permute-done((bf16[1,128,1024]{2,1,0:T(8,128)(2,1)S(1)}, bf16[1,128,1024]{2,1,0:T(8,128)(2,1)S(1)}, u32[]{:S(2)}, u32[]{:S(2)}) %collective-permute-start.29) | collective-permute-done | bytes 262176 | tf_op jit(solution)/shard_map/ppermute | solution.py:325
  345.1 7.1 %shard_map.284 = (bf16[16,32,4096]{2,1,0:T(8,128)(2,1)S(1)}, bf16[16,32,4096]{2,1,0:T(8,128)(2,1)}) custom-call(s32[32]{0:T(128)S(1)} %get-tuple-element.272.places, bf16[32,32,1024]{2,1,0:T(8,128)(2,1)S(1)} %bitcast.413, bf16[32,32,1024]{2,1,0:T(8,128)(2,1)S(1)} %bitcast.414, bf16[32,32,1024]{2,1,0:T(8,128)(2,1)S(1)} %bitcast.415, ...), custom_call_target="tpu_custom_call" | custom-call | bytes 16777216 | tf_op jit(solution)/shard_map/pallas_call | solution.py:579
  398.6 10.2 %fusion.106.refs_2_ = f32[2,1024]{1,0:T(2,128)S(1)} fusion(bf16[2,8192]{1,0:T(2,128)(2,1)} %shard_map.285.refs_0_, bf16[1024,9216]{1,0:T(8,128)(2,1)} %all-gather.5.cloned.1.call-done, f32[2,10240]{1,0:T(2,128)} %copy-done.46), kind=kOutput, calls=%fused_computation.260 | convolution fusion | flops 33572864 | bytes 16826368 | tf_op jit(solution)/shard_map/dot_general | solution.py:41
  430.0 6.1 %collective-permute-done.37 = bf16[4,32,4096]{2,1,0:T(8,128)(2,1)S(1)} collective-permute-done((bf16[4,32,4096]{2,1,0:T(8,128)(2,1)S(1)}, bf16[4,32,4096]{2,1,0:T(8,128)(2,1)S(1)}, u32[]{:S(2)}, u32[]{:S(2)}) %collective-permute-start.37) | collective-permute-done | bytes 1048608 | tf_op jit(solution)/shard_map/ppermute | solution.py:325
  449.8 5.0 collective-permute-done.40
  457.9 13.7 %collective-permute-done.42 = bf16[1,32,4096]{2,1,0:T(8,128)(2,1)} collective-permute-done((bf16[1,32,4096]{2,1,0:T(8,128)(2,1)S(1)}, bf16[1,32,4096]{2,1,0:T(8,128)(2,1)}, u32[]{:S(2)}, u32[]{:S(2)}) %collective-permute-start.42) | collective-permute-done | bytes 262176 | tf_op jit(solution)/shard_map/ppermute | solution.py:325
  479.2 8.9 %shard_map.287 = (f32[32,17408]{1,0:T(8,128)}, f32[128,1024]{1,0:T(8,128)}, f32[32,1288]{1,0:T(8,128)}, f32[1,608]{1,0:T(1,128)}, f32[32,17408]{1,0:T(8,128)}, /...) custom-call(f32[32,17408]{1,0:T(8,128)} %refs_0_.3, ...), custom_call_target="tpu_custom_call" | custom-call | flops 51106880 | bytes 20442752 | tf_op jit(solution)/shard_map/pallas_call | solution.py:196
  506.7 5.5 %shard_map.288 = (f32[32,17408]{1,0:T(8,128)}, f32[128,1024]{1,0:T(8,128)}, f32[32,1288]{1,0:T(8,128)}, f32[1,608]{1,0:T(1,128)}, f32[8,128]{1,0:T(8,128)}) custom-call(f32[8,128]{1,0:T(8,128)} %copy-done.70, f32[32,17408]{1,0:T(8,128)} %refs_0_.3, f32[128,1024]{1,0:T(8,128)} %refs_1_.3, f32[32,1288]{1,0:T(8,128)} %refs_2_.3, ...), custom_call_target="tpu_custom_call" | custom-call | flops 21919040 | bytes 8767616 | tf_op jit(solution)/shard_map/pallas_call | solution.py:196
  (515 shorter events, 284.8 us)
Async XLA Ops:
  7.2 148.6 %all-gather.3.cloned.1.call-start = ((), (), s32[]{:S(2)}) async-start(), calls=%async_computation | async-start | bytes 17301504 | tf_op jit(solution)/shard_map/all_gather | solution.py:794
  10.1 388.6 %all-gather.5.cloned.1.call-start = ((), (), s32[]{:S(2)}) async-start(), calls=%async_computation.1 | async-start | bytes 19464192 | tf_op jit(solution)/shard_map/all_gather | solution.py:873
  18.8 13.9 %collective-permute-start.3 = (bf16[1,128,1024]{2,1,0:T(8,128)(2,1)S(1)}, bf16[1,128,1024]{2,1,0:T(8,128)(2,1)S(1)}, u32[]{:S(2)}, u32[]{:S(2)}) collective-permute-start(bf16[1,128,1024]{2,1,0:T(8,128)(2,1)S(1)} %get-tuple-element.193), channel_id=1, source_target_pairs={{0,24},{1,25},{2,26},{3,27},{4,28},{5,29},{6,30},{7,31},{8,0},{9,1... | collective-permute-start | bytes 786440 | tf_op jit(solution)/shard_map/ppermute | solution.py:325
  48.4 20.6 %collective-permute-start.8 = (bf16[1,128,1024]{2,1,0:T(8,128)(2,1)S(1)}, bf16[1,128,1024]{2,1,0:T(8,128)(2,1)S(1)}, u32[]{:S(2)}, u32[]{:S(2)}) collective-permute-start(bf16[1,128,1024]{2,1,0:T(8,128)(2,1)S(1)} %collective-permute-done.3), channel_id=1, source_target_pairs={{0,24},{1,25},{2,26},{3,27},{4,28},{5,29},{6,30},{7,31},{8,0},{9,1... | collective-permute-start | bytes 786440 | tf_op jit(solution)/shard_map/ppermute | solution.py:325
  85.3 20.0 %collective-permute-start.13 = (bf16[1,128,1024]{2,1,0:T(8,128)(2,1)S(1)}, bf16[1,128,1024]{2,1,0:T(8,128)(2,1)S(1)}, u32[]{:S(2)}, u32[]{:S(2)}) collective-permute-start(bf16[1,128,1024]{2,1,0:T(8,128)(2,1)S(1)} %copy-done.51), channel_id=1, source_target_pairs={{0,24},{1,25},{2,26},{3,27},{4,28},{5,29},{6,30},{7,31},{8,0},{9,1... | collective-permute-start | bytes 786440 | tf_op jit(solution)/shard_map/ppermute | solution.py:325
  105.3 17.7 %collective-permute-start.14 = (f32[1,2,8,10240]{3,2,1,0:T(8,128)S(1)}, f32[1,2,8,10240]{3,2,1,0:T(8,128)S(1)}, u32[]{:S(2)}, u32[]{:S(2)}) collective-permute-start(f32[1,2,8,10240]{3,2,1,0:T(8,128)S(1)} %constant_dynamic-slice_fusion), channel_id=1, source_target_pairs={{0,2},{1,5},{2,0},{3,7},{4,6},{5,1},{6,4},{7,3},{8,10},{9,13},{10,... | collective-permute-start | bytes 1966088 | tf_op jit(solution)/shard_map/ppermute | solution.py:325
  128.1 17.7 %collective-permute-start.19 = (bf16[4,128,1024]{2,1,0:T(8,128)(2,1)}, bf16[4,128,1024]{2,1,0:T(8,128)(2,1)}, u32[]{:S(2)}, u32[]{:S(2)}) collective-permute-start(bf16[4,128,1024]{2,1,0:T(8,128)(2,1)} %get-tuple-element.189), channel_id=1, source_target_pairs={{0,2},{1,5},{2,0},{3,7},{4,6},{5,1},{6,4},{7,3},{8,10},{9,13},{10,... | collective-permute-start | bytes 3145736 | tf_op jit(solution)/shard_map/ppermute | solution.py:325
  135.1 10.6 %collective-permute-start.17 = (f32[160,128]{1,0:T(8,128)S(1)}, f32[160,128]{1,0:T(8,128)S(1)}, u32[]{:S(2)}, u32[]{:S(2)}) collective-permute-start(f32[160,128]{1,0:T(8,128)S(1)} %get-tuple-element.198), channel_id=1, source_target_pairs={{0,16},{1,17},{2,18},{3,19},{4,20},{5,21},{6,22},{7,23},{8,24},{9,... | collective-permute-start | bytes 245768 | tf_op jit(solution)/shard_map/ppermute | solution.py:325
  151.1 30.4 %collective-permute-start.20 = (bf16[8,128,1024]{2,1,0:T(8,128)(2,1)S(1)}, bf16[8,128,1024]{2,1,0:T(8,128)(2,1)}, u32[]{:S(2)}, u32[]{:S(2)}) collective-permute-start(bf16[8,128,1024]{2,1,0:T(8,128)(2,1)S(1)} %bitcast.395), channel_id=1, source_target_pairs={{0,4},{1,3},{2,6},{3,1},{4,0},{5,7},{6,2},{7,5},{8,12},{9,11},{10,... | collective-permute-start | bytes 6291464 | tf_op jit(solution)/shard_map/ppermute | solution.py:325
  155.1 34.8 %collective-permute-start.21 = (bf16[8,128,1024]{2,1,0:T(8,128)(2,1)S(1)}, bf16[8,128,1024]{2,1,0:T(8,128)(2,1)}, u32[]{:S(2)}, u32[]{:S(2)}) collective-permute-start(bf16[8,128,1024]{2,1,0:T(8,128)(2,1)S(1)} %bitcast.396), channel_id=1, source_target_pairs={{0,1},{1,0},{2,3},{3,2},{4,5},{5,4},{6,7},{7,6},{8,9},{9,8},{10,11... | collective-permute-start | bytes 6291464 | tf_op jit(solution)/shard_map/ppermute | solution.py:325
  241.7 9.6 %collective-permute-start.23 = (bf16[16,128,1024]{2,1,0:T(8,128)(2,1)}, bf16[16,128,1024]{2,1,0:T(8,128)(2,1)}, u32[]{:S(2)}, u32[]{:S(2)}) collective-permute-start(bf16[16,128,1024]{2,1,0:T(8,128)(2,1)} %get-tuple-element.102), channel_id=1, source_target_pairs={{0,1},{1,0},{2,3},{3,2},{4,5},{5,4},{6,7},{7,6},{8,9},{9,8},{10,11... | collective-permute-start | bytes 12582920 | tf_op jit(solution)/shard_map/ppermute | solution.py:325
  254.8 26.2 %collective-permute-start.24 = (bf16[2,4,128,1024]{3,2,1,0:T(8,128)(2,1)S(1)}, bf16[2,4,128,1024]{3,2,1,0:T(8,128)(2,1)}, u32[]{:S(2)}, u32[]{:S(2)}) collective-permute-start(bf16[2,4,128,1024]{3,2,1,0:T(8,128)(2,1)S(1)} %bitcast.432), channel_id=1, source_target_pairs={{0,4},{1,3},{2,6},{3,1},{4,0},{5,7},{6,2},{7,5},{8,12},{9,11},{10,... | collective-permute-start | bytes 6291464 | tf_op jit(solution)/shard_map/ppermute | solution.py:325
  266.0 32.6 %collective-permute-start.26 = (bf16[16,32,4096]{2,1,0:T(8,128)(2,1)}, bf16[16,32,4096]{2,1,0:T(8,128)(2,1)}, u32[]{:S(2)}, u32[]{:S(2)}) collective-permute-start(bf16[16,32,4096]{2,1,0:T(8,128)(2,1)} %get-tuple-element.109), channel_id=1, source_target_pairs={{0,1},{1,0},{2,3},{3,2},{4,5},{5,4},{6,7},{7,6},{8,9},{9,8},{10,11... | collective-permute-start | bytes 12582920 | tf_op jit(solution)/shard_map/ppermute | solution.py:325
  283.6 14.9 %collective-permute-start.25 = (bf16[4,128,1024]{2,1,0:T(8,128)(2,1)S(1)}, bf16[4,128,1024]{2,1,0:T(8,128)(2,1)S(1)}, u32[]{:S(2)}, u32[]{:S(2)}) collective-permute-start(bf16[4,128,1024]{2,1,0:T(8,128)(2,1)S(1)} %fusion.26), channel_id=1, source_target_pairs={{0,2},{1,5},{2,0},{3,7},{4,6},{5,1},{6,4},{7,3},{8,10},{9,13},{10,... | collective-permute-start | bytes 3145736 | tf_op jit(solution)/shard_map/ppermute | solution.py:325
  301.3 26.1 %collective-permute-start.28 = (bf16[2,4,32,4096]{3,2,1,0:T(8,128)(2,1)S(1)}, bf16[2,4,32,4096]{3,2,1,0:T(8,128)(2,1)S(1)}, u32[]{:S(2)}, u32[]{:S(2)}) collective-permute-start(bf16[2,4,32,4096]{3,2,1,0:T(8,128)(2,1)S(1)} %bitcast.433), channel_id=1, source_target_pairs={{0,4},{1,3},{2,6},{3,1},{4,0},{5,7},{6,2},{7,5},{8,12},{9,11},{10,... | collective-permute-start | bytes 6291464 | tf_op jit(solution)/shard_map/ppermute | solution.py:325
  303.2 23.9 %collective-permute-start.27 = (bf16[2,128,1024]{2,1,0:T(8,128)(2,1)S(1)}, bf16[2,128,1024]{2,1,0:T(8,128)(2,1)S(1)}, u32[]{:S(2)}, u32[]{:S(2)}) collective-permute-start(bf16[2,128,1024]{2,1,0:T(8,128)(2,1)S(1)} %fusion.51), channel_id=1, source_target_pairs={{0,8},{1,9},{2,10},{3,11},{4,12},{5,13},{6,14},{7,15},{8,0},{9,1},... | collective-permute-start | bytes 1572872 | tf_op jit(solution)/shard_map/ppermute | solution.py:325
  329.9 15.1 %collective-permute-start.30 = (bf16[4,32,4096]{2,1,0:T(8,128)(2,1)S(1)}, bf16[4,32,4096]{2,1,0:T(8,128)(2,1)S(1)}, u32[]{:S(2)}, u32[]{:S(2)}) collective-permute-start(bf16[4,32,4096]{2,1,0:T(8,128)(2,1)S(1)} %fusion.25), channel_id=1, source_target_pairs={{0,2},{1,5},{2,0},{3,7},{4,6},{5,1},{6,4},{7,3},{8,10},{9,13},{10,... | collective-permute-start | bytes 3145736 | tf_op jit(solution)/shard_map/ppermute | solution.py:325
  332.6 12.4 %collective-permute-start.29 = (bf16[1,128,1024]{2,1,0:T(8,128)(2,1)S(1)}, bf16[1,128,1024]{2,1,0:T(8,128)(2,1)S(1)}, u32[]{:S(2)}, u32[]{:S(2)}) collective-permute-start(bf16[1,128,1024]{2,1,0:T(8,128)(2,1)S(1)} %fusion.76), channel_id=1, source_target_pairs={{0,16},{1,17},{2,18},{3,19},{4,20},{5,21},{6,22},{7,23},{8,24},{9,... | collective-permute-start | bytes 786440 | tf_op jit(solution)/shard_map/ppermute | solution.py:325
  354.2 23.0 %collective-permute-start.32 = (bf16[16,32,4096]{2,1,0:T(8,128)(2,1)}, bf16[16,32,4096]{2,1,0:T(8,128)(2,1)}, u32[]{:S(2)}, u32[]{:S(2)}) collective-permute-start(bf16[16,32,4096]{2,1,0:T(8,128)(2,1)} %get-tuple-element.122), channel_id=1, source_target_pairs={{0,1},{1,0},{2,3},{3,2},{4,5},{5,4},{6,7},{7,6},{8,9},{9,8},{10,11... | collective-permute-start | bytes 12582920 | tf_op jit(solution)/shard_map/ppermute | solution.py:325
  362.8 14.4 %collective-permute-start.31 = (bf16[2,32,4096]{2,1,0:T(8,128)(2,1)S(1)}, bf16[2,32,4096]{2,1,0:T(8,128)(2,1)S(1)}, u32[]{:S(2)}, u32[]{:S(2)}) collective-permute-start(bf16[2,32,4096]{2,1,0:T(8,128)(2,1)S(1)} %fusion.49), channel_id=1, source_target_pairs={{0,8},{1,9},{2,10},{3,11},{4,12},{5,13},{6,14},{7,15},{8,0},{9,1},... | collective-permute-start | bytes 1572872 | tf_op jit(solution)/shard_map/ppermute | solution.py:325
  390.2 26.2 %collective-permute-start.34 = (bf16[2,4,32,4096]{3,2,1,0:T(8,128)(2,1)S(1)}, bf16[2,4,32,4096]{3,2,1,0:T(8,128)(2,1)}, u32[]{:S(2)}, u32[]{:S(2)}) collective-permute-start(bf16[2,4,32,4096]{3,2,1,0:T(8,128)(2,1)S(1)} %bitcast.431), channel_id=1, source_target_pairs={{0,4},{1,3},{2,6},{3,1},{4,0},{5,7},{6,2},{7,5},{8,12},{9,11},{10,... | collective-permute-start | bytes 6291464 | tf_op jit(solution)/shard_map/ppermute | solution.py:325
  395.0 18.2 %collective-permute-start.33 = (bf16[1,32,4096]{2,1,0:T(8,128)(2,1)}, bf16[1,32,4096]{2,1,0:T(8,128)(2,1)S(1)}, u32[]{:S(2)}, u32[]{:S(2)}) collective-permute-start(bf16[1,32,4096]{2,1,0:T(8,128)(2,1)} %fusion.73), channel_id=1, source_target_pairs={{0,16},{1,17},{2,18},{3,19},{4,20},{5,21},{6,22},{7,23},{8,24},{9,... | collective-permute-start | bytes 786440 | tf_op jit(solution)/shard_map/ppermute | solution.py:325
  421.2 14.9 %collective-permute-start.37 = (bf16[4,32,4096]{2,1,0:T(8,128)(2,1)S(1)}, bf16[4,32,4096]{2,1,0:T(8,128)(2,1)S(1)}, u32[]{:S(2)}, u32[]{:S(2)}) collective-permute-start(bf16[4,32,4096]{2,1,0:T(8,128)(2,1)S(1)} %fusion.24), channel_id=1, source_target_pairs={{0,2},{1,5},{2,0},{3,7},{4,6},{5,1},{6,4},{7,3},{8,10},{9,13},{10,... | collective-permute-start | bytes 3145736 | tf_op jit(solution)/shard_map/ppermute | solution.py:325
  456.3 15.3 %collective-permute-start.42 = (bf16[1,32,4096]{2,1,0:T(8,128)(2,1)S(1)}, bf16[1,32,4096]{2,1,0:T(8,128)(2,1)}, u32[]{:S(2)}, u32[]{:S(2)}) collective-permute-start(bf16[1,32,4096]{2,1,0:T(8,128)(2,1)S(1)} %fusion.70), channel_id=1, source_target_pairs={{0,16},{1,17},{2,18},{3,19},{4,20},{5,21},{6,22},{7,23},{8,24},{9,... | collective-permute-start | bytes 786440 | tf_op jit(solution)/shard_map/ppermute | solution.py:325
  (119 other events, 838.8 us)
Sparse Core Ops, SparseCore 0:
  11.5 135.3 all-gather.2
  149.8 127.0 all-gather.4

commit v7 on v6

--- a/solution.py
+++ b/solution.py
@@ -630,7 +630,7 @@
     yield total()
 
 
-HEAD_COLS = 4 * HEAD_DIM
+HEAD_COLS = 8 * HEAD_DIM
 
 
 def head_probs(query, key):

time: 531 us -> 530 us (level)
  transfers between devices with their start and end apart: 50 -> 50, of which waited for: 35 -> 36; matrix products, arithmetic and copies ran while one was open for 35% -> 35% of each run, Pallas kernels for 10% -> 9%
where the time goes in v7:
time: 530 us; the launch traced here: 522 us
  waiting for transfers between devices  174 us (33%)
  matrix products  101 us (19%)
  other arithmetic  79.6 us (15%)
  Pallas kernels  61.3 us (12%)
  starting transfers between devices  55.8 us (11%)
  local copies, waits for them, and re-layouts  33.4 us (6%)
  between operations  16.2 us (3%)
    ppermute x48, waiting for transfers between devices, move(): return lax.ppermute(values, AXIS, pairs)  174 us
    ppermute x48, starting transfers between devices, move(): return lax.ppermute(values, AXIS, pairs)  55.7 us
    dot_general x12, matrix products, dot_tail(): lax.dot_general(left, right, (((1,), (1,)), ((), ())), preferred_element_...  46.2 us
    dot_general x7, matrix products, matmul(): return jnp.dot(left, right, preferred_element_type=jnp.float32)  33.7 us
    dot_general x10, matrix products, dot_head(): lax.dot_general(left, right, (((0,), (0,)), ((), ())), preferred_element_...  20.7 us
    pallas_call x1, Pallas kernels, attend_back(): pl.pallas_call(attend_back_kernel, grid=(D // HEAD_COLS, count), out_shap...  18.9 us
    unnamed x191, local copies, waits for them, and re-layouts  17.6 us
    convert_element_type x6, other arithmetic, scatter_bulk(): passing = (yield [grid.ahead(here.astype(jnp.bfloat16), axis, 1)])[0]  16.9 us
  transfers between devices with their start and end apart: 50, of which 36 were waited for; matrix products, arithmetic and copies ran while one was open for 35% of the time, Pallas kernels for 9%

profile of v7, /device:TPU:0, one launch (start us, length us, event | category | flops | bytes accessed | tf_op | source)
XLA Modules:
  0.0 521.5 jit_solution(10824672966884098299)
XLA Ops:
  22.5 10.2 %collective-permute-done.3 = bf16[1,128,1024]{2,1,0:T(8,128)(2,1)S(1)} collective-permute-done((bf16[1,128,1024]{2,1,0:T(8,128)(2,1)S(1)}, bf16[1,128,1024]{2,1,0:T(8,128)(2,1)S(1)}, u32[]{:S(2)}, u32[]{:S(2)}) %collective-permute-start.3) | collective-permute-done | bytes 262176 | tf_op jit(solution)/shard_map/ppermute | solution.py:325
  48.4 5.0 collective-permute-start.8
  56.1 12.9 %collective-permute-done.8 = bf16[1,128,1024]{2,1,0:T(8,128)(2,1)S(1)} collective-permute-done((bf16[1,128,1024]{2,1,0:T(8,128)(2,1)S(1)}, bf16[1,128,1024]{2,1,0:T(8,128)(2,1)S(1)}, u32[]{:S(2)}, u32[]{:S(2)}) %collective-permute-start.8) | collective-permute-done | bytes 262176 | tf_op jit(solution)/shard_map/ppermute | solution.py:325
  73.6 5.4 %collective-permute-done.10 = f32[2,32,64]{2,1,0:T(8,128)S(1)} collective-permute-done((f32[2,32,64]{2,1,0:T(8,128)S(1)}, f32[2,32,64]{2,1,0:T(8,128)S(1)}, u32[]{:S(2)}, u32[]{:S(2)}) %collective-permute-start.10) | collective-permute-done | bytes 16416 | tf_op jit(solution)/shard_map/ppermute | solution.py:325
  92.0 13.3 %collective-permute-done.13 = bf16[1,128,1024]{2,1,0:T(8,128)(2,1)S(1)} collective-permute-done((bf16[1,128,1024]{2,1,0:T(8,128)(2,1)S(1)}, bf16[1,128,1024]{2,1,0:T(8,128)(2,1)S(1)}, u32[]{:S(2)}, u32[]{:S(2)}) %collective-permute-start.13) | collective-permute-done | bytes 262176 | tf_op jit(solution)/shard_map/ppermute | solution.py:325
  107.1 16.0 %collective-permute-done.14 = f32[1,2,8,10240]{3,2,1,0:T(8,128)S(1)} collective-permute-done((f32[1,2,8,10240]{3,2,1,0:T(8,128)S(1)}, f32[1,2,8,10240]{3,2,1,0:T(8,128)S(1)}, u32[]{:S(2)}, u32[]{:S(2)}) %collective-permute-start.14) | collective-permute-done | bytes 655392 | tf_op jit(solution)/shard_map/ppermute | solution.py:325
  156.8 7.3 %add_convert_fusion.query_ref.key_ref.value_ref = bf16[512,3072]{1,0:T(8,128)(2,1)S(1)} fusion(bf16[512,1024]{1,0:T(8,128)(2,1)S(1)} %fusion.31, bf16[1024,8192]{1,0:T(8,128)(2,1)} %all-gather.3.cloned.1.call-done, f32[3072]{0:T(1024)S(1)} %pad_maximum_fusion.21), kind=kOutput, calls=%fused_computation.20 | convolution fusion | flops 3224371200 | bytes 10498048 | tf_op jit(solution)/shard_map/dot_general | solution.py:37
  164.1 6.7 %shard_map.279 = bf16[512,1024]{1,0:T(8,128)(2,1)S(1)} custom-call(bf16[512,3072]{1,0:T(8,128)(2,1)S(1)} %add_convert_fusion.query_ref.key_ref.value_ref, bf16[512,3072]{1,0:T(8,128)(2,1)S(1)} %add_convert_fusion.query_ref.key_ref.value_ref, bf16[512,3072]{1,0:T(8,128)(2,1)S(1)} %add_convert_fusion.query_ref.key_ref.value_ref), custom_call_target="tpu_custom_call" | custom-call | flops 2147483648 | bytes 12582912 | tf_op jit(solution)/shard_map/pallas_call | solution.py:701
  170.8 10.7 %collective-permute-done.20.refs_1_ = bf16[8,128,1024]{2,1,0:T(8,128)(2,1)} collective-permute-done((bf16[8,128,1024]{2,1,0:T(8,128)(2,1)S(1)}, bf16[8,128,1024]{2,1,0:T(8,128)(2,1)}, u32[]{:S(2)}, u32[]{:S(2)}) %collective-permute-start.20) | collective-permute-done | bytes 2097184 | tf_op jit(solution)/shard_map/ppermute | solution.py:325
  190.0 13.8 %fusion.7 = (f32[512,4096]{1,0:T(8,128)}, bf16[512,4096]{1,0:T(8,128)(2,1)S(1)}) fusion(f32[4096]{0:T(1024)S(1)} %slice-done.3, bf16[512,1024]{1,0:T(8,128)(2,1)S(1)} %fusion.28, bf16[1024,8192]{1,0:T(8,128)(2,1)} %all-gather.3.cloned.1.call-done), kind=kOutput, calls=%fused_computation.9 | convolution fusion | flops 4336910336 | bytes 22036480 | tf_op jit(solution)/shard_map/dot_general | solution.py:37
  208.3 5.9 %fusion.148 = (f32[512]{0:T(512)S(1)}, f32[512,1024]{1,0:T(8,128)}, f32[512,1024]{1,0:T(8,128)S(1)}) fusion(f32[512,1024]{1,0:T(8,128)S(1)} %get-tuple-element.178, f32[2,1024]{1,0:T(2,128)S(1)} %get-tuple-element.222, f32[1024]{0:T(1024)S(1)} %copy-done.68, bf16[512,4096]{1,0:T(8,128)(2,1)S(1)} %get-tuple-element.97, bf16[4096,1024]{1,0:T(8,128)(2,1)S(1)} %bitcast.391), kind=kOutput, calls=%fused_computation.385 | convolution fusion | flops 4297063936 | bytes 18888704 | tf_op jit(solution)/shard_map/dot_general | solution.py:37
  226.2 6.7 %convolution_convert_fusion.1 = bf16[4096,1024]{1,0:T(8,128)(2,1)} fusion(bf16[512,4096]{1,0:T(8,128)(2,1)S(1)} %copy-done.28, bf16[512,1024]{1,0:T(8,128)(2,1)S(1)} %bitcast.441), kind=kOutput, calls=%fused_computation.12 | convolution fusion | flops 4299161600 | bytes 13631488 | tf_op jit(solution)/shard_map/dot_general | solution.py:47
  242.4 9.1 %fusion.152 = (f32[4096]{0:T(1024)S(1)}, bf16[512,4096]{1,0:T(8,128)(2,1)}) fusion(f32[512,4096]{1,0:T(8,128)} %get-tuple-element.101, bf16[512,1024]{1,0:T(8,128)(2,1)} %bitcast.442, bf16[4096,1024]{1,0:T(8,128)(2,1)S(1)} %bitcast.394), kind=kOutput, calls=%fused_computation.387 | convolution fusion | flops 4301254656 | bytes 22036480 | tf_op jit(solution)/shard_map/dot_general | solution.py:41
  266.3 8.3 %fusion.8 = f32[512,1024]{1,0:T(8,128)S(1)} fusion(bf16[512,4096]{1,0:T(8,128)(2,1)} %get-tuple-element.104, bf16[1024,8192]{1,0:T(8,128)(2,1)} %all-gather.3.cloned.1.call-done), kind=kOutput, calls=%fused_computation.13 | convolution fusion | flops 4294967296 | bytes 14680064 | tf_op jit(solution)/shard_map/dot_general | solution.py:41
  274.6 6.7 %collective-permute-done.24 = bf16[2,4,128,1024]{3,2,1,0:T(8,128)(2,1)} collective-permute-done((bf16[2,4,128,1024]{3,2,1,0:T(8,128)(2,1)S(1)}, bf16[2,4,128,1024]{3,2,1,0:T(8,128)(2,1)}, u32[]{:S(2)}, u32[]{:S(2)}) %collective-permute-start.24) | collective-permute-done | bytes 2097184 | tf_op jit(solution)/shard_map/ppermute | solution.py:325
  293.3 5.4 %collective-permute-done.25 = bf16[4,128,1024]{2,1,0:T(8,128)(2,1)S(1)} collective-permute-done((bf16[4,128,1024]{2,1,0:T(8,128)(2,1)S(1)}, bf16[4,128,1024]{2,1,0:T(8,128)(2,1)S(1)}, u32[]{:S(2)}, u32[]{:S(2)}) %collective-permute-start.25) | collective-permute-done | bytes 1048608 | tf_op jit(solution)/shard_map/ppermute | solution.py:325
  306.9 18.9 %shard_map.283 = (bf16[3,512,1024]{2,1,0:T(8,128)(2,1)S(1)}, f32[8,1024]{1,0:T(8,128)S(1)}) custom-call(bf16[512,3072]{1,0:T(8,128)(2,1)S(1)} %copy-done.2, bf16[512,3072]{1,0:T(8,128)(2,1)S(1)} %copy-done.2, bf16[512,3072]{1,0:T(8,128)(2,1)S(1)} %copy-done.2, bf16[512,1024]{1,0:T(8,128)(2,1)S(1)} %fusion.41.grad_ref), custom_call_target="tpu_custom_call" | custom-call | flops 4831838208 | bytes 25165824 | tf_op jit(solution)/shard_map/pallas_call | solution.py:718
  338.7 6.0 %collective-permute-done.29 = bf16[1,128,1024]{2,1,0:T(8,128)(2,1)S(1)} collective-permute-done((bf16[1,128,1024]{2,1,0:T(8,128)(2,1)S(1)}, bf16[1,128,1024]{2,1,0:T(8,128)(2,1)S(1)}, u32[]{:S(2)}, u32[]{:S(2)}) %collective-permute-start.29) | collective-permute-done | bytes 262176 | tf_op jit(solution)/shard_map/ppermute | solution.py:325
  345.0 6.9 %shard_map.284 = (bf16[16,32,4096]{2,1,0:T(8,128)(2,1)S(1)}, bf16[16,32,4096]{2,1,0:T(8,128)(2,1)}) custom-call(s32[32]{0:T(128)S(1)} %get-tuple-element.272.places, bf16[32,32,1024]{2,1,0:T(8,128)(2,1)S(1)} %bitcast.413, bf16[32,32,1024]{2,1,0:T(8,128)(2,1)S(1)} %bitcast.414, bf16[32,32,1024]{2,1,0:T(8,128)(2,1)S(1)} %bitcast.415, ...), custom_call_target="tpu_custom_call" | custom-call | bytes 16777216 | tf_op jit(solution)/shard_map/pallas_call | solution.py:579
  398.5 10.2 %fusion.106.refs_2_ = f32[2,1024]{1,0:T(2,128)S(1)} fusion(bf16[2,8192]{1,0:T(2,128)(2,1)} %shard_map.285.refs_0_, bf16[1024,9216]{1,0:T(8,128)(2,1)} %all-gather.5.cloned.1.call-done, f32[2,10240]{1,0:T(2,128)} %copy-done.46), kind=kOutput, calls=%fused_computation.260 | convolution fusion | flops 33572864 | bytes 16826368 | tf_op jit(solution)/shard_map/dot_general | solution.py:41
  429.9 6.2 %collective-permute-done.37 = bf16[4,32,4096]{2,1,0:T(8,128)(2,1)S(1)} collective-permute-done((bf16[4,32,4096]{2,1,0:T(8,128)(2,1)S(1)}, bf16[4,32,4096]{2,1,0:T(8,128)(2,1)S(1)}, u32[]{:S(2)}, u32[]{:S(2)}) %collective-permute-start.37) | collective-permute-done | bytes 1048608 | tf_op jit(solution)/shard_map/ppermute | solution.py:325
  457.9 13.3 %collective-permute-done.42 = bf16[1,32,4096]{2,1,0:T(8,128)(2,1)} collective-permute-done((bf16[1,32,4096]{2,1,0:T(8,128)(2,1)S(1)}, bf16[1,32,4096]{2,1,0:T(8,128)(2,1)}, u32[]{:S(2)}, u32[]{:S(2)}) %collective-permute-start.42) | collective-permute-done | bytes 262176 | tf_op jit(solution)/shard_map/ppermute | solution.py:325
  478.8 8.9 %shard_map.287 = (f32[32,17408]{1,0:T(8,128)}, f32[128,1024]{1,0:T(8,128)}, f32[32,1288]{1,0:T(8,128)}, f32[1,608]{1,0:T(1,128)}, f32[32,17408]{1,0:T(8,128)}, /...) custom-call(f32[32,17408]{1,0:T(8,128)} %refs_0_.3, ...), custom_call_target="tpu_custom_call" | custom-call | flops 51106880 | bytes 20442752 | tf_op jit(solution)/shard_map/pallas_call | solution.py:196
  506.3 5.5 %shard_map.288 = (f32[32,17408]{1,0:T(8,128)}, f32[128,1024]{1,0:T(8,128)}, f32[32,1288]{1,0:T(8,128)}, f32[1,608]{1,0:T(1,128)}, f32[8,128]{1,0:T(8,128)}) custom-call(f32[8,128]{1,0:T(8,128)} %copy-done.70, f32[32,17408]{1,0:T(8,128)} %refs_0_.3, f32[128,1024]{1,0:T(8,128)} %refs_1_.3, f32[32,1288]{1,0:T(8,128)} %refs_2_.3, ...), custom_call_target="tpu_custom_call" | custom-call | flops 21919040 | bytes 8767616 | tf_op jit(solution)/shard_map/pallas_call | solution.py:196
  (515 shorter events, 286.2 us)
Async XLA Ops:
  7.2 148.6 %all-gather.3.cloned.1.call-start = ((), (), s32[]{:S(2)}) async-start(), calls=%async_computation | async-start | bytes 17301504 | tf_op jit(solution)/shard_map/all_gather | solution.py:794
  10.1 388.4 %all-gather.5.cloned.1.call-start = ((), (), s32[]{:S(2)}) async-start(), calls=%async_computation.1 | async-start | bytes 19464192 | tf_op jit(solution)/shard_map/all_gather | solution.py:873
  18.8 13.9 %collective-permute-start.3 = (bf16[1,128,1024]{2,1,0:T(8,128)(2,1)S(1)}, bf16[1,128,1024]{2,1,0:T(8,128)(2,1)S(1)}, u32[]{:S(2)}, u32[]{:S(2)}) collective-permute-start(bf16[1,128,1024]{2,1,0:T(8,128)(2,1)S(1)} %get-tuple-element.193), channel_id=1, source_target_pairs={{0,24},{1,25},{2,26},{3,27},{4,28},{5,29},{6,30},{7,31},{8,0},{9,1... | collective-permute-start | bytes 786440 | tf_op jit(solution)/shard_map/ppermute | solution.py:325
  48.4 20.6 %collective-permute-start.8 = (bf16[1,128,1024]{2,1,0:T(8,128)(2,1)S(1)}, bf16[1,128,1024]{2,1,0:T(8,128)(2,1)S(1)}, u32[]{:S(2)}, u32[]{:S(2)}) collective-permute-start(bf16[1,128,1024]{2,1,0:T(8,128)(2,1)S(1)} %collective-permute-done.3), channel_id=1, source_target_pairs={{0,24},{1,25},{2,26},{3,27},{4,28},{5,29},{6,30},{7,31},{8,0},{9,1... | collective-permute-start | bytes 786440 | tf_op jit(solution)/shard_map/ppermute | solution.py:325
  85.3 20.0 %collective-permute-start.13 = (bf16[1,128,1024]{2,1,0:T(8,128)(2,1)S(1)}, bf16[1,128,1024]{2,1,0:T(8,128)(2,1)S(1)}, u32[]{:S(2)}, u32[]{:S(2)}) collective-permute-start(bf16[1,128,1024]{2,1,0:T(8,128)(2,1)S(1)} %copy-done.51), channel_id=1, source_target_pairs={{0,24},{1,25},{2,26},{3,27},{4,28},{5,29},{6,30},{7,31},{8,0},{9,1... | collective-permute-start | bytes 786440 | tf_op jit(solution)/shard_map/ppermute | solution.py:325
  105.3 17.7 %collective-permute-start.14 = (f32[1,2,8,10240]{3,2,1,0:T(8,128)S(1)}, f32[1,2,8,10240]{3,2,1,0:T(8,128)S(1)}, u32[]{:S(2)}, u32[]{:S(2)}) collective-permute-start(f32[1,2,8,10240]{3,2,1,0:T(8,128)S(1)} %constant_dynamic-slice_fusion), channel_id=1, source_target_pairs={{0,2},{1,5},{2,0},{3,7},{4,6},{5,1},{6,4},{7,3},{8,10},{9,13},{10,... | collective-permute-start | bytes 1966088 | tf_op jit(solution)/shard_map/ppermute | solution.py:325
  128.1 17.7 %collective-permute-start.19 = (bf16[4,128,1024]{2,1,0:T(8,128)(2,1)}, bf16[4,128,1024]{2,1,0:T(8,128)(2,1)}, u32[]{:S(2)}, u32[]{:S(2)}) collective-permute-start(bf16[4,128,1024]{2,1,0:T(8,128)(2,1)} %get-tuple-element.189), channel_id=1, source_target_pairs={{0,2},{1,5},{2,0},{3,7},{4,6},{5,1},{6,4},{7,3},{8,10},{9,13},{10,... | collective-permute-start | bytes 3145736 | tf_op jit(solution)/shard_map/ppermute | solution.py:325
  135.1 10.6 %collective-permute-start.17 = (f32[160,128]{1,0:T(8,128)S(1)}, f32[160,128]{1,0:T(8,128)S(1)}, u32[]{:S(2)}, u32[]{:S(2)}) collective-permute-start(f32[160,128]{1,0:T(8,128)S(1)} %get-tuple-element.198), channel_id=1, source_target_pairs={{0,16},{1,17},{2,18},{3,19},{4,20},{5,21},{6,22},{7,23},{8,24},{9,... | collective-permute-start | bytes 245768 | tf_op jit(solution)/shard_map/ppermute | solution.py:325
  151.1 30.4 %collective-permute-start.20 = (bf16[8,128,1024]{2,1,0:T(8,128)(2,1)S(1)}, bf16[8,128,1024]{2,1,0:T(8,128)(2,1)}, u32[]{:S(2)}, u32[]{:S(2)}) collective-permute-start(bf16[8,128,1024]{2,1,0:T(8,128)(2,1)S(1)} %bitcast.395), channel_id=1, source_target_pairs={{0,4},{1,3},{2,6},{3,1},{4,0},{5,7},{6,2},{7,5},{8,12},{9,11},{10,... | collective-permute-start | bytes 6291464 | tf_op jit(solution)/shard_map/ppermute | solution.py:325
  155.1 34.8 %collective-permute-start.21 = (bf16[8,128,1024]{2,1,0:T(8,128)(2,1)S(1)}, bf16[8,128,1024]{2,1,0:T(8,128)(2,1)}, u32[]{:S(2)}, u32[]{:S(2)}) collective-permute-start(bf16[8,128,1024]{2,1,0:T(8,128)(2,1)S(1)} %bitcast.396), channel_id=1, source_target_pairs={{0,1},{1,0},{2,3},{3,2},{4,5},{5,4},{6,7},{7,6},{8,9},{9,8},{10,11... | collective-permute-start | bytes 6291464 | tf_op jit(solution)/shard_map/ppermute | solution.py:325
  241.8 9.7 %collective-permute-start.23 = (bf16[16,128,1024]{2,1,0:T(8,128)(2,1)}, bf16[16,128,1024]{2,1,0:T(8,128)(2,1)}, u32[]{:S(2)}, u32[]{:S(2)}) collective-permute-start(bf16[16,128,1024]{2,1,0:T(8,128)(2,1)} %get-tuple-element.102), channel_id=1, source_target_pairs={{0,1},{1,0},{2,3},{3,2},{4,5},{5,4},{6,7},{7,6},{8,9},{9,8},{10,11... | collective-permute-start | bytes 12582920 | tf_op jit(solution)/shard_map/ppermute | solution.py:325
  255.0 26.2 %collective-permute-start.24 = (bf16[2,4,128,1024]{3,2,1,0:T(8,128)(2,1)S(1)}, bf16[2,4,128,1024]{3,2,1,0:T(8,128)(2,1)}, u32[]{:S(2)}, u32[]{:S(2)}) collective-permute-start(bf16[2,4,128,1024]{3,2,1,0:T(8,128)(2,1)S(1)} %bitcast.432), channel_id=1, source_target_pairs={{0,4},{1,3},{2,6},{3,1},{4,0},{5,7},{6,2},{7,5},{8,12},{9,11},{10,... | collective-permute-start | bytes 6291464 | tf_op jit(solution)/shard_map/ppermute | solution.py:325
  266.1 32.6 %collective-permute-start.26 = (bf16[16,32,4096]{2,1,0:T(8,128)(2,1)}, bf16[16,32,4096]{2,1,0:T(8,128)(2,1)}, u32[]{:S(2)}, u32[]{:S(2)}) collective-permute-start(bf16[16,32,4096]{2,1,0:T(8,128)(2,1)} %get-tuple-element.109), channel_id=1, source_target_pairs={{0,1},{1,0},{2,3},{3,2},{4,5},{5,4},{6,7},{7,6},{8,9},{9,8},{10,11... | collective-permute-start | bytes 12582920 | tf_op jit(solution)/shard_map/ppermute | solution.py:325
  283.9 14.9 %collective-permute-start.25 = (bf16[4,128,1024]{2,1,0:T(8,128)(2,1)S(1)}, bf16[4,128,1024]{2,1,0:T(8,128)(2,1)S(1)}, u32[]{:S(2)}, u32[]{:S(2)}) collective-permute-start(bf16[4,128,1024]{2,1,0:T(8,128)(2,1)S(1)} %fusion.26), channel_id=1, source_target_pairs={{0,2},{1,5},{2,0},{3,7},{4,6},{5,1},{6,4},{7,3},{8,10},{9,13},{10,... | collective-permute-start | bytes 3145736 | tf_op jit(solution)/shard_map/ppermute | solution.py:325
  301.5 26.1 %collective-permute-start.28 = (bf16[2,4,32,4096]{3,2,1,0:T(8,128)(2,1)S(1)}, bf16[2,4,32,4096]{3,2,1,0:T(8,128)(2,1)S(1)}, u32[]{:S(2)}, u32[]{:S(2)}) collective-permute-start(bf16[2,4,32,4096]{3,2,1,0:T(8,128)(2,1)S(1)} %bitcast.433), channel_id=1, source_target_pairs={{0,4},{1,3},{2,6},{3,1},{4,0},{5,7},{6,2},{7,5},{8,12},{9,11},{10,... | collective-permute-start | bytes 6291464 | tf_op jit(solution)/shard_map/ppermute | solution.py:325
  303.4 22.5 %collective-permute-start.27 = (bf16[2,128,1024]{2,1,0:T(8,128)(2,1)S(1)}, bf16[2,128,1024]{2,1,0:T(8,128)(2,1)S(1)}, u32[]{:S(2)}, u32[]{:S(2)}) collective-permute-start(bf16[2,128,1024]{2,1,0:T(8,128)(2,1)S(1)} %fusion.51), channel_id=1, source_target_pairs={{0,8},{1,9},{2,10},{3,11},{4,12},{5,13},{6,14},{7,15},{8,0},{9,1},... | collective-permute-start | bytes 1572872 | tf_op jit(solution)/shard_map/ppermute | solution.py:325
  330.1 14.9 %collective-permute-start.30 = (bf16[4,32,4096]{2,1,0:T(8,128)(2,1)S(1)}, bf16[4,32,4096]{2,1,0:T(8,128)(2,1)S(1)}, u32[]{:S(2)}, u32[]{:S(2)}) collective-permute-start(bf16[4,32,4096]{2,1,0:T(8,128)(2,1)S(1)} %fusion.25), channel_id=1, source_target_pairs={{0,2},{1,5},{2,0},{3,7},{4,6},{5,1},{6,4},{7,3},{8,10},{9,13},{10,... | collective-permute-start | bytes 3145736 | tf_op jit(solution)/shard_map/ppermute | solution.py:325
  332.4 12.4 %collective-permute-start.29 = (bf16[1,128,1024]{2,1,0:T(8,128)(2,1)S(1)}, bf16[1,128,1024]{2,1,0:T(8,128)(2,1)S(1)}, u32[]{:S(2)}, u32[]{:S(2)}) collective-permute-start(bf16[1,128,1024]{2,1,0:T(8,128)(2,1)S(1)} %fusion.76), channel_id=1, source_target_pairs={{0,16},{1,17},{2,18},{3,19},{4,20},{5,21},{6,22},{7,23},{8,24},{9,... | collective-permute-start | bytes 786440 | tf_op jit(solution)/shard_map/ppermute | solution.py:325
  353.9 23.0 %collective-permute-start.32 = (bf16[16,32,4096]{2,1,0:T(8,128)(2,1)}, bf16[16,32,4096]{2,1,0:T(8,128)(2,1)}, u32[]{:S(2)}, u32[]{:S(2)}) collective-permute-start(bf16[16,32,4096]{2,1,0:T(8,128)(2,1)} %get-tuple-element.122), channel_id=1, source_target_pairs={{0,1},{1,0},{2,3},{3,2},{4,5},{5,4},{6,7},{7,6},{8,9},{9,8},{10,11... | collective-permute-start | bytes 12582920 | tf_op jit(solution)/shard_map/ppermute | solution.py:325
  362.5 14.4 %collective-permute-start.31 = (bf16[2,32,4096]{2,1,0:T(8,128)(2,1)S(1)}, bf16[2,32,4096]{2,1,0:T(8,128)(2,1)S(1)}, u32[]{:S(2)}, u32[]{:S(2)}) collective-permute-start(bf16[2,32,4096]{2,1,0:T(8,128)(2,1)S(1)} %fusion.49), channel_id=1, source_target_pairs={{0,8},{1,9},{2,10},{3,11},{4,12},{5,13},{6,14},{7,15},{8,0},{9,1},... | collective-permute-start | bytes 1572872 | tf_op jit(solution)/shard_map/ppermute | solution.py:325
  390.0 26.2 %collective-permute-start.34 = (bf16[2,4,32,4096]{3,2,1,0:T(8,128)(2,1)S(1)}, bf16[2,4,32,4096]{3,2,1,0:T(8,128)(2,1)}, u32[]{:S(2)}, u32[]{:S(2)}) collective-permute-start(bf16[2,4,32,4096]{3,2,1,0:T(8,128)(2,1)S(1)} %bitcast.431), channel_id=1, source_target_pairs={{0,4},{1,3},{2,6},{3,1},{4,0},{5,7},{6,2},{7,5},{8,12},{9,11},{10,... | collective-permute-start | bytes 6291464 | tf_op jit(solution)/shard_map/ppermute | solution.py:325
  394.1 18.9 %collective-permute-start.33 = (bf16[1,32,4096]{2,1,0:T(8,128)(2,1)}, bf16[1,32,4096]{2,1,0:T(8,128)(2,1)S(1)}, u32[]{:S(2)}, u32[]{:S(2)}) collective-permute-start(bf16[1,32,4096]{2,1,0:T(8,128)(2,1)} %fusion.73), channel_id=1, source_target_pairs={{0,16},{1,17},{2,18},{3,19},{4,20},{5,21},{6,22},{7,23},{8,24},{9,... | collective-permute-start | bytes 786440 | tf_op jit(solution)/shard_map/ppermute | solution.py:325
  421.3 14.9 %collective-permute-start.37 = (bf16[4,32,4096]{2,1,0:T(8,128)(2,1)S(1)}, bf16[4,32,4096]{2,1,0:T(8,128)(2,1)S(1)}, u32[]{:S(2)}, u32[]{:S(2)}) collective-permute-start(bf16[4,32,4096]{2,1,0:T(8,128)(2,1)S(1)} %fusion.24), channel_id=1, source_target_pairs={{0,2},{1,5},{2,0},{3,7},{4,6},{5,1},{6,4},{7,3},{8,10},{9,13},{10,... | collective-permute-start | bytes 3145736 | tf_op jit(solution)/shard_map/ppermute | solution.py:325
  456.2 15.0 %collective-permute-start.42 = (bf16[1,32,4096]{2,1,0:T(8,128)(2,1)S(1)}, bf16[1,32,4096]{2,1,0:T(8,128)(2,1)}, u32[]{:S(2)}, u32[]{:S(2)}) collective-permute-start(bf16[1,32,4096]{2,1,0:T(8,128)(2,1)S(1)} %fusion.70), channel_id=1, source_target_pairs={{0,16},{1,17},{2,18},{3,19},{4,20},{5,21},{6,22},{7,23},{8,24},{9,... | collective-permute-start | bytes 786440 | tf_op jit(solution)/shard_map/ppermute | solution.py:325
  (119 other events, 828.6 us)
Sparse Core Ops, SparseCore 0:
  11.5 135.6 all-gather.2
  150.1 126.7 all-gather.4

commit v8 on v7

--- a/solution.py
+++ b/solution.py
@@ -353,14 +353,15 @@
     return values
 
 
-def scatter_axis(grid, values, axis, dim):
+def scatter_axis(grid, values, axis, dim, kind=jnp.float32):
     bit = grid.sizes[axis]
     while bit > 1:
         bit //= 2
         upper = grid.coords[axis] // bit % 2
         kept = lax.dynamic_slice_in_dim(values, upper * bit, bit, dim)
         sent = lax.dynamic_slice_in_dim(values, (1 - upper) * bit, bit, dim)
-        values = kept + grid.flip(sent, axis, bit)
+        sent = grid.flip(sent.astype(kind), axis, bit)
+        values = kept + sent.astype(jnp.float32)
     return lax.squeeze(values, (dim,))
 
 
@@ -843,7 +844,7 @@
     )
     mods = mods.reshape(sizes[CORE], sizes[X_AXIS], sizes[Y_AXIS], sizes[Z_AXIS] * count, 10 * D)
     mods = meet(scatter_axis(grid, mods, CORE, 0), get)
-    mods = scatter_axis(grid, mods, MIX_P, 0)
+    mods = scatter_axis(grid, mods, MIX_P, 0, bf16)
     mods = scatter_axis(grid, mods, MIX_Q, 0)
     mods = mods.reshape(sizes[Z_AXIS], count * 10 * D // 128, 128)
     total = lax.dynamic_index_in_dim(mods, grid.coords[Z_AXIS], 0, keepdims=False)

time: 530 us -> 529 us (level)
  waiting for transfers between devices: 174 us -> 168 us
  starting transfers between devices: 55.8 us -> 61.2 us
    ppermute x48, waiting for transfers between devices: 174 us -> 168 us  [move(): return lax.ppermute(values, AXIS, pairs)]
    ppermute x48, starting transfers between devices: 55.7 us -> 61.2 us  [move(): return lax.ppermute(values, AXIS, pairs)]
  transfers between devices with their start and end apart: 50 -> 50, of which waited for: 36 -> 34; matrix products, arithmetic and copies ran while one was open for 35% -> 35% of each run, Pallas kernels for 9% -> 9%
where the time goes in v8:
time: 529 us; the launch traced here: 520 us
  waiting for transfers between devices  168 us (32%)
  matrix products  102 us (19%)
  other arithmetic  79.1 us (15%)
  Pallas kernels  61.3 us (12%)
  starting transfers between devices  61.2 us (12%)
  local copies, waits for them, and re-layouts  32.8 us (6%)
  between operations  16.2 us (3%)
    ppermute x48, waiting for transfers between devices, move(): return lax.ppermute(values, AXIS, pairs)  168 us
    ppermute x48, starting transfers between devices, move(): return lax.ppermute(values, AXIS, pairs)  61.2 us
    dot_general x12, matrix products, dot_tail(): lax.dot_general(left, right, (((1,), (1,)), ((), ())), preferred_element_...  46.5 us
    dot_general x7, matrix products, matmul(): return jnp.dot(left, right, preferred_element_type=jnp.float32)  34.2 us
    dot_general x10, matrix products, dot_head(): lax.dot_general(left, right, (((0,), (0,)), ((), ())), preferred_element_...  20.7 us
    pallas_call x1, Pallas kernels, attend_back(): pl.pallas_call(attend_back_kernel, grid=(D // HEAD_COLS, count), out_shap...  18.9 us
    unnamed x191, local copies, waits for them, and re-layouts  17 us
    convert_element_type x6, other arithmetic, scatter_bulk(): passing = (yield [grid.ahead(here.astype(jnp.bfloat16), axis, 1)])[0]  16.9 us
  transfers between devices with their start and end apart: 50, of which 34 were waited for; matrix products, arithmetic and copies ran while one was open for 35% of the time, Pallas kernels for 9%

profile of v8, /device:TPU:0, one launch (start us, length us, event | category | flops | bytes accessed | tf_op | source)
XLA Modules:
  0.0 520.4 jit_solution(12265910308802341806)
XLA Ops:
  22.5 10.2 %collective-permute-done.3 = bf16[1,128,1024]{2,1,0:T(8,128)(2,1)S(1)} collective-permute-done((bf16[1,128,1024]{2,1,0:T(8,128)(2,1)S(1)}, bf16[1,128,1024]{2,1,0:T(8,128)(2,1)S(1)}, u32[]{:S(2)}, u32[]{:S(2)}) %collective-permute-start.3) | collective-permute-done | bytes 262176 | tf_op jit(solution)/shard_map/ppermute | solution.py:325
  48.4 5.0 collective-permute-start.8
  56.1 12.9 %collective-permute-done.8 = bf16[1,128,1024]{2,1,0:T(8,128)(2,1)S(1)} collective-permute-done((bf16[1,128,1024]{2,1,0:T(8,128)(2,1)S(1)}, bf16[1,128,1024]{2,1,0:T(8,128)(2,1)S(1)}, u32[]{:S(2)}, u32[]{:S(2)}) %collective-permute-start.8) | collective-permute-done | bytes 262176 | tf_op jit(solution)/shard_map/ppermute | solution.py:325
  73.6 5.4 %collective-permute-done.10 = f32[2,32,64]{2,1,0:T(8,128)S(1)} collective-permute-done((f32[2,32,64]{2,1,0:T(8,128)S(1)}, f32[2,32,64]{2,1,0:T(8,128)S(1)}, u32[]{:S(2)}, u32[]{:S(2)}) %collective-permute-start.10) | collective-permute-done | bytes 16416 | tf_op jit(solution)/shard_map/ppermute | solution.py:325
  92.0 13.3 %collective-permute-done.13 = bf16[1,128,1024]{2,1,0:T(8,128)(2,1)S(1)} collective-permute-done((bf16[1,128,1024]{2,1,0:T(8,128)(2,1)S(1)}, bf16[1,128,1024]{2,1,0:T(8,128)(2,1)S(1)}, u32[]{:S(2)}, u32[]{:S(2)}) %collective-permute-start.13) | collective-permute-done | bytes 262176 | tf_op jit(solution)/shard_map/ppermute | solution.py:325
  107.1 12.3 %collective-permute-done.14 = bf16[1,2,8,10240]{3,2,1,0:T(8,128)(2,1)S(1)} collective-permute-done((bf16[1,2,8,10240]{3,2,1,0:T(8,128)(2,1)S(1)}, bf16[1,2,8,10240]{3,2,1,0:T(8,128)(2,1)S(1)}, u32[]{:S(2)}, u32[]{:S(2)}) %collective-permute-start.14) | collective-permute-done | bytes 327712 | tf_op jit(solution)/shard_map/ppermute | solution.py:325
  155.5 7.3 %add_convert_fusion.query_ref.key_ref.value_ref = bf16[512,3072]{1,0:T(8,128)(2,1)S(1)} fusion(bf16[512,1024]{1,0:T(8,128)(2,1)S(1)} %fusion.31, bf16[1024,8192]{1,0:T(8,128)(2,1)} %all-gather.3.cloned.1.call-done, f32[3072]{0:T(1024)S(1)} %pad_maximum_fusion.21), kind=kOutput, calls=%fused_computation.20 | convolution fusion | flops 3224371200 | bytes 10498048 | tf_op jit(solution)/shard_map/dot_general | solution.py:37
  162.8 6.7 %shard_map.279 = bf16[512,1024]{1,0:T(8,128)(2,1)S(1)} custom-call(bf16[512,3072]{1,0:T(8,128)(2,1)S(1)} %add_convert_fusion.query_ref.key_ref.value_ref, bf16[512,3072]{1,0:T(8,128)(2,1)S(1)} %add_convert_fusion.query_ref.key_ref.value_ref, bf16[512,3072]{1,0:T(8,128)(2,1)S(1)} %add_convert_fusion.query_ref.key_ref.value_ref), custom_call_target="tpu_custom_call" | custom-call | flops 2147483648 | bytes 12582912 | tf_op jit(solution)/shard_map/pallas_call | solution.py:702
  169.5 9.0 %collective-permute-done.20.refs_1_ = bf16[8,128,1024]{2,1,0:T(8,128)(2,1)} collective-permute-done((bf16[8,128,1024]{2,1,0:T(8,128)(2,1)S(1)}, bf16[8,128,1024]{2,1,0:T(8,128)(2,1)}, u32[]{:S(2)}, u32[]{:S(2)}) %collective-permute-start.20) | collective-permute-done | bytes 2097184 | tf_op jit(solution)/shard_map/ppermute | solution.py:325
  187.4 13.8 %fusion.7 = (f32[512,4096]{1,0:T(8,128)}, bf16[512,4096]{1,0:T(8,128)(2,1)S(1)}) fusion(f32[4096]{0:T(1024)S(1)} %slice-done.3, bf16[512,1024]{1,0:T(8,128)(2,1)S(1)} %fusion.28, bf16[1024,8192]{1,0:T(8,128)(2,1)} %all-gather.3.cloned.1.call-done), kind=kOutput, calls=%fused_computation.9 | convolution fusion | flops 4336910336 | bytes 22036480 | tf_op jit(solution)/shard_map/dot_general | solution.py:37
  205.7 5.9 %fusion.148 = (f32[512]{0:T(512)S(1)}, f32[512,1024]{1,0:T(8,128)}, f32[512,1024]{1,0:T(8,128)S(1)}) fusion(f32[512,1024]{1,0:T(8,128)S(1)} %get-tuple-element.178, f32[2,1024]{1,0:T(2,128)S(1)} %get-tuple-element.222, f32[1024]{0:T(1024)S(1)} %copy-done.68, bf16[512,4096]{1,0:T(8,128)(2,1)S(1)} %get-tuple-element.97, bf16[4096,1024]{1,0:T(8,128)(2,1)S(1)} %bitcast.391), kind=kOutput, calls=%fused_computation.385 | convolution fusion | flops 4297063936 | bytes 18888704 | tf_op jit(solution)/shard_map/dot_general | solution.py:37
  223.2 6.7 %convolution_convert_fusion.1 = bf16[4096,1024]{1,0:T(8,128)(2,1)} fusion(bf16[512,4096]{1,0:T(8,128)(2,1)S(1)} %copy-done.27, bf16[512,1024]{1,0:T(8,128)(2,1)S(1)} %bitcast.441), kind=kOutput, calls=%fused_computation.12 | convolution fusion | flops 4299161600 | bytes 13631488 | tf_op jit(solution)/shard_map/dot_general | solution.py:47
  239.4 9.1 %fusion.152 = (f32[4096]{0:T(1024)S(1)}, bf16[512,4096]{1,0:T(8,128)(2,1)}) fusion(f32[512,4096]{1,0:T(8,128)} %get-tuple-element.101, bf16[512,1024]{1,0:T(8,128)(2,1)} %bitcast.442, bf16[4096,1024]{1,0:T(8,128)(2,1)S(1)} %bitcast.394), kind=kOutput, calls=%fused_computation.387 | convolution fusion | flops 4301254656 | bytes 22036480 | tf_op jit(solution)/shard_map/dot_general | solution.py:41
  264.2 8.5 %fusion.8 = f32[512,1024]{1,0:T(8,128)S(1)} fusion(bf16[512,4096]{1,0:T(8,128)(2,1)} %get-tuple-element.104, bf16[1024,8192]{1,0:T(8,128)(2,1)} %all-gather.3.cloned.1.call-done), kind=kOutput, calls=%fused_computation.13 | convolution fusion | flops 4294967296 | bytes 14680064 | tf_op jit(solution)/shard_map/dot_general | solution.py:41
  272.7 5.4 %collective-permute-done.24 = bf16[2,4,128,1024]{3,2,1,0:T(8,128)(2,1)} collective-permute-done((bf16[2,4,128,1024]{3,2,1,0:T(8,128)(2,1)S(1)}, bf16[2,4,128,1024]{3,2,1,0:T(8,128)(2,1)}, u32[]{:S(2)}, u32[]{:S(2)}) %collective-permute-start.24) | collective-permute-done | bytes 2097184 | tf_op jit(solution)/shard_map/ppermute | solution.py:325
  306.1 18.9 %shard_map.283 = (bf16[3,512,1024]{2,1,0:T(8,128)(2,1)S(1)}, f32[8,1024]{1,0:T(8,128)S(1)}) custom-call(bf16[512,3072]{1,0:T(8,128)(2,1)S(1)} %copy-done.2, bf16[512,3072]{1,0:T(8,128)(2,1)S(1)} %copy-done.2, bf16[512,3072]{1,0:T(8,128)(2,1)S(1)} %copy-done.2, bf16[512,1024]{1,0:T(8,128)(2,1)S(1)} %fusion.41.grad_ref), custom_call_target="tpu_custom_call" | custom-call | flops 4831838208 | bytes 25165824 | tf_op jit(solution)/shard_map/pallas_call | solution.py:719
  335.8 7.4 %collective-permute-done.29 = bf16[1,128,1024]{2,1,0:T(8,128)(2,1)S(1)} collective-permute-done((bf16[1,128,1024]{2,1,0:T(8,128)(2,1)S(1)}, bf16[1,128,1024]{2,1,0:T(8,128)(2,1)S(1)}, u32[]{:S(2)}, u32[]{:S(2)}) %collective-permute-start.29) | collective-permute-done | bytes 262176 | tf_op jit(solution)/shard_map/ppermute | solution.py:325
  343.2 6.9 %shard_map.284 = (bf16[16,32,4096]{2,1,0:T(8,128)(2,1)S(1)}, bf16[16,32,4096]{2,1,0:T(8,128)(2,1)}) custom-call(s32[32]{0:T(128)S(1)} %get-tuple-element.272.places, bf16[32,32,1024]{2,1,0:T(8,128)(2,1)S(1)} %bitcast.413, bf16[32,32,1024]{2,1,0:T(8,128)(2,1)S(1)} %bitcast.414, bf16[32,32,1024]{2,1,0:T(8,128)(2,1)S(1)} %bitcast.415, ...), custom_call_target="tpu_custom_call" | custom-call | bytes 16777216 | tf_op jit(solution)/shard_map/pallas_call | solution.py:580
  396.0 10.2 %fusion.106.refs_2_ = f32[2,1024]{1,0:T(2,128)S(1)} fusion(bf16[2,8192]{1,0:T(2,128)(2,1)} %shard_map.285.refs_0_, bf16[1024,9216]{1,0:T(8,128)(2,1)} %all-gather.5.cloned.1.call-done, f32[2,10240]{1,0:T(2,128)} %copy-done.46), kind=kOutput, calls=%fused_computation.261 | convolution fusion | flops 33572864 | bytes 16826368 | tf_op jit(solution)/shard_map/dot_general | solution.py:41
  427.8 6.3 %collective-permute-done.37 = bf16[4,32,4096]{2,1,0:T(8,128)(2,1)S(1)} collective-permute-done((bf16[4,32,4096]{2,1,0:T(8,128)(2,1)S(1)}, bf16[4,32,4096]{2,1,0:T(8,128)(2,1)S(1)}, u32[]{:S(2)}, u32[]{:S(2)}) %collective-permute-start.37) | collective-permute-done | bytes 1048608 | tf_op jit(solution)/shard_map/ppermute | solution.py:325
  447.8 5.5 %collective-permute-done.40 = bf16[2,32,4096]{2,1,0:T(8,128)(2,1)S(1)} collective-permute-done((bf16[2,32,4096]{2,1,0:T(8,128)(2,1)S(1)}, bf16[2,32,4096]{2,1,0:T(8,128)(2,1)S(1)}, u32[]{:S(2)}, u32[]{:S(2)}) %collective-permute-start.40) | collective-permute-done | bytes 524320 | tf_op jit(solution)/shard_map/ppermute | solution.py:325
  456.7 13.4 %collective-permute-done.42 = bf16[1,32,4096]{2,1,0:T(8,128)(2,1)} collective-permute-done((bf16[1,32,4096]{2,1,0:T(8,128)(2,1)S(1)}, bf16[1,32,4096]{2,1,0:T(8,128)(2,1)}, u32[]{:S(2)}, u32[]{:S(2)}) %collective-permute-start.42) | collective-permute-done | bytes 262176 | tf_op jit(solution)/shard_map/ppermute | solution.py:325
  477.7 8.9 %shard_map.287 = (f32[32,17408]{1,0:T(8,128)}, f32[128,1024]{1,0:T(8,128)}, f32[32,1288]{1,0:T(8,128)}, f32[1,608]{1,0:T(1,128)}, f32[32,17408]{1,0:T(8,128)}, /...) custom-call(f32[32,17408]{1,0:T(8,128)} %refs_0_.3, ...), custom_call_target="tpu_custom_call" | custom-call | flops 51106880 | bytes 20442752 | tf_op jit(solution)/shard_map/pallas_call | solution.py:196
  505.2 5.5 %shard_map.288 = (f32[32,17408]{1,0:T(8,128)}, f32[128,1024]{1,0:T(8,128)}, f32[32,1288]{1,0:T(8,128)}, f32[1,608]{1,0:T(1,128)}, f32[8,128]{1,0:T(8,128)}) custom-call(f32[8,128]{1,0:T(8,128)} %copy-done.70, f32[32,17408]{1,0:T(8,128)} %refs_0_.3, f32[128,1024]{1,0:T(8,128)} %refs_1_.3, f32[32,1288]{1,0:T(8,128)} %refs_2_.3, ...), custom_call_target="tpu_custom_call" | custom-call | flops 21919040 | bytes 8767616 | tf_op jit(solution)/shard_map/pallas_call | solution.py:196
  (515 shorter events, 289.8 us)
Async XLA Ops:
  7.2 147.3 %all-gather.3.cloned.1.call-start = ((), (), s32[]{:S(2)}) async-start(), calls=%async_computation | async-start | bytes 17301504 | tf_op jit(solution)/shard_map/all_gather | solution.py:795
  10.1 386.0 %all-gather.5.cloned.1.call-start = ((), (), s32[]{:S(2)}) async-start(), calls=%async_computation.1 | async-start | bytes 19464192 | tf_op jit(solution)/shard_map/all_gather | solution.py:874
  18.8 13.9 %collective-permute-start.3 = (bf16[1,128,1024]{2,1,0:T(8,128)(2,1)S(1)}, bf16[1,128,1024]{2,1,0:T(8,128)(2,1)S(1)}, u32[]{:S(2)}, u32[]{:S(2)}) collective-permute-start(bf16[1,128,1024]{2,1,0:T(8,128)(2,1)S(1)} %get-tuple-element.193), channel_id=1, source_target_pairs={{0,24},{1,25},{2,26},{3,27},{4,28},{5,29},{6,30},{7,31},{8,0},{9,1... | collective-permute-start | bytes 786440 | tf_op jit(solution)/shard_map/ppermute | solution.py:325
  48.4 20.6 %collective-permute-start.8 = (bf16[1,128,1024]{2,1,0:T(8,128)(2,1)S(1)}, bf16[1,128,1024]{2,1,0:T(8,128)(2,1)S(1)}, u32[]{:S(2)}, u32[]{:S(2)}) collective-permute-start(bf16[1,128,1024]{2,1,0:T(8,128)(2,1)S(1)} %collective-permute-done.3), channel_id=1, source_target_pairs={{0,24},{1,25},{2,26},{3,27},{4,28},{5,29},{6,30},{7,31},{8,0},{9,1... | collective-permute-start | bytes 786440 | tf_op jit(solution)/shard_map/ppermute | solution.py:325
  85.3 20.0 %collective-permute-start.13 = (bf16[1,128,1024]{2,1,0:T(8,128)(2,1)S(1)}, bf16[1,128,1024]{2,1,0:T(8,128)(2,1)S(1)}, u32[]{:S(2)}, u32[]{:S(2)}) collective-permute-start(bf16[1,128,1024]{2,1,0:T(8,128)(2,1)S(1)} %copy-done.51), channel_id=1, source_target_pairs={{0,24},{1,25},{2,26},{3,27},{4,28},{5,29},{6,30},{7,31},{8,0},{9,1... | collective-permute-start | bytes 786440 | tf_op jit(solution)/shard_map/ppermute | solution.py:325
  105.3 14.0 %collective-permute-start.14 = (bf16[1,2,8,10240]{3,2,1,0:T(8,128)(2,1)S(1)}, bf16[1,2,8,10240]{3,2,1,0:T(8,128)(2,1)S(1)}, u32[]{:S(2)}, u32[]{:S(2)}) collective-permute-start(bf16[1,2,8,10240]{3,2,1,0:T(8,128)(2,1)S(1)} %dynamic-slice_convert_fusion), channel_id=1, source_target_pairs={{0,2},{1,5},{2,0},{3,7},{4,6},{5,1},{6,4},{7,3},{8,10},{9,13},{10,... | collective-permute-start | bytes 983048 | tf_op jit(solution)/shard_map/ppermute | solution.py:325
  124.4 18.4 %collective-permute-start.19 = (bf16[4,128,1024]{2,1,0:T(8,128)(2,1)}, bf16[4,128,1024]{2,1,0:T(8,128)(2,1)}, u32[]{:S(2)}, u32[]{:S(2)}) collective-permute-start(bf16[4,128,1024]{2,1,0:T(8,128)(2,1)} %get-tuple-element.189), channel_id=1, source_target_pairs={{0,2},{1,5},{2,0},{3,7},{4,6},{5,1},{6,4},{7,3},{8,10},{9,13},{10,... | collective-permute-start | bytes 3145736 | tf_op jit(solution)/shard_map/ppermute | solution.py:325
  131.1 11.6 %collective-permute-start.17 = (f32[160,128]{1,0:T(8,128)S(1)}, f32[160,128]{1,0:T(8,128)S(1)}, u32[]{:S(2)}, u32[]{:S(2)}) collective-permute-start(f32[160,128]{1,0:T(8,128)S(1)} %get-tuple-element.198), channel_id=1, source_target_pairs={{0,16},{1,17},{2,18},{3,19},{4,20},{5,21},{6,22},{7,23},{8,24},{9,... | collective-permute-start | bytes 245768 | tf_op jit(solution)/shard_map/ppermute | solution.py:325
  148.0 30.4 %collective-permute-start.20 = (bf16[8,128,1024]{2,1,0:T(8,128)(2,1)S(1)}, bf16[8,128,1024]{2,1,0:T(8,128)(2,1)}, u32[]{:S(2)}, u32[]{:S(2)}) collective-permute-start(bf16[8,128,1024]{2,1,0:T(8,128)(2,1)S(1)} %bitcast.395), channel_id=1, source_target_pairs={{0,4},{1,3},{2,6},{3,1},{4,0},{5,7},{6,2},{7,5},{8,12},{9,11},{10,... | collective-permute-start | bytes 6291464 | tf_op jit(solution)/shard_map/ppermute | solution.py:325
  153.8 33.6 %collective-permute-start.21 = (bf16[8,128,1024]{2,1,0:T(8,128)(2,1)S(1)}, bf16[8,128,1024]{2,1,0:T(8,128)(2,1)}, u32[]{:S(2)}, u32[]{:S(2)}) collective-permute-start(bf16[8,128,1024]{2,1,0:T(8,128)(2,1)S(1)} %bitcast.396), channel_id=1, source_target_pairs={{0,1},{1,0},{2,3},{3,2},{4,5},{5,4},{6,7},{7,6},{8,9},{9,8},{10,11... | collective-permute-start | bytes 6291464 | tf_op jit(solution)/shard_map/ppermute | solution.py:325
  251.9 26.2 %collective-permute-start.24 = (bf16[2,4,128,1024]{3,2,1,0:T(8,128)(2,1)S(1)}, bf16[2,4,128,1024]{3,2,1,0:T(8,128)(2,1)}, u32[]{:S(2)}, u32[]{:S(2)}) collective-permute-start(bf16[2,4,128,1024]{3,2,1,0:T(8,128)(2,1)S(1)} %bitcast.432), channel_id=1, source_target_pairs={{0,4},{1,3},{2,6},{3,1},{4,0},{5,7},{6,2},{7,5},{8,12},{9,11},{10,... | collective-permute-start | bytes 6291464 | tf_op jit(solution)/shard_map/ppermute | solution.py:325
  264.1 31.5 %collective-permute-start.26 = (bf16[16,32,4096]{2,1,0:T(8,128)(2,1)}, bf16[16,32,4096]{2,1,0:T(8,128)(2,1)}, u32[]{:S(2)}, u32[]{:S(2)}) collective-permute-start(bf16[16,32,4096]{2,1,0:T(8,128)(2,1)} %get-tuple-element.109), channel_id=1, source_target_pairs={{0,1},{1,0},{2,3},{3,2},{4,5},{5,4},{6,7},{7,6},{8,9},{9,8},{10,11... | collective-permute-start | bytes 12582920 | tf_op jit(solution)/shard_map/ppermute | solution.py:325
  280.8 14.9 %collective-permute-start.25 = (bf16[4,128,1024]{2,1,0:T(8,128)(2,1)S(1)}, bf16[4,128,1024]{2,1,0:T(8,128)(2,1)S(1)}, u32[]{:S(2)}, u32[]{:S(2)}) collective-permute-start(bf16[4,128,1024]{2,1,0:T(8,128)(2,1)S(1)} %fusion.26), channel_id=1, source_target_pairs={{0,2},{1,5},{2,0},{3,7},{4,6},{5,1},{6,4},{7,3},{8,10},{9,13},{10,... | collective-permute-start | bytes 3145736 | tf_op jit(solution)/shard_map/ppermute | solution.py:325
  298.4 26.6 %collective-permute-start.28 = (bf16[2,4,32,4096]{3,2,1,0:T(8,128)(2,1)S(1)}, bf16[2,4,32,4096]{3,2,1,0:T(8,128)(2,1)S(1)}, u32[]{:S(2)}, u32[]{:S(2)}) collective-permute-start(bf16[2,4,32,4096]{3,2,1,0:T(8,128)(2,1)S(1)} %bitcast.433), channel_id=1, source_target_pairs={{0,4},{1,3},{2,6},{3,1},{4,0},{5,7},{6,2},{7,5},{8,12},{9,11},{10,... | collective-permute-start | bytes 6291464 | tf_op jit(solution)/shard_map/ppermute | solution.py:325
  302.0 23.0 %collective-permute-start.27 = (bf16[2,128,1024]{2,1,0:T(8,128)(2,1)S(1)}, bf16[2,128,1024]{2,1,0:T(8,128)(2,1)S(1)}, u32[]{:S(2)}, u32[]{:S(2)}) collective-permute-start(bf16[2,128,1024]{2,1,0:T(8,128)(2,1)S(1)} %fusion.51), channel_id=1, source_target_pairs={{0,8},{1,9},{2,10},{3,11},{4,12},{5,13},{6,14},{7,15},{8,0},{9,1},... | collective-permute-start | bytes 1572872 | tf_op jit(solution)/shard_map/ppermute | solution.py:325
  327.7 15.5 %collective-permute-start.30 = (bf16[4,32,4096]{2,1,0:T(8,128)(2,1)S(1)}, bf16[4,32,4096]{2,1,0:T(8,128)(2,1)S(1)}, u32[]{:S(2)}, u32[]{:S(2)}) collective-permute-start(bf16[4,32,4096]{2,1,0:T(8,128)(2,1)S(1)} %fusion.25), channel_id=1, source_target_pairs={{0,2},{1,5},{2,0},{3,7},{4,6},{5,1},{6,4},{7,3},{8,10},{9,13},{10,... | collective-permute-start | bytes 3145736 | tf_op jit(solution)/shard_map/ppermute | solution.py:325
  330.5 12.7 %collective-permute-start.29 = (bf16[1,128,1024]{2,1,0:T(8,128)(2,1)S(1)}, bf16[1,128,1024]{2,1,0:T(8,128)(2,1)S(1)}, u32[]{:S(2)}, u32[]{:S(2)}) collective-permute-start(bf16[1,128,1024]{2,1,0:T(8,128)(2,1)S(1)} %fusion.76), channel_id=1, source_target_pairs={{0,16},{1,17},{2,18},{3,19},{4,20},{5,21},{6,22},{7,23},{8,24},{9,... | collective-permute-start | bytes 786440 | tf_op jit(solution)/shard_map/ppermute | solution.py:325
  352.1 23.0 %collective-permute-start.32 = (bf16[16,32,4096]{2,1,0:T(8,128)(2,1)}, bf16[16,32,4096]{2,1,0:T(8,128)(2,1)}, u32[]{:S(2)}, u32[]{:S(2)}) collective-permute-start(bf16[16,32,4096]{2,1,0:T(8,128)(2,1)} %get-tuple-element.122), channel_id=1, source_target_pairs={{0,1},{1,0},{2,3},{3,2},{4,5},{5,4},{6,7},{7,6},{8,9},{9,8},{10,11... | collective-permute-start | bytes 12582920 | tf_op jit(solution)/shard_map/ppermute | solution.py:325
  360.7 14.4 %collective-permute-start.31 = (bf16[2,32,4096]{2,1,0:T(8,128)(2,1)S(1)}, bf16[2,32,4096]{2,1,0:T(8,128)(2,1)S(1)}, u32[]{:S(2)}, u32[]{:S(2)}) collective-permute-start(bf16[2,32,4096]{2,1,0:T(8,128)(2,1)S(1)} %fusion.49), channel_id=1, source_target_pairs={{0,8},{1,9},{2,10},{3,11},{4,12},{5,13},{6,14},{7,15},{8,0},{9,1},... | collective-permute-start | bytes 1572872 | tf_op jit(solution)/shard_map/ppermute | solution.py:325
  388.2 26.2 %collective-permute-start.34 = (bf16[2,4,32,4096]{3,2,1,0:T(8,128)(2,1)S(1)}, bf16[2,4,32,4096]{3,2,1,0:T(8,128)(2,1)}, u32[]{:S(2)}, u32[]{:S(2)}) collective-permute-start(bf16[2,4,32,4096]{3,2,1,0:T(8,128)(2,1)S(1)} %bitcast.431), channel_id=1, source_target_pairs={{0,4},{1,3},{2,6},{3,1},{4,0},{5,7},{6,2},{7,5},{8,12},{9,11},{10,... | collective-permute-start | bytes 6291464 | tf_op jit(solution)/shard_map/ppermute | solution.py:325
  393.0 17.5 %collective-permute-start.33 = (bf16[1,32,4096]{2,1,0:T(8,128)(2,1)}, bf16[1,32,4096]{2,1,0:T(8,128)(2,1)S(1)}, u32[]{:S(2)}, u32[]{:S(2)}) collective-permute-start(bf16[1,32,4096]{2,1,0:T(8,128)(2,1)} %fusion.73), channel_id=1, source_target_pairs={{0,16},{1,17},{2,18},{3,19},{4,20},{5,21},{6,22},{7,23},{8,24},{9,... | collective-permute-start | bytes 786440 | tf_op jit(solution)/shard_map/ppermute | solution.py:325
  419.3 14.9 %collective-permute-start.37 = (bf16[4,32,4096]{2,1,0:T(8,128)(2,1)S(1)}, bf16[4,32,4096]{2,1,0:T(8,128)(2,1)S(1)}, u32[]{:S(2)}, u32[]{:S(2)}) collective-permute-start(bf16[4,32,4096]{2,1,0:T(8,128)(2,1)S(1)} %fusion.24), channel_id=1, source_target_pairs={{0,2},{1,5},{2,0},{3,7},{4,6},{5,1},{6,4},{7,3},{8,10},{9,13},{10,... | collective-permute-start | bytes 3145736 | tf_op jit(solution)/shard_map/ppermute | solution.py:325
  443.2 10.1 %collective-permute-start.40 = (bf16[2,32,4096]{2,1,0:T(8,128)(2,1)S(1)}, bf16[2,32,4096]{2,1,0:T(8,128)(2,1)S(1)}, u32[]{:S(2)}, u32[]{:S(2)}) collective-permute-start(bf16[2,32,4096]{2,1,0:T(8,128)(2,1)S(1)} %fusion.47), channel_id=1, source_target_pairs={{0,8},{1,9},{2,10},{3,11},{4,12},{5,13},{6,14},{7,15},{8,0},{9,1},... | collective-permute-start | bytes 1572872 | tf_op jit(solution)/shard_map/ppermute | solution.py:325
  454.8 15.3 %collective-permute-start.42 = (bf16[1,32,4096]{2,1,0:T(8,128)(2,1)S(1)}, bf16[1,32,4096]{2,1,0:T(8,128)(2,1)}, u32[]{:S(2)}, u32[]{:S(2)}) collective-permute-start(bf16[1,32,4096]{2,1,0:T(8,128)(2,1)S(1)} %fusion.70), channel_id=1, source_target_pairs={{0,16},{1,17},{2,18},{3,19},{4,20},{5,21},{6,22},{7,23},{8,24},{9,... | collective-permute-start | bytes 786440 | tf_op jit(solution)/shard_map/ppermute | solution.py:325
  (119 other events, 841.0 us)
Sparse Core Ops, SparseCore 0:
  11.5 135.5 all-gather.2
  150.0 125.2 all-gather.4
